TPU v7x, 32 devices: a whole 2x2x4 slice. The times are simulated.
32 devices in a mesh: wide: 8 (over y, x, core), narrow: 4 (over z).
Axes of the slice: x: 2, y: 2, z: 4, core: 2. Of those that a mesh axis runs over, the one named last changes fastest.
Arguments:
- prior_states: bfloat16 [8, 2, 83, 8192], P('wide', None, None, 'narrow'), may hold values from -6 to 6
- target: bfloat16 [8, 83, 8192], P('wide', None, 'narrow'), may hold values from -6 to 6
- noise_draw: bfloat16 [8, 83, 8192], P('wide', None, 'narrow'), may hold values from -6 to 6
- level_index: int32 [8], P('wide'), may hold values from 0 to 7
- g2m_edges: int32 [8, 4096, 4], P('wide', 'narrow'), may hold values from 0 to 8191
- neighbours: int32 [8, 4096, 32], P('wide', 'narrow'), may hold values from 0 to 4095
- m2g_edges: int32 [8, 8192, 3], P('wide', 'narrow'), may hold values from 0 to 4095
- valid_mask: int32 [8, 8192], P('wide', 'narrow'), may hold values from 0 to 1, as said below
- channel_weights: float32 [83], replicated, may hold values from 0.25 to 2
- w_embed: float32 [249, 512], replicated, may hold values from -0.375 to 0.375
- w_cond: float32 [32, 2048], replicated, may hold values from -0.75 to 0.75
- w_attn: float32 [512, 2048], P(None, 'narrow'), may hold values from -0.375 to 0.375
- w_up: float32 [512, 2048], P(None, 'narrow'), may hold values from -0.25 to 0.25
- w_down: float32 [2048, 512], P('narrow'), may hold values from -0.125 to 0.125
- w_dec: float32 [512, 83], replicated, may hold values from -0.25 to 0.25
- biases: float32 [2643], replicated, may hold values from -0.75 to 0.75
- mom_attn: float32 [512, 2048], P(None, 'narrow'), may hold values from -0.00015258789 to 0.00015258789
- mom_up: float32 [512, 2048], P(None, 'narrow'), may hold values from -0.00015258789 to 0.00015258789
- mom_down: float32 [2048, 512], P('narrow'), may hold values from -0.00015258789 to 0.00015258789
- m_embed: float32 [249, 512], replicated, may hold values from -1.9073486e-05 to 1.9073486e-05
- v_embed: float32 [249, 512], replicated, may hold values from 5.910356e-12 to 4.7282848e-11
- m_cond: float32 [32, 2048], replicated, may hold values from -1.9073486e-05 to 1.9073486e-05
- v_cond: float32 [32, 2048], replicated, may hold values from 5.910356e-12 to 4.7282848e-11
- m_dec: float32 [512, 83], replicated, may hold values from -1.9073486e-05 to 1.9073486e-05
- v_dec: float32 [512, 83], replicated, may hold values from 5.910356e-12 to 4.7282848e-11
- m_bias: float32 [2643], replicated, may hold values from -5.340576e-05 to 5.340576e-05
- v_bias: float32 [2643], replicated, may hold values from 5.9103555e-11 to 4.7282844e-10
- ema_embed: float32 [249, 512], replicated, may hold values from -0.375 to 0.375
- ema_cond: float32 [32, 2048], replicated, may hold values from -0.75 to 0.75
- ema_attn: float32 [512, 2048], P(None, 'narrow'), may hold values from -0.375 to 0.375
- ema_up: float32 [512, 2048], P(None, 'narrow'), may hold values from -0.25 to 0.25
- ema_down: float32 [2048, 512], P('narrow'), may hold values from -0.125 to 0.125
- ema_dec: float32 [512, 83], replicated, may hold values from -0.25 to 0.25
- ema_bias: float32 [2643], replicated, may hold values from -0.75 to 0.75
Outputs:
- new_attn: float32 [512, 2048], P(None, 'narrow')
- new_up: float32 [512, 2048], P(None, 'narrow')
- new_down: float32 [2048, 512], P('narrow')
- moment_attn: float32 [512, 2048], P(None, 'narrow')
- moment_up: float32 [512, 2048], P(None, 'narrow')
- moment_down: float32 [2048, 512], P('narrow')
- new_embed: float32 [249, 512], replicated
- new_cond: float32 [32, 2048], replicated
- new_dec: float32 [512, 83], replicated
- new_bias: float32 [2643], replicated
- first_embed: float32 [249, 512], replicated
- second_embed: float32 [249, 512], replicated
- first_cond: float32 [32, 2048], replicated
- second_cond: float32 [32, 2048], replicated
- first_dec: float32 [512, 83], replicated
- second_dec: float32 [512, 83], replicated
- first_bias: float32 [2643], replicated
- second_bias: float32 [2643], replicated
- average_embed: float32 [249, 512], replicated
- average_cond: float32 [32, 2048], replicated
- average_attn: float32 [512, 2048], P(None, 'narrow')
- average_up: float32 [512, 2048], P(None, 'narrow')
- average_down: float32 [2048, 512], P('narrow')
- average_dec: float32 [512, 83], replicated
- average_bias: float32 [2643], replicated
- loss_sum: float32 [], replicated
- weight_total: float32 [], replicated
- grad_norm: float32 [], replicated
Inputs may be any that keep to these rules, and one draw needn't show every extreme that they name: `g2m_edges`: pixel numbers within the date. `neighbours`: node numbers within the date. `m2g_edges`: node numbers within the date. `valid_mask`: 1 where a pixel counts in the loss.
All inputs are finite; a program needn't handle non-finite values.
Results may differ from a plain program's by a relative error of at most 0.0062.
Values may be sent and summed in bfloat16 or wider, within the bound.
No kernel may reach another device: no remote copies, remote signals or barrier semaphores. Data moves between devices by JAX's collectives and lax.ppermute only.
A program may use at most 384 MiB of HBM per device.

v0:
```python
import math

import jax
import jax.numpy as jnp
from jax import lax
from jax.sharding import PartitionSpec as P

LATENT_WIDTH = 512
HEADS = 4
HEAD_WIDTH = 128
FF = 2048
COND = 32
NBR = 32
G2M_K = 4
M2G_K = 3
NS_ITERS = 5
SIGMA_LEVELS = 8
STEP_NUMBER = 10


highest_precision = lax.Precision.HIGHEST
sigma_low = 0.25
sigma_high = 4.0
clip_bound = 0.02
muon_rate = 0.5
muon_decay = 0.95
adam_rate = 0.03
beta_one = 0.9
beta_two = 0.95
adam_eps = 1e-08
decay_rate = 0.01
ema_keep = 0.9
coef_a = 3.4445
coef_b = -4.775
coef_c = 2.0315


def sigma_terms(level):
    fraction = level.astype(jnp.float32) / (SIGMA_LEVELS - 1)
    noise_level = sigma_low * (sigma_high / sigma_low) ** fraction
    square = noise_level * noise_level + 1.0
    scale_in = lax.rsqrt(square)
    return (
        noise_level,
        scale_in,
        1.0 / square,
        noise_level * scale_in,
        square / (noise_level * noise_level),
    )


def cond_features(noise_level):
    frequencies = 1.0 + jnp.arange(COND // 2).astype(jnp.float32)
    phases = jnp.log(noise_level) * frequencies
    return jnp.concatenate([jnp.sin(phases), jnp.cos(phases)])


def lat_weights(first_row, row_count, pixel_total):
    row_ids = (first_row + jnp.arange(row_count, dtype=jnp.int32)).astype(jnp.float32)
    return jnp.cos(math.pi * ((row_ids + 0.5) / pixel_total - 0.5))


def norm_stats(values):
    centred = values - jnp.mean(values, axis=-1, keepdims=True)
    inverse = lax.rsqrt(jnp.mean(centred * centred, axis=-1, keepdims=True) + 1e-05)
    return (centred * inverse, inverse)


def norm_back(grad_normed, normed, inverse):
    first_mean = jnp.mean(grad_normed, axis=-1, keepdims=True)
    second_mean = jnp.mean(grad_normed * normed, axis=-1, keepdims=True)
    return inverse * (grad_normed - first_mean - normed * second_mean)


def silu_slope(values):
    sigmoid_values = jax.nn.sigmoid(values)
    return sigmoid_values * (1.0 + values * (1.0 - sigmoid_values))


def contract_rows(left, right):
    return lax.dot_general(
        left, right, (((0,), (0,)), ((), ())), preferred_element_type=jnp.float32
    )


def contract_last(left, right):
    return lax.dot_general(
        left, right, (((1,), (1,)), ((), ())), preferred_element_type=jnp.float32
    )


def spread_rows(row_count, index_rows, grads):
    widened = jnp.broadcast_to(grads[:, None, :], index_rows.shape + (grads.shape[1],))
    return jnp.zeros((row_count, grads.shape[1]), jnp.float32).at[index_rows].add(widened)


def gram_sums(first_part, second_part, third_part):
    return lax.psum(
        (
            jnp.dot(first_part, first_part.T, precision=highest_precision),
            jnp.dot(second_part, second_part.T, precision=highest_precision),
            jnp.dot(third_part, third_part.T, precision=highest_precision),
        ),
        "narrow",
    )


def orthogonalize_shared(first_part, second_part, third_part):
    part_pieces = [first_part, second_part, third_part]
    gram_list = list(gram_sums(part_pieces[0], part_pieces[1], part_pieces[2]))
    scale_factors = [
        1.0 / (jnp.sqrt(jnp.trace(gram_product)) + 1e-07) for gram_product in gram_list
    ]
    part_pieces = [
        weight_matrix * scale_factor
        for weight_matrix, scale_factor in zip(part_pieces, scale_factors)
    ]
    gram_list = [
        gram_product * (scale_factor * scale_factor)
        for gram_product, scale_factor in zip(gram_list, scale_factors)
    ]
    for iteration in range(NS_ITERS):
        if iteration > 0:
            gram_list = list(gram_sums(part_pieces[0], part_pieces[1], part_pieces[2]))
        part_pieces = [
            coef_a * weight_matrix
            + jnp.dot(
                coef_b * gram_product
                + coef_c * jnp.dot(gram_product, gram_product, precision=highest_precision),
                weight_matrix,
                precision=highest_precision,
            )
            for weight_matrix, gram_product in zip(part_pieces, gram_list)
        ]
    return part_pieces


def adam_update(weight, grad, first, second):
    first_new = beta_one * first + (1.0 - beta_one) * grad
    second_new = beta_two * second + (1.0 - beta_two) * grad * grad
    first_hat = first_new / (1.0 - beta_one**STEP_NUMBER)
    second_hat = second_new / (1.0 - beta_two**STEP_NUMBER)
    weight_new = weight - adam_rate * (
        first_hat / (jnp.sqrt(second_hat) + adam_eps) + decay_rate * weight
    )
    return (weight_new, first_new, second_new)


def on_device(
    prior_states,
    target,
    noise_draw,
    level_index,
    g2m_edges,
    neighbours,
    m2g_edges,
    valid_mask,
    channel_weights,
    w_embed,
    w_cond,
    w_attn,
    w_up,
    w_down,
    w_dec,
    biases,
    mom_attn,
    mom_up,
    mom_down,
    m_embed,
    v_embed,
    m_cond,
    v_cond,
    m_dec,
    v_dec,
    m_bias,
    v_bias,
    ema_embed,
    ema_cond,
    ema_attn,
    ema_up,
    ema_down,
    ema_dec,
    ema_bias,
):
    narrow_pos = lax.axis_index("narrow")
    narrow_count = lax.axis_size("narrow")
    pixel_local = valid_mask.shape[1]
    node_local = neighbours.shape[1]
    pixel_total = pixel_local * narrow_count
    node_total = node_local * narrow_count
    lat_weight = lat_weights(narrow_pos * pixel_local, pixel_local, pixel_total)
    pixel_weight = lat_weight * valid_mask[0].astype(jnp.float32)
    weight_total = lax.psum(jnp.sum(pixel_weight), ("wide", "narrow"))
    attn_full, up_full, down_full = (
        lax.all_gather(w_attn.astype(jnp.bfloat16), "narrow", axis=1, tiled=True),
        lax.all_gather(w_up.astype(jnp.bfloat16), "narrow", axis=1, tiled=True),
        lax.all_gather(w_down.astype(jnp.bfloat16), "narrow", axis=0, tiled=True),
    )
    embed_low = w_embed.astype(jnp.bfloat16)
    dec_low = w_dec.astype(jnp.bfloat16)
    bias_embed = biases[:LATENT_WIDTH]
    bias_up = biases[LATENT_WIDTH : LATENT_WIDTH + FF]
    bias_out = biases[LATENT_WIDTH + FF :]
    noise_level, scale_in, skip_scale, out_scale, loss_scale = sigma_terms(level_index[0])
    target_rows = target[0].astype(jnp.float32)
    noisy = target_rows + noise_level * noise_draw[0].astype(jnp.float32)
    features = jnp.concatenate(
        [prior_states[0, 0], prior_states[0, 1], (scale_in * noisy).astype(jnp.bfloat16)], axis=0
    )
    embed_pre = contract_rows(features, embed_low) + bias_embed
    embedded = jax.nn.silu(embed_pre).astype(jnp.bfloat16)
    pixel_rows = lax.all_gather(embedded, "narrow", axis=0, tiled=True)
    node_in = jnp.sum(pixel_rows[g2m_edges[0]].astype(jnp.float32), axis=1) / G2M_K
    conditioning = cond_features(noise_level)
    modulation = jnp.dot(conditioning, w_cond, precision=highest_precision)
    normed_one, inverse_one = norm_stats(node_in)
    attn_in = (
        normed_one * (1.0 + modulation[:LATENT_WIDTH]) + modulation[LATENT_WIDTH : 2 * LATENT_WIDTH]
    ).astype(jnp.bfloat16)
    qkv_rows = jnp.dot(
        attn_in, attn_full[:, : 3 * LATENT_WIDTH], preferred_element_type=jnp.float32
    ).astype(jnp.bfloat16)
    query_rows = qkv_rows[:, :LATENT_WIDTH].reshape(node_local, HEADS, HEAD_WIDTH)
    key_rows, value_rows = (
        lax.all_gather(qkv_rows[:, LATENT_WIDTH : 2 * LATENT_WIDTH], "narrow", axis=0, tiled=True),
        lax.all_gather(qkv_rows[:, 2 * LATENT_WIDTH :], "narrow", axis=0, tiled=True),
    )
    neighbour_key_rows = key_rows[neighbours[0]].reshape(node_local, NBR, HEADS, HEAD_WIDTH)
    neighbour_value_rows = value_rows[neighbours[0]].reshape(node_local, NBR, HEADS, HEAD_WIDTH)
    attention_scores = jnp.einsum(
        "tzp,tvzp->tzv", query_rows, neighbour_key_rows, preferred_element_type=jnp.float32
    ) / math.sqrt(HEAD_WIDTH)
    softmax_weights = jax.nn.softmax(attention_scores, axis=-1)
    softmax_lowered = softmax_weights.astype(jnp.bfloat16)
    attended_rows = jnp.einsum(
        "ika,iakv->ikv", softmax_lowered, neighbour_value_rows, preferred_element_type=jnp.float32
    )
    attended_rows = attended_rows.reshape(node_local, LATENT_WIDTH).astype(jnp.bfloat16)
    node_mid = node_in + jnp.dot(
        attended_rows, attn_full[:, 3 * LATENT_WIDTH :], preferred_element_type=jnp.float32
    )
    normed_two, inverse_two = norm_stats(node_mid)
    mlp_in = (
        normed_two * (1.0 + modulation[2 * LATENT_WIDTH : 3 * LATENT_WIDTH])
        + modulation[3 * LATENT_WIDTH :]
    ).astype(jnp.bfloat16)
    up_pre = jnp.dot(mlp_in, up_full, preferred_element_type=jnp.float32) + bias_up
    hidden = jax.nn.silu(up_pre).astype(jnp.bfloat16)
    node_out = node_mid + jnp.dot(hidden, down_full, preferred_element_type=jnp.float32)
    node_rows = lax.all_gather(node_out.astype(jnp.bfloat16), "narrow", axis=0, tiled=True)
    decoded = (jnp.sum(node_rows[m2g_edges[0]].astype(jnp.float32), axis=1) / M2G_K).astype(
        jnp.bfloat16
    )
    raw_output = lax.dot_general(
        dec_low, decoded, (((0,), (1,)), ((), ())), preferred_element_type=jnp.float32
    )
    raw_output = raw_output + bias_out[:, None]
    errors = skip_scale * noisy + out_scale * raw_output - target_rows
    weighted = channel_weights[:, None] * pixel_weight[None, :]
    loss_local = loss_scale * jnp.sum(weighted * errors * errors)
    grad_raw = (2.0 * loss_scale * out_scale / weight_total * weighted * errors).astype(
        jnp.bfloat16
    )
    grad_out_bias = jnp.sum(grad_raw.astype(jnp.float32), axis=1)
    grad_dec = lax.dot_general(
        decoded, grad_raw, (((0,), (1,)), ((), ())), preferred_element_type=jnp.float32
    )
    grad_decoded = lax.dot_general(
        grad_raw, dec_low, (((0,), (1,)), ((), ())), preferred_element_type=jnp.float32
    )
    node_spread = spread_rows(node_total, m2g_edges[0], grad_decoded / M2G_K)
    grad_node_out = lax.psum_scatter(node_spread, "narrow", scatter_dimension=0, tiled=True)
    grad_mlp = grad_node_out.astype(jnp.bfloat16)
    grad_down = contract_rows(hidden, grad_mlp)
    grad_hidden = contract_last(grad_mlp, down_full)
    grad_up_pre = (grad_hidden * silu_slope(up_pre)).astype(jnp.bfloat16)
    grad_up_bias = jnp.sum(grad_up_pre.astype(jnp.float32), axis=0)
    grad_up = contract_rows(mlp_in, grad_up_pre)
    grad_mlp_in = contract_last(grad_up_pre, up_full)
    grad_node_mid = grad_node_out + norm_back(
        grad_mlp_in * (1.0 + modulation[2 * LATENT_WIDTH : 3 * LATENT_WIDTH]),
        normed_two,
        inverse_two,
    )
    grad_proj_out = grad_node_mid.astype(jnp.bfloat16)
    grad_proj = contract_rows(attended_rows, grad_proj_out)
    gradient_attended = (
        contract_last(grad_proj_out, attn_full[:, 3 * LATENT_WIDTH :])
        .astype(jnp.bfloat16)
        .reshape(node_local, HEADS, HEAD_WIDTH)
    )
    grad_soft = jnp.einsum(
        "tzp,tvzp->tzv", gradient_attended, neighbour_value_rows, preferred_element_type=jnp.float32
    )
    grad_near_values = jnp.einsum(
        "vwg,vwl->vgwl", softmax_lowered, gradient_attended, preferred_element_type=jnp.float32
    )
    gradient_scores = softmax_weights * (
        grad_soft - jnp.sum(softmax_weights * grad_soft, axis=-1, keepdims=True)
    )
    gradient_scores = gradient_scores.astype(jnp.bfloat16)
    grad_queries = jnp.einsum(
        "ika,iakv->ikv", gradient_scores, neighbour_key_rows, preferred_element_type=jnp.float32
    ) / math.sqrt(HEAD_WIDTH)
    grad_near_keys = jnp.einsum(
        "vwg,vwl->vgwl", gradient_scores, query_rows, preferred_element_type=jnp.float32
    ) / math.sqrt(HEAD_WIDTH)
    widened_ids = neighbours[0]
    key_spread = (
        jnp.zeros((node_total, LATENT_WIDTH), jnp.float32)
        .at[widened_ids]
        .add(grad_near_keys.reshape(node_local, NBR, LATENT_WIDTH))
    )
    value_spread = (
        jnp.zeros((node_total, LATENT_WIDTH), jnp.float32)
        .at[widened_ids]
        .add(grad_near_values.reshape(node_local, NBR, LATENT_WIDTH))
    )
    grad_key_rows, grad_value_rows = (
        lax.psum_scatter(key_spread, "narrow", scatter_dimension=0, tiled=True),
        lax.psum_scatter(value_spread, "narrow", scatter_dimension=0, tiled=True),
    )
    grad_qkv_rows = jnp.concatenate(
        [grad_queries.reshape(node_local, LATENT_WIDTH), grad_key_rows, grad_value_rows], axis=1
    )
    grad_qkv_rows = grad_qkv_rows.astype(jnp.bfloat16)
    grad_qkv = contract_rows(attn_in, grad_qkv_rows)
    grad_attn_in = contract_last(grad_qkv_rows, attn_full[:, : 3 * LATENT_WIDTH])
    grad_node_in = grad_node_mid + norm_back(
        grad_attn_in * (1.0 + modulation[:LATENT_WIDTH]), normed_one, inverse_one
    )
    grad_modulation = jnp.concatenate(
        [
            jnp.sum(grad_attn_in * normed_one, axis=0),
            jnp.sum(grad_attn_in, axis=0),
            jnp.sum(grad_mlp_in * normed_two, axis=0),
            jnp.sum(grad_mlp_in, axis=0),
        ]
    )
    grad_cond = conditioning[:, None] * grad_modulation[None, :]
    pixel_spread = spread_rows(pixel_total, g2m_edges[0], grad_node_in / G2M_K)
    grad_embedded = lax.psum_scatter(pixel_spread, "narrow", scatter_dimension=0, tiled=True)
    grad_embed_pre = (grad_embedded * silu_slope(embed_pre)).astype(jnp.bfloat16)
    grad_embed_bias = jnp.sum(grad_embed_pre.astype(jnp.float32), axis=0)
    grad_embed = lax.dot_general(
        features, grad_embed_pre, (((1,), (0,)), ((), ())), preferred_element_type=jnp.float32
    )
    grad_attn = jnp.concatenate([grad_qkv, grad_proj], axis=1)
    grad_bias = jnp.concatenate([grad_embed_bias, grad_up_bias, grad_out_bias])
    attn_cols = w_attn.shape[1]
    up_cols = w_up.shape[1]
    down_rows = w_down.shape[0]
    summed = lax.psum(
        (grad_embed, grad_cond, grad_attn, grad_up, grad_down, grad_dec, grad_bias, loss_local),
        ("wide", "narrow"),
    )
    sum_embed, sum_cond, sum_attn, sum_up, sum_down, sum_dec, sum_bias, loss_sum = summed
    square_sum = (
        jnp.sum(sum_embed * sum_embed)
        + jnp.sum(sum_cond * sum_cond)
        + jnp.sum(sum_attn * sum_attn)
        + jnp.sum(sum_up * sum_up)
        + jnp.sum(sum_down * sum_down)
        + jnp.sum(sum_dec * sum_dec)
        + jnp.sum(sum_bias * sum_bias)
    )
    attn_share = lax.dynamic_slice_in_dim(sum_attn, narrow_pos * attn_cols, attn_cols, 1)
    up_share = lax.dynamic_slice_in_dim(sum_up, narrow_pos * up_cols, up_cols, 1)
    down_share = lax.dynamic_slice_in_dim(sum_down, narrow_pos * down_rows, down_rows, 0)
    grad_norm = jnp.sqrt(square_sum)
    factor = jnp.minimum(1.0, clip_bound / (grad_norm + 1e-06))
    moment_attn = muon_decay * mom_attn + factor * attn_share
    moment_up = muon_decay * mom_up + factor * up_share
    moment_down = muon_decay * mom_down + factor * down_share
    attn_orth, up_orth, down_orth = orthogonalize_shared(moment_attn, moment_up, moment_down.T)
    new_attn = (
        w_attn - muon_rate * math.sqrt(max(1.0, LATENT_WIDTH / (4 * LATENT_WIDTH))) * attn_orth
    )
    new_up = w_up - muon_rate * math.sqrt(max(1.0, LATENT_WIDTH / FF)) * up_orth
    new_down = w_down - muon_rate * math.sqrt(max(1.0, FF / LATENT_WIDTH)) * down_orth.T
    new_embed, first_embed, second_embed = adam_update(
        w_embed, factor * sum_embed, m_embed, v_embed
    )
    new_cond, first_cond, second_cond = adam_update(w_cond, factor * sum_cond, m_cond, v_cond)
    new_dec, first_dec, second_dec = adam_update(w_dec, factor * sum_dec, m_dec, v_dec)
    new_bias, first_bias, second_bias = adam_update(biases, factor * sum_bias, m_bias, v_bias)
    keep_rest = 1.0 - ema_keep
    return (
        new_attn,
        new_up,
        new_down,
        moment_attn,
        moment_up,
        moment_down,
        new_embed,
        new_cond,
        new_dec,
        new_bias,
        first_embed,
        second_embed,
        first_cond,
        second_cond,
        first_dec,
        second_dec,
        first_bias,
        second_bias,
        ema_keep * ema_embed + keep_rest * new_embed,
        ema_keep * ema_cond + keep_rest * new_cond,
        ema_keep * ema_attn + keep_rest * new_attn,
        ema_keep * ema_up + keep_rest * new_up,
        ema_keep * ema_down + keep_rest * new_down,
        ema_keep * ema_dec + keep_rest * new_dec,
        ema_keep * ema_bias + keep_rest * new_bias,
        loss_sum,
        weight_total,
        grad_norm,
    )


def solution(mesh):
    in_specs = (
        P("wide", None, None, "narrow"),
        P("wide", None, "narrow"),
        P("wide", None, "narrow"),
        P("wide"),
        P("wide", "narrow", None),
        P("wide", "narrow", None),
        P("wide", "narrow", None),
        P("wide", "narrow"),
        P(),
        P(),
        P(),
        P(None, "narrow"),
        P(None, "narrow"),
        P("narrow", None),
        P(),
        P(),
        P(None, "narrow"),
        P(None, "narrow"),
        P("narrow", None),
        P(),
        P(),
        P(),
        P(),
        P(),
        P(),
        P(),
        P(),
        P(),
        P(),
        P(None, "narrow"),
        P(None, "narrow"),
        P("narrow", None),
        P(),
        P(),
    )
    out_specs = (
        P(None, "narrow"),
        P(None, "narrow"),
        P("narrow", None),
        P(None, "narrow"),
        P(None, "narrow"),
        P("narrow", None),
        P(),
        P(),
        P(),
        P(),
        P(),
        P(),
        P(),
        P(),
        P(),
        P(),
        P(),
        P(),
        P(),
        P(),
        P(None, "narrow"),
        P(None, "narrow"),
        P("narrow", None),
        P(),
        P(),
        P(),
        P(),
        P(),
    )
    return jax.shard_map(
        on_device, mesh=mesh, in_specs=in_specs, out_specs=out_specs, check_vma=False
    )
```

profile of v0, /device:TPU:0, one launch (start us, length us, event | category | flops | bytes accessed | tf_op | source)
XLA Modules:
  0.0 3294.9 jit_solution(6916876713721533525)
XLA Ops:
  18.7 149.7 %all-gather.8.cloned.1.call-done = bf16[8192,512]{1,0:T(8,128)(2,1)} async-done(((bf16[2048,512]{1,0:T(8,128)(2,1)}), bf16[8192,512]{1,0:T(8,128)(2,1)}) %all-gather.8.cloned.1.call-update) | async-done | bytes 8388624 | tf_op jit(solution)/shard_map/all_gather | solution.py:212
  168.5 21.8 gather_fusion
  190.3 8.5 reshape.344
  198.8 9.7 reduce_sum.275
  228.3 71.3 %all-gather.12.cloned.1.call-done = bf16[4096,512]{1,0:T(8,128)(2,1)} async-done(((bf16[1024,512]{1,0:T(8,128)(2,1)}), bf16[4096,512]{1,0:T(8,128)(2,1)}) %all-gather.12.cloned.1.call-update) | async-done | bytes 4194320 | tf_op jit(solution)/shard_map/all_gather | solution.py:225
  299.6 134.8 %gather_fusion.1 = bf16[32768,512]{1,0:T(8,128)(2,1)} fusion(bf16[4096,512]{1,0:T(8,128)(2,1)} %all-gather.12.cloned.1.call-done, s32[32768]{0:T(1024)S(1)} %broadcast_clamp_fusion), kind=kCustom, calls=%fused_computation.1 | custom fusion | bytes 67239936 | tf_op jit(solution)/shard_map/gather | solution.py:228
  434.4 46.2 %reshape.259 = bf16[1024,32,4,128]{3,2,1,0:T(4,128)(2,1)} reshape(bf16[32768,512]{1,0:T(8,128)(2,1)} %gather_fusion.1) | data formatting | bytes 67108864 | tf_op jit(solution)/shard_map/reshape | solution.py:228
  480.6 21.3 fusion.13
  501.9 12.0 copy.188
  513.9 20.0 fusion.19
  533.9 15.7 convert_convert_fusion
  549.7 16.9 copy.189
  566.6 134.8 %gather_fusion.2 = bf16[32768,512]{1,0:T(8,128)(2,1)} fusion(bf16[4096,512]{1,0:T(8,128)(2,1)} %all-gather.14.cloned.1.call-done, s32[32768]{0:T(1024)S(1)} %broadcast_clamp_fusion), kind=kCustom, calls=%fused_computation.2 | custom fusion | bytes 67239936 | tf_op jit(solution)/shard_map/gather | solution.py:229
  701.4 46.2 %reshape.260 = bf16[1024,32,4,128]{3,2,1,0:T(4,128)(2,1)} reshape(bf16[32768,512]{1,0:T(8,128)(2,1)} %gather_fusion.2) | data formatting | bytes 67108864 | tf_op jit(solution)/shard_map/reshape | solution.py:229
  747.6 15.0 fusion.9
  766.8 8.6 multiply_convert_fusion.2
  782.4 44.4 %psum.168 = f32[]{:T(128)} all-reduce(f32[]{:T(128)} %multiply_reduce_fusion.18), channel_id=1, replica_groups=mesh['wide'=8,'narrow'=4] {'wide','narrow'}, use_global_device_ids=true, to_apply=%region_1.0 | all-reduce | flops 1 | bytes 8 | tf_op jit(solution)/shard_map/psum | solution.py:193
  829.7 32.5 all-gather.20.cloned.1.call-done
  862.1 6.5 copy.151
  868.6 28.3 gather_fusion.3
  896.9 18.1 reshape.345
  915.0 16.2 reduce_sum.281
  936.5 7.5 broadcast_in_dim.12
  944.0 19.7 reshape.304
  963.8 40.9 %scatter_custom_fusion = f32[4096,512]{1,0:T(8,128)} fusion(s32[6144]{0:T(1024)S(1)} %reshape.302, f32[6144,512]{1,0:T(8,128)} %reshape.304, f32[]{:T(128)} %constant.46.clone.1), kind=kCustom, calls=%fused_computation.53 | custom fusion | flops 3145728 | bytes 8389120 | tf_op jit(solution)/shard_map/scatter-add | solution.py:94
  1004.7 9.1 copy.152
  1013.9 143.0 %reduce-scatter.5.cloned.1.call-done = f32[1024,512]{0,1:T(8,128)} async-done(((f32[4096,512]{0,1:T(8,128)}), f32[1024,512]{0,1:T(8,128)}) %reduce-scatter.5.cloned.1.call-update) | async-done | bytes 2097168 | tf_op jit(solution)/shard_map/reduce_scatter | solution.py:272
  1156.9 8.5 convert_reduce_fusion
  1180.1 85.4 %multiply_reduce_fusion = (f32[1024,4,32]{1,2,0:T(8,128)}, f32[1024,4,128,32]{2,1,3,0:T(4,128)}) fusion(f32[1024,4,128]{2,1,0:T(4,128)S(1)} %copy.210, bf16[1024,32,4,128]{3,2,1,0:T(4,128)(2,1)} %reshape.260, f32[1024,4,32]{1,2,0:T(8,128)} %get-tuple-element.161), kind=kLoop, calls=%fused_computation.17 | loop fusion | flops 66977792 | bytes 103809024 | tf_op jit(solution)/shard_map/tzp,tvzp->tzv/dot_general | solution.py:292
  1265.5 214.0 %scatter_custom_fusion.2 = f32[4096,512]{1,0:T(8,128)} fusion(s32[32768]{0:T(1024)} %copy-done.80, f32[4096,8,4,128]{3,2,1,0:T(4,128)} %bitcast.42, f32[]{:T(128)} %constant.46.clone.1), kind=kCustom, calls=%fused_computation.11 | custom fusion | flops 16777216 | bytes 75497984 | tf_op jit(solution)/shard_map/scatter-add | solution.py:317
  1481.2 33.1 %fusion.125 = (f32[1024,4,32]{1,2,0:T(8,128)}, bf16[1024,4,32]{1,2,0:T(8,128)(2,1)}) fusion(f32[1024,4,32]{1,2,0:T(8,128)} %fusion.19, f32[1024,4,32]{1,2,0:T(8,128)} %get-tuple-element.166), kind=kOutput, calls=%fused_computation.268 | output fusion | flops 659487 | bytes 1835008 | tf_op jit(solution)/shard_map/sub | solution.py:299
  1514.3 42.4 %multiply_multiply_fusion = f32[1024,4,128,32]{2,1,3,0:T(4,128)} fusion(f32[1024,4,32]{1,2,0:T(8,128)} %get-tuple-element.181, f32[1024,4,128]{2,1,0:T(4,128)S(1)} %convert.24), kind=kLoop, calls=%fused_computation.18 | loop fusion | flops 33554432 | bytes 69730304 | tf_op jit(solution)/shard_map/div | solution.py:305
  1556.7 213.7 %scatter_custom_fusion.1 = f32[4096,512]{1,0:T(8,128)} fusion(s32[32768]{0:T(1024)} %copy-done.80, f32[4096,8,4,128]{3,2,1,0:T(4,128)} %bitcast.39, f32[]{:T(128)} %constant.46.clone.1), kind=kCustom, calls=%fused_computation.14 | custom fusion | flops 16777216 | bytes 75497984 | tf_op jit(solution)/shard_map/scatter-add | solution.py:312
  1770.4 17.1 copy.198
  1787.5 14.6 fusion.11
  1805.1 110.7 %reduce-scatter.7.cloned.1.call-done = f32[1024,512]{1,0:T(8,128)} async-done(((f32[4096,512]{1,0:T(8,128)}), f32[1024,512]{1,0:T(8,128)}) %reduce-scatter.7.cloned.1.call-update) | async-done | bytes 2097168 | tf_op jit(solution)/shard_map/reduce_scatter | solution.py:320
  1933.4 6.3 broadcast_in_dim.13
  1939.7 10.0 reshape.328
  1949.8 32.2 scatter_custom_fusion.3
  1987.3 7.5 fusion.87
  2004.8 258.4 %reduce-scatter.11.cloned.1.call-done = f32[2048,512]{1,0:T(8,128)} async-done(((f32[8192,512]{1,0:T(8,128)}), f32[2048,512]{1,0:T(8,128)}) %reduce-scatter.11.cloned.1.call-update) | async-done | bytes 4194320 | tf_op jit(solution)/shard_map/reduce_scatter | solution.py:342
  2276.3 43.1 %all-reduce = (f32[2643]{0:T(1024)S(1)}, f32[]{:T(128)}) all-reduce(f32[2643]{0:T(1024)S(1)} %pad_maximum_fusion.7, f32[]{:T(128)S(6)} %mul.908), channel_id=1, replica_groups=mesh['wide'=8,'narrow'=4] {'wide','narrow'}, use_global_device_ids=true, to_apply=%region_42.43 | all-reduce | flops 2644 | bytes 21152 | tf_op jit(solution)/shard_map/psum | solution.py:353
  2320.0 199.3 %all-reduce.14.cloned.1.call-done = (f32[512,2048]{1,0:T(8,128)}, f32[249,512]{1,0:T(8,128)}, f32[32,2048]{1,0:T(8,128)}, f32[512,2048]{0,1:T(8,128)}, f32[2048,512]{0,1:T(8,128)}, /*index=5*/f32[512,83]{0,1:T(8,128)}) async-done(((f32[512,2048]{1,0:T(8,128)}, f32[249,512]{1,0:T(8,128)}, f32[32,2048]{1,0:T(8,128)}, f32[512,2048]{0,1:T(8,128)}, f32[2048,512]{0,1:T(8,128)}, /*index=5*/f32[512,83]{0,1:T(8,128)}), ...) | async-done | bytes 13525008 | tf_op jit(solution)/shard_map/psum | solution.py:353
  2549.3 121.3 %all-reduce.24.cloned.1.call-done = (f32[512,512]{1,0:T(8,128)}, f32[512,512]{1,0:T(8,128)}, f32[512,512]{1,0:T(8,128)}) async-done(((f32[512,512]{1,0:T(8,128)}, f32[512,512]{1,0:T(8,128)}, f32[512,512]{1,0:T(8,128)}), (f32[512,512]{1,0:T(8,128)}, f32[512,512]{1,0:T(8,128)}, f32[512,512]{1,0:T(8,128)})) %all-reduce.24.cloned.1.call-update) | async-done | bytes 3145744 | tf_op jit(solution)/shard_map/psum | solution.py:98
  2706.9 120.9 %all-reduce.22.cloned.1.call-done = (f32[512,512]{1,0:T(8,128)}, f32[512,512]{1,0:T(8,128)}, f32[512,512]{1,0:T(8,128)}) async-done(((f32[512,512]{1,0:T(8,128)}, f32[512,512]{1,0:T(8,128)}, f32[512,512]{1,0:T(8,128)}), (f32[512,512]{1,0:T(8,128)}, f32[512,512]{1,0:T(8,128)}, f32[512,512]{1,0:T(8,128)})) %all-reduce.22.cloned.1.call-update) | async-done | bytes 3145744 | tf_op jit(solution)/shard_map/psum | solution.py:98
  2851.0 120.9 %all-reduce.20.cloned.1.call-done = (f32[512,512]{1,0:T(8,128)}, f32[512,512]{1,0:T(8,128)}, f32[512,512]{1,0:T(8,128)}) async-done(((f32[512,512]{1,0:T(8,128)}, f32[512,512]{1,0:T(8,128)}, f32[512,512]{1,0:T(8,128)}), (f32[512,512]{1,0:T(8,128)}, f32[512,512]{1,0:T(8,128)}, f32[512,512]{1,0:T(8,128)})) %all-reduce.20.cloned.1.call-update) | async-done | bytes 3145744 | tf_op jit(solution)/shard_map/psum | solution.py:98
  2995.5 120.9 %all-reduce.18.cloned.1.call-done = (f32[512,512]{1,0:T(8,128)}, f32[512,512]{1,0:T(8,128)}, f32[512,512]{1,0:T(8,128)}) async-done(((f32[512,512]{1,0:T(8,128)}, f32[512,512]{1,0:T(8,128)}, f32[512,512]{1,0:T(8,128)}), (f32[512,512]{1,0:T(8,128)}, f32[512,512]{1,0:T(8,128)}, f32[512,512]{1,0:T(8,128)})) %all-reduce.18.cloned.1.call-update) | async-done | bytes 3145744 | tf_op jit(solution)/shard_map/psum | solution.py:98
  3155.9 105.1 %all-reduce.16.cloned.1.call-done = (f32[512,512]{1,0:T(8,128)}, f32[512,512]{1,0:T(8,128)}, f32[512,512]{1,0:T(8,128)}) async-done(((f32[512,512]{1,0:T(8,128)}, f32[512,512]{1,0:T(8,128)}, f32[512,512]{1,0:T(8,128)}), (f32[512,512]{1,0:T(8,128)}, f32[512,512]{1,0:T(8,128)}, f32[512,512]{1,0:T(8,128)})) %all-reduce.16.cloned.1.call-update) | async-done | bytes 3145744 | tf_op jit(solution)/shard_map/psum | solution.py:98
  (444 shorter events, 284.4 us)
Async XLA Ops:
  7.2 161.2 %all-gather.8.cloned.1.call-start = ((), (), s32[]{:S(2)}) async-start(), calls=%async_computation.4 | async-start | bytes 10485760 | tf_op jit(solution)/shard_map/all_gather | solution.py:212
  16.0 198.8 %all-gather.10.cloned.1.call-start = ((), (), s32[]{:S(2)}) async-start(), calls=%async_computation.5 | async-start | bytes 2621440 | tf_op jit(solution)/shard_map/all_gather | solution.py:195
  16.9 282.7 %all-gather.12.cloned.1.call-start = ((), (), s32[]{:S(2)}) async-start(), calls=%async_computation.6 | async-start | bytes 5242880 | tf_op jit(solution)/shard_map/all_gather | solution.py:225
  17.7 172.6 %copy-start.95 = (s32[4096]{0:T(1024)}, s32[4096]{0:T(1024)S(1)}, u32[]{:S(2)}) copy-start(s32[4096]{0:T(1024)S(1)} %reshape.326) | copy-start | bytes 49156
  17.9 172.4 %copy-start.116 = (f32[32]{0:T(128)}, f32[32]{0:T(128)S(1)}, u32[]{:S(2)}) copy-start(f32[32]{0:T(128)S(1)} %pad_maximum_fusion.9) | copy-start | bytes 388
  18.7 196.1 %copy-start.104 = (f32[512]{0:T(512)}, f32[512]{0:T(512)S(1)}, u32[]{:S(2)}) copy-start(f32[512]{0:T(512)S(1)} %get-tuple-element.174) | copy-start | bytes 6148
  18.7 196.1 %copy-start.119 = (f32[512]{0:T(512)}, f32[512]{0:T(512)S(1)}, u32[]{:S(2)}) copy-start(f32[512]{0:T(512)S(1)} %get-tuple-element.173) | copy-start | bytes 6148
  219.9 8.4 copy-start.30
  219.9 346.7 %all-gather.14.cloned.1.call-start = ((), (), s32[]{:S(2)}) async-start(), calls=%async_computation.7 | async-start | bytes 5242880 | tf_op jit(solution)/shard_map/all_gather | solution.py:226
  220.5 546.2 %all-gather.16.cloned.1.call-start = ((), (), s32[]{:S(2)}) async-start(), calls=%async_computation.8 | async-start | bytes 2621440 | tf_op jit(solution)/shard_map/all_gather | solution.py:196
  222.8 552.7 %all-gather.18.cloned.1.call-start = ((), (), s32[]{:S(2)}) async-start(), calls=%async_computation.9 | async-start | bytes 2621440 | tf_op jit(solution)/shard_map/all_gather | solution.py:197
  223.7 638.4 %all-gather.20.cloned.1.call-start = ((), (), s32[]{:S(2)}) async-start(), calls=%async_computation.10 | async-start | bytes 5242880 | tf_op jit(solution)/shard_map/all_gather | solution.py:250
  225.0 209.4 %copy-start.80 = (s32[32768]{0:T(1024)}, s32[32768]{0:T(1024)S(1)}, u32[]{:S(2)}) copy-start(s32[32768]{0:T(1024)S(1)} %reshape.278) | copy-start | bytes 393220
  766.4 409.3 %copy-start.6 = (f32[1024,512]{0,1:T(8,128)}, f32[1024,512]{0,1:T(8,128)S(1)}, u32[]{:S(2)}) copy-start(f32[1024,512]{0,1:T(8,128)S(1)} %get-tuple-element.178) | copy-start | bytes 6291460
  766.4 409.3 %copy-start.93 = (f32[1024]{0:T(1024)}, f32[1024]{0:T(1024)S(1)}, u32[]{:S(2)}) copy-start(f32[1024]{0:T(1024)S(1)} %broadcast_multiply_fusion.7) | copy-start | bytes 12292
  766.7 409.0 %copy-start.100 = (f32[1024]{0:T(1024)}, f32[1024]{0:T(1024)S(1)}, u32[]{:S(2)}) copy-start(f32[1024]{0:T(1024)S(1)} %add_rsqrt_fusion) | copy-start | bytes 12292
  775.4 52.2 %copy-start.103 = (s32[1,2048,3]{1,0,2:T(1,128)S(1)}, s32[1,2048,3]{1,0,2:T(1,128)}, u32[]{:S(2)}) copy-start(s32[1,2048,3]{1,0,2:T(1,128)} %param.40) | copy-start | bytes 73732
  781.7 375.2 %reduce-scatter.5.cloned.1.call-start = ((), (), s32[]{:S(2)}) async-start(), calls=%async_computation.11 | async-start | bytes 10485760 | tf_op jit(solution)/shard_map/reduce_scatter | solution.py:272
  915.0 16.2 copy-start.59
  915.0 16.2 copy-start.62
  915.0 16.2 copy-start.64
  915.0 16.2 copy-start.124
  1013.8 789.1 %reduce-scatter.9.cloned.1.call-start = ((), (), s32[]{:S(2)}) async-start(), calls=%async_computation.13 | async-start | bytes 10485760 | tf_op jit(solution)/shard_map/reduce_scatter | solution.py:321
  1156.9 8.5 copy-start.125
  1479.5 436.2 %reduce-scatter.7.cloned.1.call-start = ((), (), s32[]{:S(2)}) async-start(), calls=%async_computation.12 | async-start | bytes 10485760 | tf_op jit(solution)/shard_map/reduce_scatter | solution.py:320
  1770.4 492.8 %reduce-scatter.11.cloned.1.call-start = ((), (), s32[]{:S(2)}) async-start(), calls=%async_computation.14 | async-start | bytes 20971520 | tf_op jit(solution)/shard_map/reduce_scatter | solution.py:342
  1802.9 114.6 %copy-start.76 = (bf16[128,8,4,128]{3,1,2,0:T(8,128)(2,1)}, bf16[128,8,4,128]{3,1,2,0:T(8,128)(2,1)S(1)}, u32[]{:S(2)}) copy-start(bf16[128,8,4,128]{3,1,2,0:T(8,128)(2,1)S(1)} %copy.243) | copy-start | bytes 3145732
  1805.0 112.4 %copy-start.67 = (bf16[1024,512]{1,0:T(8,128)(2,1)}, bf16[1024,512]{1,0:T(8,128)(2,1)S(1)}, u32[]{:S(2)}) copy-start(bf16[1024,512]{1,0:T(8,128)(2,1)S(1)} %convert.29) | copy-start | bytes 3145732
  1982.0 537.3 %all-reduce.14.cloned.1.call-start = ((), (), s32[]{:S(2)}) async-start(), calls=%async_computation.15 | async-start | bytes 27099136 | tf_op jit(solution)/shard_map/psum | solution.py:353
  2001.6 261.6 %copy-start.113 = (f32[512]{0:T(512)S(1)}, f32[512]{0:T(512)}, u32[]{:S(2)}) copy-start(f32[512]{0:T(512)} %copy-done.112) | copy-start | bytes 6148
  2269.5 401.1 %all-reduce.24.cloned.1.call-start = ((), (), s32[]{:S(2)}) async-start(), calls=%async_computation.20 | async-start | bytes 6291456 | tf_op jit(solution)/shard_map/psum | solution.py:98
  2537.7 152.4 %copy-start.8 = (f32[512,512]{0,1:T(8,128)}, f32[512,512]{0,1:T(8,128)S(1)}, u32[]{:S(2)}) copy-start(f32[512,512]{0,1:T(8,128)S(1)} %multiply_add_fusion.9) | copy-start | bytes 3145732
  2549.0 278.7 %all-reduce.22.cloned.1.call-start = ((), (), s32[]{:S(2)}) async-start(), calls=%async_computation.19 | async-start | bytes 6291456 | tf_op jit(solution)/shard_map/psum | solution.py:98
  2682.6 9.4 copy-start.52
  2706.8 265.1 %all-reduce.20.cloned.1.call-start = ((), (), s32[]{:S(2)}) async-start(), calls=%async_computation.18 | async-start | bytes 6291456 | tf_op jit(solution)/shard_map/psum | solution.py:98
  2827.8 8.8 copy-start.47
  2848.1 127.9 %copy-start.17 = (f32[512,512]{1,0:T(8,128)S(1)}, f32[512,512]{1,0:T(8,128)}, u32[]{:S(2)}) copy-start(f32[512,512]{1,0:T(8,128)} %copy-done.16) | copy-start | bytes 3145732
  2851.0 265.4 %all-reduce.18.cloned.1.call-start = ((), (), s32[]{:S(2)}) async-start(), calls=%async_computation.17 | async-start | bytes 6291456 | tf_op jit(solution)/shard_map/psum | solution.py:98
  2971.9 8.8 copy-start.48
  2992.5 128.0 %copy-start.21 = (f32[512,512]{1,0:T(8,128)S(1)}, f32[512,512]{1,0:T(8,128)}, u32[]{:S(2)}) copy-start(f32[512,512]{1,0:T(8,128)} %copy-done.20) | copy-start | bytes 3145732
  2995.5 265.5 %all-reduce.16.cloned.1.call-start = ((), (), s32[]{:S(2)}) async-start(), calls=%async_computation.16 | async-start | bytes 6291456 | tf_op jit(solution)/shard_map/psum | solution.py:98
  3116.4 8.8 copy-start.49
  3140.0 8.0 copy-start.60
  3261.0 9.7 copy-start.11
  3261.0 9.7 copy-start.33
  3261.0 9.7 copy-start.36
  3261.0 9.7 copy-start.40
  3261.0 9.7 copy-start.51
  (97 other events, 476.1 us)
Sparse Core Ops, SparseCore 0:
  16.1 152.3 all-gather.7
  170.6 44.1 all-gather.9
  220.1 79.4 all-gather.11
  301.6 79.2 all-gather.13
  382.9 44.4 all-gather.15
  429.4 44.6 all-gather.17
  781.8 80.2 all-gather.19
  1014.0 142.8 reduce-scatter.4
  1479.6 145.2 reduce-scatter.8
  1770.5 145.1 reduce-scatter.6
  1982.2 281.0 reduce-scatter.10
  2271.2 248.0 all-reduce.13
  2549.2 121.3 all-reduce.23
  2707.0 120.7 all-reduce.21
  2851.1 120.7 all-reduce.19
  2995.6 120.7 all-reduce.17
  3140.2 120.7 all-reduce.15
where the time goes:
time: 3300 us; the launch traced here: 3290 us
  waiting for transfers between devices  1560 us (47%)
  other arithmetic  782 us (24%)
  local copies, waits for them, and re-layouts  593 us (18%)
  matrix products  246 us (7%)
  blocking collectives  87.5 us (3%)
    psum x5, waiting for transfers between devices, gram_sums(): lax.psum((jnp.dot(first_part, first_part.T, precision=highest_precision),...  589 us
    reduce_scatter x1, waiting for transfers between devices, on_device(): lax.psum_scatter(pixel_spread, 'narrow', scatter_dimension=0, tiled=True)  258 us
    scatter-add x1, other arithmetic, on_device(): value_spread = jnp.zeros((node_total, LATENT_WIDTH), jnp.float32).at[wide...  214 us
    scatter-add x1, other arithmetic, on_device(): key_spread = jnp.zeros((node_total, LATENT_WIDTH), jnp.float32).at[widene...  214 us
    psum x1, waiting for transfers between devices, on_device(): lax.psum((grad_embed, grad_cond, grad_attn, grad_up, grad_down, grad_dec,...  199 us
    all_gather x1, waiting for transfers between devices, on_device(): pixel_rows = lax.all_gather(embedded, 'narrow', axis=0, tiled=True)  150 us
    reduce_scatter x1, waiting for transfers between devices, on_device(): lax.psum_scatter(node_spread, 'narrow', scatter_dimension=0, tiled=True)  143 us
    gather x1, local copies, waits for them, and re-layouts, on_device(): value_rows[neighbours[0]].reshape(node_local, NBR, HEADS, HEAD_WIDTH)  135 us
  transfers between devices with their start and end apart: 17, of which 13 were waited for; matrix products, arithmetic and copies ran while one was open for 27% of the time, Pallas kernels for 0%

commit v1 on v0

v1 whole, which is shorter than its diff:
```python
import math

import jax
import jax.numpy as jnp
from jax import lax
from jax.sharding import PartitionSpec as P

LATENT_WIDTH = 512
HEADS = 4
HEAD_WIDTH = 128
FF = 2048
COND = 32
NBR = 32
G2M_K = 4
M2G_K = 3
NS_ITERS = 5
SIGMA_LEVELS = 8
STEP_NUMBER = 10


highest_precision = lax.Precision.HIGHEST
sigma_low = 0.25
sigma_high = 4.0
clip_bound = 0.02
muon_rate = 0.5
muon_decay = 0.95
adam_rate = 0.03
beta_one = 0.9
beta_two = 0.95
adam_eps = 1e-08
decay_rate = 0.01
ema_keep = 0.9
coef_a = 3.4445
coef_b = -4.775
coef_c = 2.0315


def sigma_terms(level):
    fraction = level.astype(jnp.float32) / (SIGMA_LEVELS - 1)
    noise_level = sigma_low * (sigma_high / sigma_low) ** fraction
    square = noise_level * noise_level + 1.0
    scale_in = lax.rsqrt(square)
    return (
        noise_level,
        scale_in,
        1.0 / square,
        noise_level * scale_in,
        square / (noise_level * noise_level),
    )


def cond_features(noise_level):
    frequencies = 1.0 + jnp.arange(COND // 2).astype(jnp.float32)
    phases = jnp.log(noise_level) * frequencies
    return jnp.concatenate([jnp.sin(phases), jnp.cos(phases)])


def lat_weights(first_row, row_count, pixel_total):
    row_ids = (first_row + jnp.arange(row_count, dtype=jnp.int32)).astype(jnp.float32)
    return jnp.cos(math.pi * ((row_ids + 0.5) / pixel_total - 0.5))


def norm_stats(values):
    centred = values - jnp.mean(values, axis=-1, keepdims=True)
    inverse = lax.rsqrt(jnp.mean(centred * centred, axis=-1, keepdims=True) + 1e-05)
    return (centred * inverse, inverse)


def norm_back(grad_normed, normed, inverse):
    first_mean = jnp.mean(grad_normed, axis=-1, keepdims=True)
    second_mean = jnp.mean(grad_normed * normed, axis=-1, keepdims=True)
    return inverse * (grad_normed - first_mean - normed * second_mean)


def silu_slope(values):
    sigmoid_values = jax.nn.sigmoid(values)
    return sigmoid_values * (1.0 + values * (1.0 - sigmoid_values))


def contract_rows(left, right):
    return lax.dot_general(
        left, right, (((0,), (0,)), ((), ())), preferred_element_type=jnp.float32
    )


def contract_last(left, right):
    return lax.dot_general(
        left, right, (((1,), (1,)), ((), ())), preferred_element_type=jnp.float32
    )


def bit_swap(values, axis_name, bit):
    size = lax.axis_size(axis_name)
    return lax.ppermute(values, axis_name, [(i, i ^ (1 << bit)) for i in range(size)])


def axis_bits(axis_name):
    bits = []
    reach = 1
    while reach < lax.axis_size(axis_name):
        bits.append((axis_name, len(bits)))
        reach *= 2
    return bits


def small_sum(values):
    for axis_name, bit in axis_bits("wide") + axis_bits("narrow"):
        values = values + bit_swap(values, axis_name, bit)
    return values


def large_sum(values, sent_type):
    steps = axis_bits("wide") + axis_bits("narrow")
    for axis_name, bit in steps:
        half = values.shape[0] // 2
        mine = (lax.axis_index(axis_name) >> bit) & 1
        kept = lax.dynamic_slice_in_dim(values, mine * half, half, 0)
        sent = lax.dynamic_slice_in_dim(values, (1 - mine) * half, half, 0)
        values = kept + bit_swap(sent.astype(sent_type), axis_name, bit).astype(jnp.float32)
    values = values.astype(sent_type)
    for axis_name, bit in steps[::-1]:
        mine = (lax.axis_index(axis_name) >> bit) & 1
        other = bit_swap(values, axis_name, bit)
        is_high = mine == 1
        values = jnp.concatenate(
            [jnp.where(is_high, other, values), jnp.where(is_high, values, other)], axis=0
        )
    return values.astype(jnp.float32)


def ring_slots(values):
    size = lax.axis_size("narrow")
    slots = [values]
    for shift in range(1, size):
        slots.append(
            lax.ppermute(values, "narrow", [((i + shift) % size, i) for i in range(size)])
        )
    return slots


def line_slots(values):
    size = lax.axis_size("narrow")
    pos = lax.axis_index("narrow")
    up = [(i, i + 1) for i in range(size - 1)]
    down = [(i + 1, i) for i in range(size - 1)]
    from_low, from_high = values, values
    low_list, high_list = [], []
    for _ in range(size - 1):
        from_low = lax.ppermute(from_low, "narrow", up)
        from_high = lax.ppermute(from_high, "narrow", down)
        low_list.append(from_low)
        high_list.append(from_high)
    slots = [values]
    for shift in range(1, size):
        slots.append(
            jnp.where(pos + shift < size, high_list[shift - 1], low_list[size - shift - 1])
        )
    return slots


def ring_sum(parts):
    size = lax.axis_size("narrow")
    total = parts[0]
    for shift in range(1, size):
        arrived = lax.ppermute(
            parts[shift].astype(jnp.bfloat16),
            "narrow",
            [(i, (i + shift) % size) for i in range(size)],
        )
        total = total + arrived.astype(jnp.float32)
    return total


def count_matrix(index_rows, first, column_count):
    columns = first + jnp.arange(column_count, dtype=jnp.int32)[None, :]
    total = jnp.zeros((index_rows.shape[0], column_count), jnp.float32)
    for slot in range(index_rows.shape[1]):
        total = total + (index_rows[:, slot : slot + 1] == columns).astype(jnp.float32)
    return total.astype(jnp.bfloat16)


def wide_gather(block, axis):
    rows = block.shape[0] // lax.axis_size("wide")
    own = lax.dynamic_slice_in_dim(block, lax.axis_index("wide") * rows, rows, 0)
    if axis == 1:
        across = lax.all_gather(own, "narrow", axis=1, tiled=True)
        return lax.all_gather(across, "wide", axis=0, tiled=True)
    across = lax.all_gather(own, "narrow", axis=0)
    whole = lax.all_gather(across, "wide", axis=1)
    return whole.reshape(-1, block.shape[1])


def high_dot(left, right):
    return jnp.dot(left, right, precision=highest_precision)


def orthogonal_map(gram):
    scale = 1.0 / (jnp.sqrt(jnp.trace(gram)) + 1e-07)
    gram = gram * (scale * scale)
    eye = jnp.eye(gram.shape[0], dtype=jnp.float32)
    mapped = None
    for iteration in range(NS_ITERS):
        poly = coef_a * eye + coef_b * gram + coef_c * high_dot(gram, gram)
        if iteration < NS_ITERS - 1:
            gram = high_dot(poly, high_dot(poly, gram))
        mapped = poly * scale if mapped is None else high_dot(poly, mapped)
    return mapped


def adam_update(weight, grad, first, second):
    first_new = beta_one * first + (1.0 - beta_one) * grad
    second_new = beta_two * second + (1.0 - beta_two) * grad * grad
    first_hat = first_new / (1.0 - beta_one**STEP_NUMBER)
    second_hat = second_new / (1.0 - beta_two**STEP_NUMBER)
    weight_new = weight - adam_rate * (
        first_hat / (jnp.sqrt(second_hat) + adam_eps) + decay_rate * weight
    )
    return (weight_new, first_new, second_new)


def on_device(
    prior_states,
    target,
    noise_draw,
    level_index,
    g2m_edges,
    neighbours,
    m2g_edges,
    valid_mask,
    channel_weights,
    w_embed,
    w_cond,
    w_attn,
    w_up,
    w_down,
    w_dec,
    biases,
    mom_attn,
    mom_up,
    mom_down,
    m_embed,
    v_embed,
    m_cond,
    v_cond,
    m_dec,
    v_dec,
    m_bias,
    v_bias,
    ema_embed,
    ema_cond,
    ema_attn,
    ema_up,
    ema_down,
    ema_dec,
    ema_bias,
):
    narrow_pos = lax.axis_index("narrow")
    narrow_count = lax.axis_size("narrow")
    pixel_local = valid_mask.shape[1]
    node_local = neighbours.shape[1]
    pixel_total = pixel_local * narrow_count
    node_total = node_local * narrow_count
    embed_low = w_embed.astype(jnp.bfloat16)
    dec_low = w_dec.astype(jnp.bfloat16)
    bias_embed = biases[:LATENT_WIDTH]
    bias_up = biases[LATENT_WIDTH : LATENT_WIDTH + FF]
    bias_out = biases[LATENT_WIDTH + FF :]
    noise_level, scale_in, skip_scale, out_scale, loss_scale = sigma_terms(level_index[0])
    target_rows = target[0].astype(jnp.float32)
    noisy = target_rows + noise_level * noise_draw[0].astype(jnp.float32)
    features = jnp.concatenate(
        [prior_states[0, 0], prior_states[0, 1], (scale_in * noisy).astype(jnp.bfloat16)], axis=0
    )
    feature_slots = line_slots(features)
    g2m_slots = ring_slots(g2m_edges[0].T)
    attn_full = wide_gather(w_attn.astype(jnp.bfloat16), 1)
    up_full = wide_gather(w_up.astype(jnp.bfloat16), 1)
    down_full = wide_gather(w_down.astype(jnp.bfloat16), 0)
    mom_attn_full = wide_gather(mom_attn, 1)
    mom_up_full = wide_gather(mom_up, 1)
    mom_down_full = wide_gather(mom_down, 0)
    lat_weight = lat_weights(narrow_pos * pixel_local, pixel_local, pixel_total)
    pixel_weight = lat_weight * valid_mask[0].astype(jnp.float32)
    weight_total = small_sum(jnp.sum(pixel_weight).reshape(1, 1))[0, 0]

    g2m_ids = (jnp.concatenate(g2m_slots, axis=1) - narrow_pos * pixel_local) % pixel_total
    g2m_ids = g2m_ids.T
    near_ids = (neighbours[0] - narrow_pos * node_local) % node_total
    m2g_ids = (m2g_edges[0] - narrow_pos * node_local) % node_total
    g2m_counts = [
        count_matrix(g2m_ids, slot * pixel_local, pixel_local) for slot in range(narrow_count)
    ]
    near_counts = count_matrix(near_ids, 0, node_total)
    m2g_counts = count_matrix(m2g_ids, 0, node_total)

    embed_pres = []
    node_in = None
    for slot in range(narrow_count):
        embed_pre = contract_rows(feature_slots[slot], embed_low) + bias_embed
        embedded = jax.nn.silu(embed_pre).astype(jnp.bfloat16)
        part = jnp.dot(g2m_counts[slot], embedded, preferred_element_type=jnp.float32)
        node_in = part if node_in is None else node_in + part
        embed_pres.append(embed_pre)
    node_in = node_in / G2M_K
    conditioning = cond_features(noise_level)
    modulation = jnp.dot(conditioning, w_cond, precision=highest_precision)
    gain_one = 1.0 + modulation[:LATENT_WIDTH]
    gain_two = 1.0 + modulation[2 * LATENT_WIDTH : 3 * LATENT_WIDTH]
    normed_one, inverse_one = norm_stats(node_in)
    attn_in = (normed_one * gain_one + modulation[LATENT_WIDTH : 2 * LATENT_WIDTH]).astype(
        jnp.bfloat16
    )
    attn_own = attn_in[:node_local]
    query_map = attn_full[:, :LATENT_WIDTH]
    pair_map = attn_full[:, LATENT_WIDTH : 3 * LATENT_WIDTH]
    proj_map = attn_full[:, 3 * LATENT_WIDTH :]
    query_rows = jnp.dot(attn_own, query_map, preferred_element_type=jnp.float32).astype(
        jnp.bfloat16
    )
    pair_rows = jnp.dot(attn_in, pair_map, preferred_element_type=jnp.float32).astype(
        jnp.bfloat16
    )
    key_rows = pair_rows[:, :LATENT_WIDTH]
    value_rows = pair_rows[:, LATENT_WIDTH:]

    counts = near_counts.astype(jnp.float32)
    attended_heads = []
    prob_heads = []
    for head in range(HEADS):
        part = slice(head * HEAD_WIDTH, (head + 1) * HEAD_WIDTH)
        scores = contract_last(query_rows[:, part], key_rows[:, part]) / math.sqrt(HEAD_WIDTH)
        scores = jnp.where(counts > 0, scores, -jnp.inf)
        raised = jnp.exp(scores - jnp.max(scores, axis=1, keepdims=True))
        prob = raised / jnp.sum(raised * counts, axis=1, keepdims=True)
        lowered = (prob.astype(jnp.bfloat16).astype(jnp.float32) * counts).astype(jnp.bfloat16)
        prob_heads.append((prob, lowered))
        attended_heads.append(
            jnp.dot(lowered, value_rows[:, part], preferred_element_type=jnp.float32)
        )
    attended_rows = jnp.concatenate(attended_heads, axis=1).astype(jnp.bfloat16)
    node_mid = node_in[:node_local] + jnp.dot(
        attended_rows, proj_map, preferred_element_type=jnp.float32
    )
    normed_two, inverse_two = norm_stats(node_mid)
    mlp_in = (normed_two * gain_two + modulation[3 * LATENT_WIDTH :]).astype(jnp.bfloat16)
    up_pre = jnp.dot(mlp_in, up_full, preferred_element_type=jnp.float32) + bias_up
    hidden = jax.nn.silu(up_pre).astype(jnp.bfloat16)
    node_out = node_mid + jnp.dot(hidden, down_full, preferred_element_type=jnp.float32)
    node_low = node_out.astype(jnp.bfloat16)
    node_raw = lax.dot_general(
        dec_low, node_low, (((0,), (1,)), ((), ())), preferred_element_type=jnp.float32
    ).astype(jnp.bfloat16)
    all_raw = jnp.concatenate(ring_slots(node_raw), axis=1)
    raw_output = contract_last(all_raw, m2g_counts) / M2G_K + bias_out[:, None]
    errors = skip_scale * noisy + out_scale * raw_output - target_rows
    weighted = channel_weights[:, None] * pixel_weight[None, :]
    loss_local = loss_scale * jnp.sum(weighted * errors * errors)
    grad_raw = (2.0 * loss_scale * out_scale / weight_total * weighted * errors).astype(
        jnp.bfloat16
    )
    grad_out_bias = jnp.sum(grad_raw.astype(jnp.float32), axis=1)
    raw_spread = jnp.dot(grad_raw, m2g_counts, preferred_element_type=jnp.float32)
    grad_node_raw = (
        ring_sum(
            [
                raw_spread[:, slot * node_local : (slot + 1) * node_local]
                for slot in range(narrow_count)
            ]
        )
        / M2G_K
    )
    grad_dec = lax.dot_general(
        node_low.astype(jnp.float32),
        grad_node_raw,
        (((0,), (1,)), ((), ())),
        precision=highest_precision,
    )
    grad_node_out = lax.dot_general(
        grad_node_raw,
        dec_low.astype(jnp.float32),
        (((0,), (1,)), ((), ())),
        precision=highest_precision,
    )
    grad_mlp = grad_node_out.astype(jnp.bfloat16)
    grad_down = contract_rows(hidden, grad_mlp)
    grad_hidden = contract_last(grad_mlp, down_full)
    grad_up_pre = (grad_hidden * silu_slope(up_pre)).astype(jnp.bfloat16)
    grad_up_bias = jnp.sum(grad_up_pre.astype(jnp.float32), axis=0)
    grad_up = contract_rows(mlp_in, grad_up_pre)
    grad_mlp_in = contract_last(grad_up_pre, up_full)
    grad_node_mid = grad_node_out + norm_back(grad_mlp_in * gain_two, normed_two, inverse_two)
    grad_proj_out = grad_node_mid.astype(jnp.bfloat16)
    grad_proj = contract_rows(attended_rows, grad_proj_out)
    sum_down = large_sum(grad_down, jnp.bfloat16)
    sum_up = large_sum(grad_up, jnp.bfloat16)
    sum_proj = large_sum(grad_proj, jnp.bfloat16)
    gradient_attended = contract_last(grad_proj_out, proj_map).astype(jnp.bfloat16)

    query_grads, key_grads, value_grads = [], [], []
    for head in range(HEADS):
        part = slice(head * HEAD_WIDTH, (head + 1) * HEAD_WIDTH)
        prob, lowered = prob_heads[head]
        grad_head = gradient_attended[:, part]
        grad_prob = contract_last(grad_head, value_rows[:, part])
        weighted_prob = prob * counts
        inner = jnp.sum(weighted_prob * grad_prob, axis=1, keepdims=True)
        grad_scores = (
            (prob * (grad_prob - inner)).astype(jnp.bfloat16).astype(jnp.float32) * counts
        ).astype(jnp.bfloat16)
        query_grads.append(
            jnp.dot(grad_scores, key_rows[:, part], preferred_element_type=jnp.float32)
        )
        key_grads.append(contract_rows(grad_scores, query_rows[:, part]))
        value_grads.append(contract_rows(lowered, grad_head))
    grad_query_rows = (jnp.concatenate(query_grads, axis=1) / math.sqrt(HEAD_WIDTH)).astype(
        jnp.bfloat16
    )
    grad_pair_rows = jnp.concatenate(
        [jnp.concatenate(key_grads, axis=1) / math.sqrt(HEAD_WIDTH)] + value_grads, axis=1
    ).astype(jnp.bfloat16)

    grad_qkv = jnp.concatenate(
        [contract_rows(attn_own, grad_query_rows), contract_rows(attn_in, grad_pair_rows)], axis=1
    )
    sum_qkv = large_sum(grad_qkv, jnp.bfloat16)
    grad_attn_in = contract_last(grad_pair_rows, pair_map)
    grad_attn_in = grad_attn_in.at[:node_local].add(contract_last(grad_query_rows, query_map))
    grad_node_in = norm_back(grad_attn_in * gain_one, normed_one, inverse_one)
    grad_node_in = grad_node_in.at[:node_local].add(grad_node_mid)
    grad_modulation = jnp.concatenate(
        [
            jnp.sum(grad_attn_in * normed_one, axis=0),
            jnp.sum(grad_attn_in, axis=0),
            jnp.sum(grad_mlp_in * normed_two, axis=0),
            jnp.sum(grad_mlp_in, axis=0),
        ]
    )
    grad_cond = conditioning[:, None] * grad_modulation[None, :]
    node_grads = (grad_node_in / G2M_K).astype(jnp.bfloat16)
    grad_embed = None
    grad_embed_bias = None
    for slot in range(narrow_count):
        grad_embedded = contract_rows(g2m_counts[slot], node_grads)
        grad_pre = (grad_embedded * silu_slope(embed_pres[slot])).astype(jnp.bfloat16)
        bias_part = jnp.sum(grad_pre.astype(jnp.float32), axis=0)
        embed_part = jnp.dot(feature_slots[slot], grad_pre, preferred_element_type=jnp.float32)
        grad_embed = embed_part if grad_embed is None else grad_embed + embed_part
        grad_embed_bias = bias_part if grad_embed_bias is None else grad_embed_bias + bias_part

    grad_bias = jnp.concatenate([grad_embed_bias, grad_up_bias, grad_out_bias])
    pieces = [grad_embed, grad_cond, grad_dec, grad_bias, loss_local]
    flat = jnp.concatenate([piece.reshape(-1) for piece in pieces])
    row_total = -(-flat.shape[0] // (LATENT_WIDTH * 256)) * 256
    flat = jnp.pad(flat, (0, row_total * LATENT_WIDTH - flat.shape[0]))
    flat = large_sum(flat.reshape(row_total, LATENT_WIDTH), jnp.float32).reshape(-1)
    sums = []
    place = 0
    for piece in pieces:
        sums.append(flat[place : place + piece.size].reshape(piece.shape))
        place += piece.size
    sum_embed, sum_cond, sum_dec, sum_bias, loss_sum = sums
    sum_attn = jnp.concatenate([sum_qkv, sum_proj], axis=1)
    square_sum = (
        jnp.sum(sum_embed * sum_embed)
        + jnp.sum(sum_cond * sum_cond)
        + jnp.sum(sum_attn * sum_attn)
        + jnp.sum(sum_up * sum_up)
        + jnp.sum(sum_down * sum_down)
        + jnp.sum(sum_dec * sum_dec)
        + jnp.sum(sum_bias * sum_bias)
    )
    grad_norm = jnp.sqrt(square_sum)
    factor = jnp.minimum(1.0, clip_bound / (grad_norm + 1e-06))
    attn_cols = w_attn.shape[1]
    up_cols = w_up.shape[1]
    down_rows = w_down.shape[0]
    all_attn = muon_decay * mom_attn_full + factor * sum_attn
    all_up = muon_decay * mom_up_full + factor * sum_up
    all_down = muon_decay * mom_down_full + factor * sum_down
    moment_attn = lax.dynamic_slice_in_dim(all_attn, narrow_pos * attn_cols, attn_cols, 1)
    moment_up = lax.dynamic_slice_in_dim(all_up, narrow_pos * up_cols, up_cols, 1)
    moment_down = lax.dynamic_slice_in_dim(all_down, narrow_pos * down_rows, down_rows, 0)
    map_attn = orthogonal_map(high_dot(all_attn, all_attn.T))
    map_up = orthogonal_map(high_dot(all_up, all_up.T))
    map_down = orthogonal_map(
        lax.dot_general(
            all_down, all_down, (((0,), (0,)), ((), ())), precision=highest_precision
        )
    )
    attn_orth = high_dot(map_attn, moment_attn)
    up_orth = high_dot(map_up, moment_up)
    down_orth = lax.dot_general(
        moment_down, map_down, (((1,), (1,)), ((), ())), precision=highest_precision
    )
    new_attn = (
        w_attn - muon_rate * math.sqrt(max(1.0, LATENT_WIDTH / (4 * LATENT_WIDTH))) * attn_orth
    )
    new_up = w_up - muon_rate * math.sqrt(max(1.0, LATENT_WIDTH / FF)) * up_orth
    new_down = w_down - muon_rate * math.sqrt(max(1.0, FF / LATENT_WIDTH)) * down_orth
    new_embed, first_embed, second_embed = adam_update(
        w_embed, factor * sum_embed, m_embed, v_embed
    )
    new_cond, first_cond, second_cond = adam_update(w_cond, factor * sum_cond, m_cond, v_cond)
    new_dec, first_dec, second_dec = adam_update(w_dec, factor * sum_dec, m_dec, v_dec)
    new_bias, first_bias, second_bias = adam_update(biases, factor * sum_bias, m_bias, v_bias)
    keep_rest = 1.0 - ema_keep
    return (
        new_attn,
        new_up,
        new_down,
        moment_attn,
        moment_up,
        moment_down,
        new_embed,
        new_cond,
        new_dec,
        new_bias,
        first_embed,
        second_embed,
        first_cond,
        second_cond,
        first_dec,
        second_dec,
        first_bias,
        second_bias,
        ema_keep * ema_embed + keep_rest * new_embed,
        ema_keep * ema_cond + keep_rest * new_cond,
        ema_keep * ema_attn + keep_rest * new_attn,
        ema_keep * ema_up + keep_rest * new_up,
        ema_keep * ema_down + keep_rest * new_down,
        ema_keep * ema_dec + keep_rest * new_dec,
        ema_keep * ema_bias + keep_rest * new_bias,
        loss_sum,
        weight_total,
        grad_norm,
    )


def solution(mesh):
    in_specs = (
        P("wide", None, None, "narrow"),
        P("wide", None, "narrow"),
        P("wide", None, "narrow"),
        P("wide"),
        P("wide", "narrow", None),
        P("wide", "narrow", None),
        P("wide", "narrow", None),
        P("wide", "narrow"),
        P(),
        P(),
        P(),
        P(None, "narrow"),
        P(None, "narrow"),
        P("narrow", None),
        P(),
        P(),
        P(None, "narrow"),
        P(None, "narrow"),
        P("narrow", None),
        P(),
        P(),
        P(),
        P(),
        P(),
        P(),
        P(),
        P(),
        P(),
        P(),
        P(None, "narrow"),
        P(None, "narrow"),
        P("narrow", None),
        P(),
        P(),
    )
    out_specs = (
        P(None, "narrow"),
        P(None, "narrow"),
        P("narrow", None),
        P(None, "narrow"),
        P(None, "narrow"),
        P("narrow", None),
        P(),
        P(),
        P(),
        P(),
        P(),
        P(),
        P(),
        P(),
        P(),
        P(),
        P(),
        P(),
        P(),
        P(),
        P(None, "narrow"),
        P(None, "narrow"),
        P("narrow", None),
        P(),
        P(),
        P(),
        P(),
        P(),
    )
    return jax.shard_map(
        on_device, mesh=mesh, in_specs=in_specs, out_specs=out_specs, check_vma=False
    )
```

time: 3300 us -> 1320 us (0.40)
  waiting for transfers between devices: 1560 us -> 94.4 us
  other arithmetic: 782 us -> 236 us
  local copies, waits for them, and re-layouts: 593 us -> 52.6 us
  matrix products: 246 us -> 696 us
  starting transfers between devices: 1.35 us -> 86.3 us
    psum x6 -> x0, waiting for transfers between devices: 788 us -> none  [the longest x5 589 us: gram_sums(): lax.psum((jnp.dot(first_part, first_part.T, precision=highest_precision),...]
    reduce_scatter x4 -> x0, waiting for transfers between devices: 512 us -> none  [the longest x1 258 us: on_device(): lax.psum_scatter(pixel_spread, 'narrow', scatter_dimension=0, tiled=True)]
    scatter-add x4 -> x1, other arithmetic: 501 us -> 0.54 us  [on_device(): grad_node_in = grad_node_in.at[:node_local].add(grad_node_mid)]
    gather x4 -> x0, local copies, waits for them, and re-layouts: 320 us -> none  [the longest x1 135 us: on_device(): value_rows[neighbours[0]].reshape(node_local, NBR, HEADS, HEAD_WIDTH)]
    all_gather x7 -> x6, waiting for transfers between devices: 257 us -> 0.09 us  [the longest x4 0.06 us: wide_gather(): return lax.all_gather(across, 'wide', axis=0, tiled=True)]
    dot_general x5 -> x21, matrix products: 18.9 us -> 194 us  [contract_rows(): lax.dot_general(left, right, (((0,), (0,)), ((), ())), preferred_element_...]
    dot_general x54 -> x80, matrix products: 192 us -> 348 us  [the longest x55 134 us: high_dot(): return jnp.dot(left, right, precision=highest_precision)]
    dot_general x4 -> x14, matrix products: 19.5 us -> 140 us  [contract_last(): lax.dot_general(left, right, (((1,), (1,)), ((), ())), preferred_element_...]
  transfers between devices with their start and end apart: 17 -> 76, of which waited for: 13 -> 33; matrix products, arithmetic and copies ran while one was open for 27% -> 64% of each run, Pallas kernels for 0% -> 0%
where the time goes in v1:
time: 1320 us; the launch traced here: 1310 us
  matrix products  696 us (53%)
  other arithmetic  236 us (18%)
  blocking collectives  111 us (8%)
  waiting for transfers between devices  94.4 us (7%)
  starting transfers between devices  86.3 us (7%)
  local copies, waits for them, and re-layouts  52.6 us (4%)
  between operations  33.1 us (3%)
    dot_general x21, matrix products, contract_rows(): lax.dot_general(left, right, (((0,), (0,)), ((), ())), preferred_element_...  194 us
    dot_general x14, matrix products, contract_last(): lax.dot_general(left, right, (((1,), (1,)), ((), ())), preferred_element_...  140 us
    dot_general x55, matrix products, high_dot(): return jnp.dot(left, right, precision=highest_precision)  134 us
    dot_general x4, matrix products, on_device(): jnp.dot(g2m_counts[slot], embedded, preferred_element_type=jnp.float32)  98.1 us
    ppermute x55, waiting for transfers between devices, bit_swap(): lax.ppermute(values, axis_name, [(i, i ^ 1 << bit) for i in range(size)])  94.1 us
    all_gather x4, blocking collectives, wide_gather(): across = lax.all_gather(own, 'narrow', axis=1, tiled=True)  80.8 us
    gt x1, other arithmetic, on_device(): scores = jnp.where(counts > 0, scores, -jnp.inf)  80.6 us
    convert_element_type x2, other arithmetic, on_device(): grad_scores = ((prob * (grad_prob - inner)).astype(jnp.bfloat16).astype(j...  60 us
  transfers between devices with their start and end apart: 76, of which 33 were waited for; matrix products, arithmetic and copies ran while one was open for 64% of the time, Pallas kernels for 0%

profile of v1, /device:TPU:0, one launch (start us, length us, event | category | flops | bytes accessed | tf_op | source)
XLA Modules:
  0.0 1309.1 jit_solution(1917147301161323724)
XLA Ops:
  8.4 16.3 %all_gather.50 = bf16[64,2048]{1,0:T(8,128)(2,1)} all-gather(bf16[64,512]{1,0:T(8,128)(2,1)S(1)} %dynamic-slice_convert_fusion.15), channel_id=1, replica_groups=mesh['wide'=8,'narrow'=4] {'narrow'}, dimensions={1}, use_global_device_ids=true | all-gather | bytes 327680 | tf_op jit(solution)/shard_map/all_gather | solution.py:186
  25.7 15.1 %all_gather.52 = bf16[64,2048]{1,0:T(8,128)(2,1)} all-gather(bf16[64,512]{1,0:T(8,128)(2,1)S(1)} %dynamic-slice_convert_fusion.14), channel_id=1, replica_groups=mesh['wide'=8,'narrow'=4] {'narrow'}, dimensions={1}, use_global_device_ids=true | all-gather | bytes 327680 | tf_op jit(solution)/shard_map/all_gather | solution.py:186
  41.8 15.1 %all-gather = bf16[256,512]{1,0:T(8,128)(2,1)} all-gather(bf16[64,512]{1,0:T(8,128)(2,1)S(1)} %dynamic-slice_convert_fusion.13), channel_id=2, replica_groups=mesh['wide'=8,'narrow'=4] {'narrow'}, dimensions={0}, use_global_device_ids=true | all-gather | bytes 327680 | tf_op jit(solution)/shard_map/all_gather | solution.py:188
  57.0 15.7 %all-gather.2 = f32[256,512]{1,0:T(8,128)} all-gather(f32[64,512]{1,0:T(8,128)S(1)} %constant_dynamic-slice_fusion), channel_id=4, replica_groups=mesh['wide'=8,'narrow'=4] {'narrow'}, dimensions={0}, use_global_device_ids=true | all-gather | bytes 655360 | tf_op jit(solution)/shard_map/all_gather | solution.py:188
  89.7 27.4 %all_gather.48 = f32[64,2048]{1,0:T(8,128)} all-gather(f32[64,512]{1,0:T(8,128)S(1)} %constant_dynamic-slice_fusion.9), channel_id=1, replica_groups=mesh['wide'=8,'narrow'=4] {'narrow'}, dimensions={1}, use_global_device_ids=true | all-gather | bytes 655360 | tf_op jit(solution)/shard_map/all_gather | solution.py:186
  124.1 80.6 %convert_compare_fusion = (pred[1024,4096]{1,0:T(32,128)(4,1)}, bf16[1024,4096]{1,0:T(8,128)(2,1)}) fusion(s32[1024]{0:T(1024)S(1)} %bitcast.255, s32[1024]{0:T(1024)S(1)} %bitcast.256, s32[1024]{0:T(1024)S(1)} %bitcast.257, s32[1024]{0:T(1024)S(1)} %bitcast.258, s32[1024]{0:T(1024)S(1)} %bitcast.259, s32[1024]{0:T(1024)S(1)} %bitcast.260, ...), kind=kLoop, calls=%fused_computation.16 | loop fusion | flops 411041792 | bytes 12713984 | tf_op jit(solution)/shard_map/gt | solution.py:332
  208.5 27.1 %fusion.23 = f32[4096,512]{0,1:T(8,128)} fusion(s32[4096]{0:T(1024)S(1)} %bitcast.298, s32[4096]{0:T(1024)S(1)} %bitcast.306, s32[4096]{0:T(1024)S(1)} %bitcast.314, s32[4096]{0:T(1024)S(1)} %bitcast.290, f32[2048,512]{1,0:T(8,128)} %fusion.254, f32[512]{0:T(512)S(1)} %slice.320), kind=kOutput, calls=%fused_computation.97 | convolution fusion | flops 8696889344 | bytes 12650496 | tf_op jit(solution)/shard_map/dot_general | solution.py:301
  245.5 23.5 %fusion.31 = f32[4096,512]{0,1:T(8,128)} fusion(s32[2048]{0:T(1024)S(1)} %iota_add_fusion.1, s32[4096]{0:T(1024)S(1)} %bitcast.299, s32[4096]{0:T(1024)S(1)} %bitcast.307, s32[4096]{0:T(1024)S(1)} %bitcast.315, s32[4096]{0:T(1024)S(1)} %bitcast.291, f32[2048,512]{1,0:T(8,128)} %fusion.165, f32[512]{0:T(512)S(1)} %slice.320), kind=kOutput, calls=%fused_computation.105 | convolution fusion | flops 8696889344 | bytes 12658688 | tf_op jit(solution)/shard_map/dot_general | solution.py:301
  273.1 23.8 %fusion.29 = f32[4096,512]{0,1:T(8,128)} fusion(s32[2048]{0:T(1024)S(1)} %iota_add_fusion.2, s32[4096]{0:T(1024)S(1)} %bitcast.300, s32[4096]{0:T(1024)S(1)} %bitcast.308, s32[4096]{0:T(1024)S(1)} %bitcast.316, s32[4096]{0:T(1024)S(1)} %bitcast.292, f32[2048,512]{1,0:T(8,128)} %fusion.164, f32[512]{0:T(512)S(1)} %slice.320), kind=kOutput, calls=%fused_computation.103 | convolution fusion | flops 8696889344 | bytes 12658688 | tf_op jit(solution)/shard_map/dot_general | solution.py:301
  298.9 23.7 %fusion.246 = (f32[4096]{0:T(1024)S(1)}, f32[4096,512]{0,1:T(8,128)S(1)}) fusion(f32[2048,512]{1,0:T(8,128)S(1)} %fusion.166, f32[512]{0:T(512)S(1)} %slice.320, s32[2048]{0:T(1024)S(1)} %iota_add_fusion, s32[4096]{0:T(1024)S(1)} %bitcast.301, s32[4096]{0:T(1024)S(1)} %bitcast.309, s32[4096]{0:T(1024)S(1)} %bitcast.317, s32[4096]{0:T(1024)S(1)} %bitcast.293, ...), kind=kOutput, calls=%fused_computation.602 | convolution fusion | flops 8707371008 | bytes 37840896 | tf_op jit(solution)/shard_map/dot_general | solution.py:301
  331.6 7.5 convolution_convert_fusion
  339.1 8.0 fusion.250
  347.1 7.5 fusion.249
  354.6 7.5 fusion.248
  362.1 7.7 fusion.247
  369.9 23.6 %fusion = (f32[1024]{0:T(1024)S(1)}, f32[1024]{0:T(1024)S(1)}, f32[1024]{0:T(1024)S(1)}, f32[1024]{0:T(1024)S(1)}) fusion(bf16[1024,4096]{1,0:T(8,128)(2,1)S(1)} %bitcast.240, f32[1024,4096]{1,0:T(8,128)} %get-tuple-element.219, f32[1024]{0:T(1024)S(1)} %get-tuple-element.218, f32[1024,4096]{1,0:T(8,128)} %get-tuple-element.221, ...), kind=kLoop, calls=%fused_computation.29 | loop fusion | flops 54521856 | bytes 75530240 | tf_op jit(solution)/shard_map/reduce_sum | solution.py:334
  393.5 8.6 convolution_convert_fusion.10
  402.2 8.7 convolution_convert_fusion.9
  410.9 11.5 convolution_convert_fusion.8
  422.5 7.7 convolution_convert_fusion.7
  433.2 8.3 multiply_convert_fusion.6
  474.1 15.7 %fusion.136 = (f32[]{:T(128)}, f32[83]{0:T(128)}, f32[83,2048]{1,0:T(8,128)S(1)}) fusion(f32[2048]{0:T(1024)S(1)} %bitcast.322, f32[83]{0:T(128)S(1)} %copy-done.157, f32[]{:T(128)S(6)} %div.228, f32[83]{0:T(128)S(1)} %slice.378, s32[2048]{0:T(1024)S(1)} %bitcast.326, s32[2048]{0:T(1024)S(1)} %bitcast.328, s32[2048]{0:T(1024)S(1)} %bitcast.324, ...), kind=kOutput, calls=%fused_computation.351 | convolution fusion | flops 1473955712 | bytes 2073592 | tf_op jit(solution)/shard_map/dot_general | solution.py:87
  489.9 15.1 %fusion.252 = (bf16[83,4096]{1,0:T(8,128)(2,1)S(1)}, f32[83,4096]{1,0:T(8,128)}) fusion(s32[2048]{0:T(1024)S(1)} %bitcast.327, s32[2048]{0:T(1024)S(1)} %bitcast.329, s32[2048]{0:T(1024)S(1)} %bitcast.325, f32[83,2048]{1,0:T(8,128)S(1)} %get-tuple-element.245, f32[2048]{0:T(1024)S(1)} %bitcast.323, f32[83]{0:T(128)S(1)} %copy-done.157, f32[]{:T(128)S(6)} %div.228), kind=kOutput, calls=%fused_computation.608 | convolution fusion | flops 1469026304 | bytes 2752848 | tf_op jit(solution)/shard_map/dot_general | solution.py:362
  509.6 21.9 %all_gather.58 = f32[64,2048]{1,0:T(8,128)} all-gather(f32[64,512]{1,0:T(8,128)S(1)} %constant_dynamic-slice_fusion.2), channel_id=1, replica_groups=mesh['wide'=8,'narrow'=4] {'narrow'}, dimensions={1}, use_global_device_ids=true | all-gather | bytes 655360 | tf_op jit(solution)/shard_map/all_gather | solution.py:186
  545.3 8.3 convert_reduce_fusion
  574.9 9.8 fusion.104
  584.7 9.5 fusion.110
  594.2 9.5 fusion.116
  603.8 44.6 %fusion.9 = (f32[1024]{0:T(1024)S(1)}, f32[1024]{0:T(1024)S(1)}, f32[1024]{0:T(1024)S(1)}, f32[1024]{0:T(1024)S(1)}, f32[1024,4096]{1,0:T(8,128)}) fusion(bf16[1024,4096]{1,0:T(8,128)(2,1)S(1)} %bitcast.242, f32[1024]{0:T(1024)S(1)} %copy-done.120, f32[1024,4096]{1,0:T(8,128)} %get-tuple-element.219, f32[1024]{0:T(1024)S(1)} %copy-done.108, ...), kind=kOutput, calls=%fused_computation.38 | convolution fusion | flops 1161818112 | bytes 143966208 | tf_op jit(solution)/shard_map/dot_general | solution.py:87
  648.4 45.7 %fusion.10 = (bf16[1024,4096]{1,0:T(8,128)(2,1)}, bf16[1024,4096]{1,0:T(8,128)(2,1)}, bf16[1024,4096]{1,0:T(8,128)(2,1)}) fusion(bf16[1024,4096]{1,0:T(8,128)(2,1)} %get-tuple-element.114, f32[1024,4096]{1,0:T(8,128)} %get-tuple-element.232, f32[1024]{0:T(1024)S(1)} %get-tuple-element.84, f32[1024]{0:T(1024)S(1)} %copy-done.120, ...), kind=kLoop, calls=%fused_computation.39 | loop fusion | flops 104857600 | bytes 134254592 | tf_op jit(solution)/shard_map/convert_element_type | solution.py:409
  694.1 7.5 fusion.125
  716.4 14.3 %fusion.19 = bf16[1024,4096]{1,0:T(8,128)(2,1)} fusion(bf16[1024,4096]{1,0:T(8,128)(2,1)} %get-tuple-element.114, f32[1024,4096]{1,0:T(8,128)} %fusion.104, f32[1024]{0:T(1024)S(1)} %get-tuple-element.87, f32[1024]{0:T(1024)S(1)} %get-tuple-element.91, f32[1024,4096]{1,0:T(8,128)S(1)} %bitcast.236, f32[1024]{0:T(1024)S(1)} %get-tuple-element.224), kind=kLoop, calls=%fused_computation.48 | loop fusion | flops 37748736 | bytes 50343936 | tf_op jit(solution)/shard_map/convert_element_type | solution.py:409
  730.8 7.4 fusion.107
  757.5 11.8 fusion.38
  769.3 11.7 fusion.37
  781.0 12.2 fusion.36
  793.1 8.7 fusion.35
  801.8 8.5 fusion.256
  827.8 22.4 %convert_reduce_fusion.1 = (f32[512]{0:T(512)S(1)}, bf16[2048,512]{1,0:T(8,128)(2,1)}) fusion(f32[2048,512]{1,0:T(8,128)} %copy-done.12, f32[512]{0:T(512)S(1)} %copy-done.153, bf16[4096,512]{0,1:T(8,128)(2,1)} %multiply_convert_fusion.4, s32[2048]{0:T(1024)S(1)} %copy-done.143, s32[4096]{0:T(1024)S(1)} %bitcast.302, s32[4096]{0:T(1024)S(1)} %bitcast.310, ...), kind=kOutput, calls=%fused_computation.161 | convolution fusion | flops 8703180800 | bytes 10563584 | tf_op jit(solution)/shard_map/dot_general | solution.py:81
  850.3 21.5 %convert_reduce_fusion.2 = (f32[512]{0:T(512)S(1)}, bf16[2048,512]{1,0:T(8,128)(2,1)}) fusion(f32[2048,512]{1,0:T(8,128)S(1)} %copy-done.11, f32[512]{0:T(512)S(1)} %copy-done.153, bf16[4096,512]{0,1:T(8,128)(2,1)} %multiply_convert_fusion.4, s32[2048]{0:T(1024)S(1)} %copy-done.141, s32[4096]{0:T(1024)S(1)} %bitcast.303, s32[4096]{0:T(1024)S(1)} %bitcast.311, ...), kind=kOutput, calls=%fused_computation.162 | convolution fusion | flops 8703180800 | bytes 10563584 | tf_op jit(solution)/shard_map/dot_general | solution.py:81
  871.7 23.2 %convert_reduce_fusion.3 = (f32[512]{0:T(512)}, bf16[2048,512]{1,0:T(8,128)(2,1)}) fusion(f32[2048,512]{1,0:T(8,128)} %fusion.164, f32[512]{0:T(512)S(1)} %copy-done.153, bf16[4096,512]{0,1:T(8,128)(2,1)} %multiply_convert_fusion.4, s32[2048]{0:T(1024)S(1)} %copy-done.139, s32[4096]{0:T(1024)S(1)} %bitcast.304, s32[4096]{0:T(1024)S(1)} %bitcast.312, ...), kind=kOutput, calls=%fused_computation.163 | convolution fusion | flops 8703180800 | bytes 10563584 | tf_op jit(solution)/shard_map/dot_general | solution.py:81
  894.9 26.4 %convert_reduce_fusion.4 = (f32[512]{0:T(512)}, bf16[2048,512]{1,0:T(8,128)(2,1)}) fusion(f32[2048,512]{1,0:T(8,128)S(1)} %copy-done.13, f32[512]{0:T(512)S(1)} %copy-done.153, bf16[4096,512]{0,1:T(8,128)(2,1)} %multiply_convert_fusion.4, s32[4096]{0:T(1024)S(1)} %bitcast.305, s32[4096]{0:T(1024)S(1)} %bitcast.313, s32[4096]{0:T(1024)S(1)} %bitcast.321, ...), kind=kOutput, calls=%fused_computation.164 | convolution fusion | flops 8703180800 | bytes 10555392 | tf_op jit(solution)/shard_map/dot_general | solution.py:81
  955.9 7.9 concatenate.129
  1028.4 8.4 collective-permute-done.28
  1092.4 11.1 collective-permute-done.58
  1136.0 8.4 select_reduce_fusion.2
  1168.4 7.7 select_reduce_fusion.1
  1191.2 8.5 select_reduce_fusion
  (785 shorter events, 493.6 us)
Async XLA Ops:
  7.3 322.2 %all-gather.13.cloned.1.call-start = ((), (), s32[]{:S(2)}) async-start(), calls=%async_computation.1 | async-start | bytes 2359296 | tf_op jit(solution)/shard_map/all_gather | solution.py:187
  24.7 408.5 %all-gather.15.cloned.1.call-start = ((), (), s32[]{:S(2)}) async-start(), calls=%async_computation.2 | async-start | bytes 2359296 | tf_op jit(solution)/shard_map/all_gather | solution.py:187
  40.9 400.7 %all-gather.19.cloned.1.call-start = ((), (), s32[]{:S(2)}) async-start(), calls=%async_computation.4 | async-start | bytes 2359296 | tf_op jit(solution)/shard_map/all_gather | solution.py:189
  56.9 1056.8 %all-gather.21.cloned.1.call-start = ((), (), s32[]{:S(2)}) async-start(), calls=%async_computation.5 | async-start | bytes 4718592 | tf_op jit(solution)/shard_map/all_gather | solution.py:189
  72.7 1058.0 %all-gather.11.cloned.1.call-start = ((), (), s32[]{:S(2)}) async-start(), calls=%async_computation | async-start | bytes 4718592 | tf_op jit(solution)/shard_map/all_gather | solution.py:187
  72.7 132.7 %collective-permute-start.2 = (s32[4,1024]{1,0:T(4,128)}, s32[4,1024]{1,0:T(4,128)S(1)}, u32[]{:S(2)}, u32[]{:S(2)}) collective-permute-start(s32[4,1024]{1,0:T(4,128)} %bitcast.286), channel_id=1, source_target_pairs={{3,0},{0,1},{1,2},{2,3},{7,4},{4,5},{5,6},{6,7},{11,8},{8,9},{9,10... | collective-permute-start | bytes 49160 | tf_op jit(solution)/shard_map/ppermute | solution.py:136
  74.9 130.5 %collective-permute-start.1 = (s32[4,1024]{1,0:T(4,128)}, s32[4,1024]{1,0:T(4,128)S(1)}, u32[]{:S(2)}, u32[]{:S(2)}) collective-permute-start(s32[4,1024]{1,0:T(4,128)} %bitcast.287), channel_id=1, source_target_pairs={{2,0},{3,1},{0,2},{1,3},{6,4},{7,5},{4,6},{5,7},{10,8},{11,9},{8,1... | collective-permute-start | bytes 49160 | tf_op jit(solution)/shard_map/ppermute | solution.py:136
  77.4 128.0 %collective-permute-start = (s32[4,1024]{1,0:T(4,128)}, s32[4,1024]{1,0:T(4,128)S(1)}, u32[]{:S(2)}, u32[]{:S(2)}) collective-permute-start(s32[4,1024]{1,0:T(4,128)} %bitcast.288), channel_id=1, source_target_pairs={{1,0},{2,1},{3,2},{0,3},{5,4},{6,5},{7,6},{4,7},{9,8},{10,9},{11,1... | collective-permute-start | bytes 49160 | tf_op jit(solution)/shard_map/ppermute | solution.py:136
  83.5 122.1 %collective-permute-start.4 = (bf16[249,2048]{1,0:T(8,128)(2,1)}, bf16[249,2048]{1,0:T(8,128)(2,1)S(1)}, u32[]{:S(2)}, u32[]{:S(2)}) collective-permute-start(bf16[249,2048]{1,0:T(8,128)(2,1)} %pad_maximum_fusion.3), channel_id=1, source_target_pairs={{0,1},{1,2},{2,3},{4,5},{5,6},{6,7},{8,9},{9,10},{10,11},{12,13},{... | collective-permute-start | bytes 3059720 | tf_op jit(solution)/shard_map/ppermute | solution.py:149
  87.5 119.5 %collective-permute-start.3 = (bf16[249,2048]{1,0:T(8,128)(2,1)}, bf16[249,2048]{1,0:T(8,128)(2,1)S(1)}, u32[]{:S(2)}, u32[]{:S(2)}) collective-permute-start(bf16[249,2048]{1,0:T(8,128)(2,1)} %pad_maximum_fusion.3), channel_id=1, source_target_pairs={{1,0},{2,1},{3,2},{5,4},{6,5},{7,6},{9,8},{10,9},{11,10},{13,12},{... | collective-permute-start | bytes 3059720 | tf_op jit(solution)/shard_map/ppermute | solution.py:150
  117.1 1047.1 %all-gather.17.cloned.1.call-start = ((), (), s32[]{:S(2)}) async-start(), calls=%async_computation.3 | async-start | bytes 4718592 | tf_op jit(solution)/shard_map/all_gather | solution.py:187
  205.4 249.4 %collective-permute-start.9 = (f32[1,1]{1,0:T(1,128)}, f32[1,1]{1,0:T(1,128)}, u32[]{:S(2)}, u32[]{:S(2)}) collective-permute-start(f32[1,1]{1,0:T(1,128)} %bitcast.50), channel_id=1, source_target_pairs={{0,4},{4,0},{8,12},{12,8},{16,20},{20,16},{24,28},{28,24},{1,5},{5... | collective-permute-start | bytes 20 | tf_op jit(solution)/shard_map/ppermute | solution.py:94
  205.6 30.0 %collective-permute-start.5 = (bf16[249,2048]{1,0:T(8,128)(2,1)S(1)}, bf16[249,2048]{1,0:T(8,128)(2,1)S(1)}, u32[]{:S(2)}, u32[]{:S(2)}) collective-permute-start(bf16[249,2048]{1,0:T(8,128)(2,1)S(1)} %collective-permute-done.4), channel_id=1, source_target_pairs={{0,1},{1,2},{2,3},{4,5},{5,6},{6,7},{8,9},{9,10},{10,11},{12,13},{... | collective-permute-start | bytes 3059720 | tf_op jit(solution)/shard_map/ppermute | solution.py:149
  207.0 34.6 %collective-permute-start.7 = (bf16[249,2048]{1,0:T(8,128)(2,1)S(1)}, bf16[249,2048]{1,0:T(8,128)(2,1)}, u32[]{:S(2)}, u32[]{:S(2)}) collective-permute-start(bf16[249,2048]{1,0:T(8,128)(2,1)S(1)} %collective-permute-done.3), channel_id=1, source_target_pairs={{1,0},{2,1},{3,2},{5,4},{6,5},{7,6},{9,8},{10,9},{11,10},{13,12},{... | collective-permute-start | bytes 3059720 | tf_op jit(solution)/shard_map/ppermute | solution.py:150
  235.6 34.8 %collective-permute-start.6 = (bf16[249,2048]{1,0:T(8,128)(2,1)S(1)}, bf16[249,2048]{1,0:T(8,128)(2,1)}, u32[]{:S(2)}, u32[]{:S(2)}) collective-permute-start(bf16[249,2048]{1,0:T(8,128)(2,1)S(1)} %collective-permute-done.5), channel_id=1, source_target_pairs={{0,1},{1,2},{2,3},{4,5},{5,6},{6,7},{8,9},{9,10},{10,11},{12,13},{... | collective-permute-start | bytes 3059720 | tf_op jit(solution)/shard_map/ppermute | solution.py:149
  269.1 27.8 %collective-permute-start.8 = (bf16[249,2048]{1,0:T(8,128)(2,1)}, bf16[249,2048]{1,0:T(8,128)(2,1)}, u32[]{:S(2)}, u32[]{:S(2)}) collective-permute-start(bf16[249,2048]{1,0:T(8,128)(2,1)} %collective-permute-done.7), channel_id=1, source_target_pairs={{1,0},{2,1},{3,2},{5,4},{6,5},{7,6},{9,8},{10,9},{11,10},{13,12},{... | collective-permute-start | bytes 3059720 | tf_op jit(solution)/shard_map/ppermute | solution.py:150
  448.0 26.1 %collective-permute-start.16 = (bf16[83,1024]{1,0:T(8,128)(2,1)}, bf16[83,1024]{1,0:T(8,128)(2,1)}, u32[]{:S(2)}, u32[]{:S(2)}) collective-permute-start(bf16[83,1024]{1,0:T(8,128)(2,1)} %fusion.87), channel_id=1, source_target_pairs={{3,0},{0,1},{1,2},{2,3},{7,4},{4,5},{5,6},{6,7},{11,8},{8,9},{9,10... | collective-permute-start | bytes 509960 | tf_op jit(solution)/shard_map/ppermute | solution.py:136
  449.4 24.7 %collective-permute-start.15 = (bf16[83,1024]{1,0:T(8,128)(2,1)}, bf16[83,1024]{1,0:T(8,128)(2,1)}, u32[]{:S(2)}, u32[]{:S(2)}) collective-permute-start(bf16[83,1024]{1,0:T(8,128)(2,1)} %fusion.87), channel_id=1, source_target_pairs={{2,0},{3,1},{0,2},{1,3},{6,4},{7,5},{4,6},{5,7},{10,8},{11,9},{8,1... | collective-permute-start | bytes 509960 | tf_op jit(solution)/shard_map/ppermute | solution.py:136
  452.2 21.9 %collective-permute-start.14 = (bf16[83,1024]{1,0:T(8,128)(2,1)}, bf16[83,1024]{1,0:T(8,128)(2,1)}, u32[]{:S(2)}, u32[]{:S(2)}) collective-permute-start(bf16[83,1024]{1,0:T(8,128)(2,1)} %fusion.87), channel_id=1, source_target_pairs={{1,0},{2,1},{3,2},{0,3},{5,4},{6,5},{7,6},{4,7},{9,8},{10,9},{11,1... | collective-permute-start | bytes 509960 | tf_op jit(solution)/shard_map/ppermute | solution.py:136
  505.8 26.4 %collective-permute-start.17 = (bf16[83,1024]{1,0:T(8,128)(2,1)}, bf16[83,1024]{1,0:T(8,128)(2,1)S(1)}, u32[]{:S(2)}, u32[]{:S(2)}) collective-permute-start(bf16[83,1024]{1,0:T(8,128)(2,1)} %get-tuple-element.132), channel_id=1, source_target_pairs={{0,1},{1,2},{2,3},{3,0},{4,5},{5,6},{6,7},{7,4},{8,9},{9,10},{10,1... | collective-permute-start | bytes 509960 | tf_op jit(solution)/shard_map/ppermute | solution.py:165
  507.3 24.9 %collective-permute-start.19 = (bf16[83,1024]{1,0:T(8,128)(2,1)}, bf16[83,1024]{1,0:T(8,128)(2,1)S(1)}, u32[]{:S(2)}, u32[]{:S(2)}) collective-permute-start(bf16[83,1024]{1,0:T(8,128)(2,1)} %get-tuple-element.133), channel_id=1, source_target_pairs={{0,3},{1,0},{2,1},{3,2},{4,7},{5,4},{6,5},{7,6},{8,11},{9,8},{10,9... | collective-permute-start | bytes 509960 | tf_op jit(solution)/shard_map/ppermute | solution.py:165
  509.6 22.7 %collective-permute-start.18 = (bf16[83,1024]{1,0:T(8,128)(2,1)S(1)}, bf16[83,1024]{1,0:T(8,128)(2,1)S(1)}, u32[]{:S(2)}, u32[]{:S(2)}) collective-permute-start(bf16[83,1024]{1,0:T(8,128)(2,1)S(1)} %get-tuple-element.134), channel_id=1, source_target_pairs={{0,2},{1,3},{2,0},{3,1},{4,6},{5,7},{6,4},{7,5},{8,10},{9,11},{10,... | collective-permute-start | bytes 509960 | tf_op jit(solution)/shard_map/ppermute | solution.py:165
  927.3 79.1 %collective-permute-start.50 = (bf16[256,2048]{1,0:T(8,128)(2,1)}, bf16[256,2048]{1,0:T(8,128)(2,1)}, u32[]{:S(2)}, u32[]{:S(2)}) collective-permute-start(bf16[256,2048]{1,0:T(8,128)(2,1)} %dynamic-slice_convert_fusion.1), channel_id=1, source_target_pairs={{0,4},{4,0},{8,12},{12,8},{16,20},{20,16},{24,28},{28,24},{1,5},{5... | collective-permute-start | bytes 3145736 | tf_op jit(solution)/shard_map/ppermute | solution.py:94
  930.2 80.3 %collective-permute-start.60 = (bf16[1024,512]{1,0:T(8,128)(2,1)}, bf16[1024,512]{1,0:T(8,128)(2,1)}, u32[]{:S(2)}, u32[]{:S(2)}) collective-permute-start(bf16[1024,512]{1,0:T(8,128)(2,1)} %dynamic-slice_convert_fusion), channel_id=1, source_target_pairs={{0,4},{4,0},{8,12},{12,8},{16,20},{20,16},{24,28},{28,24},{1,5},{5... | collective-permute-start | bytes 3145736 | tf_op jit(solution)/shard_map/ppermute | solution.py:94
  931.7 8.9 collective-permute-start.40
  951.6 14.7 %collective-permute-start.43 = (bf16[32,512]{1,0:T(8,128)(2,1)}, bf16[32,512]{1,0:T(8,128)(2,1)}, u32[]{:S(2)}, u32[]{:S(2)}) collective-permute-start(bf16[32,512]{1,0:T(8,128)(2,1)} %dynamic-slice_convert_fusion.20), channel_id=1, source_target_pairs={{0,1},{1,0},{2,3},{3,2},{4,5},{5,4},{6,7},{7,6},{8,9},{9,8},{10,11... | collective-permute-start | bytes 98312 | tf_op jit(solution)/shard_map/ppermute | solution.py:94
  975.6 20.0 %collective-permute-start.30 = (bf16[256,1536]{1,0:T(8,128)(2,1)S(1)}, bf16[256,1536]{1,0:T(8,128)(2,1)S(1)}, u32[]{:S(2)}, u32[]{:S(2)}) collective-permute-start(bf16[256,1536]{1,0:T(8,128)(2,1)S(1)} %fusion.64), channel_id=1, source_target_pairs={{0,4},{4,0},{8,12},{12,8},{16,20},{20,16},{24,28},{28,24},{1,5},{5... | collective-permute-start | bytes 2359304 | tf_op jit(solution)/shard_map/ppermute | solution.py:94
  982.2 7.9 collective-permute-start.21
  991.6 14.0 %collective-permute-start.49 = (bf16[256,512]{1,0:T(8,128)(2,1)S(1)}, bf16[256,512]{1,0:T(8,128)(2,1)S(1)}, u32[]{:S(2)}, u32[]{:S(2)}) collective-permute-start(bf16[256,512]{1,0:T(8,128)(2,1)S(1)} %pad_maximum_fusion.13), channel_id=1, source_target_pairs={{0,4},{4,0},{8,12},{12,8},{16,20},{20,16},{24,28},{28,24},{1,5},{5... | collective-permute-start | bytes 786440 | tf_op jit(solution)/shard_map/ppermute | solution.py:94
  1000.9 14.0 %collective-permute-start.31 = (bf16[128,1536]{1,0:T(8,128)(2,1)S(1)}, bf16[128,1536]{1,0:T(8,128)(2,1)S(1)}, u32[]{:S(2)}, u32[]{:S(2)}) collective-permute-start(bf16[128,1536]{1,0:T(8,128)(2,1)S(1)} %dynamic-slice_convert_fusion.4), channel_id=1, source_target_pairs={{0,8},{4,12},{8,0},{12,4},{16,24},{20,28},{24,16},{28,20},{1,9},{5... | collective-permute-start | bytes 1179656 | tf_op jit(solution)/shard_map/ppermute | solution.py:94
  1008.2 31.0 %collective-permute-start.51 = (bf16[128,2048]{1,0:T(8,128)(2,1)S(1)}, bf16[128,2048]{1,0:T(8,128)(2,1)S(1)}, u32[]{:S(2)}, u32[]{:S(2)}) collective-permute-start(bf16[128,2048]{1,0:T(8,128)(2,1)S(1)} %dynamic-slice_convert_fusion.3), channel_id=1, source_target_pairs={{0,8},{4,12},{8,0},{12,4},{16,24},{20,28},{24,16},{28,20},{1,9},{5... | collective-permute-start | bytes 1572872 | tf_op jit(solution)/shard_map/ppermute | solution.py:94
  1012.2 30.9 %collective-permute-start.61 = (bf16[512,512]{1,0:T(8,128)(2,1)S(1)}, bf16[512,512]{1,0:T(8,128)(2,1)S(1)}, u32[]{:S(2)}, u32[]{:S(2)}) collective-permute-start(bf16[512,512]{1,0:T(8,128)(2,1)S(1)} %dynamic-slice_convert_fusion.2), channel_id=1, source_target_pairs={{0,8},{4,12},{8,0},{12,4},{16,24},{20,28},{24,16},{28,20},{1,9},{5... | collective-permute-start | bytes 1572872 | tf_op jit(solution)/shard_map/ppermute | solution.py:94
  1022.4 14.4 %collective-permute-start.28 = (f32[128,512]{1,0:T(8,128)S(1)}, f32[128,512]{1,0:T(8,128)S(1)}, u32[]{:S(2)}, u32[]{:S(2)}) collective-permute-start(f32[128,512]{1,0:T(8,128)S(1)} %pad_maximum_fusion.12), channel_id=1, source_target_pairs={{0,8},{4,12},{8,0},{12,4},{16,24},{20,28},{24,16},{28,20},{1,9},{5... | collective-permute-start | bytes 786440 | tf_op jit(solution)/shard_map/ppermute | solution.py:94
  1026.1 10.8 collective-permute-start.34
  1036.9 25.7 %collective-permute-start.29 = (f32[256,512]{1,0:T(8,128)S(1)}, f32[256,512]{1,0:T(8,128)S(1)}, u32[]{:S(2)}, u32[]{:S(2)}) collective-permute-start(f32[256,512]{1,0:T(8,128)S(1)} %pad_maximum_fusion.8), channel_id=1, source_target_pairs={{0,4},{4,0},{8,12},{12,8},{16,20},{20,16},{24,28},{28,24},{1,5},{5... | collective-permute-start | bytes 1572872 | tf_op jit(solution)/shard_map/ppermute | solution.py:94
  1039.4 9.2 collective-permute-start.52
  1043.3 11.0 collective-permute-start.62
  1047.9 9.8 collective-permute-start.37
  1048.7 10.6 collective-permute-start.53
  1057.8 25.2 %collective-permute-start.38 = (bf16[128,1536]{1,0:T(8,128)(2,1)S(1)}, bf16[128,1536]{1,0:T(8,128)(2,1)S(1)}, u32[]{:S(2)}, u32[]{:S(2)}) collective-permute-start(bf16[128,1536]{1,0:T(8,128)(2,1)S(1)} %pad_maximum_fusion.11), channel_id=1, source_target_pairs={{0,8},{4,12},{8,0},{12,4},{16,24},{20,28},{24,16},{28,20},{1,9},{5... | collective-permute-start | bytes 1179656 | tf_op jit(solution)/shard_map/ppermute | solution.py:94
  1067.2 8.1 collective-permute-start.55
  1080.8 8.1 collective-permute-start.57
  1082.2 9.5 collective-permute-start.67
  1089.0 14.5 %collective-permute-start.58 = (bf16[128,2048]{1,0:T(8,128)(2,1)S(1)}, bf16[128,2048]{1,0:T(8,128)(2,1)S(1)}, u32[]{:S(2)}, u32[]{:S(2)}) collective-permute-start(bf16[128,2048]{1,0:T(8,128)(2,1)S(1)} %pad_maximum_fusion.9), channel_id=1, source_target_pairs={{0,8},{4,12},{8,0},{12,4},{16,24},{20,28},{24,16},{28,20},{1,9},{5... | collective-permute-start | bytes 1572872 | tf_op jit(solution)/shard_map/ppermute | solution.py:94
  1089.7 21.3 %collective-permute-start.39 = (bf16[256,1536]{1,0:T(8,128)(2,1)S(1)}, bf16[256,1536]{1,0:T(8,128)(2,1)S(1)}, u32[]{:S(2)}, u32[]{:S(2)}) collective-permute-start(bf16[256,1536]{1,0:T(8,128)(2,1)S(1)} %pad_maximum_fusion.7), channel_id=1, source_target_pairs={{0,4},{4,0},{8,12},{12,8},{16,20},{20,16},{24,28},{28,24},{1,5},{5... | collective-permute-start | bytes 2359304 | tf_op jit(solution)/shard_map/ppermute | solution.py:94
  1091.8 17.7 %collective-permute-start.68 = (bf16[512,512]{1,0:T(8,128)(2,1)S(1)}, bf16[512,512]{1,0:T(8,128)(2,1)S(1)}, u32[]{:S(2)}, u32[]{:S(2)}) collective-permute-start(bf16[512,512]{1,0:T(8,128)(2,1)S(1)} %pad_maximum_fusion.10), channel_id=1, source_target_pairs={{0,8},{4,12},{8,0},{12,4},{16,24},{20,28},{24,16},{28,20},{1,9},{5... | collective-permute-start | bytes 1572872 | tf_op jit(solution)/shard_map/ppermute | solution.py:94
  1104.9 13.6 %collective-permute-start.59 = (bf16[256,2048]{1,0:T(8,128)(2,1)}, bf16[256,2048]{1,0:T(8,128)(2,1)}, u32[]{:S(2)}, u32[]{:S(2)}) collective-permute-start(bf16[256,2048]{1,0:T(8,128)(2,1)} %pad_maximum_fusion.5), channel_id=1, source_target_pairs={{0,4},{4,0},{8,12},{12,8},{16,20},{20,16},{24,28},{28,24},{1,5},{5... | collective-permute-start | bytes 3145736 | tf_op jit(solution)/shard_map/ppermute | solution.py:94
  1110.8 12.5 collective-permute-start.69
  (208 other events, 3974.8 us)
Sparse Core Ops, SparseCore 0:
  24.8 29.4 all-gather.12
  56.2 27.8 all-gather.14
  86.1 27.8 all-gather.18
  115.7 36.7 all-gather.20
  154.2 36.7 all-gather.10
  531.6 38.7 all-gather.16

commit v2 on v1

--- a/solution.py
+++ b/solution.py
@@ -1,8 +1,11 @@
+import functools
 import math
 
 import jax
 import jax.numpy as jnp
 from jax import lax
+from jax.experimental import pallas as pl
+from jax.experimental.pallas import tpu as pltpu
 from jax.sharding import PartitionSpec as P
 
 LATENT_WIDTH = 512
@@ -109,23 +112,56 @@
     return values
 
 
+def sum_stages():
+    wide_bits = len(axis_bits("wide"))
+    stages = [("wide", 0, 1)]
+    first = 1
+    while first < wide_bits:
+        stages.append(("wide", first, min(2, wide_bits - first)))
+        first += 2
+    stages.append(("narrow", 0, len(axis_bits("narrow"))))
+    return stages
+
+
+def partner_swap(values, axis_name, distance):
+    size = lax.axis_size(axis_name)
+    return lax.ppermute(values, axis_name, [(i, i ^ distance) for i in range(size)])
+
+
 def large_sum(values, sent_type):
-    steps = axis_bits("wide") + axis_bits("narrow")
-    for axis_name, bit in steps:
-        half = values.shape[0] // 2
-        mine = (lax.axis_index(axis_name) >> bit) & 1
-        kept = lax.dynamic_slice_in_dim(values, mine * half, half, 0)
-        sent = lax.dynamic_slice_in_dim(values, (1 - mine) * half, half, 0)
-        values = kept + bit_swap(sent.astype(sent_type), axis_name, bit).astype(jnp.float32)
+    stages = sum_stages()
+    for axis_name, first, width in stages:
+        members = 1 << width
+        block = values.shape[0] // members
+        mine = (lax.axis_index(axis_name) >> first) & (members - 1)
+        arrived = [
+            partner_swap(
+                lax.dynamic_slice_in_dim(values, (mine ^ far) * block, block, 0).astype(sent_type),
+                axis_name,
+                far << first,
+            )
+            for far in range(1, members)
+        ]
+        values = lax.dynamic_slice_in_dim(values, mine * block, block, 0)
+        for piece in arrived:
+            values = values + piece.astype(jnp.float32)
     values = values.astype(sent_type)
-    for axis_name, bit in steps[::-1]:
-        mine = (lax.axis_index(axis_name) >> bit) & 1
-        other = bit_swap(values, axis_name, bit)
-        is_high = mine == 1
-        values = jnp.concatenate(
-            [jnp.where(is_high, other, values), jnp.where(is_high, values, other)], axis=0
-        )
-    return values.astype(jnp.float32)
+    for axis_name, first, width in stages[::-1]:
+        members = 1 << width
+        block = values.shape[0]
+        mine = (lax.axis_index(axis_name) >> first) & (members - 1)
+        pieces = [values] + [
+            partner_swap(values, axis_name, far << first) for far in range(1, members)
+        ]
+        for bit in range(width):
+            is_high = ((mine >> bit) & 1) == 1
+            step = 1 << bit
+            pieces = [
+                jnp.where(is_high, pieces[place ^ step], pieces[place])
+                for place in range(members)
+            ]
+        values = jnp.concatenate(pieces, axis=0)
+    return values
 
 
 def ring_slots(values):
@@ -141,13 +177,13 @@
 def line_slots(values):
     size = lax.axis_size("narrow")
     pos = lax.axis_index("narrow")
-    up = [(i, i + 1) for i in range(size - 1)]
-    down = [(i + 1, i) for i in range(size - 1)]
     from_low, from_high = values, values
     low_list, high_list = [], []
-    for _ in range(size - 1):
-        from_low = lax.ppermute(from_low, "narrow", up)
-        from_high = lax.ppermute(from_high, "narrow", down)
+    for step in range(size - 1):
+        from_low = lax.ppermute(from_low, "narrow", [(i, i + 1) for i in range(step, size - 1)])
+        from_high = lax.ppermute(
+            from_high, "narrow", [(i, i - 1) for i in range(1, size - step)]
+        )
         low_list.append(from_low)
         high_list.append(from_high)
     slots = [values]
@@ -171,23 +207,208 @@
     return total
 
 
-def count_matrix(index_rows, first, column_count):
-    columns = first + jnp.arange(column_count, dtype=jnp.int32)[None, :]
-    total = jnp.zeros((index_rows.shape[0], column_count), jnp.float32)
-    for slot in range(index_rows.shape[1]):
-        total = total + (index_rows[:, slot : slot + 1] == columns).astype(jnp.float32)
-    return total.astype(jnp.bfloat16)
-
-
-def wide_gather(block, axis):
-    rows = block.shape[0] // lax.axis_size("wide")
-    own = lax.dynamic_slice_in_dim(block, lax.axis_index("wide") * rows, rows, 0)
-    if axis == 1:
-        across = lax.all_gather(own, "narrow", axis=1, tiled=True)
-        return lax.all_gather(across, "wide", axis=0, tiled=True)
+def wide_gather(blocks):
+    wide_count = lax.axis_size("wide")
+    own = []
+    for block in blocks:
+        rows = block.shape[0] // wide_count
+        own.append(lax.dynamic_slice_in_dim(block, lax.axis_index("wide") * rows, rows, 0))
+    own = jnp.stack(own)
     across = lax.all_gather(own, "narrow", axis=0)
-    whole = lax.all_gather(across, "wide", axis=1)
-    return whole.reshape(-1, block.shape[1])
+    whole = lax.all_gather(across, "wide", axis=0)
+    side = whole[:, :, :-1].transpose(2, 0, 3, 1, 4)
+    side = side.reshape(side.shape[0], blocks[0].shape[0], -1)
+    last = whole[:, :, -1].transpose(1, 0, 2, 3).reshape(-1, blocks[-1].shape[1])
+    return [side[place] for place in range(side.shape[0])] + [last]
+
+
+VMEM_LIMIT = 60 * 1024 * 1024
+SCORE_SCALE = math.log2(math.e) / math.sqrt(HEAD_WIDTH)
+MASKED = -1e30
+
+
+def kernel_params():
+    return pltpu.CompilerParams(vmem_limit_bytes=VMEM_LIMIT)
+
+
+def count_kernel(ids_ref, out_ref):
+    first = pl.program_id(0) * out_ref.shape[1]
+    columns = lax.broadcasted_iota(jnp.int32, out_ref.shape, 1).astype(jnp.int16)
+    ids = (ids_ref[...] - first).astype(jnp.int16)
+    one = jnp.ones(out_ref.shape, jnp.bfloat16)
+    zero = jnp.zeros(out_ref.shape, jnp.bfloat16)
+    total = zero
+    for slot in range(ids.shape[1]):
+        total = total + jnp.where(ids[:, slot : slot + 1] == columns, one, zero)
+    out_ref[...] = total
+
+
+def count_matrix(ids, column_count, rows=1024, columns=2048):
+    row_count, slots = ids.shape
+    rows = min(rows, row_count)
+    columns = min(columns, column_count)
+    return pl.pallas_call(
+        count_kernel,
+        grid=(column_count // columns, row_count // rows),
+        in_specs=[pl.BlockSpec((rows, slots), lambda j, i: (i, 0))],
+        out_specs=pl.BlockSpec((rows, columns), lambda j, i: (i, j)),
+        out_shape=jax.ShapeDtypeStruct((row_count, column_count), jnp.bfloat16),
+        cost_estimate=pl.CostEstimate(
+            flops=4 * slots * row_count * column_count,
+            bytes_accessed=2 * row_count * column_count,
+            transcendentals=0,
+        ),
+        compiler_params=kernel_params(),
+    )(ids)
+
+
+def bias_kernel(row_ref, lane_ref, out_ref):
+    groups, width = row_ref.shape
+    blocks = out_ref.shape[1] // 128
+    row_iota = lax.broadcasted_iota(jnp.int32, (8 * blocks, width), 0)
+    lane_iota = lax.broadcasted_iota(jnp.int32, (128, width), 0)
+    for group in range(groups):
+        left = jnp.where(row_iota == row_ref[group : group + 1, :], 1.0, 0.0)
+        right = jnp.where(lane_iota == lane_ref[group : group + 1, :], 1.0, 0.0)
+        counts = contract_last(left.astype(jnp.bfloat16), right.astype(jnp.bfloat16))
+        bias = jnp.where(counts > 0.5, jnp.log2(counts), MASKED)
+        for block in range(blocks):
+            out_ref[group * 8 : (group + 1) * 8, block * 128 : (block + 1) * 128] = bias[
+                block * 8 : (block + 1) * 8, :
+            ]
+
+
+def count_bias(ids, total, per_step=32):
+    row_count, slots = ids.shape
+    groups = row_count // 8
+    member = (jnp.arange(row_count, dtype=jnp.int32) % 8)[:, None]
+    row_keys = ((ids // 128) * 8 + member).reshape(groups, 8 * slots)
+    lane_keys = (ids % 128).reshape(groups, 8 * slots)
+    spec = pl.BlockSpec((per_step, 8 * slots), lambda i: (i, 0))
+    return pl.pallas_call(
+        bias_kernel,
+        grid=(groups // per_step,),
+        in_specs=[spec, spec],
+        out_specs=pl.BlockSpec((8 * per_step, total), lambda i: (i, 0)),
+        out_shape=jax.ShapeDtypeStruct((row_count, total), jnp.float32),
+        cost_estimate=pl.CostEstimate(
+            flops=16 * row_count * total, bytes_accessed=4 * row_count * total, transcendentals=0
+        ),
+        compiler_params=kernel_params(),
+    )(row_keys, lane_keys)
+
+
+def attend_kernel(chunk, q_ref, k_ref, v_ref, bias_ref, att_ref, mass_ref, score_ref):
+    q = q_ref[...]
+    total = k_ref.shape[0]
+    top = None
+    for start in range(0, total, chunk):
+        part = pl.ds(start, chunk)
+        scores = contract_last(q, k_ref[part, :]) * SCORE_SCALE + bias_ref[:, part]
+        score_ref[:, part] = scores
+        highest = jnp.max(scores, axis=1, keepdims=True)
+        top = highest if top is None else jnp.maximum(top, highest)
+    mass = jnp.zeros((q.shape[0], 1), jnp.float32)
+    attended = jnp.zeros(att_ref.shape, jnp.float32)
+    for start in range(0, total, chunk):
+        part = pl.ds(start, chunk)
+        raised = jnp.exp2(score_ref[:, part] - top)
+        mass = mass + jnp.sum(raised, axis=1, keepdims=True)
+        attended = attended + jnp.dot(
+            raised.astype(jnp.bfloat16), v_ref[part, :], preferred_element_type=jnp.float32
+        )
+    att_ref[...] = attended / mass
+    mass_ref[...] = jnp.broadcast_to(top + jnp.log2(mass), mass_ref.shape)
+
+
+def attend(queries, pairs, bias, rows=256, chunk=512):
+    row_count = queries.shape[0]
+    total = pairs.shape[0]
+    block = pl.BlockSpec((rows, HEAD_WIDTH), lambda h, r: (r, h))
+    return pl.pallas_call(
+        functools.partial(attend_kernel, chunk),
+        grid=(HEADS, row_count // rows),
+        in_specs=[
+            block,
+            pl.BlockSpec((total, HEAD_WIDTH), lambda h, r: (0, h)),
+            pl.BlockSpec((total, HEAD_WIDTH), lambda h, r: (0, HEADS + h)),
+            pl.BlockSpec((rows, total), lambda h, r: (r, 0)),
+        ],
+        out_specs=[block, block],
+        out_shape=[jax.ShapeDtypeStruct(queries.shape, jnp.float32)] * 2,
+        scratch_shapes=[pltpu.VMEM((rows, total), jnp.float32)],
+        cost_estimate=pl.CostEstimate(
+            flops=16 * row_count * total * HEAD_WIDTH * HEADS,
+            bytes_accessed=16 * row_count * total,
+            transcendentals=HEADS * row_count * total,
+        ),
+        compiler_params=kernel_params(),
+    )(queries, pairs, pairs, bias)
+
+
+def attend_back_kernel(
+    chunk, q_ref, k_ref, v_ref, bias_ref, mass_ref, att_ref, g_ref, dq_ref, dk_ref, dv_ref, dk_sum, dv_sum
+):
+    step = pl.program_id(1)
+    q = q_ref[...]
+    g = g_ref[...]
+    total = k_ref.shape[0]
+    mass = mass_ref[:, :1]
+    inner = jnp.sum(att_ref[...] * g.astype(jnp.float32), axis=1, keepdims=True)
+
+    @pl.when(step == 0)
+    def _():
+        dk_sum[...] = jnp.zeros_like(dk_sum)
+        dv_sum[...] = jnp.zeros_like(dv_sum)
+
+    dq = jnp.zeros(q.shape, jnp.float32)
+    for start in range(0, total, chunk):
+        part = pl.ds(start, chunk)
+        k = k_ref[part, :]
+        v = v_ref[part, :]
+        prob = jnp.exp2(contract_last(q, k) * SCORE_SCALE + (bias_ref[:, part] - mass))
+        grad_scores = (prob * (contract_last(g, v) - inner)).astype(jnp.bfloat16)
+        dq = dq + jnp.dot(grad_scores, k, preferred_element_type=jnp.float32)
+        dk_sum[part, :] += contract_rows(grad_scores, q)
+        dv_sum[part, :] += contract_rows(prob.astype(jnp.bfloat16), g)
+    shrink = 1.0 / math.sqrt(HEAD_WIDTH)
+    dq_ref[...] = (dq * shrink).astype(jnp.bfloat16)
+
+    @pl.when(step == pl.num_programs(1) - 1)
+    def _():
+        dk_ref[...] = (dk_sum[...] * shrink).astype(jnp.bfloat16)
+        dv_ref[...] = dv_sum[...].astype(jnp.bfloat16)
+
+
+def attend_back(queries, pairs, bias, mass, attended, grads, rows=1024, chunk=256):
+    row_count = queries.shape[0]
+    total = pairs.shape[0]
+    rows = min(rows, row_count)
+    block = pl.BlockSpec((rows, HEAD_WIDTH), lambda h, r: (r, h))
+    column = pl.BlockSpec((total, HEAD_WIDTH), lambda h, r: (0, h))
+    key_shape = jax.ShapeDtypeStruct((total, LATENT_WIDTH), jnp.bfloat16)
+    return pl.pallas_call(
+        functools.partial(attend_back_kernel, chunk),
+        grid=(HEADS, row_count // rows),
+        in_specs=[
+            block,
+            column,
+            pl.BlockSpec((total, HEAD_WIDTH), lambda h, r: (0, HEADS + h)),
+            pl.BlockSpec((rows, total), lambda h, r: (r, 0)),
+            block,
+            block,
+            block,
+        ],
+        out_specs=[block, column, column],
+        out_shape=[jax.ShapeDtypeStruct(queries.shape, jnp.bfloat16), key_shape, key_shape],
+        scratch_shapes=[pltpu.VMEM((total, HEAD_WIDTH), jnp.float32)] * 2,
+        cost_estimate=pl.CostEstimate(
+            flops=24 * row_count * total * HEAD_WIDTH * HEADS,
+            bytes_accessed=16 * row_count * total,
+            transcendentals=HEADS * row_count * total,
+        ),
+        compiler_params=kernel_params(),
+    )(queries, pairs, pairs, bias, mass, attended, grads)
 
 
 def high_dot(left, right):
@@ -271,14 +492,11 @@
     features = jnp.concatenate(
         [prior_states[0, 0], prior_states[0, 1], (scale_in * noisy).astype(jnp.bfloat16)], axis=0
     )
+    g2m_slots = ring_slots(g2m_edges[0].T)
     feature_slots = line_slots(features)
-    g2m_slots = ring_slots(g2m_edges[0].T)
-    attn_full = wide_gather(w_attn.astype(jnp.bfloat16), 1)
-    up_full = wide_gather(w_up.astype(jnp.bfloat16), 1)
-    down_full = wide_gather(w_down.astype(jnp.bfloat16), 0)
-    mom_attn_full = wide_gather(mom_attn, 1)
-    mom_up_full = wide_gather(mom_up, 1)
-    mom_down_full = wide_gather(mom_down, 0)
+    attn_full, up_full, down_full = wide_gather(
+        [w_attn.astype(jnp.bfloat16), w_up.astype(jnp.bfloat16), w_down.astype(jnp.bfloat16)]
+    )
     lat_weight = lat_weights(narrow_pos * pixel_local, pixel_local, pixel_total)
     pixel_weight = lat_weight * valid_mask[0].astype(jnp.float32)
     weight_total = small_sum(jnp.sum(pixel_weight).reshape(1, 1))[0, 0]
@@ -287,11 +505,11 @@
     g2m_ids = g2m_ids.T
     near_ids = (neighbours[0] - narrow_pos * node_local) % node_total
     m2g_ids = (m2g_edges[0] - narrow_pos * node_local) % node_total
+    near_bias = count_bias(near_ids, node_total)
+    m2g_counts = count_matrix(m2g_ids, node_total)
     g2m_counts = [
-        count_matrix(g2m_ids, slot * pixel_local, pixel_local) for slot in range(narrow_count)
+        count_matrix(g2m_ids - slot * pixel_local, pixel_local) for slot in range(narrow_count)
     ]
-    near_counts = count_matrix(near_ids, 0, node_total)
-    m2g_counts = count_matrix(m2g_ids, 0, node_total)
 
     embed_pres = []
     node_in = None
@@ -320,24 +538,10 @@
     pair_rows = jnp.dot(attn_in, pair_map, preferred_element_type=jnp.float32).astype(
         jnp.bfloat16
     )
-    key_rows = pair_rows[:, :LATENT_WIDTH]
-    value_rows = pair_rows[:, LATENT_WIDTH:]
-
-    counts = near_counts.astype(jnp.float32)
-    attended_heads = []
-    prob_heads = []
-    for head in range(HEADS):
-        part = slice(head * HEAD_WIDTH, (head + 1) * HEAD_WIDTH)
-        scores = contract_last(query_rows[:, part], key_rows[:, part]) / math.sqrt(HEAD_WIDTH)
-        scores = jnp.where(counts > 0, scores, -jnp.inf)
-        raised = jnp.exp(scores - jnp.max(scores, axis=1, keepdims=True))
-        prob = raised / jnp.sum(raised * counts, axis=1, keepdims=True)
-        lowered = (prob.astype(jnp.bfloat16).astype(jnp.float32) * counts).astype(jnp.bfloat16)
-        prob_heads.append((prob, lowered))
-        attended_heads.append(
-            jnp.dot(lowered, value_rows[:, part], preferred_element_type=jnp.float32)
-        )
-    attended_rows = jnp.concatenate(attended_heads, axis=1).astype(jnp.bfloat16)
+    attended, mass = attend(query_rows, pair_rows, near_bias)
+    attended_rows = attended.astype(jnp.bfloat16)
+    mom_blocks, _ = lax.optimization_barrier(((mom_attn, mom_up, mom_down), attended))
+    mom_attn_full, mom_up_full, mom_down_full = wide_gather(mom_blocks)
     node_mid = node_in[:node_local] + jnp.dot(
         attended_rows, proj_map, preferred_element_type=jnp.float32
     )
@@ -391,39 +595,25 @@
     grad_node_mid = grad_node_out + norm_back(grad_mlp_in * gain_two, normed_two, inverse_two)
     grad_proj_out = grad_node_mid.astype(jnp.bfloat16)
     grad_proj = contract_rows(attended_rows, grad_proj_out)
-    sum_down = large_sum(grad_down, jnp.bfloat16)
-    sum_up = large_sum(grad_up, jnp.bfloat16)
-    sum_proj = large_sum(grad_proj, jnp.bfloat16)
+    sum_down = large_sum(grad_down, jnp.bfloat16).astype(jnp.float32)
+    sum_up = large_sum(grad_up, jnp.bfloat16).astype(jnp.float32)
+    sum_proj = large_sum(grad_proj, jnp.bfloat16).astype(jnp.float32)
     gradient_attended = contract_last(grad_proj_out, proj_map).astype(jnp.bfloat16)
 
-    query_grads, key_grads, value_grads = [], [], []
-    for head in range(HEADS):
-        part = slice(head * HEAD_WIDTH, (head + 1) * HEAD_WIDTH)
-        prob, lowered = prob_heads[head]
-        grad_head = gradient_attended[:, part]
-        grad_prob = contract_last(grad_head, value_rows[:, part])
-        weighted_prob = prob * counts
-        inner = jnp.sum(weighted_prob * grad_prob, axis=1, keepdims=True)
-        grad_scores = (
-            (prob * (grad_prob - inner)).astype(jnp.bfloat16).astype(jnp.float32) * counts
-        ).astype(jnp.bfloat16)
-        query_grads.append(
-            jnp.dot(grad_scores, key_rows[:, part], preferred_element_type=jnp.float32)
-        )
-        key_grads.append(contract_rows(grad_scores, query_rows[:, part]))
-        value_grads.append(contract_rows(lowered, grad_head))
-    grad_query_rows = (jnp.concatenate(query_grads, axis=1) / math.sqrt(HEAD_WIDTH)).astype(
-        jnp.bfloat16
-    )
-    grad_pair_rows = jnp.concatenate(
-        [jnp.concatenate(key_grads, axis=1) / math.sqrt(HEAD_WIDTH)] + value_grads, axis=1
-    ).astype(jnp.bfloat16)
-
+    grad_query_rows, grad_key_rows, grad_value_rows = attend_back(
+        query_rows, pair_rows, near_bias, mass, attended, gradient_attended
+    )
     grad_qkv = jnp.concatenate(
-        [contract_rows(attn_own, grad_query_rows), contract_rows(attn_in, grad_pair_rows)], axis=1
-    )
-    sum_qkv = large_sum(grad_qkv, jnp.bfloat16)
-    grad_attn_in = contract_last(grad_pair_rows, pair_map)
+        [
+            contract_rows(attn_own, grad_query_rows),
+            contract_rows(attn_in, grad_key_rows),
+            contract_rows(attn_in, grad_value_rows),
+        ],
+        axis=1,
+    )
+    sum_qkv = large_sum(grad_qkv, jnp.bfloat16).astype(jnp.float32)
+    grad_attn_in = contract_last(grad_key_rows, pair_map[:, :LATENT_WIDTH])
+    grad_attn_in = grad_attn_in + contract_last(grad_value_rows, pair_map[:, LATENT_WIDTH:])
     grad_attn_in = grad_attn_in.at[:node_local].add(contract_last(grad_query_rows, query_map))
     grad_node_in = norm_back(grad_attn_in * gain_one, normed_one, inverse_one)
     grad_node_in = grad_node_in.at[:node_local].add(grad_node_mid)
@@ -447,18 +637,36 @@
         grad_embed = embed_part if grad_embed is None else grad_embed + embed_part
         grad_embed_bias = bias_part if grad_embed_bias is None else grad_embed_bias + bias_part
 
-    grad_bias = jnp.concatenate([grad_embed_bias, grad_up_bias, grad_out_bias])
-    pieces = [grad_embed, grad_cond, grad_dec, grad_bias, loss_local]
-    flat = jnp.concatenate([piece.reshape(-1) for piece in pieces])
-    row_total = -(-flat.shape[0] // (LATENT_WIDTH * 256)) * 256
-    flat = jnp.pad(flat, (0, row_total * LATENT_WIDTH - flat.shape[0]))
-    flat = large_sum(flat.reshape(row_total, LATENT_WIDTH), jnp.float32).reshape(-1)
-    sums = []
-    place = 0
-    for piece in pieces:
-        sums.append(flat[place : place + piece.size].reshape(piece.shape))
-        place += piece.size
-    sum_embed, sum_cond, sum_dec, sum_bias, loss_sum = sums
+    width = LATENT_WIDTH
+    channels = w_dec.shape[1]
+    late_rows = jnp.concatenate(
+        [
+            grad_embed,
+            grad_embed_bias.reshape(1, width),
+            grad_up_bias.reshape(FF // width, width),
+            jnp.pad(
+                jnp.concatenate([grad_out_bias, loss_local.reshape(1)]), (0, width - channels - 1)
+            ).reshape(1, width),
+            grad_dec.T,
+        ]
+        + [grad_cond[:, place * width : (place + 1) * width] for place in range(4)],
+        axis=0,
+    )
+    device_count = lax.axis_size("wide") * narrow_count
+    late_rows = jnp.pad(late_rows, ((0, -late_rows.shape[0] % (2 * device_count)), (0, 0)))
+    late_rows = large_sum(late_rows, jnp.float32)
+    embed_rows = w_embed.shape[0]
+    sum_embed = late_rows[:embed_rows]
+    place = embed_rows
+    bias_rows = late_rows[place : place + 2 + FF // width].reshape(-1)
+    sum_bias = bias_rows[: biases.shape[0]]
+    loss_sum = bias_rows[biases.shape[0]]
+    place += 2 + FF // width
+    sum_dec = late_rows[place : place + channels].T
+    place += channels
+    sum_cond = jnp.concatenate(
+        [late_rows[place + COND * part : place + COND * (part + 1)] for part in range(4)], axis=1
+    )
     sum_attn = jnp.concatenate([sum_qkv, sum_proj], axis=1)
     square_sum = (
         jnp.sum(sum_embed * sum_embed)

time: 1320 us -> 1260 us (0.955)
  matrix products: 696 us -> 402 us
  waiting for transfers between devices: 94.4 us -> 254 us
  Pallas kernels: 0 us -> 156 us
  other arithmetic: 236 us -> 103 us
  blocking collectives: 111 us -> 36.7 us
  local copies, waits for them, and re-layouts: 52.6 us -> 126 us
  starting transfers between devices: 86.3 us -> 145 us
    ppermute x6 -> x76, waiting for transfers between devices: 0.02 us -> 237 us  [the longest x70 233 us: partner_swap(): lax.ppermute(values, axis_name, [(i, i ^ distance) for i in range(size)])]
    pallas_call x0 -> x8, Pallas kernels: none -> 156 us  [the longest x1 54.8 us: attend_back(): pl.pallas_call(functools.partial(attend_back_kernel, chunk), grid=(HEADS,...]
    ppermute x6 -> x76, starting transfers between devices: 15.4 us -> 118 us  [the longest x70 106 us: partner_swap(): lax.ppermute(values, axis_name, [(i, i ^ distance) for i in range(size)])]
    dot_general x21 -> x14, matrix products: 194 us -> 91.6 us  [contract_rows(): lax.dot_general(left, right, (((0,), (0,)), ((), ())), preferred_element_...]
    dot_general x14 -> x7, matrix products: 140 us -> 38.1 us  [contract_last(): lax.dot_general(left, right, (((1,), (1,)), ((), ())), preferred_element_...]
    ppermute x55 -> x5, waiting for transfers between devices: 94.1 us -> 5.15 us  [bit_swap(): lax.ppermute(values, axis_name, [(i, i ^ 1 << bit) for i in range(size)])]
    all_gather x4 -> x0, blocking collectives: 80.8 us -> none  [wide_gather(): across = lax.all_gather(own, 'narrow', axis=1, tiled=True)]
    gt x1 -> x0, other arithmetic: 80.6 us -> none  [on_device(): scores = jnp.where(counts > 0, scores, -jnp.inf)]
  transfers between devices with their start and end apart: 76 -> 93, of which waited for: 33 -> 46; matrix products, arithmetic and copies ran while one was open for 64% -> 27% of each run, Pallas kernels for 0% -> 9%
where the time goes in v2:
time: 1260 us; the launch traced here: 1250 us
  matrix products  402 us (32%)
  waiting for transfers between devices  254 us (20%)
  Pallas kernels  156 us (12%)
  starting transfers between devices  145 us (12%)
  local copies, waits for them, and re-layouts  126 us (10%)
  other arithmetic  103 us (8%)
  blocking collectives  36.7 us (3%)
  between operations  31.5 us (2%)
    ppermute x70, waiting for transfers between devices, partner_swap(): lax.ppermute(values, axis_name, [(i, i ^ distance) for i in range(size)])  233 us
    dot_general x55, matrix products, high_dot(): return jnp.dot(left, right, precision=highest_precision)  133 us
    ppermute x70, starting transfers between devices, partner_swap(): lax.ppermute(values, axis_name, [(i, i ^ distance) for i in range(size)])  106 us
    dot_general x14, matrix products, contract_rows(): lax.dot_general(left, right, (((0,), (0,)), ((), ())), preferred_element_...  91.6 us
    dot_general x4, matrix products, on_device(): jnp.dot(g2m_counts[slot], embedded, preferred_element_type=jnp.float32)  70.4 us
    pallas_call x1, Pallas kernels, attend_back(): pl.pallas_call(functools.partial(attend_back_kernel, chunk), grid=(HEADS,...  54.8 us
    pallas_call x5, Pallas kernels, count_matrix(): pl.pallas_call(count_kernel, grid=(column_count // columns, row_count //...  53 us
    pallas_call x1, Pallas kernels, attend(): pl.pallas_call(functools.partial(attend_kernel, chunk), grid=(HEADS, row_...  39.3 us
  transfers between devices with their start and end apart: 93, of which 46 were waited for; matrix products, arithmetic and copies ran while one was open for 27% of the time, Pallas kernels for 9%

profile of v2, /device:TPU:0, one launch (start us, length us, event | category | flops | bytes accessed | tf_op | source)
XLA Modules:
  0.0 1254.7 jit_solution(3662870494813852188)
XLA Ops:
  24.8 36.7 %all-gather = bf16[12,64,512]{2,1,0:T(8,128)(2,1)} all-gather(bf16[3,64,512]{2,1,0:T(8,128)(2,1)S(1)} %pad_maximum_fusion.16), channel_id=2, replica_groups=mesh['wide'=8,'narrow'=4] {'narrow'}, dimensions={0}, use_global_device_ids=true | all-gather | bytes 983040 | tf_op jit(solution)/shard_map/all_gather | solution.py:217
  74.9 9.5 shard_map.541.bias_ref
  84.4 9.7 shard_map.543
  121.4 10.8 shard_map.537
  132.2 16.1 %fusion.10 = f32[4096,512]{0,1:T(8,128)} fusion(bf16[4096,2048]{1,0:T(8,128)(2,1)} %shard_map.537, f32[2048,512]{1,0:T(8,128)} %fusion.159, f32[512]{0:T(512)S(1)} %slice.172), kind=kOutput, calls=%fused_computation.73 | convolution fusion | flops 8596226048 | bytes 29362176 | tf_op jit(solution)/shard_map/dot_general | solution.py:519
  153.8 10.8 shard_map.539
  164.6 10.8 shard_map.538
  175.4 10.8 shard_map.540
  191.6 16.6 %fusion.12 = f32[4096,512]{0,1:T(8,128)} fusion(bf16[4096,2048]{1,0:T(8,128)(2,1)} %shard_map.539, f32[2048,512]{1,0:T(8,128)S(1)} %fusion.103, f32[512]{0:T(512)S(1)} %slice.172), kind=kOutput, calls=%fused_computation.75 | convolution fusion | flops 8596226048 | bytes 29362176 | tf_op jit(solution)/shard_map/dot_general | solution.py:519
  218.1 15.0 %fusion.11 = f32[4096,512]{0,1:T(8,128)} fusion(bf16[4096,2048]{1,0:T(8,128)(2,1)} %shard_map.538, f32[2048,512]{1,0:T(8,128)S(1)} %fusion.102, f32[512]{0:T(512)S(1)} %slice.172), kind=kOutput, calls=%fused_computation.74 | convolution fusion | flops 8596226048 | bytes 29362176 | tf_op jit(solution)/shard_map/dot_general | solution.py:519
  233.1 22.7 %fusion.155 = (f32[4096]{0:T(1024)S(1)}, f32[4096,512]{0,1:T(8,128)}) fusion(bf16[4096,2048]{1,0:T(8,128)(2,1)} %shard_map.540, f32[2048,512]{1,0:T(8,128)} %fusion.104, f32[512]{0:T(512)S(1)} %slice.172, f32[4096,512]{0,1:T(8,128)} %fusion.12, f32[4096,512]{0,1:T(8,128)} %fusion.10, f32[4096,512]{0,1:T(8,128)} %fusion.11), kind=kOutput, calls=%fused_computation.489 | convolution fusion | flops 8606707712 | bytes 54544384 | tf_op jit(solution)/shard_map/dot_general | solution.py:519
  271.7 7.1 convolution_convert_fusion.k_ref.v_ref
  283.7 39.3 %shard_map.542 = (f32[1024,512]{1,0:T(8,128)}, f32[1024,512]{1,0:T(8,128)}) custom-call(bf16[1024,512]{1,0:T(8,128)(2,1)} %convolution_convert_fusion.2.q_ref, bf16[4096,1024]{1,0:T(8,128)(2,1)} %convolution_convert_fusion.k_ref.v_ref, bf16[4096,1024]{1,0:T(8,128)(2,1)} %convolution_convert_fusion.k_ref.v_ref, f32[1024,4096]{1,0:T(8,128)} %shard_map.541.bias_ref), custom_call_target="tpu_custom_call" | custom-call | flops 34359738368 | bytes 67108864 | tf_op jit(solution)/shard_map/pallas_call | solution.py:328
  356.5 12.1 convert_reduce_fusion.5
  368.6 9.9 fusion.157
  397.1 8.4 convert_reduce_fusion
  420.7 54.8 %shard_map.544 = (bf16[1024,512]{1,0:T(8,128)(2,1)}, bf16[4096,512]{1,0:T(8,128)(2,1)}, bf16[4096,512]{1,0:T(8,128)(2,1)}) custom-call(bf16[1024,512]{1,0:T(8,128)(2,1)} %convolution_convert_fusion.2.q_ref, bf16[4096,1024]{1,0:T(8,128)(2,1)} %convolution_convert_fusion.k_ref.v_ref, bf16[4096,1024]{1,0:T(8,128)(2,1)} %convolution_convert_fusion.k_ref.v_ref, ...), custom_call_target="tpu_custom_call" | custom-call | flops 51539607552 | bytes 67108864 | tf_op jit(solution)/shard_map/pallas_call | solution.py:390
  497.1 15.7 %convert_reduce_fusion.1 = (f32[512]{0:T(512)S(1)}, bf16[2048,512]{1,0:T(8,128)(2,1)S(1)}) fusion(f32[2048,512]{1,0:T(8,128)} %fusion.104, f32[512]{0:T(512)S(1)} %copy-done.146, bf16[4096,2048]{1,0:T(8,128)(2,1)} %shard_map.540, bf16[4096,512]{0,1:T(8,128)(2,1)} %multiply_convert_fusion), kind=kOutput, calls=%fused_computation.48 | convolution fusion | flops 8602517504 | bytes 27267072 | tf_op jit(solution)/shard_map/dot_general | solution.py:84
  512.8 16.0 %convert_reduce_fusion.2 = (f32[512]{0:T(512)S(1)}, bf16[2048,512]{1,0:T(8,128)(2,1)}) fusion(f32[2048,512]{1,0:T(8,128)S(1)} %copy-done.12, f32[512]{0:T(512)S(1)} %copy-done.146, bf16[4096,2048]{1,0:T(8,128)(2,1)} %shard_map.539, bf16[4096,512]{0,1:T(8,128)(2,1)} %multiply_convert_fusion), kind=kOutput, calls=%fused_computation.49 | convolution fusion | flops 8602517504 | bytes 27267072 | tf_op jit(solution)/shard_map/dot_general | solution.py:84
  528.8 16.4 %convert_reduce_fusion.3 = (f32[512]{0:T(512)S(1)}, bf16[2048,512]{1,0:T(8,128)(2,1)}) fusion(f32[2048,512]{1,0:T(8,128)S(1)} %copy-done.14, f32[512]{0:T(512)S(1)} %copy-done.146, bf16[4096,2048]{1,0:T(8,128)(2,1)} %shard_map.538, bf16[4096,512]{0,1:T(8,128)(2,1)} %multiply_convert_fusion), kind=kOutput, calls=%fused_computation.50 | convolution fusion | flops 8602517504 | bytes 27267072 | tf_op jit(solution)/shard_map/dot_general | solution.py:84
  545.2 15.9 %convert_reduce_fusion.4 = (f32[512]{0:T(512)S(1)}, bf16[2048,512]{1,0:T(8,128)(2,1)}) fusion(f32[2048,512]{1,0:T(8,128)S(1)} %copy-done.15, f32[512]{0:T(512)S(1)} %copy-done.146, bf16[4096,2048]{1,0:T(8,128)(2,1)} %shard_map.537, bf16[4096,512]{0,1:T(8,128)(2,1)} %multiply_convert_fusion), kind=kOutput, calls=%fused_computation.51 | convolution fusion | flops 8602517504 | bytes 27267072 | tf_op jit(solution)/shard_map/dot_general | solution.py:84
  674.3 7.0 collective-permute-done.35
  681.4 9.2 collective-permute-done.36
  695.8 13.8 %collective-permute-done.38 = bf16[16,1536]{0,1:T(8,128)(2,1)S(1)} collective-permute-done((bf16[16,1536]{0,1:T(8,128)(2,1)S(1)}, bf16[16,1536]{0,1:T(8,128)(2,1)S(1)}, u32[]{:S(2)}, u32[]{:S(2)}) %collective-permute-start.38) | collective-permute-done | bytes 49184 | tf_op jit(solution)/shard_map/ppermute | solution.py:128
  709.6 11.6 collective-permute-done.39
  723.3 15.1 %collective-permute-start.42 = (bf16[16,1536]{0,1:T(8,128)(2,1)S(1)}, bf16[16,1536]{0,1:T(8,128)(2,1)S(1)}, u32[]{:S(2)}, u32[]{:S(2)}) collective-permute-start(bf16[16,1536]{0,1:T(8,128)(2,1)S(1)} %add_convert_fusion.4), channel_id=1, source_target_pairs={{0,2},{1,3},{2,0},{3,1},{4,6},{5,7},{6,4},{7,5},{8,10},{9,11},{10,... | collective-permute-start | bytes 147464 | tf_op jit(solution)/shard_map/ppermute | solution.py:128
  742.2 20.1 %collective-permute-done.42 = bf16[16,1536]{0,1:T(8,128)(2,1)S(1)} collective-permute-done((bf16[16,1536]{0,1:T(8,128)(2,1)S(1)}, bf16[16,1536]{0,1:T(8,128)(2,1)S(1)}, u32[]{:S(2)}, u32[]{:S(2)}) %collective-permute-start.42) | collective-permute-done | bytes 49184 | tf_op jit(solution)/shard_map/ppermute | solution.py:128
  767.1 9.0 collective-permute-done.44
  787.7 7.3 collective-permute-done.63
  796.3 12.1 collective-permute-done.64
  810.0 8.7 collective-permute-done.78
  820.1 7.9 collective-permute-done.66
  828.1 29.6 %collective-permute-done.67 = bf16[16,2048]{0,1:T(8,128)(2,1)S(1)} collective-permute-done((bf16[16,2048]{0,1:T(8,128)(2,1)S(1)}, bf16[16,2048]{0,1:T(8,128)(2,1)S(1)}, u32[]{:S(2)}, u32[]{:S(2)}) %collective-permute-start.67) | collective-permute-done | bytes 65568 | tf_op jit(solution)/shard_map/ppermute | solution.py:128
  862.0 20.3 %collective-permute-done.81 = bf16[64,512]{1,0:T(8,128)(2,1)S(1)} collective-permute-done((bf16[64,512]{1,0:T(8,128)(2,1)S(1)}, bf16[64,512]{1,0:T(8,128)(2,1)S(1)}, u32[]{:S(2)}, u32[]{:S(2)}) %collective-permute-start.81) | collective-permute-done | bytes 65568 | tf_op jit(solution)/shard_map/ppermute | solution.py:128
  884.0 11.1 collective-permute-start.71
  902.6 8.2 collective-permute-start.84
  910.8 10.6 collective-permute-done.70
  928.1 11.5 collective-permute-done.72
  940.1 11.4 collective-permute-done.73
  979.3 7.0 reshape.339
  996.9 7.0 reshape.341
  1018.1 19.8 %select_reduce_fusion = (f32[]{:T(128)}, f32[512,512]{1,0:T(8,128)S(1)}) fusion(f32[4,8,64,512]{3,2,1,0:T(8,128)} %bitcast.273, f32[8,4,3,64,512]{4,3,2,1,0:T(8,128)} %bitcast.261), kind=kOutput, calls=%fused_computation.169 | convolution fusion | flops 6445334528 | bytes 9437188 | tf_op jit(solution)/shard_map/dot_general | solution.py:694
  1072.6 7.7 select_reduce_fusion.1
  1099.4 7.5 select_reduce_fusion.2
  1144.8 6.9 copy.198
  1151.7 7.5 reshape.342
  1186.9 6.9 copy.195
  1193.8 7.9 reshape.340
  (730 shorter events, 555.1 us)
Async XLA Ops:
  7.2 257.8 %all-gather.8.cloned.1.call-start = ((), (), s32[]{:S(2)}) async-start(), calls=%async_computation | async-start | bytes 7077888 | tf_op jit(solution)/shard_map/all_gather | solution.py:218
  7.3 107.7 %collective-permute-start = (s32[4,1024]{1,0:T(4,128)}, s32[4,1024]{1,0:T(4,128)S(1)}, u32[]{:S(2)}, u32[]{:S(2)}) collective-permute-start(s32[4,1024]{1,0:T(4,128)} %bitcast.288), channel_id=1, source_target_pairs={{1,0},{2,1},{3,2},{0,3},{5,4},{6,5},{7,6},{4,7},{9,8},{10,9},{11,1... | collective-permute-start | bytes 49160 | tf_op jit(solution)/shard_map/ppermute | solution.py:172
  12.4 102.6 %collective-permute-start.1 = (s32[4,1024]{1,0:T(4,128)}, s32[4,1024]{1,0:T(4,128)S(1)}, u32[]{:S(2)}, u32[]{:S(2)}) collective-permute-start(s32[4,1024]{1,0:T(4,128)} %bitcast.289), channel_id=1, source_target_pairs={{2,0},{3,1},{0,2},{1,3},{6,4},{7,5},{4,6},{5,7},{10,8},{11,9},{8,1... | collective-permute-start | bytes 49160 | tf_op jit(solution)/shard_map/ppermute | solution.py:172
  12.4 102.6 %collective-permute-start.2 = (s32[4,1024]{1,0:T(4,128)}, s32[4,1024]{1,0:T(4,128)S(1)}, u32[]{:S(2)}, u32[]{:S(2)}) collective-permute-start(s32[4,1024]{1,0:T(4,128)} %bitcast.290), channel_id=1, source_target_pairs={{3,0},{0,1},{1,2},{2,3},{7,4},{4,5},{5,6},{6,7},{11,8},{8,9},{9,10... | collective-permute-start | bytes 49160 | tf_op jit(solution)/shard_map/ppermute | solution.py:172
  18.4 129.9 %collective-permute-start.4 = (bf16[249,2048]{1,0:T(8,128)(2,1)}, bf16[249,2048]{1,0:T(8,128)(2,1)S(1)}, u32[]{:S(2)}, u32[]{:S(2)}) collective-permute-start(bf16[249,2048]{1,0:T(8,128)(2,1)} %pad_maximum_fusion.4), channel_id=1, source_target_pairs={{0,1},{1,2},{2,3},{4,5},{5,6},{6,7},{8,9},{9,10},{10,11},{12,13},{... | collective-permute-start | bytes 3059720 | tf_op jit(solution)/shard_map/ppermute | solution.py:183
  61.6 517.9 %all-gather.10.cloned.1.call-start = ((), (), s32[]{:S(2)}) async-start(), calls=%async_computation.1 | async-start | bytes 1966080 | tf_op jit(solution)/shard_map/all_gather | solution.py:217
  62.3 31.7 %collective-permute-start.9 = (f32[1,1]{1,0:T(1,128)}, f32[1,1]{1,0:T(1,128)}, u32[]{:S(2)}, u32[]{:S(2)}) collective-permute-start(f32[1,1]{1,0:T(1,128)} %bitcast.26), channel_id=1, source_target_pairs={{0,4},{4,0},{8,12},{12,8},{16,20},{20,16},{24,28},{28,24},{1,5},{5... | collective-permute-start | bytes 20 | tf_op jit(solution)/shard_map/ppermute | solution.py:97
  112.7 37.3 %collective-permute-start.3 = (bf16[249,2048]{1,0:T(8,128)(2,1)}, bf16[249,2048]{1,0:T(8,128)(2,1)}, u32[]{:S(2)}, u32[]{:S(2)}) collective-permute-start(bf16[249,2048]{1,0:T(8,128)(2,1)} %pad_maximum_fusion.4), channel_id=1, source_target_pairs={{1,0},{2,1},{3,2},{5,4},{6,5},{7,6},{9,8},{10,9},{11,10},{13,12},{... | collective-permute-start | bytes 3059720 | tf_op jit(solution)/shard_map/ppermute | solution.py:184
  148.3 37.9 %collective-permute-start.5 = (bf16[249,2048]{1,0:T(8,128)(2,1)S(1)}, bf16[249,2048]{1,0:T(8,128)(2,1)}, u32[]{:S(2)}, u32[]{:S(2)}) collective-permute-start(bf16[249,2048]{1,0:T(8,128)(2,1)S(1)} %collective-permute-done.4), channel_id=1, source_target_pairs={{1,2},{2,3},{5,6},{6,7},{9,10},{10,11},{13,14},{14,15},{17,18},{18... | collective-permute-start | bytes 3059720 | tf_op jit(solution)/shard_map/ppermute | solution.py:183
  150.0 37.9 %collective-permute-start.7 = (bf16[249,2048]{1,0:T(8,128)(2,1)}, bf16[249,2048]{1,0:T(8,128)(2,1)}, u32[]{:S(2)}, u32[]{:S(2)}) collective-permute-start(bf16[249,2048]{1,0:T(8,128)(2,1)} %collective-permute-done.3), channel_id=1, source_target_pairs={{1,0},{2,1},{5,4},{6,5},{9,8},{10,9},{13,12},{14,13},{17,16},{18,1... | collective-permute-start | bytes 3059720 | tf_op jit(solution)/shard_map/ppermute | solution.py:184
  186.2 22.0 %collective-permute-start.6 = (bf16[249,2048]{1,0:T(8,128)(2,1)}, bf16[249,2048]{1,0:T(8,128)(2,1)}, u32[]{:S(2)}, u32[]{:S(2)}) collective-permute-start(bf16[249,2048]{1,0:T(8,128)(2,1)} %collective-permute-done.5), channel_id=1, source_target_pairs={{2,3},{6,7},{10,11},{14,15},{18,19},{22,23},{26,27},{30,31}} | collective-permute-start | bytes 3059720 | tf_op jit(solution)/shard_map/ppermute | solution.py:183
  187.9 26.2 %collective-permute-start.8 = (bf16[249,2048]{1,0:T(8,128)(2,1)}, bf16[249,2048]{1,0:T(8,128)(2,1)}, u32[]{:S(2)}, u32[]{:S(2)}) collective-permute-start(bf16[249,2048]{1,0:T(8,128)(2,1)} %collective-permute-done.7), channel_id=1, source_target_pairs={{1,0},{5,4},{9,8},{13,12},{17,16},{21,20},{25,24},{29,28}} | collective-permute-start | bytes 3059720 | tf_op jit(solution)/shard_map/ppermute | solution.py:184
  383.8 634.3 %all-gather.12.cloned.1.call-start = ((), (), s32[]{:S(2)}) async-start(), calls=%async_computation.2 | async-start | bytes 14155776 | tf_op jit(solution)/shard_map/all_gather | solution.py:218
  563.5 30.2 %collective-permute-start.48 = (bf16[256,512]{1,0:T(8,128)(2,1)}, bf16[256,512]{1,0:T(8,128)(2,1)}, u32[]{:S(2)}, u32[]{:S(2)}) collective-permute-start(bf16[256,512]{1,0:T(8,128)(2,1)} %dynamic-slice_convert_fusion.18), channel_id=1, source_target_pairs={{0,4},{4,0},{8,12},{12,8},{16,20},{20,16},{24,28},{28,24},{1,5},{5... | collective-permute-start | bytes 786440 | tf_op jit(solution)/shard_map/ppermute | solution.py:128
  598.5 35.2 %collective-permute-start.20 = (f32[256,512]{1,0:T(8,128)S(1)}, f32[256,512]{1,0:T(8,128)S(1)}, u32[]{:S(2)}, u32[]{:S(2)}) collective-permute-start(f32[256,512]{1,0:T(8,128)S(1)} %pad_dynamic-slice_fusion), channel_id=1, source_target_pairs={{0,4},{4,0},{8,12},{12,8},{16,20},{20,16},{24,28},{28,24},{1,5},{5... | collective-permute-start | bytes 1572872 | tf_op jit(solution)/shard_map/ppermute | solution.py:128
  613.7 124.7 %collective-permute-start.76 = (bf16[1024,512]{1,0:T(8,128)(2,1)S(1)}, bf16[1024,512]{1,0:T(8,128)(2,1)}, u32[]{:S(2)}, u32[]{:S(2)}) collective-permute-start(bf16[1024,512]{1,0:T(8,128)(2,1)S(1)} %dynamic-slice_convert_fusion), channel_id=1, source_target_pairs={{0,4},{4,0},{8,12},{12,8},{16,20},{20,16},{24,28},{28,24},{1,5},{5... | collective-permute-start | bytes 3145736 | tf_op jit(solution)/shard_map/ppermute | solution.py:128
  637.5 19.9 %collective-permute-start.61 = (bf16[256,512]{1,0:T(8,128)(2,1)S(1)}, bf16[256,512]{1,0:T(8,128)(2,1)S(1)}, u32[]{:S(2)}, u32[]{:S(2)}) collective-permute-start(bf16[256,512]{1,0:T(8,128)(2,1)S(1)} %pad_maximum_fusion.14), channel_id=1, source_target_pairs={{0,4},{4,0},{8,12},{12,8},{16,20},{20,16},{24,28},{28,24},{1,5},{5... | collective-permute-start | bytes 786440 | tf_op jit(solution)/shard_map/ppermute | solution.py:128
  661.6 78.6 %collective-permute-start.62 = (bf16[256,2048]{0,1:T(8,128)(2,1)}, bf16[256,2048]{0,1:T(8,128)(2,1)S(1)}, u32[]{:S(2)}, u32[]{:S(2)}) collective-permute-start(bf16[256,2048]{0,1:T(8,128)(2,1)} %dynamic-slice_convert_fusion.1), channel_id=1, source_target_pairs={{0,4},{4,0},{8,12},{12,8},{16,20},{20,16},{24,28},{28,24},{1,5},{5... | collective-permute-start | bytes 3145736 | tf_op jit(solution)/shard_map/ppermute | solution.py:128
  671.3 19.3 %collective-permute-start.36 = (bf16[64,1536]{0,1:T(8,128)(2,1)S(1)}, bf16[64,1536]{0,1:T(8,128)(2,1)S(1)}, u32[]{:S(2)}, u32[]{:S(2)}) collective-permute-start(bf16[64,1536]{0,1:T(8,128)(2,1)S(1)} %get-tuple-element.247), channel_id=1, source_target_pairs={{0,16},{4,20},{8,24},{12,28},{16,0},{20,4},{24,8},{28,12},{1,17},{... | collective-permute-start | bytes 589832 | tf_op jit(solution)/shard_map/ppermute | solution.py:128
  672.9 17.7 %collective-permute-start.37 = (bf16[64,1536]{0,1:T(8,128)(2,1)S(1)}, bf16[64,1536]{0,1:T(8,128)(2,1)S(1)}, u32[]{:S(2)}, u32[]{:S(2)}) collective-permute-start(bf16[64,1536]{0,1:T(8,128)(2,1)S(1)} %get-tuple-element.246), channel_id=1, source_target_pairs={{0,24},{4,28},{8,16},{12,20},{16,8},{20,12},{24,0},{28,4},{1,25},{... | collective-permute-start | bytes 589832 | tf_op jit(solution)/shard_map/ppermute | solution.py:128
  691.3 18.3 %collective-permute-start.38 = (bf16[16,1536]{0,1:T(8,128)(2,1)S(1)}, bf16[16,1536]{0,1:T(8,128)(2,1)S(1)}, u32[]{:S(2)}, u32[]{:S(2)}) collective-permute-start(bf16[16,1536]{0,1:T(8,128)(2,1)S(1)} %get-tuple-element.256), channel_id=1, source_target_pairs={{0,1},{1,0},{2,3},{3,2},{4,5},{5,4},{6,7},{7,6},{8,9},{9,8},{10,11... | collective-permute-start | bytes 147464 | tf_op jit(solution)/shard_map/ppermute | solution.py:128
  691.3 29.9 %collective-permute-start.39 = (bf16[16,1536]{0,1:T(8,128)(2,1)S(1)}, bf16[16,1536]{0,1:T(8,128)(2,1)S(1)}, u32[]{:S(2)}, u32[]{:S(2)}) collective-permute-start(bf16[16,1536]{0,1:T(8,128)(2,1)S(1)} %get-tuple-element.258), channel_id=1, source_target_pairs={{0,2},{1,3},{2,0},{3,1},{4,6},{5,7},{6,4},{7,5},{8,10},{9,11},{10,... | collective-permute-start | bytes 147464 | tf_op jit(solution)/shard_map/ppermute | solution.py:128
  693.6 27.6 %collective-permute-start.40 = (bf16[16,1536]{0,1:T(8,128)(2,1)S(1)}, bf16[16,1536]{0,1:T(8,128)(2,1)S(1)}, u32[]{:S(2)}, u32[]{:S(2)}) collective-permute-start(bf16[16,1536]{0,1:T(8,128)(2,1)S(1)} %get-tuple-element.257), channel_id=1, source_target_pairs={{0,3},{1,2},{2,1},{3,0},{4,7},{5,6},{6,5},{7,4},{8,11},{9,10},{10,... | collective-permute-start | bytes 147464 | tf_op jit(solution)/shard_map/ppermute | solution.py:128
  709.6 185.6 %collective-permute-start.33 = (f32[256,512]{1,0:T(8,128)S(1)}, f32[256,512]{1,0:T(8,128)S(1)}, u32[]{:S(2)}, u32[]{:S(2)}) collective-permute-start(f32[256,512]{1,0:T(8,128)S(1)} %pad_maximum_fusion.8), channel_id=1, source_target_pairs={{0,4},{4,0},{8,12},{12,8},{16,20},{20,16},{24,28},{28,24},{1,5},{5... | collective-permute-start | bytes 1572872 | tf_op jit(solution)/shard_map/ppermute | solution.py:128
  721.5 20.7 %collective-permute-start.41 = (bf16[16,1536]{0,1:T(8,128)(2,1)S(1)}, bf16[16,1536]{0,1:T(8,128)(2,1)S(1)}, u32[]{:S(2)}, u32[]{:S(2)}) collective-permute-start(bf16[16,1536]{0,1:T(8,128)(2,1)S(1)} %add_convert_fusion.4), channel_id=1, source_target_pairs={{0,3},{1,2},{2,1},{3,0},{4,7},{5,6},{6,5},{7,4},{8,11},{9,10},{10,... | collective-permute-start | bytes 147464 | tf_op jit(solution)/shard_map/ppermute | solution.py:128
  723.3 39.1 %collective-permute-start.42 = (bf16[16,1536]{0,1:T(8,128)(2,1)S(1)}, bf16[16,1536]{0,1:T(8,128)(2,1)S(1)}, u32[]{:S(2)}, u32[]{:S(2)}) collective-permute-start(bf16[16,1536]{0,1:T(8,128)(2,1)S(1)} %add_convert_fusion.4), channel_id=1, source_target_pairs={{0,2},{1,3},{2,0},{3,1},{4,6},{5,7},{6,4},{7,5},{8,10},{9,11},{10,... | collective-permute-start | bytes 147464 | tf_op jit(solution)/shard_map/ppermute | solution.py:128
  738.4 23.9 %collective-permute-start.43 = (bf16[16,1536]{0,1:T(8,128)(2,1)S(1)}, bf16[16,1536]{0,1:T(8,128)(2,1)S(1)}, u32[]{:S(2)}, u32[]{:S(2)}) collective-permute-start(bf16[16,1536]{0,1:T(8,128)(2,1)S(1)} %add_convert_fusion.4), channel_id=1, source_target_pairs={{0,1},{1,0},{2,3},{3,2},{4,5},{5,4},{6,7},{7,6},{8,9},{9,8},{10,11... | collective-permute-start | bytes 147464 | tf_op jit(solution)/shard_map/ppermute | solution.py:128
  740.1 69.8 %collective-permute-start.77 = (bf16[256,512]{1,0:T(8,128)(2,1)S(1)}, bf16[256,512]{1,0:T(8,128)(2,1)S(1)}, u32[]{:S(2)}, u32[]{:S(2)}) collective-permute-start(bf16[256,512]{1,0:T(8,128)(2,1)S(1)} %get-tuple-element.217), channel_id=1, source_target_pairs={{0,8},{4,12},{8,0},{12,4},{16,24},{20,28},{24,16},{28,20},{1,9},{5... | collective-permute-start | bytes 786440 | tf_op jit(solution)/shard_map/ppermute | solution.py:128
  764.8 17.6 %collective-permute-start.45 = (bf16[64,1536]{0,1:T(8,128)(2,1)S(1)}, bf16[64,1536]{0,1:T(8,128)(2,1)S(1)}, u32[]{:S(2)}, u32[]{:S(2)}) collective-permute-start(bf16[64,1536]{0,1:T(8,128)(2,1)S(1)} %pad_maximum_fusion.12), channel_id=1, source_target_pairs={{0,16},{4,20},{8,24},{12,28},{16,0},{20,4},{24,8},{28,12},{1,17},{... | collective-permute-start | bytes 589832 | tf_op jit(solution)/shard_map/ppermute | solution.py:128
  776.1 18.9 %collective-permute-start.63 = (bf16[64,2048]{0,1:T(8,128)(2,1)S(1)}, bf16[64,2048]{0,1:T(8,128)(2,1)S(1)}, u32[]{:S(2)}, u32[]{:S(2)}) collective-permute-start(bf16[64,2048]{0,1:T(8,128)(2,1)S(1)} %get-tuple-element.230), channel_id=1, source_target_pairs={{0,8},{4,12},{8,0},{12,4},{16,24},{20,28},{24,16},{28,20},{1,9},{5... | collective-permute-start | bytes 786440 | tf_op jit(solution)/shard_map/ppermute | solution.py:128
  782.4 26.0 %collective-permute-start.64 = (bf16[64,2048]{0,1:T(8,128)(2,1)S(1)}, bf16[64,2048]{0,1:T(8,128)(2,1)S(1)}, u32[]{:S(2)}, u32[]{:S(2)}) collective-permute-start(bf16[64,2048]{0,1:T(8,128)(2,1)S(1)} %get-tuple-element.232), channel_id=1, source_target_pairs={{0,16},{4,20},{8,24},{12,28},{16,0},{20,4},{24,8},{28,12},{1,17},{... | collective-permute-start | bytes 786440 | tf_op jit(solution)/shard_map/ppermute | solution.py:128
  783.7 25.4 %collective-permute-start.65 = (bf16[64,2048]{0,1:T(8,128)(2,1)S(1)}, bf16[64,2048]{0,1:T(8,128)(2,1)S(1)}, u32[]{:S(2)}, u32[]{:S(2)}) collective-permute-start(bf16[64,2048]{0,1:T(8,128)(2,1)S(1)} %get-tuple-element.231), channel_id=1, source_target_pairs={{0,24},{4,28},{8,16},{12,20},{16,8},{20,12},{24,0},{28,4},{1,25},{... | collective-permute-start | bytes 786440 | tf_op jit(solution)/shard_map/ppermute | solution.py:128
  795.0 23.8 %collective-permute-start.78 = (bf16[256,512]{1,0:T(8,128)(2,1)S(1)}, bf16[256,512]{1,0:T(8,128)(2,1)S(1)}, u32[]{:S(2)}, u32[]{:S(2)}) collective-permute-start(bf16[256,512]{1,0:T(8,128)(2,1)S(1)} %get-tuple-element.219), channel_id=1, source_target_pairs={{0,16},{4,20},{8,24},{12,28},{16,0},{20,4},{24,8},{28,12},{1,17},{... | collective-permute-start | bytes 786440 | tf_op jit(solution)/shard_map/ppermute | solution.py:128
  809.1 150.3 %collective-permute-start.47 = (bf16[256,1536]{0,1:T(8,128)(2,1)}, bf16[256,1536]{0,1:T(8,128)(2,1)}, u32[]{:S(2)}, u32[]{:S(2)}) collective-permute-start(bf16[256,1536]{0,1:T(8,128)(2,1)} %pad_maximum_fusion.7), channel_id=1, source_target_pairs={{0,4},{4,0},{8,12},{12,8},{16,20},{20,16},{24,28},{28,24},{1,5},{5... | collective-permute-start | bytes 2359304 | tf_op jit(solution)/shard_map/ppermute | solution.py:128
  809.9 18.1 %collective-permute-start.66 = (bf16[16,2048]{0,1:T(8,128)(2,1)S(1)}, bf16[16,2048]{0,1:T(8,128)(2,1)S(1)}, u32[]{:S(2)}, u32[]{:S(2)}) collective-permute-start(bf16[16,2048]{0,1:T(8,128)(2,1)S(1)} %get-tuple-element.251), channel_id=1, source_target_pairs={{0,1},{1,0},{2,3},{3,2},{4,5},{5,4},{6,7},{7,6},{8,9},{9,8},{10,11... | collective-permute-start | bytes 196616 | tf_op jit(solution)/shard_map/ppermute | solution.py:128
  818.8 38.9 %collective-permute-start.67 = (bf16[16,2048]{0,1:T(8,128)(2,1)S(1)}, bf16[16,2048]{0,1:T(8,128)(2,1)S(1)}, u32[]{:S(2)}, u32[]{:S(2)}) collective-permute-start(bf16[16,2048]{0,1:T(8,128)(2,1)S(1)} %get-tuple-element.253), channel_id=1, source_target_pairs={{0,2},{1,3},{2,0},{3,1},{4,6},{5,7},{6,4},{7,5},{8,10},{9,11},{10,... | collective-permute-start | bytes 196616 | tf_op jit(solution)/shard_map/ppermute | solution.py:128
  818.8 38.9 %collective-permute-start.68 = (bf16[16,2048]{0,1:T(8,128)(2,1)S(1)}, bf16[16,2048]{0,1:T(8,128)(2,1)S(1)}, u32[]{:S(2)}, u32[]{:S(2)}) collective-permute-start(bf16[16,2048]{0,1:T(8,128)(2,1)S(1)} %get-tuple-element.252), channel_id=1, source_target_pairs={{0,3},{1,2},{2,1},{3,0},{4,7},{5,6},{6,5},{7,4},{8,11},{9,10},{10,... | collective-permute-start | bytes 196616 | tf_op jit(solution)/shard_map/ppermute | solution.py:128
  828.0 30.5 %collective-permute-start.80 = (bf16[64,512]{1,0:T(8,128)(2,1)S(1)}, bf16[64,512]{1,0:T(8,128)(2,1)S(1)}, u32[]{:S(2)}, u32[]{:S(2)}) collective-permute-start(bf16[64,512]{1,0:T(8,128)(2,1)S(1)} %get-tuple-element.264), channel_id=1, source_target_pairs={{0,1},{1,0},{2,3},{3,2},{4,5},{5,4},{6,7},{7,6},{8,9},{9,8},{10,11... | collective-permute-start | bytes 196616 | tf_op jit(solution)/shard_map/ppermute | solution.py:128
  857.7 24.6 %collective-permute-start.81 = (bf16[64,512]{1,0:T(8,128)(2,1)S(1)}, bf16[64,512]{1,0:T(8,128)(2,1)S(1)}, u32[]{:S(2)}, u32[]{:S(2)}) collective-permute-start(bf16[64,512]{1,0:T(8,128)(2,1)S(1)} %get-tuple-element.266), channel_id=1, source_target_pairs={{0,2},{1,3},{2,0},{3,1},{4,6},{5,7},{6,4},{7,5},{8,10},{9,11},{10,... | collective-permute-start | bytes 196616 | tf_op jit(solution)/shard_map/ppermute | solution.py:128
  857.7 26.3 %collective-permute-start.82 = (bf16[64,512]{1,0:T(8,128)(2,1)S(1)}, bf16[64,512]{1,0:T(8,128)(2,1)S(1)}, u32[]{:S(2)}, u32[]{:S(2)}) collective-permute-start(bf16[64,512]{1,0:T(8,128)(2,1)S(1)} %get-tuple-element.265), channel_id=1, source_target_pairs={{0,3},{1,2},{2,1},{3,0},{4,7},{5,6},{6,5},{7,4},{8,11},{9,10},{10,... | collective-permute-start | bytes 196616 | tf_op jit(solution)/shard_map/ppermute | solution.py:128
  858.6 44.0 %collective-permute-start.69 = (bf16[16,2048]{0,1:T(8,128)(2,1)S(1)}, bf16[16,2048]{0,1:T(8,128)(2,1)}, u32[]{:S(2)}, u32[]{:S(2)}) collective-permute-start(bf16[16,2048]{0,1:T(8,128)(2,1)S(1)} %add_convert_fusion.3), channel_id=1, source_target_pairs={{0,3},{1,2},{2,1},{3,0},{4,7},{5,6},{6,5},{7,4},{8,11},{9,10},{10,... | collective-permute-start | bytes 196616 | tf_op jit(solution)/shard_map/ppermute | solution.py:128
  882.3 39.1 %collective-permute-start.70 = (bf16[16,2048]{0,1:T(8,128)(2,1)S(1)}, bf16[16,2048]{0,1:T(8,128)(2,1)}, u32[]{:S(2)}, u32[]{:S(2)}) collective-permute-start(bf16[16,2048]{0,1:T(8,128)(2,1)S(1)} %add_convert_fusion.3), channel_id=1, source_target_pairs={{0,2},{1,3},{2,0},{3,1},{4,6},{5,7},{6,4},{7,5},{8,10},{9,11},{10,... | collective-permute-start | bytes 196616 | tf_op jit(solution)/shard_map/ppermute | solution.py:128
  884.0 37.4 %collective-permute-start.71 = (bf16[16,2048]{0,1:T(8,128)(2,1)S(1)}, bf16[16,2048]{0,1:T(8,128)(2,1)}, u32[]{:S(2)}, u32[]{:S(2)}) collective-permute-start(bf16[16,2048]{0,1:T(8,128)(2,1)S(1)} %add_convert_fusion.3), channel_id=1, source_target_pairs={{0,1},{1,0},{2,3},{3,2},{4,5},{5,4},{6,7},{7,6},{8,9},{9,8},{10,11... | collective-permute-start | bytes 196616 | tf_op jit(solution)/shard_map/ppermute | solution.py:128
  895.2 29.3 %collective-permute-start.83 = (bf16[64,512]{1,0:T(8,128)(2,1)S(1)}, bf16[64,512]{1,0:T(8,128)(2,1)S(1)}, u32[]{:S(2)}, u32[]{:S(2)}) collective-permute-start(bf16[64,512]{1,0:T(8,128)(2,1)S(1)} %add_convert_fusion.5), channel_id=1, source_target_pairs={{0,3},{1,2},{2,1},{3,0},{4,7},{5,6},{6,5},{7,4},{8,11},{9,10},{10,... | collective-permute-start | bytes 196616 | tf_op jit(solution)/shard_map/ppermute | solution.py:128
  902.6 22.5 %collective-permute-start.84 = (bf16[64,512]{1,0:T(8,128)(2,1)S(1)}, bf16[64,512]{1,0:T(8,128)(2,1)S(1)}, u32[]{:S(2)}, u32[]{:S(2)}) collective-permute-start(bf16[64,512]{1,0:T(8,128)(2,1)S(1)} %add_convert_fusion.5), channel_id=1, source_target_pairs={{0,2},{1,3},{2,0},{3,1},{4,6},{5,7},{6,4},{7,5},{8,10},{9,11},{10,... | collective-permute-start | bytes 196616 | tf_op jit(solution)/shard_map/ppermute | solution.py:128
  924.5 27.0 %collective-permute-start.73 = (bf16[64,2048]{0,1:T(8,128)(2,1)S(1)}, bf16[64,2048]{0,1:T(8,128)(2,1)S(1)}, u32[]{:S(2)}, u32[]{:S(2)}) collective-permute-start(bf16[64,2048]{0,1:T(8,128)(2,1)S(1)} %pad_maximum_fusion.10), channel_id=1, source_target_pairs={{0,16},{4,20},{8,24},{12,28},{16,0},{20,4},{24,8},{28,12},{1,17},{... | collective-permute-start | bytes 786440 | tf_op jit(solution)/shard_map/ppermute | solution.py:128
  925.1 26.4 %collective-permute-start.74 = (bf16[64,2048]{0,1:T(8,128)(2,1)S(1)}, bf16[64,2048]{0,1:T(8,128)(2,1)S(1)}, u32[]{:S(2)}, u32[]{:S(2)}) collective-permute-start(bf16[64,2048]{0,1:T(8,128)(2,1)S(1)} %pad_maximum_fusion.10), channel_id=1, source_target_pairs={{0,8},{4,12},{8,0},{12,4},{16,24},{20,28},{24,16},{28,20},{1,9},{5... | collective-permute-start | bytes 786440 | tf_op jit(solution)/shard_map/ppermute | solution.py:128
  927.4 25.9 %collective-permute-start.86 = (bf16[256,512]{1,0:T(8,128)(2,1)S(1)}, bf16[256,512]{1,0:T(8,128)(2,1)S(1)}, u32[]{:S(2)}, u32[]{:S(2)}) collective-permute-start(bf16[256,512]{1,0:T(8,128)(2,1)S(1)} %pad_maximum_fusion.15), channel_id=1, source_target_pairs={{0,24},{4,28},{8,16},{12,20},{16,8},{20,12},{24,0},{28,4},{1,25},{... | collective-permute-start | bytes 786440 | tf_op jit(solution)/shard_map/ppermute | solution.py:128
  (202 other events, 2826.7 us)
Sparse Core Ops, SparseCore 0:
  61.7 45.2 all-gather.7
  383.9 36.7 all-gather.9
  579.6 87.3 all-gather.11

commit v3 on v2

--- a/solution.py
+++ b/solution.py
@@ -92,11 +92,6 @@
     )
 
 
-def bit_swap(values, axis_name, bit):
-    size = lax.axis_size(axis_name)
-    return lax.ppermute(values, axis_name, [(i, i ^ (1 << bit)) for i in range(size)])
-
-
 def axis_bits(axis_name):
     bits = []
     reach = 1
@@ -104,12 +99,6 @@
         bits.append((axis_name, len(bits)))
         reach *= 2
     return bits
-
-
-def small_sum(values):
-    for axis_name, bit in axis_bits("wide") + axis_bits("narrow"):
-        values = values + bit_swap(values, axis_name, bit)
-    return values
 
 
 def sum_stages():
@@ -128,40 +117,46 @@
     return lax.ppermute(values, axis_name, [(i, i ^ distance) for i in range(size)])
 
 
-def large_sum(values, sent_type):
+def scatter_stage(values, stage, sent_type):
+    axis_name, first, width = stage
+    members = 1 << width
+    block = values.shape[0] // members
+    mine = (lax.axis_index(axis_name) >> first) & (members - 1)
+    arrived = [
+        partner_swap(
+            lax.dynamic_slice_in_dim(values, (mine ^ far) * block, block, 0).astype(sent_type),
+            axis_name,
+            far << first,
+        )
+        for far in range(1, members)
+    ]
+    values = lax.dynamic_slice_in_dim(values, mine * block, block, 0)
+    for piece in arrived:
+        values = values + piece.astype(jnp.float32)
+    return values
+
+
+def gather_stage(values, stage):
+    axis_name, first, width = stage
+    members = 1 << width
+    mine = (lax.axis_index(axis_name) >> first) & (members - 1)
+    pieces = [values] + [
+        partner_swap(values, axis_name, far << first) for far in range(1, members)
+    ]
+    for bit in range(width):
+        is_high = ((mine >> bit) & 1) == 1
+        step = 1 << bit
+        pieces = [
+            jnp.where(is_high, pieces[place ^ step], pieces[place]) for place in range(members)
+        ]
+    return jnp.concatenate(pieces, axis=0)
+
+
+def sum_steps(sent_type):
     stages = sum_stages()
-    for axis_name, first, width in stages:
-        members = 1 << width
-        block = values.shape[0] // members
-        mine = (lax.axis_index(axis_name) >> first) & (members - 1)
-        arrived = [
-            partner_swap(
-                lax.dynamic_slice_in_dim(values, (mine ^ far) * block, block, 0).astype(sent_type),
-                axis_name,
-                far << first,
-            )
-            for far in range(1, members)
-        ]
-        values = lax.dynamic_slice_in_dim(values, mine * block, block, 0)
-        for piece in arrived:
-            values = values + piece.astype(jnp.float32)
-    values = values.astype(sent_type)
-    for axis_name, first, width in stages[::-1]:
-        members = 1 << width
-        block = values.shape[0]
-        mine = (lax.axis_index(axis_name) >> first) & (members - 1)
-        pieces = [values] + [
-            partner_swap(values, axis_name, far << first) for far in range(1, members)
-        ]
-        for bit in range(width):
-            is_high = ((mine >> bit) & 1) == 1
-            step = 1 << bit
-            pieces = [
-                jnp.where(is_high, pieces[place ^ step], pieces[place])
-                for place in range(members)
-            ]
-        values = jnp.concatenate(pieces, axis=0)
-    return values
+    steps = [functools.partial(scatter_stage, stage=s, sent_type=sent_type) for s in stages]
+    steps.append(lambda values: gather_stage(values.astype(sent_type), stages[-1]))
+    return steps + [functools.partial(gather_stage, stage=s) for s in stages[-2::-1]]
 
 
 def ring_slots(values):
@@ -178,19 +173,27 @@
     size = lax.axis_size("narrow")
     pos = lax.axis_index("narrow")
     from_low, from_high = values, values
-    low_list, high_list = [], []
+    arrived = {}
+    slots = [(values, pos)]
+    orders = [
+        sorted((s for s in range(size) if s != n), key=lambda s, n=n: (abs(s - n), s < n))
+        for n in range(size)
+    ]
     for step in range(size - 1):
         from_low = lax.ppermute(from_low, "narrow", [(i, i + 1) for i in range(step, size - 1)])
         from_high = lax.ppermute(
             from_high, "narrow", [(i, i - 1) for i in range(1, size - step)]
         )
-        low_list.append(from_low)
-        high_list.append(from_high)
-    slots = [values]
-    for shift in range(1, size):
-        slots.append(
-            jnp.where(pos + shift < size, high_list[shift - 1], low_list[size - shift - 1])
-        )
+        arrived[-1 - step] = from_low
+        arrived[1 + step] = from_high
+        offsets = [orders[n][step] - n for n in range(size)]
+        chosen = arrived[offsets[0]]
+        for offset in sorted(set(offsets) - {offsets[0]}):
+            here = functools.reduce(
+                jnp.logical_or, [pos == n for n in range(size) if offsets[n] == offset]
+            )
+            chosen = jnp.where(here, arrived[offset], chosen)
+        slots.append((chosen, pos + jnp.array(offsets, jnp.int32)[pos]))
     return slots
 
 
@@ -207,19 +210,26 @@
     return total
 
 
-def wide_gather(blocks):
-    wide_count = lax.axis_size("wide")
-    own = []
-    for block in blocks:
-        rows = block.shape[0] // wide_count
-        own.append(lax.dynamic_slice_in_dim(block, lax.axis_index("wide") * rows, rows, 0))
-    own = jnp.stack(own)
-    across = lax.all_gather(own, "narrow", axis=0)
+def own_rows(blocks):
+    rows = blocks.shape[1] // lax.axis_size("wide")
+    return lax.dynamic_slice_in_dim(blocks, lax.axis_index("wide") * rows, rows, 1)
+
+
+def spread_wide(across):
     whole = lax.all_gather(across, "wide", axis=0)
-    side = whole[:, :, :-1].transpose(2, 0, 3, 1, 4)
-    side = side.reshape(side.shape[0], blocks[0].shape[0], -1)
-    last = whole[:, :, -1].transpose(1, 0, 2, 3).reshape(-1, blocks[-1].shape[1])
-    return [side[place] for place in range(side.shape[0])] + [last]
+    count = whole.shape[2]
+    return whole.transpose(2, 1, 0, 3, 4).reshape(count, -1, whole.shape[4])
+
+
+def near_gather(own):
+    size = lax.axis_size("narrow")
+    pos = lax.axis_index("narrow")
+    across = jnp.zeros((size,) + own.shape, own.dtype)
+    for shift, piece in enumerate(ring_slots(own)):
+        across = lax.dynamic_update_slice_in_dim(
+            across, piece[None], (pos + shift) % size, 0
+        )
+    return across
 
 
 VMEM_LIMIT = 60 * 1024 * 1024
@@ -347,7 +357,19 @@
 
 
 def attend_back_kernel(
-    chunk, q_ref, k_ref, v_ref, bias_ref, mass_ref, att_ref, g_ref, dq_ref, dk_ref, dv_ref, dk_sum, dv_sum
+    chunk,
+    q_ref,
+    k_ref,
+    v_ref,
+    bias_ref,
+    mass_ref,
+    att_ref,
+    g_ref,
+    dq_ref,
+    dk_ref,
+    dv_ref,
+    dk_sum,
+    dv_sum,
 ):
     step = pl.program_id(1)
     q = q_ref[...]
@@ -411,21 +433,177 @@
     )(queries, pairs, pairs, bias, mass, attended, grads)
 
 
-def high_dot(left, right):
-    return jnp.dot(left, right, precision=highest_precision)
-
-
-def orthogonal_map(gram):
-    scale = 1.0 / (jnp.sqrt(jnp.trace(gram)) + 1e-07)
+def gather_kernel(sub, ids_ref, pixel_ref, *rest):
+    out_ref = rest[-1]
+    pixels = pixel_ref[...]
+    columns = lax.broadcasted_iota(jnp.int32, (sub, pixels.shape[0]), 1).astype(jnp.int16)
+    one = jnp.ones(columns.shape, jnp.bfloat16)
+    zero = jnp.zeros(columns.shape, jnp.bfloat16)
+    for block in range(out_ref.shape[0] // sub):
+        part = pl.ds(block * sub, sub)
+        ids = ids_ref[part, :].astype(jnp.int16)
+        counts = zero
+        for slot in range(ids.shape[1]):
+            counts = counts + jnp.where(ids[:, slot : slot + 1] == columns, one, zero)
+        rows = jnp.dot(counts, pixels, preferred_element_type=jnp.float32)
+        if len(rest) == 2:
+            rows = rows + rest[0][part, :]
+        out_ref[part, :] = rows
+
+
+def gather_sum(ids, pixels, earlier, rows=1024, sub=256):
+    row_count, slots = ids.shape
+    pixel_count, width = pixels.shape
+    block = pl.BlockSpec((rows, width), lambda i: (i, 0))
+    more = [] if earlier is None else [earlier]
+    return pl.pallas_call(
+        functools.partial(gather_kernel, sub),
+        grid=(row_count // rows,),
+        in_specs=[
+            pl.BlockSpec((rows, slots), lambda i: (i, 0)),
+            pl.BlockSpec((pixel_count, width), lambda i: (0, 0)),
+        ]
+        + [block] * len(more),
+        out_specs=block,
+        out_shape=jax.ShapeDtypeStruct((row_count, width), jnp.float32),
+        cost_estimate=pl.CostEstimate(
+            flops=2 * row_count * pixel_count * width,
+            bytes_accessed=12 * row_count * width,
+            transcendentals=0,
+        ),
+        compiler_params=kernel_params(),
+    )(ids, pixels, *more)
+
+
+def scatter_kernel(chunk, ids_ref, g_ref, pre_ref, feature_ref, grad_ref, bias_ref):
+    step = pl.program_id(0)
+    rows = pre_ref.shape[0]
+    pixel_ids = lax.broadcasted_iota(jnp.int32, (rows, chunk), 0).astype(jnp.int16)
+    one = jnp.ones((rows, chunk), jnp.bfloat16)
+    zero = jnp.zeros((rows, chunk), jnp.bfloat16)
+    spread = jnp.zeros(pre_ref.shape, jnp.float32)
+    for start in range(0, g_ref.shape[0], chunk):
+        part = pl.ds(start, chunk)
+        counts = zero
+        for slot in range(ids_ref.shape[0]):
+            ids = jnp.broadcast_to(ids_ref[slot : slot + 1, part] - step * rows, (rows, chunk))
+            counts = counts + jnp.where(ids.astype(jnp.int16) == pixel_ids, one, zero)
+        spread = spread + jnp.dot(counts, g_ref[part, :], preferred_element_type=jnp.float32)
+    pre = pre_ref[...]
+    sigmoid_values = 1.0 / (1.0 + jnp.exp(-pre))
+    lowered = (spread * (sigmoid_values * (1.0 + pre * (1.0 - sigmoid_values)))).astype(
+        jnp.bfloat16
+    )
+
+    @pl.when(step == 0)
+    def _():
+        grad_ref[...] = jnp.zeros_like(grad_ref)
+        bias_ref[...] = jnp.zeros_like(bias_ref)
+
+    grad_ref[...] += jnp.dot(feature_ref[...], lowered, preferred_element_type=jnp.float32)
+    bias_ref[...] += jnp.sum(lowered.astype(jnp.float32), axis=0, keepdims=True)
+
+
+def scatter_sum(ids, grads, pre, features, rows=512, chunk=1024):
+    slots, node_count = ids.shape
+    pixel_count, width = pre.shape
+    channels = features.shape[0]
+    return pl.pallas_call(
+        functools.partial(scatter_kernel, chunk),
+        grid=(pixel_count // rows,),
+        in_specs=[
+            pl.BlockSpec((slots, node_count), lambda i: (0, 0)),
+            pl.BlockSpec((node_count, width), lambda i: (0, 0)),
+            pl.BlockSpec((rows, width), lambda i: (i, 0)),
+            pl.BlockSpec((channels, rows), lambda i: (0, i)),
+        ],
+        out_specs=[
+            pl.BlockSpec((channels, width), lambda i: (0, 0)),
+            pl.BlockSpec((1, width), lambda i: (0, 0)),
+        ],
+        out_shape=[
+            jax.ShapeDtypeStruct((channels, width), jnp.float32),
+            jax.ShapeDtypeStruct((1, width), jnp.float32),
+        ],
+        cost_estimate=pl.CostEstimate(
+            flops=2 * node_count * pixel_count * width,
+            bytes_accessed=8 * pixel_count * width,
+            transcendentals=pixel_count * width,
+        ),
+        compiler_params=kernel_params(),
+    )(ids, grads, pre, features)
+
+
+def split_low(values):
+    upper = values.astype(jnp.bfloat16)
+    return upper, (values - upper.astype(jnp.float32)).astype(jnp.bfloat16)
+
+
+def plain_dot(left, right):
+    return jnp.dot(left, right, preferred_element_type=jnp.float32)
+
+
+def triple_dot(left, right, dot=plain_dot):
+    return dot(left[0], right[0]) + (dot(left[0], right[1]) + dot(left[1], right[0]))
+
+
+def muon_kernel(factor_ref, pos_ref, mom_ref, attn_ref, rest_ref, moment_ref, turned_ref, full_ref):
+    matrix = pl.program_id(0)
+    factor = factor_ref[0, 0]
+    own, width = moment_ref.shape[1:]
+    gram = jnp.zeros((width, width), jnp.float32)
+    for start in range(0, mom_ref.shape[1], own):
+        part = pl.ds(start, own)
+        grads = jnp.where(
+            matrix == 0,
+            attn_ref[part, :].astype(jnp.float32),
+            rest_ref[part, :].astype(jnp.float32),
+        )
+        moment = muon_decay * mom_ref[0, part, :] + factor * grads
+        full_ref[part, :] = moment
+        halves = split_low(moment)
+        gram = gram + triple_dot(halves, halves, contract_rows)
+    mine = full_ref[pl.ds(pos_ref[0, 0] * own, own), :]
+    moment_ref[0] = mine
+    row_ids = lax.broadcasted_iota(jnp.int32, gram.shape, 0)
+    eye = jnp.where(row_ids == lax.broadcasted_iota(jnp.int32, gram.shape, 1), 1.0, 0.0)
+    trace = jnp.sum(jnp.sum(gram * eye, axis=1, keepdims=True), axis=0, keepdims=True)
+    scale = 1.0 / (jnp.sqrt(trace) + 1e-07)
     gram = gram * (scale * scale)
-    eye = jnp.eye(gram.shape[0], dtype=jnp.float32)
-    mapped = None
+    turned = mine * scale
     for iteration in range(NS_ITERS):
-        poly = coef_a * eye + coef_b * gram + coef_c * high_dot(gram, gram)
+        gram_halves = split_low(gram)
+        poly = coef_a * eye + coef_b * gram + coef_c * triple_dot(gram_halves, gram_halves)
+        poly_halves = split_low(poly)
+        turned = triple_dot(split_low(turned), poly_halves)
         if iteration < NS_ITERS - 1:
-            gram = high_dot(poly, high_dot(poly, gram))
-        mapped = poly * scale if mapped is None else high_dot(poly, mapped)
-    return mapped
+            gram = triple_dot(poly_halves, split_low(triple_dot(poly_halves, gram_halves)))
+    turned_ref[0] = turned
+
+
+def muon_parts(factor, pos, mom_full, sum_attn, sum_rest, own):
+    matrices, rows, width = mom_full.shape
+    block = pl.BlockSpec((1, own, width), lambda i: (i, 0, 0))
+    scalar = pl.BlockSpec(memory_space=pltpu.SMEM)
+    shape = jax.ShapeDtypeStruct((matrices, own, width), jnp.float32)
+    return pl.pallas_call(
+        muon_kernel,
+        grid=(matrices,),
+        in_specs=[
+            scalar,
+            scalar,
+            pl.BlockSpec((1, rows, width), lambda i: (i, 0, 0)),
+            pl.BlockSpec((rows, width), lambda i: (0, 0)),
+            pl.BlockSpec((rows, width), lambda i: (jnp.maximum(i - 1, 0), 0)),
+        ],
+        out_specs=[block, block],
+        out_shape=[shape, shape],
+        scratch_shapes=[pltpu.VMEM((rows, width), jnp.float32)],
+        cost_estimate=pl.CostEstimate(
+            flops=100 * matrices * width**3, bytes_accessed=8 * matrices * rows * width, transcendentals=0
+        ),
+        compiler_params=kernel_params(),
+    )(factor.reshape(1, 1), pos.reshape(1, 1), mom_full, sum_attn, sum_rest)
 
 
 def adam_update(weight, grad, first, second):
@@ -492,32 +670,25 @@
     features = jnp.concatenate(
         [prior_states[0, 0], prior_states[0, 1], (scale_in * noisy).astype(jnp.bfloat16)], axis=0
     )
-    g2m_slots = ring_slots(g2m_edges[0].T)
+    g2m_rows = jnp.concatenate(ring_slots(g2m_edges[0].T), axis=1)
+    g2m_cols = g2m_rows.T
     feature_slots = line_slots(features)
-    attn_full, up_full, down_full = wide_gather(
-        [w_attn.astype(jnp.bfloat16), w_up.astype(jnp.bfloat16), w_down.astype(jnp.bfloat16)]
-    )
+    low_blocks = jnp.stack([w_attn.T, w_up.T, w_down]).astype(jnp.bfloat16)
+    weight_full = spread_wide(near_gather(own_rows(low_blocks)))
+    attn_rows, up_rows, down_full = weight_full[0], weight_full[1], weight_full[2]
     lat_weight = lat_weights(narrow_pos * pixel_local, pixel_local, pixel_total)
     pixel_weight = lat_weight * valid_mask[0].astype(jnp.float32)
-    weight_total = small_sum(jnp.sum(pixel_weight).reshape(1, 1))[0, 0]
-
-    g2m_ids = (jnp.concatenate(g2m_slots, axis=1) - narrow_pos * pixel_local) % pixel_total
-    g2m_ids = g2m_ids.T
     near_ids = (neighbours[0] - narrow_pos * node_local) % node_total
     m2g_ids = (m2g_edges[0] - narrow_pos * node_local) % node_total
     near_bias = count_bias(near_ids, node_total)
     m2g_counts = count_matrix(m2g_ids, node_total)
-    g2m_counts = [
-        count_matrix(g2m_ids - slot * pixel_local, pixel_local) for slot in range(narrow_count)
-    ]
 
     embed_pres = []
     node_in = None
-    for slot in range(narrow_count):
-        embed_pre = contract_rows(feature_slots[slot], embed_low) + bias_embed
+    for features_here, source in feature_slots:
+        embed_pre = contract_rows(features_here, embed_low) + bias_embed
         embedded = jax.nn.silu(embed_pre).astype(jnp.bfloat16)
-        part = jnp.dot(g2m_counts[slot], embedded, preferred_element_type=jnp.float32)
-        node_in = part if node_in is None else node_in + part
+        node_in = gather_sum(g2m_cols - source * pixel_local, embedded, node_in)
         embed_pres.append(embed_pre)
     node_in = node_in / G2M_K
     conditioning = cond_features(noise_level)
@@ -529,25 +700,21 @@
         jnp.bfloat16
     )
     attn_own = attn_in[:node_local]
-    query_map = attn_full[:, :LATENT_WIDTH]
-    pair_map = attn_full[:, LATENT_WIDTH : 3 * LATENT_WIDTH]
-    proj_map = attn_full[:, 3 * LATENT_WIDTH :]
-    query_rows = jnp.dot(attn_own, query_map, preferred_element_type=jnp.float32).astype(
-        jnp.bfloat16
-    )
-    pair_rows = jnp.dot(attn_in, pair_map, preferred_element_type=jnp.float32).astype(
-        jnp.bfloat16
-    )
+    query_map = attn_rows[:LATENT_WIDTH]
+    pair_map = attn_rows[LATENT_WIDTH : 3 * LATENT_WIDTH]
+    proj_map = attn_rows[3 * LATENT_WIDTH :]
+    query_rows = contract_last(attn_own, query_map).astype(jnp.bfloat16)
+    pair_rows = contract_last(attn_in, pair_map).astype(jnp.bfloat16)
+    mom_blocks = jnp.stack([mom_attn.T, mom_up.T, mom_down])
+    mom_blocks, pair_rows = lax.optimization_barrier((mom_blocks, pair_rows))
+    mom_full = spread_wide(lax.all_gather(own_rows(mom_blocks), "narrow", axis=0))
+
     attended, mass = attend(query_rows, pair_rows, near_bias)
     attended_rows = attended.astype(jnp.bfloat16)
-    mom_blocks, _ = lax.optimization_barrier(((mom_attn, mom_up, mom_down), attended))
-    mom_attn_full, mom_up_full, mom_down_full = wide_gather(mom_blocks)
-    node_mid = node_in[:node_local] + jnp.dot(
-        attended_rows, proj_map, preferred_element_type=jnp.float32
-    )
+    node_mid = node_in[:node_local] + contract_last(attended_rows, proj_map)
     normed_two, inverse_two = norm_stats(node_mid)
     mlp_in = (normed_two * gain_two + modulation[3 * LATENT_WIDTH :]).astype(jnp.bfloat16)
-    up_pre = jnp.dot(mlp_in, up_full, preferred_element_type=jnp.float32) + bias_up
+    up_pre = contract_last(mlp_in, up_rows) + bias_up
     hidden = jax.nn.silu(up_pre).astype(jnp.bfloat16)
     node_out = node_mid + jnp.dot(hidden, down_full, preferred_element_type=jnp.float32)
     node_low = node_out.astype(jnp.bfloat16)
@@ -559,9 +726,7 @@
     errors = skip_scale * noisy + out_scale * raw_output - target_rows
     weighted = channel_weights[:, None] * pixel_weight[None, :]
     loss_local = loss_scale * jnp.sum(weighted * errors * errors)
-    grad_raw = (2.0 * loss_scale * out_scale / weight_total * weighted * errors).astype(
-        jnp.bfloat16
-    )
+    grad_raw = (2.0 * loss_scale * out_scale * weighted * errors).astype(jnp.bfloat16)
     grad_out_bias = jnp.sum(grad_raw.astype(jnp.float32), axis=1)
     raw_spread = jnp.dot(grad_raw, m2g_counts, preferred_element_type=jnp.float32)
     grad_node_raw = (
@@ -590,31 +755,28 @@
     grad_hidden = contract_last(grad_mlp, down_full)
     grad_up_pre = (grad_hidden * silu_slope(up_pre)).astype(jnp.bfloat16)
     grad_up_bias = jnp.sum(grad_up_pre.astype(jnp.float32), axis=0)
-    grad_up = contract_rows(mlp_in, grad_up_pre)
-    grad_mlp_in = contract_last(grad_up_pre, up_full)
+    grad_up = contract_rows(grad_up_pre, mlp_in)
+    grad_mlp_in = plain_dot(grad_up_pre, up_rows)
     grad_node_mid = grad_node_out + norm_back(grad_mlp_in * gain_two, normed_two, inverse_two)
     grad_proj_out = grad_node_mid.astype(jnp.bfloat16)
-    grad_proj = contract_rows(attended_rows, grad_proj_out)
-    sum_down = large_sum(grad_down, jnp.bfloat16).astype(jnp.float32)
-    sum_up = large_sum(grad_up, jnp.bfloat16).astype(jnp.float32)
-    sum_proj = large_sum(grad_proj, jnp.bfloat16).astype(jnp.float32)
-    gradient_attended = contract_last(grad_proj_out, proj_map).astype(jnp.bfloat16)
-
+    grad_proj = contract_rows(grad_proj_out, attended_rows)
+    early = jnp.concatenate([grad_up, grad_down, grad_proj], axis=0).astype(jnp.bfloat16)
+    early = lax.psum(early, ("wide", "narrow"))
+    gradient_attended = plain_dot(grad_proj_out, proj_map).astype(jnp.bfloat16)
     grad_query_rows, grad_key_rows, grad_value_rows = attend_back(
         query_rows, pair_rows, near_bias, mass, attended, gradient_attended
     )
     grad_qkv = jnp.concatenate(
         [
-            contract_rows(attn_own, grad_query_rows),
-            contract_rows(attn_in, grad_key_rows),
-            contract_rows(attn_in, grad_value_rows),
+            contract_rows(grad_query_rows, attn_own),
+            contract_rows(grad_key_rows, attn_in),
+            contract_rows(grad_value_rows, attn_in),
         ],
-        axis=1,
-    )
-    sum_qkv = large_sum(grad_qkv, jnp.bfloat16).astype(jnp.float32)
-    grad_attn_in = contract_last(grad_key_rows, pair_map[:, :LATENT_WIDTH])
-    grad_attn_in = grad_attn_in + contract_last(grad_value_rows, pair_map[:, LATENT_WIDTH:])
-    grad_attn_in = grad_attn_in.at[:node_local].add(contract_last(grad_query_rows, query_map))
+        axis=0,
+    )
+    grad_attn_in = plain_dot(grad_key_rows, pair_map[:LATENT_WIDTH])
+    grad_attn_in = grad_attn_in + plain_dot(grad_value_rows, pair_map[LATENT_WIDTH:])
+    grad_attn_in = grad_attn_in.at[:node_local].add(plain_dot(grad_query_rows, query_map))
     grad_node_in = norm_back(grad_attn_in * gain_one, normed_one, inverse_one)
     grad_node_in = grad_node_in.at[:node_local].add(grad_node_mid)
     grad_modulation = jnp.concatenate(
@@ -629,13 +791,19 @@
     node_grads = (grad_node_in / G2M_K).astype(jnp.bfloat16)
     grad_embed = None
     grad_embed_bias = None
-    for slot in range(narrow_count):
-        grad_embedded = contract_rows(g2m_counts[slot], node_grads)
-        grad_pre = (grad_embedded * silu_slope(embed_pres[slot])).astype(jnp.bfloat16)
-        bias_part = jnp.sum(grad_pre.astype(jnp.float32), axis=0)
-        embed_part = jnp.dot(feature_slots[slot], grad_pre, preferred_element_type=jnp.float32)
+    steps = sum_steps(jnp.bfloat16)
+    grad_qkv = steps[0](grad_qkv)
+    for place, (features_here, source) in enumerate(feature_slots):
+        node_grads, grad_qkv = lax.optimization_barrier((node_grads, grad_qkv))
+        if place + 1 < len(steps):
+            grad_qkv = steps[place + 1](grad_qkv)
+        embed_part, bias_part = scatter_sum(
+            g2m_rows - source * pixel_local, node_grads, embed_pres[place], features_here
+        )
         grad_embed = embed_part if grad_embed is None else grad_embed + embed_part
         grad_embed_bias = bias_part if grad_embed_bias is None else grad_embed_bias + bias_part
+    for step in steps[len(feature_slots) + 1 :]:
+        grad_qkv = step(grad_qkv)
 
     width = LATENT_WIDTH
     channels = w_dec.shape[1]
@@ -645,7 +813,10 @@
             grad_embed_bias.reshape(1, width),
             grad_up_bias.reshape(FF // width, width),
             jnp.pad(
-                jnp.concatenate([grad_out_bias, loss_local.reshape(1)]), (0, width - channels - 1)
+                jnp.concatenate(
+                    [grad_out_bias, loss_local.reshape(1), jnp.sum(pixel_weight).reshape(1)]
+                ),
+                (0, width - channels - 2),
             ).reshape(1, width),
             grad_dec.T,
         ]
@@ -654,52 +825,37 @@
     )
     device_count = lax.axis_size("wide") * narrow_count
     late_rows = jnp.pad(late_rows, ((0, -late_rows.shape[0] % (2 * device_count)), (0, 0)))
-    late_rows = large_sum(late_rows, jnp.float32)
+    for step in sum_steps(jnp.float32):
+        late_rows = step(late_rows)
     embed_rows = w_embed.shape[0]
     sum_embed = late_rows[:embed_rows]
     place = embed_rows
     bias_rows = late_rows[place : place + 2 + FF // width].reshape(-1)
     sum_bias = bias_rows[: biases.shape[0]]
     loss_sum = bias_rows[biases.shape[0]]
+    weight_total = bias_rows[biases.shape[0] + 1]
     place += 2 + FF // width
     sum_dec = late_rows[place : place + channels].T
     place += channels
     sum_cond = jnp.concatenate(
         [late_rows[place + COND * part : place + COND * (part + 1)] for part in range(4)], axis=1
     )
-    sum_attn = jnp.concatenate([sum_qkv, sum_proj], axis=1)
+    sum_attn = jnp.concatenate([grad_qkv, early[2 * FF :]], axis=0)
     square_sum = (
         jnp.sum(sum_embed * sum_embed)
         + jnp.sum(sum_cond * sum_cond)
-        + jnp.sum(sum_attn * sum_attn)
-        + jnp.sum(sum_up * sum_up)
-        + jnp.sum(sum_down * sum_down)
+        + jnp.sum(jnp.square(grad_qkv.astype(jnp.float32)))
+        + jnp.sum(jnp.square(early.astype(jnp.float32)))
         + jnp.sum(sum_dec * sum_dec)
         + jnp.sum(sum_bias * sum_bias)
     )
-    grad_norm = jnp.sqrt(square_sum)
-    factor = jnp.minimum(1.0, clip_bound / (grad_norm + 1e-06))
-    attn_cols = w_attn.shape[1]
-    up_cols = w_up.shape[1]
-    down_rows = w_down.shape[0]
-    all_attn = muon_decay * mom_attn_full + factor * sum_attn
-    all_up = muon_decay * mom_up_full + factor * sum_up
-    all_down = muon_decay * mom_down_full + factor * sum_down
-    moment_attn = lax.dynamic_slice_in_dim(all_attn, narrow_pos * attn_cols, attn_cols, 1)
-    moment_up = lax.dynamic_slice_in_dim(all_up, narrow_pos * up_cols, up_cols, 1)
-    moment_down = lax.dynamic_slice_in_dim(all_down, narrow_pos * down_rows, down_rows, 0)
-    map_attn = orthogonal_map(high_dot(all_attn, all_attn.T))
-    map_up = orthogonal_map(high_dot(all_up, all_up.T))
-    map_down = orthogonal_map(
-        lax.dot_general(
-            all_down, all_down, (((0,), (0,)), ((), ())), precision=highest_precision
-        )
-    )
-    attn_orth = high_dot(map_attn, moment_attn)
-    up_orth = high_dot(map_up, moment_up)
-    down_orth = lax.dot_general(
-        moment_down, map_down, (((1,), (1,)), ((), ())), precision=highest_precision
-    )
+    grad_norm = jnp.sqrt(square_sum) / weight_total
+    factor = jnp.minimum(1.0, clip_bound / (grad_norm + 1e-06)) / weight_total
+    moments, turned = muon_parts(
+        factor, narrow_pos, mom_full, sum_attn, early, w_down.shape[0]
+    )
+    moment_attn, moment_up, moment_down = moments[0].T, moments[1].T, moments[2]
+    attn_orth, up_orth, down_orth = turned[0].T, turned[1].T, turned[2]
     new_attn = (
         w_attn - muon_rate * math.sqrt(max(1.0, LATENT_WIDTH / (4 * LATENT_WIDTH))) * attn_orth
     )

time: 1260 us -> 720 us (0.57)
  matrix products: 402 us -> 102 us
  waiting for transfers between devices: 254 us -> 78.4 us
  Pallas kernels: 156 us -> 292 us
  starting transfers between devices: 145 us -> 71 us
  local copies, waits for them, and re-layouts: 126 us -> 67.6 us
  blocking collectives: 36.7 us -> 0 us
  other arithmetic: 103 us -> 72.3 us
    dot_general x69 -> x5, matrix products: 254 us -> 13.7 us  [plain_dot(): return jnp.dot(left, right, preferred_element_type=jnp.float32)]
    ppermute x70 -> x28, waiting for transfers between devices: 233 us -> 25.3 us  [partner_swap(): lax.ppermute(values, axis_name, [(i, i ^ distance) for i in range(size)])]
    pallas_call x0 -> x9, Pallas kernels: none -> 179 us  [the longest x1 64.9 us: muon_parts(): pl.pallas_call(muon_kernel, grid=(matrices,), in_specs=[scalar, scalar, p...]
    ppermute x70 -> x28, starting transfers between devices: 106 us -> 44.3 us  [partner_swap(): lax.ppermute(values, axis_name, [(i, i ^ distance) for i in range(size)])]
    mul x9 -> x0, local copies, waits for them, and re-layouts: 59.5 us -> none  [the longest x4 28.7 us: on_device(): all_attn = muon_decay * mom_attn_full + factor * sum_attn]
    dot_general x14 -> x10, matrix products: 91.6 us -> 32.5 us  [contract_rows(): lax.dot_general(left, right, (((0,), (0,)), ((), ())), preferred_element_...]
    pallas_call x5 -> x1, Pallas kernels: 53 us -> 9.76 us  [count_matrix(): pl.pallas_call(count_kernel, grid=(column_count // columns, row_count //...]
    all_gather x1 -> x0, blocking collectives: 36.7 us -> none  [wide_gather(): across = lax.all_gather(own, 'narrow', axis=0)]
  transfers between devices with their start and end apart: 93 -> 50, of which waited for: 46 -> 21; matrix products, arithmetic and copies ran while one was open for 27% -> 21% of each run, Pallas kernels for 9% -> 27%
where the time goes in v3:
time: 720 us; the launch traced here: 710 us
  Pallas kernels  292 us (41%)
  matrix products  102 us (14%)
  waiting for transfers between devices  78.4 us (11%)
  other arithmetic  72.3 us (10%)
  starting transfers between devices  71 us (10%)
  local copies, waits for them, and re-layouts  67.6 us (9%)
  between operations  26 us (4%)
    pallas_call x1, Pallas kernels, muon_parts(): pl.pallas_call(muon_kernel, grid=(matrices,), in_specs=[scalar, scalar, p...  64.9 us
    pallas_call x4, Pallas kernels, scatter_sum(): pl.pallas_call(functools.partial(scatter_kernel, chunk), grid=(pixel_coun...  60 us
    pallas_call x1, Pallas kernels, attend_back(): pl.pallas_call(functools.partial(attend_back_kernel, chunk), grid=(HEADS,...  54.6 us
    pallas_call x4, Pallas kernels, gather_sum(): pl.pallas_call(functools.partial(gather_kernel, sub), grid=(row_count //...  54.2 us
    ppermute x28, starting transfers between devices, partner_swap(): lax.ppermute(values, axis_name, [(i, i ^ distance) for i in range(size)])  44.3 us
    pallas_call x1, Pallas kernels, attend(): pl.pallas_call(functools.partial(attend_kernel, chunk), grid=(HEADS, row_...  39.1 us
    dot_general x6, matrix products, contract_last(): lax.dot_general(left, right, (((1,), (1,)), ((), ())), preferred_element_...  37.7 us
    ppermute x9, waiting for transfers between devices, ring_slots(): lax.ppermute(values, 'narrow', [((i + shift) % size, i) for i in range(si...  36.1 us
  transfers between devices with their start and end apart: 50, of which 21 were waited for; matrix products, arithmetic and copies ran while one was open for 21% of the time, Pallas kernels for 27%

profile of v3, /device:TPU:0, one launch (start us, length us, event | category | flops | bytes accessed | tf_op | source)
XLA Modules:
  0.0 709.7 jit_solution(15938623705923912349)
XLA Ops:
  12.5 5.9 collective-permute-start.5
  19.7 4.7 collective-permute-start
  32.1 17.9 %collective-permute-done.9 = bf16[3,64,512]{2,1,0:T(8,128)(2,1)S(1)} collective-permute-done((bf16[3,64,512]{2,1,0:T(8,128)(2,1)}, bf16[3,64,512]{2,1,0:T(8,128)(2,1)S(1)}, u32[]{:S(2)}, u32[]{:S(2)}) %collective-permute-start.9) | collective-permute-done | bytes 196640 | tf_op jit(solution)/shard_map/ppermute | solution.py:167
  51.7 9.1 %collective-permute-done.10 = bf16[3,64,512]{2,1,0:T(8,128)(2,1)S(1)} collective-permute-done((bf16[3,64,512]{2,1,0:T(8,128)(2,1)}, bf16[3,64,512]{2,1,0:T(8,128)(2,1)S(1)}, u32[]{:S(2)}, u32[]{:S(2)}) %collective-permute-start.10) | collective-permute-done | bytes 196640 | tf_op jit(solution)/shard_map/ppermute | solution.py:167
  60.8 8.3 %collective-permute-done.11 = bf16[3,64,512]{2,1,0:T(8,128)(2,1)S(1)} collective-permute-done((bf16[3,64,512]{2,1,0:T(8,128)(2,1)}, bf16[3,64,512]{2,1,0:T(8,128)(2,1)S(1)}, u32[]{:S(2)}, u32[]{:S(2)}) %collective-permute-start.11) | collective-permute-done | bytes 196640 | tf_op jit(solution)/shard_map/ppermute | solution.py:167
  74.4 5.3 multiply_convert_fusion.3
  88.6 9.6 %shard_map.568.bias_ref = f32[1024,4096]{1,0:T(8,128)} custom-call(s32[128,256]{1,0:T(8,128)} %get-tuple-element.283.row_ref, s32[128,256]{1,0:T(8,128)} %get-tuple-element.282.lane_ref), custom_call_target="tpu_custom_call" | custom-call | flops 67108864 | bytes 16777216 | tf_op jit(solution)/shard_map/pallas_call | solution.py:298
  99.8 6.7 collective-permute-done.4
  116.7 13.1 %shard_map.564.rest_0_ = f32[4096,512]{1,0:T(8,128)} custom-call(s32[4096,4]{1,0:T(8,128)} %copy.105.ids_ref, bf16[2048,512]{1,0:T(8,128)(2,1)} %get-tuple-element.299.pixel_ref), custom_call_target="tpu_custom_call" | custom-call | flops 8589934592 | bytes 25165824 | tf_op jit(solution)/shard_map/pallas_call | solution.py:459
  134.2 4.0 multiply_convert_fusion.4
  138.1 3.9 multiply_convert_fusion.5
  142.0 4.0 multiply_convert_fusion.6
  146.0 13.6 %shard_map.565.rest_0_ = f32[4096,512]{1,0:T(8,128)} custom-call(s32[4096,4]{1,0:T(8,128)} %copy.106.ids_ref, bf16[2048,512]{1,0:T(8,128)(2,1)} %get-tuple-element.297.pixel_ref, f32[4096,512]{1,0:T(8,128)} %shard_map.564.rest_0_), custom_call_target="tpu_custom_call" | custom-call | flops 8589934592 | bytes 25165824 | tf_op jit(solution)/shard_map/pallas_call | solution.py:459
  159.5 13.6 %shard_map.566.rest_0_ = f32[4096,512]{1,0:T(8,128)} custom-call(s32[4096,4]{1,0:T(8,128)} %copy.107.ids_ref, bf16[2048,512]{1,0:T(8,128)(2,1)} %get-tuple-element.295.pixel_ref, f32[4096,512]{1,0:T(8,128)} %shard_map.565.rest_0_), custom_call_target="tpu_custom_call" | custom-call | flops 8589934592 | bytes 25165824 | tf_op jit(solution)/shard_map/pallas_call | solution.py:459
  173.1 14.0 %shard_map.567 = f32[4096,512]{1,0:T(8,128)} custom-call(s32[4096,4]{1,0:T(8,128)} %copy.108.ids_ref, bf16[2048,512]{1,0:T(8,128)(2,1)} %get-tuple-element.293.pixel_ref, f32[4096,512]{1,0:T(8,128)} %shard_map.566.rest_0_), custom_call_target="tpu_custom_call" | custom-call | flops 8589934592 | bytes 25165824 | tf_op jit(solution)/shard_map/pallas_call | solution.py:459
  187.1 4.2 fusion.64
  192.9 4.2 broadcast_multiply_fusion
  209.0 7.1 %convolution_convert_fusion.k_ref.v_ref = bf16[4096,1024]{1,0:T(8,128)(2,1)} fusion(bf16[4096,512]{1,0:T(8,128)(2,1)S(1)} %copy-done.1, bf16[1024,512]{1,0:T(8,128)(2,1)S(1)} %bitcast.183), kind=kOutput, calls=%fused_computation.12 | convolution fusion | flops 4299161600 | bytes 13631488 | tf_op jit(solution)/shard_map/dot_general | solution.py:90
  217.8 39.1 %shard_map.569 = (f32[1024,512]{1,0:T(8,128)}, f32[1024,512]{1,0:T(8,128)}) custom-call(bf16[1024,512]{1,0:T(8,128)(2,1)} %convolution_convert_fusion.4.q_ref, bf16[4096,1024]{1,0:T(8,128)(2,1)} %convolution_convert_fusion.k_ref.v_ref, bf16[4096,1024]{1,0:T(8,128)(2,1)} %convolution_convert_fusion.k_ref.v_ref, f32[1024,4096]{1,0:T(8,128)} %shard_map.568.bias_ref), custom_call_target="tpu_custom_call" | custom-call | flops 34359738368 | bytes 67108864 | tf_op jit(solution)/shard_map/pallas_call | solution.py:338
  256.9 3.2 fusion.80
  260.5 5.9 multiply_convert_fusion.2
  275.8 9.8 %shard_map.570 = bf16[2048,4096]{1,0:T(8,128)(2,1)} custom-call(s32[2048,3]{1,0:T(8,128)} %add_select_fusion.ids_ref), custom_call_target="tpu_custom_call" | custom-call | flops 100663296 | bytes 16777216 | tf_op jit(solution)/shard_map/pallas_call | solution.py:260
  287.7 12.2 %convert_reduce_fusion.1 = (f32[83]{0:T(128)S(1)}, f32[]{:T(128)}, f32[83,2048]{1,0:T(8,128)S(1)}) fusion(f32[2048]{0:T(1024)S(1)} %bitcast.190, f32[83]{0:T(128)S(1)} %copy-done.77, f32[]{:T(128)S(6)} %mul.584, f32[83]{0:T(128)S(1)} %slice.212, bf16[2048,4096]{1,0:T(8,128)(2,1)} %shard_map.570, bf16[83,1024]{1,0:T(8,128)(2,1)} %copy-done.65, ...), kind=kOutput, calls=%fused_computation.102 | convolution fusion | flops 1398458240 | bytes 18826232 | tf_op jit(solution)/shard_map/dot_general | solution.py:90
  299.9 9.8 %fusion.81 = (bf16[83,4096]{1,0:T(8,128)(2,1)S(1)}, f32[83,4096]{1,0:T(8,128)}) fusion(bf16[2048,4096]{1,0:T(8,128)(2,1)} %shard_map.570, f32[83,2048]{1,0:T(8,128)S(1)} %get-tuple-element.310, f32[2048]{0:T(1024)S(1)} %bitcast.191, f32[83]{0:T(128)S(1)} %copy-done.77, f32[]{:T(128)S(6)} %mul.584), kind=kOutput, calls=%fused_computation.274 | convolution fusion | flops 1393528832 | bytes 19505488 | tf_op jit(solution)/shard_map/dot_general | solution.py:731
  316.2 3.5 collective-permute-done.15
  319.7 4.0 collective-permute-done.16
  325.9 7.6 %convert_reduce_fusion = (f32[2048]{0:T(1024)S(1)}, bf16[1024,2048]{1,0:T(8,128)(2,1)S(1)}) fusion(f32[1024,2048]{1,0:T(8,128)} %get-tuple-element.304, f32[2048]{0:T(1024)S(1)} %slice.210, bf16[2048,512]{1,0:T(8,128)(2,1)} %bitcast.176, f32[1024,512]{1,0:T(8,128)S(1)} %fusion.46), kind=kOutput, calls=%fused_computation.2 | convolution fusion | flops 2173171712 | bytes 16793600 | tf_op jit(solution)/shard_map/dot_general | solution.py:90
  353.1 54.6 %shard_map.571 = (bf16[1024,512]{1,0:T(8,128)(2,1)}, bf16[4096,512]{1,0:T(8,128)(2,1)}, bf16[4096,512]{1,0:T(8,128)(2,1)}) custom-call(bf16[1024,512]{1,0:T(8,128)(2,1)} %convolution_convert_fusion.4.q_ref, bf16[4096,1024]{1,0:T(8,128)(2,1)} %convolution_convert_fusion.k_ref.v_ref, bf16[4096,1024]{1,0:T(8,128)(2,1)} %convolution_convert_fusion.k_ref.v_ref, ...), custom_call_target="tpu_custom_call" | custom-call | flops 51539607552 | bytes 67108864 | tf_op jit(solution)/shard_map/pallas_call | solution.py:412
  410.6 4.7 fusion.83
  420.8 4.7 fusion.82
  430.0 4.9 multiply_reduce_fusion.1
  436.8 3.9 subtract_multiply_fusion
  441.3 3.3 multiply_convert_fusion.g_ref
  449.7 14.9 %shard_map.572 = (f32[249,512]{1,0:T(8,128)}, f32[1,512]{1,0:T(1,128)}) custom-call(s32[4,4096]{1,0:T(4,128)} %copy-done.62, bf16[4096,512]{1,0:T(8,128)(2,1)} %multiply_convert_fusion.g_ref, f32[2048,512]{1,0:T(8,128)} %get-tuple-element.300.pre_ref, bf16[249,2048]{1,0:T(8,128)(2,1)} %pad_maximum_fusion.4.feature_ref), custom_call_target="tpu_custom_call" | custom-call | flops 8589934592 | bytes 8388608 | tf_op jit(solution)/shard_map/pallas_call | solution.py:511
  464.8 8.2 %collective-permute-start.22 = (bf16[48,512]{1,0:T(8,128)(2,1)S(1)}, bf16[48,512]{1,0:T(8,128)(2,1)S(1)}, u32[]{:S(2)}, u32[]{:S(2)}) collective-permute-start(bf16[48,512]{1,0:T(8,128)(2,1)S(1)} %get-tuple-element.264), channel_id=1, source_target_pairs={{0,1},{1,0},{2,3},{3,2},{4,5},{5,4},{6,7},{7,6},{8,9},{9,8},{10,11... | collective-permute-start | bytes 147464 | tf_op jit(solution)/shard_map/ppermute | solution.py:117
  472.9 4.6 collective-permute-start.23
  477.5 15.2 %shard_map.573 = (f32[249,512]{1,0:T(8,128)}, f32[1,512]{1,0:T(1,128)}) custom-call(s32[4,4096]{1,0:T(4,128)} %copy-done.59, bf16[4096,512]{1,0:T(8,128)(2,1)} %multiply_convert_fusion.g_ref, f32[2048,512]{1,0:T(8,128)} %get-tuple-element.298.pre_ref, bf16[249,2048]{1,0:T(8,128)(2,1)} %copy-done.37), custom_call_target="tpu_custom_call" | custom-call | flops 8589934592 | bytes 8388608 | tf_op jit(solution)/shard_map/pallas_call | solution.py:511
  492.7 3.9 collective-permute-start.25
  497.3 14.9 %shard_map.574 = (f32[249,512]{1,0:T(8,128)}, f32[1,512]{1,0:T(1,128)}) custom-call(s32[4,4096]{1,0:T(4,128)} %copy-done.61, bf16[4096,512]{1,0:T(8,128)(2,1)} %multiply_convert_fusion.g_ref, f32[2048,512]{1,0:T(8,128)} %get-tuple-element.296.pre_ref, bf16[249,2048]{1,0:T(8,128)(2,1)} %copy-done.36), custom_call_target="tpu_custom_call" | custom-call | flops 8589934592 | bytes 8388608 | tf_op jit(solution)/shard_map/pallas_call | solution.py:511
  512.3 15.2 %shard_map.575 = (f32[249,512]{1,0:T(8,128)}, f32[1,512]{1,0:T(1,128)}) custom-call(s32[4,4096]{1,0:T(4,128)} %copy-done.60, bf16[4096,512]{1,0:T(8,128)(2,1)} %multiply_convert_fusion.g_ref, f32[2048,512]{1,0:T(8,128)} %get-tuple-element.294.pre_ref, bf16[249,2048]{1,0:T(8,128)(2,1)} %copy-done.35), custom_call_target="tpu_custom_call" | custom-call | flops 8589934592 | bytes 8388608 | tf_op jit(solution)/shard_map/pallas_call | solution.py:511
  544.5 3.3 collective-permute-done.31
  552.0 3.3 collective-permute-start.34
  557.7 3.4 collective-permute-start.35
  569.6 6.5 collective-permute-done.38
  607.5 12.0 %copy.119 = f32[3,4,8,64,512]{4,3,2,1,0:T(8,128)} copy(f32[3,4,8,64,512]{4,3,0,1,2:T(8,128)} %bitcast.163) | data formatting | bytes 25165824 | tf_op jit(solution)/shard_map/transpose | solution.py:221
  619.5 64.9 %shard_map.576 = (f32[3,512,512]{2,1,0:T(8,128)}, f32[3,512,512]{2,1,0:T(8,128)}) custom-call(f32[1,1]{1,0:T(1,128)} %bitcast.52.factor_ref, s32[1,1]{1,0:T(1,128)} %bitcast.53.pos_ref, f32[3,2048,512]{2,1,0:T(8,128)} %bitcast.164, bf16[2048,512]{1,0:T(8,128)(2,1)} %pad_maximum_fusion.3.attn_ref, bf16[4608,512]{1,0:T(8,128)(2,1)} %all-reduce.4.cloned.1.call-done.rest_ref), custom_call_target="tpu_custom_call" | custom-call | flops 40265318400 | bytes 25165824 | tf_op jit(solution)/shard_map/pallas_call | solution.py:589
  686.8 3.6 slice_bitcast_fusion
  695.5 3.7 multiply_add_fusion.1
  (399 shorter events, 185.8 us)
Async XLA Ops:
  7.2 193.4 %all-gather.6.cloned.1.call-start = ((), (), s32[]{:S(2)}) async-start(), calls=%async_computation | async-start | bytes 7077888 | tf_op jit(solution)/shard_map/all_gather | solution.py:219
  12.5 67.3 %collective-permute-start.5 = (bf16[249,2048]{1,0:T(8,128)(2,1)}, bf16[249,2048]{1,0:T(8,128)(2,1)}, u32[]{:S(2)}, u32[]{:S(2)}) collective-permute-start(bf16[249,2048]{1,0:T(8,128)(2,1)} %pad_maximum_fusion.4.feature_ref), channel_id=1, source_target_pairs={{0,1},{1,2},{2,3},{4,5},{5,6},{6,7},{8,9},{9,10},{10,11},{12,13},{... | collective-permute-start | bytes 3059720 | tf_op jit(solution)/shard_map/ppermute | solution.py:183
  18.4 62.2 %collective-permute-start.3 = (bf16[249,2048]{1,0:T(8,128)(2,1)}, bf16[249,2048]{1,0:T(8,128)(2,1)}, u32[]{:S(2)}, u32[]{:S(2)}) collective-permute-start(bf16[249,2048]{1,0:T(8,128)(2,1)} %pad_maximum_fusion.4.feature_ref), channel_id=1, source_target_pairs={{1,0},{2,1},{3,2},{5,4},{6,5},{7,6},{9,8},{10,9},{11,10},{13,12},{... | collective-permute-start | bytes 3059720 | tf_op jit(solution)/shard_map/ppermute | solution.py:184
  19.7 78.6 %collective-permute-start = (s32[4,1024]{1,0:T(4,128)S(1)}, s32[4,1024]{1,0:T(4,128)}, u32[]{:S(2)}, u32[]{:S(2)}) collective-permute-start(s32[4,1024]{1,0:T(4,128)S(1)} %bitcast.192), channel_id=1, source_target_pairs={{1,0},{2,1},{3,2},{0,3},{5,4},{6,5},{7,6},{4,7},{9,8},{10,9},{11,1... | collective-permute-start | bytes 49160 | tf_op jit(solution)/shard_map/ppermute | solution.py:167
  24.4 73.8 %collective-permute-start.1 = (s32[4,1024]{1,0:T(4,128)S(1)}, s32[4,1024]{1,0:T(4,128)}, u32[]{:S(2)}, u32[]{:S(2)}) collective-permute-start(s32[4,1024]{1,0:T(4,128)S(1)} %bitcast.193), channel_id=1, source_target_pairs={{2,0},{3,1},{0,2},{1,3},{6,4},{7,5},{4,6},{5,7},{10,8},{11,9},{8,1... | collective-permute-start | bytes 49160 | tf_op jit(solution)/shard_map/ppermute | solution.py:167
  27.2 22.8 %collective-permute-start.9 = (bf16[3,64,512]{2,1,0:T(8,128)(2,1)}, bf16[3,64,512]{2,1,0:T(8,128)(2,1)S(1)}, u32[]{:S(2)}, u32[]{:S(2)}) collective-permute-start(bf16[3,64,512]{2,1,0:T(8,128)(2,1)} %get-tuple-element.221), channel_id=1, source_target_pairs={{1,0},{2,1},{3,2},{0,3},{5,4},{6,5},{7,6},{4,7},{9,8},{10,9},{11,1... | collective-permute-start | bytes 589832 | tf_op jit(solution)/shard_map/ppermute | solution.py:167
  50.0 10.8 %collective-permute-start.10 = (bf16[3,64,512]{2,1,0:T(8,128)(2,1)}, bf16[3,64,512]{2,1,0:T(8,128)(2,1)S(1)}, u32[]{:S(2)}, u32[]{:S(2)}) collective-permute-start(bf16[3,64,512]{2,1,0:T(8,128)(2,1)} %get-tuple-element.221), channel_id=1, source_target_pairs={{2,0},{3,1},{0,2},{1,3},{6,4},{7,5},{4,6},{5,7},{10,8},{11,9},{8,1... | collective-permute-start | bytes 589832 | tf_op jit(solution)/shard_map/ppermute | solution.py:167
  60.8 8.4 %collective-permute-start.11 = (bf16[3,64,512]{2,1,0:T(8,128)(2,1)}, bf16[3,64,512]{2,1,0:T(8,128)(2,1)S(1)}, u32[]{:S(2)}, u32[]{:S(2)}) collective-permute-start(bf16[3,64,512]{2,1,0:T(8,128)(2,1)} %get-tuple-element.221), channel_id=1, source_target_pairs={{3,0},{0,1},{1,2},{2,3},{7,4},{4,5},{5,6},{6,7},{11,8},{8,9},{9,10... | collective-permute-start | bytes 589832 | tf_op jit(solution)/shard_map/ppermute | solution.py:167
  69.2 29.1 %collective-permute-start.2 = (s32[4,1024]{1,0:T(4,128)S(1)}, s32[4,1024]{1,0:T(4,128)S(1)}, u32[]{:S(2)}, u32[]{:S(2)}) collective-permute-start(s32[4,1024]{1,0:T(4,128)S(1)} %bitcast.194), channel_id=1, source_target_pairs={{3,0},{0,1},{1,2},{2,3},{7,4},{4,5},{5,6},{6,7},{11,8},{8,9},{9,10... | collective-permute-start | bytes 49160 | tf_op jit(solution)/shard_map/ppermute | solution.py:167
  70.1 283.0 %all-gather.8.cloned.1.call-start = ((), (), s32[]{:S(2)}) async-start(), calls=%async_computation.2 | async-start | bytes 1966080 | tf_op jit(solution)/shard_map/all_gather | solution.py:710
  79.8 19.3 %collective-permute-start.6 = (bf16[249,2048]{1,0:T(8,128)(2,1)}, bf16[249,2048]{1,0:T(8,128)(2,1)S(1)}, u32[]{:S(2)}, u32[]{:S(2)}) collective-permute-start(bf16[249,2048]{1,0:T(8,128)(2,1)} %collective-permute-done.5), channel_id=1, source_target_pairs={{1,2},{2,3},{5,6},{6,7},{9,10},{10,11},{13,14},{14,15},{17,18},{18... | collective-permute-start | bytes 3059720 | tf_op jit(solution)/shard_map/ppermute | solution.py:183
  80.6 25.9 %collective-permute-start.4 = (bf16[249,2048]{1,0:T(8,128)(2,1)}, bf16[249,2048]{1,0:T(8,128)(2,1)}, u32[]{:S(2)}, u32[]{:S(2)}) collective-permute-start(bf16[249,2048]{1,0:T(8,128)(2,1)} %collective-permute-done.3), channel_id=1, source_target_pairs={{1,0},{2,1},{5,4},{6,5},{9,8},{10,9},{13,12},{14,13},{17,16},{18,1... | collective-permute-start | bytes 3059720 | tf_op jit(solution)/shard_map/ppermute | solution.py:184
  99.1 30.7 %collective-permute-start.7 = (bf16[249,2048]{1,0:T(8,128)(2,1)S(1)}, bf16[249,2048]{1,0:T(8,128)(2,1)S(1)}, u32[]{:S(2)}, u32[]{:S(2)}) collective-permute-start(bf16[249,2048]{1,0:T(8,128)(2,1)S(1)} %collective-permute-done.6), channel_id=1, source_target_pairs={{2,3},{6,7},{10,11},{14,15},{18,19},{22,23},{26,27},{30,31}} | collective-permute-start | bytes 3059720 | tf_op jit(solution)/shard_map/ppermute | solution.py:183
  106.5 25.4 %collective-permute-start.8 = (bf16[249,2048]{1,0:T(8,128)(2,1)}, bf16[249,2048]{1,0:T(8,128)(2,1)S(1)}, u32[]{:S(2)}, u32[]{:S(2)}) collective-permute-start(bf16[249,2048]{1,0:T(8,128)(2,1)} %collective-permute-done.4), channel_id=1, source_target_pairs={{1,0},{5,4},{9,8},{13,12},{17,16},{21,20},{25,24},{29,28}} | collective-permute-start | bytes 3059720 | tf_op jit(solution)/shard_map/ppermute | solution.py:184
  270.2 15.4 %collective-permute-start.12 = (bf16[83,1024]{1,0:T(8,128)(2,1)S(1)}, bf16[83,1024]{1,0:T(8,128)(2,1)S(1)}, u32[]{:S(2)}, u32[]{:S(2)}) collective-permute-start(bf16[83,1024]{1,0:T(8,128)(2,1)S(1)} %fusion.6), channel_id=1, source_target_pairs={{1,0},{2,1},{3,2},{0,3},{5,4},{6,5},{7,6},{4,7},{9,8},{10,9},{11,1... | collective-permute-start | bytes 509960 | tf_op jit(solution)/shard_map/ppermute | solution.py:167
  271.7 14.7 %collective-permute-start.13 = (bf16[83,1024]{1,0:T(8,128)(2,1)S(1)}, bf16[83,1024]{1,0:T(8,128)(2,1)S(1)}, u32[]{:S(2)}, u32[]{:S(2)}) collective-permute-start(bf16[83,1024]{1,0:T(8,128)(2,1)S(1)} %fusion.6), channel_id=1, source_target_pairs={{2,0},{3,1},{0,2},{1,3},{6,4},{7,5},{4,6},{5,7},{10,8},{11,9},{8,1... | collective-permute-start | bytes 509960 | tf_op jit(solution)/shard_map/ppermute | solution.py:167
  272.9 13.5 %collective-permute-start.14 = (bf16[83,1024]{1,0:T(8,128)(2,1)S(1)}, bf16[83,1024]{1,0:T(8,128)(2,1)S(1)}, u32[]{:S(2)}, u32[]{:S(2)}) collective-permute-start(bf16[83,1024]{1,0:T(8,128)(2,1)S(1)} %fusion.6), channel_id=1, source_target_pairs={{3,0},{0,1},{1,2},{2,3},{7,4},{4,5},{5,6},{6,7},{11,8},{8,9},{9,10... | collective-permute-start | bytes 509960 | tf_op jit(solution)/shard_map/ppermute | solution.py:167
  310.5 9.1 %collective-permute-start.15 = (bf16[83,1024]{1,0:T(8,128)(2,1)}, bf16[83,1024]{1,0:T(8,128)(2,1)S(1)}, u32[]{:S(2)}, u32[]{:S(2)}) collective-permute-start(bf16[83,1024]{1,0:T(8,128)(2,1)} %get-tuple-element.249), channel_id=1, source_target_pairs={{0,1},{1,2},{2,3},{3,0},{4,5},{5,6},{6,7},{7,4},{8,9},{9,10},{10,1... | collective-permute-start | bytes 509960 | tf_op jit(solution)/shard_map/ppermute | solution.py:204
  310.5 13.1 %collective-permute-start.16 = (bf16[83,1024]{1,0:T(8,128)(2,1)}, bf16[83,1024]{1,0:T(8,128)(2,1)S(1)}, u32[]{:S(2)}, u32[]{:S(2)}) collective-permute-start(bf16[83,1024]{1,0:T(8,128)(2,1)} %get-tuple-element.251), channel_id=1, source_target_pairs={{0,2},{1,3},{2,0},{3,1},{4,6},{5,7},{6,4},{7,5},{8,10},{9,11},{10,... | collective-permute-start | bytes 509960 | tf_op jit(solution)/shard_map/ppermute | solution.py:204
  312.3 11.4 %collective-permute-start.17 = (bf16[83,1024]{1,0:T(8,128)(2,1)S(1)}, bf16[83,1024]{1,0:T(8,128)(2,1)S(1)}, u32[]{:S(2)}, u32[]{:S(2)}) collective-permute-start(bf16[83,1024]{1,0:T(8,128)(2,1)S(1)} %get-tuple-element.250), channel_id=1, source_target_pairs={{0,3},{1,0},{2,1},{3,2},{4,7},{5,4},{6,5},{7,6},{8,11},{9,8},{10,9... | collective-permute-start | bytes 509960 | tf_op jit(solution)/shard_map/ppermute | solution.py:204
  316.1 267.3 %all-reduce.4.cloned.1.call-start = ((), (), s32[]{:S(2)}) async-start(), calls=%async_computation.1 | async-start | bytes 9437184 | tf_op jit(solution)/shard_map/psum | solution.py:764
  348.7 258.9 %all-gather.10.cloned.1.call-start = ((), (), s32[]{:S(2)}) async-start(), calls=%async_computation.3 | async-start | bytes 14155776 | tf_op jit(solution)/shard_map/all_gather | solution.py:219
  420.7 23.9 %collective-permute-start.18 = (bf16[768,512]{1,0:T(8,128)(2,1)}, bf16[768,512]{1,0:T(8,128)(2,1)}, u32[]{:S(2)}, u32[]{:S(2)}) collective-permute-start(bf16[768,512]{1,0:T(8,128)(2,1)} %dynamic-slice_convert_fusion), channel_id=1, source_target_pairs={{0,4},{4,0},{8,12},{12,8},{16,20},{20,16},{24,28},{28,24},{1,5},{5... | collective-permute-start | bytes 2359304 | tf_op jit(solution)/shard_map/ppermute | solution.py:117
  446.2 18.4 %collective-permute-start.19 = (bf16[192,512]{1,0:T(8,128)(2,1)S(1)}, bf16[192,512]{1,0:T(8,128)(2,1)S(1)}, u32[]{:S(2)}, u32[]{:S(2)}) collective-permute-start(bf16[192,512]{1,0:T(8,128)(2,1)S(1)} %get-tuple-element.239), channel_id=1, source_target_pairs={{0,8},{4,12},{8,0},{12,4},{16,24},{20,28},{24,16},{28,20},{1,9},{5... | collective-permute-start | bytes 589832 | tf_op jit(solution)/shard_map/ppermute | solution.py:117
  447.7 16.9 %collective-permute-start.20 = (bf16[192,512]{1,0:T(8,128)(2,1)S(1)}, bf16[192,512]{1,0:T(8,128)(2,1)S(1)}, u32[]{:S(2)}, u32[]{:S(2)}) collective-permute-start(bf16[192,512]{1,0:T(8,128)(2,1)S(1)} %get-tuple-element.241), channel_id=1, source_target_pairs={{0,16},{4,20},{8,24},{12,28},{16,0},{20,4},{24,8},{28,12},{1,17},{... | collective-permute-start | bytes 589832 | tf_op jit(solution)/shard_map/ppermute | solution.py:117
  449.2 15.4 %collective-permute-start.21 = (bf16[192,512]{1,0:T(8,128)(2,1)S(1)}, bf16[192,512]{1,0:T(8,128)(2,1)S(1)}, u32[]{:S(2)}, u32[]{:S(2)}) collective-permute-start(bf16[192,512]{1,0:T(8,128)(2,1)S(1)} %get-tuple-element.240), channel_id=1, source_target_pairs={{0,24},{4,28},{8,16},{12,20},{16,8},{20,12},{24,0},{28,4},{1,25},{... | collective-permute-start | bytes 589832 | tf_op jit(solution)/shard_map/ppermute | solution.py:117
  464.8 27.9 %collective-permute-start.22 = (bf16[48,512]{1,0:T(8,128)(2,1)S(1)}, bf16[48,512]{1,0:T(8,128)(2,1)S(1)}, u32[]{:S(2)}, u32[]{:S(2)}) collective-permute-start(bf16[48,512]{1,0:T(8,128)(2,1)S(1)} %get-tuple-element.264), channel_id=1, source_target_pairs={{0,1},{1,0},{2,3},{3,2},{4,5},{5,4},{6,7},{7,6},{8,9},{9,8},{10,11... | collective-permute-start | bytes 147464 | tf_op jit(solution)/shard_map/ppermute | solution.py:117
  472.9 19.7 %collective-permute-start.23 = (bf16[48,512]{1,0:T(8,128)(2,1)S(1)}, bf16[48,512]{1,0:T(8,128)(2,1)S(1)}, u32[]{:S(2)}, u32[]{:S(2)}) collective-permute-start(bf16[48,512]{1,0:T(8,128)(2,1)S(1)} %get-tuple-element.266), channel_id=1, source_target_pairs={{0,2},{1,3},{2,0},{3,1},{4,6},{5,7},{6,4},{7,5},{8,10},{9,11},{10,... | collective-permute-start | bytes 147464 | tf_op jit(solution)/shard_map/ppermute | solution.py:117
  477.5 15.2 %collective-permute-start.24 = (bf16[48,512]{1,0:T(8,128)(2,1)S(1)}, bf16[48,512]{1,0:T(8,128)(2,1)S(1)}, u32[]{:S(2)}, u32[]{:S(2)}) collective-permute-start(bf16[48,512]{1,0:T(8,128)(2,1)S(1)} %get-tuple-element.265), channel_id=1, source_target_pairs={{0,3},{1,2},{2,1},{3,0},{4,7},{5,6},{6,5},{7,4},{8,11},{9,10},{10,... | collective-permute-start | bytes 147464 | tf_op jit(solution)/shard_map/ppermute | solution.py:117
  492.7 19.5 %collective-permute-start.25 = (bf16[48,512]{1,0:T(8,128)(2,1)S(1)}, bf16[48,512]{1,0:T(8,128)(2,1)S(1)}, u32[]{:S(2)}, u32[]{:S(2)}) collective-permute-start(bf16[48,512]{1,0:T(8,128)(2,1)S(1)} %convert_add_fusion.3), channel_id=1, source_target_pairs={{0,3},{1,2},{2,1},{3,0},{4,7},{5,6},{6,5},{7,4},{8,11},{9,10},{10,... | collective-permute-start | bytes 147464 | tf_op jit(solution)/shard_map/ppermute | solution.py:117
  496.7 15.5 %collective-permute-start.26 = (bf16[48,512]{1,0:T(8,128)(2,1)S(1)}, bf16[48,512]{1,0:T(8,128)(2,1)S(1)}, u32[]{:S(2)}, u32[]{:S(2)}) collective-permute-start(bf16[48,512]{1,0:T(8,128)(2,1)S(1)} %convert_add_fusion.3), channel_id=1, source_target_pairs={{0,2},{1,3},{2,0},{3,1},{4,6},{5,7},{6,4},{7,5},{8,10},{9,11},{10,... | collective-permute-start | bytes 147464 | tf_op jit(solution)/shard_map/ppermute | solution.py:117
  496.7 15.5 %collective-permute-start.27 = (bf16[48,512]{1,0:T(8,128)(2,1)S(1)}, bf16[48,512]{1,0:T(8,128)(2,1)S(1)}, u32[]{:S(2)}, u32[]{:S(2)}) collective-permute-start(bf16[48,512]{1,0:T(8,128)(2,1)S(1)} %convert_add_fusion.3), channel_id=1, source_target_pairs={{0,1},{1,0},{2,3},{3,2},{4,5},{5,4},{6,7},{7,6},{8,9},{9,8},{10,11... | collective-permute-start | bytes 147464 | tf_op jit(solution)/shard_map/ppermute | solution.py:117
  532.7 9.2 %collective-permute-start.29 = (f32[64,512]{1,0:T(8,128)S(1)}, f32[64,512]{1,0:T(8,128)S(1)}, u32[]{:S(2)}, u32[]{:S(2)}) collective-permute-start(f32[64,512]{1,0:T(8,128)S(1)} %get-tuple-element.261), channel_id=1, source_target_pairs={{0,8},{4,12},{8,0},{12,4},{16,24},{20,28},{24,16},{28,20},{1,9},{5... | collective-permute-start | bytes 393224 | tf_op jit(solution)/shard_map/ppermute | solution.py:117
  534.2 10.3 %collective-permute-start.30 = (f32[64,512]{1,0:T(8,128)S(1)}, f32[64,512]{1,0:T(8,128)S(1)}, u32[]{:S(2)}, u32[]{:S(2)}) collective-permute-start(f32[64,512]{1,0:T(8,128)S(1)} %get-tuple-element.263), channel_id=1, source_target_pairs={{0,16},{4,20},{8,24},{12,28},{16,0},{20,4},{24,8},{28,12},{1,17},{... | collective-permute-start | bytes 393224 | tf_op jit(solution)/shard_map/ppermute | solution.py:117
  536.3 11.6 %collective-permute-start.31 = (f32[64,512]{1,0:T(8,128)S(1)}, f32[64,512]{1,0:T(8,128)S(1)}, u32[]{:S(2)}, u32[]{:S(2)}) collective-permute-start(f32[64,512]{1,0:T(8,128)S(1)} %get-tuple-element.262), channel_id=1, source_target_pairs={{0,24},{4,28},{8,16},{12,20},{16,8},{20,12},{24,0},{28,4},{1,25},{... | collective-permute-start | bytes 393224 | tf_op jit(solution)/shard_map/ppermute | solution.py:117
  536.3 15.7 %collective-permute-start.42 = (bf16[192,512]{1,0:T(8,128)(2,1)S(1)}, bf16[192,512]{1,0:T(8,128)(2,1)S(1)}, u32[]{:S(2)}, u32[]{:S(2)}) collective-permute-start(bf16[192,512]{1,0:T(8,128)(2,1)S(1)} %pad_maximum_fusion.8), channel_id=1, source_target_pairs={{0,24},{4,28},{8,16},{12,20},{16,8},{20,12},{24,0},{28,4},{1,25},{... | collective-permute-start | bytes 589832 | tf_op jit(solution)/shard_map/ppermute | solution.py:117
  539.2 16.5 %collective-permute-start.43 = (bf16[192,512]{1,0:T(8,128)(2,1)S(1)}, bf16[192,512]{1,0:T(8,128)(2,1)S(1)}, u32[]{:S(2)}, u32[]{:S(2)}) collective-permute-start(bf16[192,512]{1,0:T(8,128)(2,1)S(1)} %pad_maximum_fusion.8), channel_id=1, source_target_pairs={{0,16},{4,20},{8,24},{12,28},{16,0},{20,4},{24,8},{28,12},{1,17},{... | collective-permute-start | bytes 589832 | tf_op jit(solution)/shard_map/ppermute | solution.py:117
  541.9 13.8 %collective-permute-start.44 = (bf16[192,512]{1,0:T(8,128)(2,1)S(1)}, bf16[192,512]{1,0:T(8,128)(2,1)S(1)}, u32[]{:S(2)}, u32[]{:S(2)}) collective-permute-start(bf16[192,512]{1,0:T(8,128)(2,1)S(1)} %pad_maximum_fusion.8), channel_id=1, source_target_pairs={{0,8},{4,12},{8,0},{12,4},{16,24},{20,28},{24,16},{28,20},{1,9},{5... | collective-permute-start | bytes 589832 | tf_op jit(solution)/shard_map/ppermute | solution.py:117
  547.9 7.8 %collective-permute-start.32 = (f32[16,512]{1,0:T(8,128)S(1)}, f32[16,512]{1,0:T(8,128)S(1)}, u32[]{:S(2)}, u32[]{:S(2)}) collective-permute-start(f32[16,512]{1,0:T(8,128)S(1)} %get-tuple-element.279), channel_id=1, source_target_pairs={{0,1},{1,0},{2,3},{3,2},{4,5},{5,4},{6,7},{7,6},{8,9},{9,8},{10,11... | collective-permute-start | bytes 98312 | tf_op jit(solution)/shard_map/ppermute | solution.py:117
  549.5 6.3 collective-permute-start.33
  552.0 5.7 collective-permute-start.34
  557.7 5.9 collective-permute-start.35
  561.1 4.8 collective-permute-start.36
  562.3 18.3 %collective-permute-start.45 = (bf16[768,512]{1,0:T(8,128)(2,1)S(1)}, bf16[768,512]{1,0:T(8,128)(2,1)}, u32[]{:S(2)}, u32[]{:S(2)}) collective-permute-start(bf16[768,512]{1,0:T(8,128)(2,1)S(1)} %pad_maximum_fusion.5), channel_id=1, source_target_pairs={{0,4},{4,0},{8,12},{12,8},{16,20},{20,16},{24,28},{28,24},{1,5},{5... | collective-permute-start | bytes 2359304 | tf_op jit(solution)/shard_map/ppermute | solution.py:117
  566.0 10.1 %collective-permute-start.38 = (f32[64,512]{1,0:T(8,128)S(1)}, f32[64,512]{1,0:T(8,128)S(1)}, u32[]{:S(2)}, u32[]{:S(2)}) collective-permute-start(f32[64,512]{1,0:T(8,128)S(1)} %pad_maximum_fusion.10), channel_id=1, source_target_pairs={{0,24},{4,28},{8,16},{12,20},{16,8},{20,12},{24,0},{28,4},{1,25},{... | collective-permute-start | bytes 393224 | tf_op jit(solution)/shard_map/ppermute | solution.py:117
  566.7 10.2 %collective-permute-start.39 = (f32[64,512]{1,0:T(8,128)S(1)}, f32[64,512]{1,0:T(8,128)S(1)}, u32[]{:S(2)}, u32[]{:S(2)}) collective-permute-start(f32[64,512]{1,0:T(8,128)S(1)} %pad_maximum_fusion.10), channel_id=1, source_target_pairs={{0,16},{4,20},{8,24},{12,28},{16,0},{20,4},{24,8},{28,12},{1,17},{... | collective-permute-start | bytes 393224 | tf_op jit(solution)/shard_map/ppermute | solution.py:117
  568.2 11.5 %collective-permute-start.40 = (f32[64,512]{1,0:T(8,128)S(1)}, f32[64,512]{1,0:T(8,128)S(1)}, u32[]{:S(2)}, u32[]{:S(2)}) collective-permute-start(f32[64,512]{1,0:T(8,128)S(1)} %pad_maximum_fusion.10), channel_id=1, source_target_pairs={{0,8},{4,12},{8,0},{12,4},{16,24},{20,28},{24,16},{28,20},{1,9},{5... | collective-permute-start | bytes 393224 | tf_op jit(solution)/shard_map/ppermute | solution.py:117
  580.6 9.3 %collective-permute-start.41 = (f32[256,512]{1,0:T(8,128)}, f32[256,512]{1,0:T(8,128)}, u32[]{:S(2)}, u32[]{:S(2)}) collective-permute-start(f32[256,512]{1,0:T(8,128)} %pad_maximum_fusion.6), channel_id=1, source_target_pairs={{0,4},{4,0},{8,12},{12,8},{16,20},{20,16},{24,28},{28,24},{1,5},{5... | collective-permute-start | bytes 1572872 | tf_op jit(solution)/shard_map/ppermute | solution.py:117
  (92 other events, 885.7 us)
Sparse Core Ops, SparseCore 0:
  70.2 46.9 all-gather.5
  316.3 36.7 all-gather.7
  358.7 153.9 all-reduce.3
  514.6 88.4 all-gather.9

commit v4 on v3

--- a/solution.py
+++ b/solution.py
@@ -117,46 +117,57 @@
     return lax.ppermute(values, axis_name, [(i, i ^ distance) for i in range(size)])
 
 
-def scatter_stage(values, stage, sent_type):
-    axis_name, first, width = stage
-    members = 1 << width
-    block = values.shape[0] // members
-    mine = (lax.axis_index(axis_name) >> first) & (members - 1)
-    arrived = [
-        partner_swap(
-            lax.dynamic_slice_in_dim(values, (mine ^ far) * block, block, 0).astype(sent_type),
-            axis_name,
-            far << first,
-        )
-        for far in range(1, members)
-    ]
-    values = lax.dynamic_slice_in_dim(values, mine * block, block, 0)
-    for piece in arrived:
-        values = values + piece.astype(jnp.float32)
-    return values
-
-
-def gather_stage(values, stage):
-    axis_name, first, width = stage
-    members = 1 << width
-    mine = (lax.axis_index(axis_name) >> first) & (members - 1)
-    pieces = [values] + [
-        partner_swap(values, axis_name, far << first) for far in range(1, members)
-    ]
-    for bit in range(width):
-        is_high = ((mine >> bit) & 1) == 1
-        step = 1 << bit
-        pieces = [
-            jnp.where(is_high, pieces[place ^ step], pieces[place]) for place in range(members)
+def joint_pieces(coarse, fine):
+    upper = fine.astype(jnp.bfloat16)
+    lower = (fine - lax.optimization_barrier(upper).astype(jnp.float32)).astype(jnp.bfloat16)
+    return jnp.concatenate([coarse.astype(jnp.bfloat16), upper, lower], axis=1)
+
+
+def joint_split(pieces, coarse_width):
+    coarse = pieces[:, :coarse_width]
+    fine_width = (pieces.shape[1] - coarse_width) // 2
+    upper = pieces[:, coarse_width : coarse_width + fine_width].astype(jnp.float32)
+    return coarse, upper + pieces[:, coarse_width + fine_width :].astype(jnp.float32)
+
+
+def joint_sum(coarse, fine, beside):
+    coarse_width = coarse.shape[1]
+    stages = sum_stages()
+    for axis_name, first, width in stages:
+        members = 1 << width
+        block = fine.shape[0] // members
+        mine = (lax.axis_index(axis_name) >> first) & (members - 1)
+        arrived = []
+        for far in range(1, members):
+            begin = (mine ^ far) * block
+            piece = joint_pieces(
+                lax.dynamic_slice_in_dim(coarse, begin, block, 0),
+                lax.dynamic_slice_in_dim(fine, begin, block, 0),
+            )
+            arrived.append(partner_swap(piece, axis_name, far << first))
+        coarse = lax.dynamic_slice_in_dim(coarse, mine * block, block, 0)
+        fine = lax.dynamic_slice_in_dim(fine, mine * block, block, 0)
+        for piece in arrived:
+            more_coarse, more_fine = joint_split(piece, coarse_width)
+            coarse = coarse + more_coarse.astype(jnp.float32)
+            fine = fine + more_fine
+    values = joint_pieces(coarse, fine)
+    values, beside = lax.optimization_barrier((values, beside))
+    for axis_name, first, width in stages[::-1]:
+        members = 1 << width
+        mine = (lax.axis_index(axis_name) >> first) & (members - 1)
+        pieces = [values] + [
+            partner_swap(values, axis_name, far << first) for far in range(1, members)
         ]
-    return jnp.concatenate(pieces, axis=0)
-
-
-def sum_steps(sent_type):
-    stages = sum_stages()
-    steps = [functools.partial(scatter_stage, stage=s, sent_type=sent_type) for s in stages]
-    steps.append(lambda values: gather_stage(values.astype(sent_type), stages[-1]))
-    return steps + [functools.partial(gather_stage, stage=s) for s in stages[-2::-1]]
+        for bit in range(width):
+            is_high = ((mine >> bit) & 1) == 1
+            step = 1 << bit
+            pieces = [
+                jnp.where(is_high, pieces[place ^ step], pieces[place])
+                for place in range(members)
+            ]
+        values = jnp.concatenate(pieces, axis=0)
+    return values, *beside
 
 
 def ring_slots(values):
@@ -169,21 +180,32 @@
     return slots
 
 
-def line_slots(values):
+def line_slots(values, use_slot, later):
     size = lax.axis_size("narrow")
     pos = lax.axis_index("narrow")
     from_low, from_high = values, values
     arrived = {}
-    slots = [(values, pos)]
     orders = [
         sorted((s for s in range(size) if s != n), key=lambda s, n=n: (abs(s - n), s < n))
         for n in range(size)
     ]
-    for step in range(size - 1):
-        from_low = lax.ppermute(from_low, "narrow", [(i, i + 1) for i in range(step, size - 1)])
-        from_high = lax.ppermute(
-            from_high, "narrow", [(i, i - 1) for i in range(1, size - step)]
-        )
+    chosen, source = values, pos
+    for step in range(size):
+        if step < size - 1:
+            from_low = lax.ppermute(
+                from_low, "narrow", [(i, i + 1) for i in range(step, size - 1)]
+            )
+            from_high = lax.ppermute(
+                from_high, "narrow", [(i, i - 1) for i in range(1, size - step)]
+            )
+        result = use_slot(chosen, source)
+        if step == size - 1:
+            return later
+        if step == 0:
+            result = (result, later)
+        from_low, from_high, result = lax.optimization_barrier((from_low, from_high, result))
+        if step == 0:
+            later = result[1]
         arrived[-1 - step] = from_low
         arrived[1 + step] = from_high
         offsets = [orders[n][step] - n for n in range(size)]
@@ -193,8 +215,7 @@
                 jnp.logical_or, [pos == n for n in range(size) if offsets[n] == offset]
             )
             chosen = jnp.where(here, arrived[offset], chosen)
-        slots.append((chosen, pos + jnp.array(offsets, jnp.int32)[pos]))
-    return slots
+        source = pos + jnp.array(offsets, jnp.int32)[pos]
 
 
 def ring_sum(parts):
@@ -210,31 +231,13 @@
     return total
 
 
-def own_rows(blocks):
-    rows = blocks.shape[1] // lax.axis_size("wide")
-    return lax.dynamic_slice_in_dim(blocks, lax.axis_index("wide") * rows, rows, 1)
-
-
-def spread_wide(across):
-    whole = lax.all_gather(across, "wide", axis=0)
-    count = whole.shape[2]
-    return whole.transpose(2, 1, 0, 3, 4).reshape(count, -1, whole.shape[4])
-
-
-def near_gather(own):
-    size = lax.axis_size("narrow")
-    pos = lax.axis_index("narrow")
-    across = jnp.zeros((size,) + own.shape, own.dtype)
-    for shift, piece in enumerate(ring_slots(own)):
-        across = lax.dynamic_update_slice_in_dim(
-            across, piece[None], (pos + shift) % size, 0
-        )
-    return across
-
-
 VMEM_LIMIT = 60 * 1024 * 1024
 SCORE_SCALE = math.log2(math.e) / math.sqrt(HEAD_WIDTH)
 MASKED = -1e30
+
+
+def small_cost():
+    return pl.CostEstimate(flops=1 << 20, bytes_accessed=1 << 20, transcendentals=0)
 
 
 def kernel_params():
@@ -263,11 +266,7 @@
         in_specs=[pl.BlockSpec((rows, slots), lambda j, i: (i, 0))],
         out_specs=pl.BlockSpec((rows, columns), lambda j, i: (i, j)),
         out_shape=jax.ShapeDtypeStruct((row_count, column_count), jnp.bfloat16),
-        cost_estimate=pl.CostEstimate(
-            flops=4 * slots * row_count * column_count,
-            bytes_accessed=2 * row_count * column_count,
-            transcendentals=0,
-        ),
+        cost_estimate=small_cost(),
         compiler_params=kernel_params(),
     )(ids)
 
@@ -301,9 +300,7 @@
         in_specs=[spec, spec],
         out_specs=pl.BlockSpec((8 * per_step, total), lambda i: (i, 0)),
         out_shape=jax.ShapeDtypeStruct((row_count, total), jnp.float32),
-        cost_estimate=pl.CostEstimate(
-            flops=16 * row_count * total, bytes_accessed=4 * row_count * total, transcendentals=0
-        ),
+        cost_estimate=small_cost(),
         compiler_params=kernel_params(),
     )(row_keys, lane_keys)
 
@@ -347,11 +344,7 @@
         out_specs=[block, block],
         out_shape=[jax.ShapeDtypeStruct(queries.shape, jnp.float32)] * 2,
         scratch_shapes=[pltpu.VMEM((rows, total), jnp.float32)],
-        cost_estimate=pl.CostEstimate(
-            flops=16 * row_count * total * HEAD_WIDTH * HEADS,
-            bytes_accessed=16 * row_count * total,
-            transcendentals=HEADS * row_count * total,
-        ),
+        cost_estimate=small_cost(),
         compiler_params=kernel_params(),
     )(queries, pairs, pairs, bias)
 
@@ -424,72 +417,78 @@
         out_specs=[block, column, column],
         out_shape=[jax.ShapeDtypeStruct(queries.shape, jnp.bfloat16), key_shape, key_shape],
         scratch_shapes=[pltpu.VMEM((total, HEAD_WIDTH), jnp.float32)] * 2,
-        cost_estimate=pl.CostEstimate(
-            flops=24 * row_count * total * HEAD_WIDTH * HEADS,
-            bytes_accessed=16 * row_count * total,
-            transcendentals=HEADS * row_count * total,
-        ),
+        cost_estimate=small_cost(),
         compiler_params=kernel_params(),
     )(queries, pairs, pairs, bias, mass, attended, grads)
 
 
-def gather_kernel(sub, ids_ref, pixel_ref, *rest):
-    out_ref = rest[-1]
+def gather_kernel(sub, first_ref, ids_ref, feature_ref, map_ref, bias_ref, *rest):
+    out_ref, pixel_ref = rest[-2:]
+
+    @pl.when(pl.program_id(0) == 0)
+    def _():
+        pre = contract_rows(feature_ref[...], map_ref[...]) + bias_ref[...]
+        pixel_ref[...] = (pre / (1.0 + jnp.exp(-pre))).astype(jnp.bfloat16)
+
     pixels = pixel_ref[...]
     columns = lax.broadcasted_iota(jnp.int32, (sub, pixels.shape[0]), 1).astype(jnp.int16)
     one = jnp.ones(columns.shape, jnp.bfloat16)
     zero = jnp.zeros(columns.shape, jnp.bfloat16)
     for block in range(out_ref.shape[0] // sub):
         part = pl.ds(block * sub, sub)
-        ids = ids_ref[part, :].astype(jnp.int16)
+        ids = (ids_ref[part, :] - first_ref[0, 0]).astype(jnp.int16)
         counts = zero
         for slot in range(ids.shape[1]):
             counts = counts + jnp.where(ids[:, slot : slot + 1] == columns, one, zero)
         rows = jnp.dot(counts, pixels, preferred_element_type=jnp.float32)
-        if len(rest) == 2:
+        if len(rest) == 3:
             rows = rows + rest[0][part, :]
         out_ref[part, :] = rows
 
 
-def gather_sum(ids, pixels, earlier, rows=1024, sub=256):
+def gather_sum(first, ids, features, embed_map, embed_bias, earlier, rows=1024, sub=256):
     row_count, slots = ids.shape
-    pixel_count, width = pixels.shape
+    channels, pixel_count = features.shape
+    width = embed_map.shape[1]
     block = pl.BlockSpec((rows, width), lambda i: (i, 0))
     more = [] if earlier is None else [earlier]
     return pl.pallas_call(
         functools.partial(gather_kernel, sub),
         grid=(row_count // rows,),
         in_specs=[
+            pl.BlockSpec(memory_space=pltpu.SMEM),
             pl.BlockSpec((rows, slots), lambda i: (i, 0)),
-            pl.BlockSpec((pixel_count, width), lambda i: (0, 0)),
+            pl.BlockSpec((channels, pixel_count), lambda i: (0, 0)),
+            pl.BlockSpec((channels, width), lambda i: (0, 0)),
+            pl.BlockSpec((1, width), lambda i: (0, 0)),
         ]
         + [block] * len(more),
         out_specs=block,
         out_shape=jax.ShapeDtypeStruct((row_count, width), jnp.float32),
-        cost_estimate=pl.CostEstimate(
-            flops=2 * row_count * pixel_count * width,
-            bytes_accessed=12 * row_count * width,
-            transcendentals=0,
-        ),
+        scratch_shapes=[pltpu.VMEM((pixel_count, width), jnp.bfloat16)],
+        cost_estimate=small_cost(),
         compiler_params=kernel_params(),
-    )(ids, pixels, *more)
-
-
-def scatter_kernel(chunk, ids_ref, g_ref, pre_ref, feature_ref, grad_ref, bias_ref):
+    )(first.reshape(1, 1), ids, features, embed_map, embed_bias, *more)
+
+
+def scatter_kernel(
+    chunk, first_ref, ids_ref, g_ref, feature_ref, map_ref, shift_ref, grad_ref, bias_ref
+):
     step = pl.program_id(0)
-    rows = pre_ref.shape[0]
+    rows = feature_ref.shape[1]
     pixel_ids = lax.broadcasted_iota(jnp.int32, (rows, chunk), 0).astype(jnp.int16)
     one = jnp.ones((rows, chunk), jnp.bfloat16)
     zero = jnp.zeros((rows, chunk), jnp.bfloat16)
-    spread = jnp.zeros(pre_ref.shape, jnp.float32)
+    spread = jnp.zeros((rows, g_ref.shape[1]), jnp.float32)
     for start in range(0, g_ref.shape[0], chunk):
         part = pl.ds(start, chunk)
         counts = zero
         for slot in range(ids_ref.shape[0]):
-            ids = jnp.broadcast_to(ids_ref[slot : slot + 1, part] - step * rows, (rows, chunk))
+            ids = ids_ref[slot : slot + 1, part] - (first_ref[0, 0] + step * rows)
+            ids = jnp.broadcast_to(ids, (rows, chunk))
             counts = counts + jnp.where(ids.astype(jnp.int16) == pixel_ids, one, zero)
         spread = spread + jnp.dot(counts, g_ref[part, :], preferred_element_type=jnp.float32)
-    pre = pre_ref[...]
+    pre = contract_rows(feature_ref[...], map_ref[...]) + shift_ref[...]
     sigmoid_values = 1.0 / (1.0 + jnp.exp(-pre))
     lowered = (spread * (sigmoid_values * (1.0 + pre * (1.0 - sigmoid_values)))).astype(
         jnp.bfloat16
@@ -504,18 +503,20 @@
     bias_ref[...] += jnp.sum(lowered.astype(jnp.float32), axis=0, keepdims=True)
 
 
-def scatter_sum(ids, grads, pre, features, rows=512, chunk=1024):
+def scatter_sum(first, ids, grads, features, embed_map, embed_bias, rows=512, chunk=1024):
     slots, node_count = ids.shape
-    pixel_count, width = pre.shape
-    channels = features.shape[0]
+    width = grads.shape[1]
+    channels, pixel_count = features.shape
     return pl.pallas_call(
         functools.partial(scatter_kernel, chunk),
         grid=(pixel_count // rows,),
         in_specs=[
+            pl.BlockSpec(memory_space=pltpu.SMEM),
             pl.BlockSpec((slots, node_count), lambda i: (0, 0)),
             pl.BlockSpec((node_count, width), lambda i: (0, 0)),
-            pl.BlockSpec((rows, width), lambda i: (i, 0)),
             pl.BlockSpec((channels, rows), lambda i: (0, i)),
+            pl.BlockSpec((channels, width), lambda i: (0, 0)),
+            pl.BlockSpec((1, width), lambda i: (0, 0)),
         ],
         out_specs=[
             pl.BlockSpec((channels, width), lambda i: (0, 0)),
@@ -525,13 +526,135 @@
             jax.ShapeDtypeStruct((channels, width), jnp.float32),
             jax.ShapeDtypeStruct((1, width), jnp.float32),
         ],
-        cost_estimate=pl.CostEstimate(
-            flops=2 * node_count * pixel_count * width,
-            bytes_accessed=8 * pixel_count * width,
-            transcendentals=pixel_count * width,
-        ),
+        cost_estimate=small_cost(),
         compiler_params=kernel_params(),
-    )(ids, grads, pre, features)
+    )(first.reshape(1, 1), ids, grads, features, embed_map, embed_bias)
+
+
+def row_norm(sums):
+    values = sums * (1.0 / G2M_K)
+    centred = values - jnp.mean(values, axis=1, keepdims=True)
+    inverse = lax.rsqrt(jnp.mean(centred * centred, axis=1, keepdims=True) + 1e-05)
+    return centred * inverse, inverse
+
+
+def project_kernel(sum_ref, shift_ref, map_ref, attn_ref, query_ref, pair_ref):
+    width = sum_ref.shape[1]
+    normed, _ = row_norm(sum_ref[...])
+    attn_in = (normed * shift_ref[0:1, :] + shift_ref[1:2, :]).astype(jnp.bfloat16)
+    attn_ref[...] = attn_in
+    for place in range(2):
+        part = pl.ds(place * width, width)
+        weights = map_ref[pl.ds((place + 1) * width, width), :]
+        pair_ref[:, part] = contract_last(attn_in, weights).astype(jnp.bfloat16)
+
+    @pl.when(pl.program_id(0) == 0)
+    def _():
+        query_ref[...] = contract_last(attn_in, map_ref[pl.ds(0, width), :]).astype(jnp.bfloat16)
+
+
+def project(sums, shifts, attn_map, rows):
+    row_count, width = sums.shape
+    block = pl.BlockSpec((rows, width), lambda i: (i, 0))
+    return pl.pallas_call(
+        project_kernel,
+        grid=(row_count // rows,),
+        in_specs=[
+            block,
+            pl.BlockSpec(shifts.shape, lambda i: (0, 0)),
+            pl.BlockSpec(attn_map.shape, lambda i: (0, 0)),
+        ],
+        out_specs=[
+            block,
+            pl.BlockSpec((rows, width), lambda i: (0, 0)),
+            pl.BlockSpec((rows, 2 * width), lambda i: (i, 0)),
+        ],
+        out_shape=[
+            jax.ShapeDtypeStruct((row_count, width), jnp.bfloat16),
+            jax.ShapeDtypeStruct((rows, width), jnp.bfloat16),
+            jax.ShapeDtypeStruct((row_count, 2 * width), jnp.bfloat16),
+        ],
+        cost_estimate=small_cost(),
+        compiler_params=kernel_params(),
+    )(sums, shifts, attn_map)
+
+
+def project_back_kernel(
+    dq_ref,
+    dk_ref,
+    dv_ref,
+    sum_ref,
+    attn_ref,
+    mid_ref,
+    shift_ref,
+    map_ref,
+    node_ref,
+    grad_ref,
+    column_ref,
+    back_ref,
+):
+    step = pl.program_id(0)
+    width = sum_ref.shape[1]
+    attn_in = attn_ref[...]
+    dk, dv = dk_ref[...], dv_ref[...]
+    back_ref[...] = plain_dot(dk, map_ref[pl.ds(width, width), :]) + plain_dot(
+        dv, map_ref[pl.ds(2 * width, width), :]
+    )
+
+    @pl.when(step == 0)
+    def _():
+        grad_ref[...] = jnp.zeros_like(grad_ref)
+        column_ref[...] = jnp.zeros_like(column_ref)
+        dq = dq_ref[...]
+        back_ref[...] += plain_dot(dq, map_ref[pl.ds(0, width), :])
+        grad_ref[:, pl.ds(0, width)] = contract_rows(dq, attn_in)
+
+    grad_ref[:, pl.ds(width, width)] += contract_rows(dk, attn_in)
+    grad_ref[:, pl.ds(2 * width, width)] += contract_rows(dv, attn_in)
+    back = back_ref[...]
+    normed, inverse = row_norm(sum_ref[...])
+    column_ref[0:1, :] += jnp.sum(back * normed, axis=0, keepdims=True)
+    column_ref[1:2, :] += jnp.sum(back, axis=0, keepdims=True)
+    grads = back * shift_ref[0:1, :]
+    first_mean = jnp.mean(grads, axis=1, keepdims=True)
+    second_mean = jnp.mean(grads * normed, axis=1, keepdims=True)
+    grads = inverse * (grads - first_mean - normed * second_mean)
+    own_share = jnp.where(step == 0, 1.0, 0.0)
+    node_ref[...] = ((grads + own_share * mid_ref[...]) * (1.0 / G2M_K)).astype(jnp.bfloat16)
+
+
+def project_back(dq, dk, dv, sums, attn_in, mid, shifts, attn_map):
+    row_count, width = sums.shape
+    rows = dq.shape[0]
+    block = pl.BlockSpec((rows, width), lambda i: (i, 0))
+    own = pl.BlockSpec((rows, width), lambda i: (0, 0))
+    return pl.pallas_call(
+        project_back_kernel,
+        grid=(row_count // rows,),
+        in_specs=[
+            own,
+            block,
+            block,
+            block,
+            block,
+            own,
+            pl.BlockSpec(shifts.shape, lambda i: (0, 0)),
+            pl.BlockSpec(attn_map.shape, lambda i: (0, 0)),
+        ],
+        out_specs=[
+            block,
+            pl.BlockSpec((width, 3 * width), lambda i: (0, 0)),
+            pl.BlockSpec((8, width), lambda i: (0, 0)),
+        ],
+        out_shape=[
+            jax.ShapeDtypeStruct((row_count, width), jnp.bfloat16),
+            jax.ShapeDtypeStruct((width, 3 * width), jnp.float32),
+            jax.ShapeDtypeStruct((8, width), jnp.float32),
+        ],
+        scratch_shapes=[pltpu.VMEM((rows, width), jnp.float32)],
+        cost_estimate=small_cost(),
+        compiler_params=kernel_params(),
+    )(dq, dk, dv, sums, attn_in, mid, shifts, attn_map)
 
 
 def split_low(values):
@@ -547,30 +670,30 @@
     return dot(left[0], right[0]) + (dot(left[0], right[1]) + dot(left[1], right[0]))
 
 
-def muon_kernel(factor_ref, pos_ref, mom_ref, attn_ref, rest_ref, moment_ref, turned_ref, full_ref):
-    matrix = pl.program_id(0)
+def muon_kernel(choice_ref, factor_ref, mom_ref, qkv_ref, proj_ref, rest_ref, turned_ref, full_ref):
+    matrix, pos = choice_ref[0], choice_ref[1]
     factor = factor_ref[0, 0]
-    own, width = moment_ref.shape[1:]
+    own, width = turned_ref.shape
     gram = jnp.zeros((width, width), jnp.float32)
-    for start in range(0, mom_ref.shape[1], own):
-        part = pl.ds(start, own)
+    for place in range(FF // width):
+        part = pl.ds(place * width, width)
+        if place < 3:
+            first = qkv_ref[:, part]
+        else:
+            first = proj_ref[...]
         grads = jnp.where(
-            matrix == 0,
-            attn_ref[part, :].astype(jnp.float32),
-            rest_ref[part, :].astype(jnp.float32),
+            matrix == 0, first.astype(jnp.float32), rest_ref[part, :].astype(jnp.float32)
         )
-        moment = muon_decay * mom_ref[0, part, :] + factor * grads
+        moment = muon_decay * mom_ref[0, part, :].astype(jnp.float32) + factor * grads
         full_ref[part, :] = moment
         halves = split_low(moment)
         gram = gram + triple_dot(halves, halves, contract_rows)
-    mine = full_ref[pl.ds(pos_ref[0, 0] * own, own), :]
-    moment_ref[0] = mine
     row_ids = lax.broadcasted_iota(jnp.int32, gram.shape, 0)
     eye = jnp.where(row_ids == lax.broadcasted_iota(jnp.int32, gram.shape, 1), 1.0, 0.0)
     trace = jnp.sum(jnp.sum(gram * eye, axis=1, keepdims=True), axis=0, keepdims=True)
     scale = 1.0 / (jnp.sqrt(trace) + 1e-07)
     gram = gram * (scale * scale)
-    turned = mine * scale
+    turned = full_ref[pl.ds(pos * own, own), :] * scale
     for iteration in range(NS_ITERS):
         gram_halves = split_low(gram)
         poly = coef_a * eye + coef_b * gram + coef_c * triple_dot(gram_halves, gram_halves)
@@ -578,32 +701,122 @@
         turned = triple_dot(split_low(turned), poly_halves)
         if iteration < NS_ITERS - 1:
             gram = triple_dot(poly_halves, split_low(triple_dot(poly_halves, gram_halves)))
-    turned_ref[0] = turned
-
-
-def muon_parts(factor, pos, mom_full, sum_attn, sum_rest, own):
-    matrices, rows, width = mom_full.shape
-    block = pl.BlockSpec((1, own, width), lambda i: (i, 0, 0))
-    scalar = pl.BlockSpec(memory_space=pltpu.SMEM)
-    shape = jax.ShapeDtypeStruct((matrices, own, width), jnp.float32)
+    turned_ref[...] = turned.astype(jnp.bfloat16)
+
+
+def turn_moment(matrix, pos, factor, mom_full, sum_qkv, sum_rest, own):
+    rows, width = mom_full.shape[1:]
     return pl.pallas_call(
         muon_kernel,
-        grid=(matrices,),
-        in_specs=[
-            scalar,
-            scalar,
-            pl.BlockSpec((1, rows, width), lambda i: (i, 0, 0)),
-            pl.BlockSpec((rows, width), lambda i: (0, 0)),
-            pl.BlockSpec((rows, width), lambda i: (jnp.maximum(i - 1, 0), 0)),
-        ],
-        out_specs=[block, block],
-        out_shape=[shape, shape],
-        scratch_shapes=[pltpu.VMEM((rows, width), jnp.float32)],
-        cost_estimate=pl.CostEstimate(
-            flops=100 * matrices * width**3, bytes_accessed=8 * matrices * rows * width, transcendentals=0
+        grid_spec=pltpu.PrefetchScalarGridSpec(
+            num_scalar_prefetch=1,
+            grid=(1,),
+            in_specs=[
+                pl.BlockSpec(memory_space=pltpu.SMEM),
+                pl.BlockSpec((1, rows, width), lambda i, choice: (choice[0], 0, 0)),
+                pl.BlockSpec((width, 3 * width), lambda i, choice: (0, 0)),
+                pl.BlockSpec((width, width), lambda i, choice: (2 * FF // width, 0)),
+                pl.BlockSpec(
+                    (rows, width), lambda i, choice: (jnp.maximum(choice[0] - 1, 0), 0)
+                ),
+            ],
+            out_specs=pl.BlockSpec((own, width), lambda i, choice: (0, 0)),
+            scratch_shapes=[pltpu.VMEM((rows, width), jnp.float32)],
         ),
+        out_shape=jax.ShapeDtypeStruct((own, width), jnp.bfloat16),
+        cost_estimate=small_cost(),
         compiler_params=kernel_params(),
-    )(factor.reshape(1, 1), pos.reshape(1, 1), mom_full, sum_attn, sum_rest)
+    )(jnp.stack([matrix, pos]), factor.reshape(1, 1), mom_full, sum_qkv, sum_rest, sum_rest)
+
+
+def share_turned(turned, group, moments):
+    across = partner_swap(turned, "wide", 2)
+    across, moments = lax.optimization_barrier((across, moments))
+    beside = partner_swap(turned, "wide", 1)
+    corner = partner_swap(across, "wide", 1)
+    low_side = group < 2
+    even = group % 2 == 0
+    first = jnp.where(even, turned, beside)
+    second = jnp.where(even, beside, turned)
+    far_first = jnp.where(even, across, corner)
+    far_second = jnp.where(even, corner, across)
+    return (
+        jnp.where(low_side, first, far_first),
+        jnp.where(low_side, second, far_second),
+        jnp.where(low_side, across, turned),
+    ), moments
+
+
+def moment_kernel(pos_ref, factor_ref, qkv_ref, proj_ref, up_ref, down_ref, *refs):
+    own_refs, moment_refs = refs[:3], refs[3:]
+    pos = pos_ref[0]
+    factor = factor_ref[0, 0]
+    own = own_refs[2].shape[0]
+    proj_share = jnp.where(pos == FF // own - 1, 1.0, 0.0)
+    first = jnp.where(
+        proj_share > 0.5, proj_ref[...].astype(jnp.float32), qkv_ref[...].astype(jnp.float32)
+    )
+    moment_refs[0][...] = muon_decay * own_refs[0][...] + factor * first.T
+    second = up_ref[...].astype(jnp.float32)
+    moment_refs[1][...] = muon_decay * own_refs[1][...] + factor * second.T
+    third = down_ref[...].astype(jnp.float32)
+    moment_refs[2][...] = muon_decay * own_refs[2][...] + factor * third
+
+
+def own_moments(pos, factor, sum_qkv, sum_rest, moms):
+    own, width = moms[2].shape
+    parts = FF // own
+    whole = pl.BlockSpec((own, width), lambda i, pos: (0, 0))
+    return pl.pallas_call(
+        moment_kernel,
+        grid_spec=pltpu.PrefetchScalarGridSpec(
+            num_scalar_prefetch=1,
+            grid=(1,),
+            in_specs=[
+                pl.BlockSpec(memory_space=pltpu.SMEM),
+                pl.BlockSpec((width, width), lambda i, pos: (0, jnp.minimum(pos[0], 2))),
+                pl.BlockSpec((width, width), lambda i, pos: (2 * FF // width, 0)),
+                pl.BlockSpec((own, width), lambda i, pos: (pos[0], 0)),
+                pl.BlockSpec((own, width), lambda i, pos: (parts + pos[0], 0)),
+            ]
+            + [whole] * 3,
+            out_specs=[whole] * 3,
+        ),
+        out_shape=[jax.ShapeDtypeStruct((own, width), jnp.float32)] * 3,
+        cost_estimate=small_cost(),
+        compiler_params=kernel_params(),
+    )(
+        pos.reshape(1),
+        factor.reshape(1, 1),
+        sum_qkv,
+        sum_rest,
+        sum_rest,
+        sum_rest,
+        *moms,
+    )
+
+
+def step_kernel(*refs):
+    rates = [
+        muon_rate * math.sqrt(max(1.0, LATENT_WIDTH / FF)),
+        muon_rate * math.sqrt(max(1.0, LATENT_WIDTH / FF)),
+        muon_rate * math.sqrt(max(1.0, FF / LATENT_WIDTH)),
+    ]
+    for place in range(3):
+        turned = refs[place][...].astype(jnp.float32)
+        change = turned if place == 2 else turned.T
+        new = refs[3 + place][...] - rates[place] * change
+        refs[9 + place][...] = new
+        refs[12 + place][...] = ema_keep * refs[6 + place][...] + (1.0 - ema_keep) * new
+
+
+def take_step(turned, weights, averages):
+    return pl.pallas_call(
+        step_kernel,
+        out_shape=[jax.ShapeDtypeStruct(weights[0].shape, jnp.float32)] * 6,
+        cost_estimate=small_cost(),
+        compiler_params=kernel_params(),
+    )(*turned, *weights, *averages)
 
 
 def adam_update(weight, grad, first, second):
@@ -661,7 +874,7 @@
     node_total = node_local * narrow_count
     embed_low = w_embed.astype(jnp.bfloat16)
     dec_low = w_dec.astype(jnp.bfloat16)
-    bias_embed = biases[:LATENT_WIDTH]
+    bias_embed = biases[:LATENT_WIDTH].reshape(1, LATENT_WIDTH)
     bias_up = biases[LATENT_WIDTH : LATENT_WIDTH + FF]
     bias_out = biases[LATENT_WIDTH + FF :]
     noise_level, scale_in, skip_scale, out_scale, loss_scale = sigma_terms(level_index[0])
@@ -671,11 +884,6 @@
         [prior_states[0, 0], prior_states[0, 1], (scale_in * noisy).astype(jnp.bfloat16)], axis=0
     )
     g2m_rows = jnp.concatenate(ring_slots(g2m_edges[0].T), axis=1)
-    g2m_cols = g2m_rows.T
-    feature_slots = line_slots(features)
-    low_blocks = jnp.stack([w_attn.T, w_up.T, w_down]).astype(jnp.bfloat16)
-    weight_full = spread_wide(near_gather(own_rows(low_blocks)))
-    attn_rows, up_rows, down_full = weight_full[0], weight_full[1], weight_full[2]
     lat_weight = lat_weights(narrow_pos * pixel_local, pixel_local, pixel_total)
     pixel_weight = lat_weight * valid_mask[0].astype(jnp.float32)
     near_ids = (neighbours[0] - narrow_pos * node_local) % node_total
@@ -683,35 +891,50 @@
     near_bias = count_bias(near_ids, node_total)
     m2g_counts = count_matrix(m2g_ids, node_total)
 
-    embed_pres = []
-    node_in = None
-    for features_here, source in feature_slots:
-        embed_pre = contract_rows(features_here, embed_low) + bias_embed
-        embedded = jax.nn.silu(embed_pre).astype(jnp.bfloat16)
-        node_in = gather_sum(g2m_cols - source * pixel_local, embedded, node_in)
-        embed_pres.append(embed_pre)
-    node_in = node_in / G2M_K
+    feature_slots, node_sums = [], []
+
+    def use_slot(features_here, source):
+        node_sums.append(
+            gather_sum(
+                source * pixel_local,
+                g2m_cols,
+                features_here,
+                embed_low,
+                bias_embed,
+                node_sums[-1] if node_sums else None,
+            )
+        )
+        feature_slots.append((features_here, source))
+        return node_sums[-1], near_bias
+
+    g2m_cols = g2m_rows.T
+    piece_rows = LATENT_WIDTH // lax.axis_size("wide")
+    piece_first = lax.axis_index("wide") * piece_rows
+    low_own = jnp.stack(
+        [
+            lax.dynamic_slice_in_dim(one, piece_first, piece_rows, 0)
+            if place % 3 == 2
+            else lax.dynamic_slice_in_dim(one, piece_first, piece_rows, 1).T
+            for place, one in enumerate((w_attn, w_up, w_down, mom_attn, mom_up, mom_down))
+        ]
+    ).astype(jnp.bfloat16)
+    near_blocks = lax.all_gather(low_own, "narrow", axis=0)
+    near_blocks = line_slots(features, use_slot, near_blocks)
+    weight_all = lax.all_gather(near_blocks[:, :3], "wide", axis=0)
+    mom_near, _ = lax.optimization_barrier((near_blocks, node_sums[3]))
+    mom_all = lax.all_gather(mom_near[:, 3:], "wide", axis=0)
+    weight_full = weight_all.transpose(2, 1, 0, 3, 4).reshape(3, -1, LATENT_WIDTH)
+    attn_rows, up_rows, down_full = weight_full[0], weight_full[1], weight_full[2]
     conditioning = cond_features(noise_level)
     modulation = jnp.dot(conditioning, w_cond, precision=highest_precision)
-    gain_one = 1.0 + modulation[:LATENT_WIDTH]
     gain_two = 1.0 + modulation[2 * LATENT_WIDTH : 3 * LATENT_WIDTH]
-    normed_one, inverse_one = norm_stats(node_in)
-    attn_in = (normed_one * gain_one + modulation[LATENT_WIDTH : 2 * LATENT_WIDTH]).astype(
-        jnp.bfloat16
-    )
-    attn_own = attn_in[:node_local]
-    query_map = attn_rows[:LATENT_WIDTH]
-    pair_map = attn_rows[LATENT_WIDTH : 3 * LATENT_WIDTH]
+    shifts = modulation.reshape(4, LATENT_WIDTH) + jnp.array([[1.0], [0.0], [1.0], [0.0]])
+    node_sum = node_sums[-1]
     proj_map = attn_rows[3 * LATENT_WIDTH :]
-    query_rows = contract_last(attn_own, query_map).astype(jnp.bfloat16)
-    pair_rows = contract_last(attn_in, pair_map).astype(jnp.bfloat16)
-    mom_blocks = jnp.stack([mom_attn.T, mom_up.T, mom_down])
-    mom_blocks, pair_rows = lax.optimization_barrier((mom_blocks, pair_rows))
-    mom_full = spread_wide(lax.all_gather(own_rows(mom_blocks), "narrow", axis=0))
-
+    attn_in, query_rows, pair_rows = project(node_sum, shifts, attn_rows, node_local)
     attended, mass = attend(query_rows, pair_rows, near_bias)
     attended_rows = attended.astype(jnp.bfloat16)
-    node_mid = node_in[:node_local] + contract_last(attended_rows, proj_map)
+    node_mid = node_sum[:node_local] / G2M_K + contract_last(attended_rows, proj_map)
     normed_two, inverse_two = norm_stats(node_mid)
     mlp_in = (normed_two * gain_two + modulation[3 * LATENT_WIDTH :]).astype(jnp.bfloat16)
     up_pre = contract_last(mlp_in, up_rows) + bias_up
@@ -750,6 +973,7 @@
         (((0,), (1,)), ((), ())),
         precision=highest_precision,
     )
+    grad_node_out, mom_all = lax.optimization_barrier((grad_node_out, mom_all))
     grad_mlp = grad_node_out.astype(jnp.bfloat16)
     grad_down = contract_rows(hidden, grad_mlp)
     grad_hidden = contract_last(grad_mlp, down_full)
@@ -761,50 +985,39 @@
     grad_proj_out = grad_node_mid.astype(jnp.bfloat16)
     grad_proj = contract_rows(grad_proj_out, attended_rows)
     early = jnp.concatenate([grad_up, grad_down, grad_proj], axis=0).astype(jnp.bfloat16)
+    gradient_attended = plain_dot(grad_proj_out, proj_map).astype(jnp.bfloat16)
+    early, gradient_attended = lax.optimization_barrier((early, gradient_attended))
     early = lax.psum(early, ("wide", "narrow"))
-    gradient_attended = plain_dot(grad_proj_out, proj_map).astype(jnp.bfloat16)
     grad_query_rows, grad_key_rows, grad_value_rows = attend_back(
         query_rows, pair_rows, near_bias, mass, attended, gradient_attended
     )
-    grad_qkv = jnp.concatenate(
-        [
-            contract_rows(grad_query_rows, attn_own),
-            contract_rows(grad_key_rows, attn_in),
-            contract_rows(grad_value_rows, attn_in),
-        ],
-        axis=0,
-    )
-    grad_attn_in = plain_dot(grad_key_rows, pair_map[:LATENT_WIDTH])
-    grad_attn_in = grad_attn_in + plain_dot(grad_value_rows, pair_map[LATENT_WIDTH:])
-    grad_attn_in = grad_attn_in.at[:node_local].add(plain_dot(grad_query_rows, query_map))
-    grad_node_in = norm_back(grad_attn_in * gain_one, normed_one, inverse_one)
-    grad_node_in = grad_node_in.at[:node_local].add(grad_node_mid)
+    node_grads, grad_qkv, column_sums = project_back(
+        grad_query_rows,
+        grad_key_rows,
+        grad_value_rows,
+        node_sum,
+        attn_in,
+        grad_node_mid,
+        shifts,
+        attn_rows,
+    )
     grad_modulation = jnp.concatenate(
         [
-            jnp.sum(grad_attn_in * normed_one, axis=0),
-            jnp.sum(grad_attn_in, axis=0),
+            column_sums[0],
+            column_sums[1],
             jnp.sum(grad_mlp_in * normed_two, axis=0),
             jnp.sum(grad_mlp_in, axis=0),
         ]
     )
     grad_cond = conditioning[:, None] * grad_modulation[None, :]
-    node_grads = (grad_node_in / G2M_K).astype(jnp.bfloat16)
     grad_embed = None
     grad_embed_bias = None
-    steps = sum_steps(jnp.bfloat16)
-    grad_qkv = steps[0](grad_qkv)
-    for place, (features_here, source) in enumerate(feature_slots):
-        node_grads, grad_qkv = lax.optimization_barrier((node_grads, grad_qkv))
-        if place + 1 < len(steps):
-            grad_qkv = steps[place + 1](grad_qkv)
+    for features_here, source in feature_slots:
         embed_part, bias_part = scatter_sum(
-            g2m_rows - source * pixel_local, node_grads, embed_pres[place], features_here
+            source * pixel_local, g2m_rows, node_grads, features_here, embed_low, bias_embed
         )
         grad_embed = embed_part if grad_embed is None else grad_embed + embed_part
         grad_embed_bias = bias_part if grad_embed_bias is None else grad_embed_bias + bias_part
-    for step in steps[len(feature_slots) + 1 :]:
-        grad_qkv = step(grad_qkv)
-
     width = LATENT_WIDTH
     channels = w_dec.shape[1]
     late_rows = jnp.concatenate(
@@ -812,55 +1025,58 @@
             grad_embed,
             grad_embed_bias.reshape(1, width),
             grad_up_bias.reshape(FF // width, width),
-            jnp.pad(
-                jnp.concatenate(
-                    [grad_out_bias, loss_local.reshape(1), jnp.sum(pixel_weight).reshape(1)]
-                ),
-                (0, width - channels - 2),
-            ).reshape(1, width),
+            jnp.pad(grad_out_bias, (0, width - channels)).reshape(1, width),
             grad_dec.T,
         ]
-        + [grad_cond[:, place * width : (place + 1) * width] for place in range(4)],
+        + [grad_cond[:, place * width : (place + 1) * width] for place in range(4)]
+        + [
+            jnp.pad(
+                jnp.concatenate([loss_local.reshape(1), jnp.sum(pixel_weight).reshape(1)]),
+                (0, width - 2),
+            ).reshape(1, width),
+        ],
         axis=0,
     )
-    device_count = lax.axis_size("wide") * narrow_count
-    late_rows = jnp.pad(late_rows, ((0, -late_rows.shape[0] % (2 * device_count)), (0, 0)))
-    for step in sum_steps(jnp.float32):
-        late_rows = step(late_rows)
+    scalar_row = late_rows.shape[0] - 1
+    late_rows = jnp.pad(late_rows, ((0, width - late_rows.shape[0]), (0, 0)))
+    late_rows, grad_qkv, early = lax.optimization_barrier((late_rows, grad_qkv, early))
+    early_square = jnp.sum(jnp.square(early.astype(jnp.float32)))
+    late_rows, mom_all = lax.optimization_barrier((late_rows, mom_all))
+    mom_full = mom_all.transpose(2, 1, 0, 3, 4).reshape(3, -1, LATENT_WIDTH)
+    joint, early_square, mom_full = joint_sum(grad_qkv, late_rows, (early_square, mom_full))
+    sum_qkv, late_rows = joint_split(joint, 3 * LATENT_WIDTH)
     embed_rows = w_embed.shape[0]
     sum_embed = late_rows[:embed_rows]
     place = embed_rows
     bias_rows = late_rows[place : place + 2 + FF // width].reshape(-1)
     sum_bias = bias_rows[: biases.shape[0]]
-    loss_sum = bias_rows[biases.shape[0]]
-    weight_total = bias_rows[biases.shape[0] + 1]
+    loss_sum = late_rows[scalar_row, 0]
+    weight_total = late_rows[scalar_row, 1]
     place += 2 + FF // width
     sum_dec = late_rows[place : place + channels].T
     place += channels
     sum_cond = jnp.concatenate(
         [late_rows[place + COND * part : place + COND * (part + 1)] for part in range(4)], axis=1
     )
-    sum_attn = jnp.concatenate([grad_qkv, early[2 * FF :]], axis=0)
     square_sum = (
-        jnp.sum(sum_embed * sum_embed)
-        + jnp.sum(sum_cond * sum_cond)
-        + jnp.sum(jnp.square(grad_qkv.astype(jnp.float32)))
-        + jnp.sum(jnp.square(early.astype(jnp.float32)))
-        + jnp.sum(sum_dec * sum_dec)
-        + jnp.sum(sum_bias * sum_bias)
+        jnp.sum(jnp.square(late_rows[:scalar_row]))
+        + jnp.sum(jnp.square(sum_qkv.astype(jnp.float32)))
+        + early_square
     )
     grad_norm = jnp.sqrt(square_sum) / weight_total
     factor = jnp.minimum(1.0, clip_bound / (grad_norm + 1e-06)) / weight_total
-    moments, turned = muon_parts(
-        factor, narrow_pos, mom_full, sum_attn, early, w_down.shape[0]
-    )
-    moment_attn, moment_up, moment_down = moments[0].T, moments[1].T, moments[2]
-    attn_orth, up_orth, down_orth = turned[0].T, turned[1].T, turned[2]
-    new_attn = (
-        w_attn - muon_rate * math.sqrt(max(1.0, LATENT_WIDTH / (4 * LATENT_WIDTH))) * attn_orth
-    )
-    new_up = w_up - muon_rate * math.sqrt(max(1.0, LATENT_WIDTH / FF)) * up_orth
-    new_down = w_down - muon_rate * math.sqrt(max(1.0, FF / LATENT_WIDTH)) * down_orth
+    group = lax.axis_index("wide") % 4
+    turned = turn_moment(
+        jnp.minimum(group, 2), narrow_pos, factor, mom_full, joint, early, w_down.shape[0]
+    )
+    moments = own_moments(
+        narrow_pos, factor, joint, early, (mom_attn, mom_up, mom_down)
+    )
+    turned, moments = share_turned(turned, group, moments)
+    moment_attn, moment_up, moment_down = moments
+    new_attn, new_up, new_down, average_attn, average_up, average_down = take_step(
+        turned, (w_attn, w_up, w_down), (ema_attn, ema_up, ema_down)
+    )
     new_embed, first_embed, second_embed = adam_update(
         w_embed, factor * sum_embed, m_embed, v_embed
     )
@@ -889,9 +1105,9 @@
         second_bias,
         ema_keep * ema_embed + keep_rest * new_embed,
         ema_keep * ema_cond + keep_rest * new_cond,
-        ema_keep * ema_attn + keep_rest * new_attn,
-        ema_keep * ema_up + keep_rest * new_up,
-        ema_keep * ema_down + keep_rest * new_down,
+        average_attn,
+        average_up,
+        average_down,
         ema_keep * ema_dec + keep_rest * new_dec,
         ema_keep * ema_bias + keep_rest * new_bias,
         loss_sum,

time: 720 us -> 619 us (0.86)
  matrix products: 102 us -> 57.5 us
  local copies, waits for them, and re-layouts: 67.6 us -> 38.7 us
  other arithmetic: 72.3 us -> 46 us
  starting transfers between devices: 71 us -> 45.6 us
  Pallas kernels: 292 us -> 306 us
  waiting for transfers between devices: 78.4 us -> 92.3 us
    ppermute x9 -> x6, waiting for transfers between devices: 36.1 us -> 0.02 us  [ring_slots(): lax.ppermute(values, 'narrow', [((i + shift) % size, i) for i in range(si...]
    dot_general x10 -> x3, matrix products: 32.5 us -> 5.81 us  [contract_rows(): lax.dot_general(left, right, (((0,), (0,)), ((), ())), preferred_element_...]
    ppermute x28 -> x17, starting transfers between devices: 44.3 us -> 19.7 us  [partner_swap(): lax.ppermute(values, axis_name, [(i, i ^ distance) for i in range(size)])]
    ppermute x28 -> x17, waiting for transfers between devices: 25.3 us -> 47 us  [partner_swap(): lax.ppermute(values, axis_name, [(i, i ^ distance) for i in range(size)])]
    ppermute x3, waiting for transfers between devices: 8.92 us -> 22.9 us  [line_slots(): lax.ppermute(from_high, 'narrow', [(i, i - 1) for i in range(1, size - st...]
    unnamed x187 -> x144, local copies, waits for them, and re-layouts: 21.4 us -> 8.17 us
    ppermute x3, waiting for transfers between devices: 0.01 us -> 12.6 us  [line_slots(): lax.ppermute(from_low, 'narrow', [(i, i + 1) for i in range(step, size -...]
    transpose x1, local copies, waits for them, and re-layouts: 12 us -> 1.94 us  [on_device(): g2m_cols = g2m_rows.T]
  transfers between devices with their start and end apart: 50 -> 36, of which waited for: 21 -> 17; matrix products, arithmetic and copies ran while one was open for 21% -> 15% of each run, Pallas kernels for 27% -> 44%
where the time goes in v4:
time: 619 us; the launch traced here: 610 us
  Pallas kernels  306 us (49%)
  waiting for transfers between devices  92.3 us (15%)
  matrix products  57.5 us (9%)
  other arithmetic  46 us (7%)
  starting transfers between devices  45.6 us (7%)
  local copies, waits for them, and re-layouts  38.7 us (6%)
  between operations  23.4 us (4%)
    pallas_call x4, Pallas kernels, scatter_sum(): pl.pallas_call(functools.partial(scatter_kernel, chunk), grid=(pixel_coun...  62.2 us
    pallas_call x4, Pallas kernels, gather_sum(): pl.pallas_call(functools.partial(gather_kernel, sub), grid=(row_count //...  58.3 us
    pallas_call x1, Pallas kernels, attend_back(): pl.pallas_call(functools.partial(attend_back_kernel, chunk), grid=(HEADS,...  55.3 us
    ppermute x17, waiting for transfers between devices, partner_swap(): lax.ppermute(values, axis_name, [(i, i ^ distance) for i in range(size)])  47 us
    pallas_call x1, Pallas kernels, attend(): pl.pallas_call(functools.partial(attend_kernel, chunk), grid=(HEADS, row_...  39.9 us
    dot_general x4, matrix products, contract_last(): lax.dot_general(left, right, (((1,), (1,)), ((), ())), preferred_element_...  30.7 us
    pallas_call x1, Pallas kernels, turn_moment(): pl.pallas_call(muon_kernel, grid_spec=pltpu.PrefetchScalarGridSpec(num_sc...  24.6 us
    pallas_call x1, Pallas kernels, project_back(): pl.pallas_call(project_back_kernel, grid=(row_count // rows,), in_specs=[...  22.9 us
  transfers between devices with their start and end apart: 36, of which 17 were waited for; matrix products, arithmetic and copies ran while one was open for 15% of the time, Pallas kernels for 44%

profile of v4, /device:TPU:0, one launch (start us, length us, event | category | flops | bytes accessed | tf_op | source)
XLA Modules:
  0.0 609.8 jit_solution(490901363522593540)
XLA Ops:
  7.3 5.1 collective-permute-start
  21.4 4.6 collective-permute-start.3
  30.1 9.5 %shard_map.574.bias_ref = f32[1024,4096]{1,0:T(8,128)} custom-call(s32[128,256]{1,0:T(8,128)} %get-tuple-element.205.row_ref, s32[128,256]{1,0:T(8,128)} %get-tuple-element.204.lane_ref), custom_call_target="tpu_custom_call" | custom-call | flops 1048576 | bytes 1048576 | tf_op jit(solution)/shard_map/pallas_call | solution.py:297
  42.9 13.9 %shard_map.573.rest_0_ = f32[4096,512]{1,0:T(8,128)} custom-call(s32[1,1]{1,0:T(1,128)} %bitcast.2.first_ref, s32[4096,4]{1,0:T(8,128)} %copy.108.ids_ref, bf16[249,2048]{1,0:T(8,128)(2,1)} %copy-done.4, bf16[249,512]{1,0:T(8,128)(2,1)} %convert_element_type.289.map_ref, f32[1,512]{1,0:T(1,128)} %bitcast.128), custom_call_target="tpu_custom_call" | custom-call | flops 1048576 | bytes 1048576 | tf_op jit(solution)/shard_map/pallas_call | solution.py:455
  56.8 12.6 %collective-permute-done.3 = bf16[249,2048]{1,0:T(8,128)(2,1)S(1)} collective-permute-done((bf16[249,2048]{1,0:T(8,128)(2,1)S(1)}, bf16[249,2048]{1,0:T(8,128)(2,1)S(1)}, u32[]{:S(2)}, u32[]{:S(2)}) %collective-permute-start.3) | collective-permute-done | bytes 1019936 | tf_op jit(solution)/shard_map/ppermute | solution.py:195
  69.4 7.6 %collective-permute-done.4 = bf16[249,2048]{1,0:T(8,128)(2,1)} collective-permute-done((bf16[249,2048]{1,0:T(8,128)(2,1)S(1)}, bf16[249,2048]{1,0:T(8,128)(2,1)}, u32[]{:S(2)}, u32[]{:S(2)}) %collective-permute-start.4) | collective-permute-done | bytes 1019936 | tf_op jit(solution)/shard_map/ppermute | solution.py:198
  85.0 15.1 %shard_map.575.rest_0_ = f32[4096,512]{1,0:T(8,128)} custom-call(s32[1,1]{1,0:T(1,128)} %bitcast.28.first_ref, s32[4096,4]{1,0:T(8,128)} %copy.108.ids_ref, bf16[249,2048]{1,0:T(8,128)(2,1)} %broadcast_select_fusion.2.feature_ref, bf16[249,512]{1,0:T(8,128)(2,1)} %convert_element_type.289.map_ref, f32[1,512]{1,0:T(1,128)} %bitcast.129, ...), custom_call_target="tpu_custom_call" | custom-call | flops 1048576 | bytes 1048576 | tf_op jit(solution)/shard_map/pallas_call | solution.py:455
  100.0 8.3 %collective-permute-done.6 = bf16[249,2048]{1,0:T(8,128)(2,1)S(1)} collective-permute-done((bf16[249,2048]{1,0:T(8,128)(2,1)}, bf16[249,2048]{1,0:T(8,128)(2,1)S(1)}, u32[]{:S(2)}, u32[]{:S(2)}) %collective-permute-start.6) | collective-permute-done | bytes 1019936 | tf_op jit(solution)/shard_map/ppermute | solution.py:198
  114.9 14.6 %shard_map.576.rest_0_ = f32[4096,512]{1,0:T(8,128)} custom-call(s32[1,1]{1,0:T(1,128)} %bitcast.30.first_ref, s32[4096,4]{1,0:T(8,128)} %copy.108.ids_ref, bf16[249,2048]{1,0:T(8,128)(2,1)} %select_select_fusion.1.feature_ref, bf16[249,512]{1,0:T(8,128)(2,1)} %convert_element_type.289.map_ref, f32[1,512]{1,0:T(1,128)} %bitcast.130, ...), custom_call_target="tpu_custom_call" | custom-call | flops 1048576 | bytes 1048576 | tf_op jit(solution)/shard_map/pallas_call | solution.py:455
  129.5 6.9 %collective-permute-done.8 = bf16[249,2048]{1,0:T(8,128)(2,1)} collective-permute-done((bf16[249,2048]{1,0:T(8,128)(2,1)S(1)}, bf16[249,2048]{1,0:T(8,128)(2,1)}, u32[]{:S(2)}, u32[]{:S(2)}) %collective-permute-start.8) | collective-permute-done | bytes 1019936 | tf_op jit(solution)/shard_map/ppermute | solution.py:198
  138.8 14.8 %shard_map.577.sum_ref = f32[4096,512]{1,0:T(8,128)} custom-call(s32[1,1]{1,0:T(1,128)} %bitcast.7.first_ref, s32[4096,4]{1,0:T(8,128)} %copy.108.ids_ref, bf16[249,2048]{1,0:T(8,128)(2,1)} %select_select_fusion.feature_ref, bf16[249,512]{1,0:T(8,128)(2,1)} %convert_element_type.289.map_ref, f32[1,512]{1,0:T(1,128)} %bitcast.131, f32[4096,512]{1,0:T(8,128)} %shard_map.576.rest_0_), custom_call_target="tpu_custom_call" | custom-call | flops 1048576 | bytes 1048576 | tf_op jit(solution)/shard_map/pallas_call | solution.py:455
  157.7 3.9 copy.123
  161.7 2.9 fusion.67
  164.6 13.2 %shard_map.578 = (bf16[4096,512]{1,0:T(8,128)(2,1)}, bf16[1024,512]{1,0:T(8,128)(2,1)}, bf16[4096,1024]{1,0:T(8,128)(2,1)}) custom-call(f32[4096,512]{1,0:T(8,128)} %shard_map.577.sum_ref, f32[4,512]{1,0:T(4,128)} %broadcast_add_fusion.shift_ref, bf16[2048,512]{1,0:T(8,128)(2,1)} %bitcast.115), custom_call_target="tpu_custom_call" | custom-call | flops 1048576 | bytes 1048576 | tf_op jit(solution)/shard_map/pallas_call | solution.py:559
  177.7 39.9 %shard_map.579 = (f32[1024,512]{1,0:T(8,128)}, f32[1024,512]{1,0:T(8,128)}) custom-call(bf16[1024,512]{1,0:T(8,128)(2,1)} %get-tuple-element.87.q_ref, bf16[4096,1024]{1,0:T(8,128)(2,1)} %get-tuple-element.88.k_ref.v_ref, bf16[4096,1024]{1,0:T(8,128)(2,1)} %get-tuple-element.88.k_ref.v_ref, f32[1024,4096]{1,0:T(8,128)} %shard_map.574.bias_ref), custom_call_target="tpu_custom_call" | custom-call | flops 1048576 | bytes 1048576 | tf_op jit(solution)/shard_map/pallas_call | solution.py:335
  217.6 3.0 fusion.74
  223.0 5.7 multiply_convert_fusion.1
  232.7 4.2 collective-permute-start.9
  237.7 9.8 %shard_map.580 = bf16[2048,4096]{1,0:T(8,128)(2,1)} custom-call(s32[2048,3]{1,0:T(8,128)} %add_select_fusion.ids_ref), custom_call_target="tpu_custom_call" | custom-call | flops 1048576 | bytes 1048576 | tf_op jit(solution)/shard_map/pallas_call | solution.py:263
  248.9 12.3 %fusion.11 = (f32[]{:T(128)}, f32[83]{0:T(128)}, f32[83,2048]{1,0:T(8,128)S(1)}) fusion(f32[2048]{0:T(1024)S(1)} %bitcast.126, f32[83]{0:T(128)} %param.46, f32[]{:T(128)S(6)} %mul.440, f32[83]{0:T(128)} %slice.200, bf16[2048,4096]{1,0:T(8,128)(2,1)} %shard_map.580, bf16[83,1024]{1,0:T(8,128)(2,1)} %copy-done.34, bf16[83,1024]{1,0:T(8,128)(2,1)} %copy-done.33, ...), kind=kOutput, calls=%fused_computation.60 | convolution fusion | flops 1398458240 | bytes 18826232 | tf_op jit(solution)/shard_map/dot_general | solution.py:90
  261.2 8.7 %fusion.75 = (bf16[83,4096]{1,0:T(8,128)(2,1)S(1)}, f32[83,4096]{1,0:T(8,128)S(1)}) fusion(bf16[2048,4096]{1,0:T(8,128)(2,1)} %shard_map.580, f32[83,2048]{1,0:T(8,128)S(1)} %get-tuple-element.221, f32[2048]{0:T(1024)S(1)} %bitcast.127, f32[83]{0:T(128)} %param.46, f32[]{:T(128)S(6)} %mul.440), kind=kOutput, calls=%fused_computation.234 | convolution fusion | flops 1393528832 | bytes 19505488 | tf_op jit(solution)/shard_map/dot_general | solution.py:954
  271.2 2.8 collective-permute-start.14
  274.0 5.4 collective-permute-done.12
  279.4 4.2 collective-permute-done.13
  286.0 9.8 %convert_reduce_fusion = (f32[2048]{0:T(1024)}, bf16[1024,2048]{1,0:T(8,128)(2,1)S(1)}) fusion(f32[1024,2048]{1,0:T(8,128)} %get-tuple-element.215, f32[2048]{0:T(1024)} %copy-done.49, bf16[2048,512]{1,0:T(8,128)(2,1)} %bitcast.123, f32[1024,512]{1,0:T(8,128)} %fusion.43), kind=kOutput, calls=%fused_computation.1 | convolution fusion | flops 2173171712 | bytes 16793600 | tf_op jit(solution)/shard_map/dot_general | solution.py:90
  295.8 3.4 multiply_reduce_fusion.2
  299.3 2.6 convolution_convert_fusion.1
  315.2 55.3 %shard_map.581 = (bf16[1024,512]{1,0:T(8,128)(2,1)}, bf16[4096,512]{1,0:T(8,128)(2,1)}, bf16[4096,512]{1,0:T(8,128)(2,1)}) custom-call(bf16[1024,512]{1,0:T(8,128)(2,1)} %get-tuple-element.87.q_ref, bf16[4096,1024]{1,0:T(8,128)(2,1)} %get-tuple-element.88.k_ref.v_ref, bf16[4096,1024]{1,0:T(8,128)(2,1)} %get-tuple-element.88.k_ref.v_ref, ...), custom_call_target="tpu_custom_call" | custom-call | flops 1048576 | bytes 1048576 | tf_op jit(solution)/shard_map/pallas_call | solution.py:405
  370.5 22.9 %shard_map.582 = (bf16[4096,512]{1,0:T(8,128)(2,1)}, f32[512,1536]{1,0:T(8,128)}, f32[8,512]{1,0:T(8,128)}) custom-call(bf16[1024,512]{1,0:T(8,128)(2,1)} %get-tuple-element.94.dq_ref, bf16[4096,512]{1,0:T(8,128)(2,1)} %get-tuple-element.95.dk_ref, bf16[4096,512]{1,0:T(8,128)(2,1)} %get-tuple-element.96.dv_ref, f32[4096,512]{1,0:T(8,128)} %shard_map.577.sum_ref, ...), custom_call_target="tpu_custom_call" | custom-call | flops 1048576 | bytes 1048576 | tf_op jit(solution)/shard_map/pallas_call | solution.py:631
  393.4 15.5 %shard_map.584 = (f32[249,512]{1,0:T(8,128)}, f32[1,512]{1,0:T(1,128)}) custom-call(s32[1,1]{1,0:T(1,128)} %bitcast.28.first_ref, s32[4,4096]{1,0:T(4,128)} %get-tuple-element.207.ids_ref, bf16[4096,512]{1,0:T(8,128)(2,1)} %get-tuple-element.98.g_ref, bf16[249,2048]{1,0:T(8,128)(2,1)} %broadcast_select_fusion.2.feature_ref, ...), custom_call_target="tpu_custom_call" | custom-call | flops 1048576 | bytes 1048576 | tf_op jit(solution)/shard_map/pallas_call | solution.py:510
  408.9 15.6 %shard_map.583 = (f32[249,512]{1,0:T(8,128)}, f32[1,512]{1,0:T(1,128)}) custom-call(s32[1,1]{1,0:T(1,128)} %bitcast.2.first_ref, s32[4,4096]{1,0:T(4,128)} %get-tuple-element.207.ids_ref, bf16[4096,512]{1,0:T(8,128)(2,1)} %get-tuple-element.98.g_ref, bf16[249,2048]{1,0:T(8,128)(2,1)} %copy-done.4, bf16[249,512]{1,0:T(8,128)(2,1)} %convert_element_type.289.map_ref, ...), custom_call_target="tpu_custom_call" | custom-call | flops 1048576 | bytes 1048576 | tf_op jit(solution)/shard_map/pallas_call | solution.py:510
  424.5 15.5 %shard_map.585 = (f32[249,512]{1,0:T(8,128)}, f32[1,512]{1,0:T(1,128)}) custom-call(s32[1,1]{1,0:T(1,128)} %bitcast.30.first_ref, s32[4,4096]{1,0:T(4,128)} %get-tuple-element.207.ids_ref, bf16[4096,512]{1,0:T(8,128)(2,1)} %get-tuple-element.98.g_ref, bf16[249,2048]{1,0:T(8,128)(2,1)} %select_select_fusion.1.feature_ref, ...), custom_call_target="tpu_custom_call" | custom-call | flops 1048576 | bytes 1048576 | tf_op jit(solution)/shard_map/pallas_call | solution.py:510
  440.1 15.7 %shard_map.586 = (f32[249,512]{1,0:T(8,128)}, f32[1,512]{1,0:T(1,128)}) custom-call(s32[1,1]{1,0:T(1,128)} %bitcast.7.first_ref, s32[4,4096]{1,0:T(4,128)} %get-tuple-element.207.ids_ref, bf16[4096,512]{1,0:T(8,128)(2,1)} %get-tuple-element.98.g_ref, bf16[249,2048]{1,0:T(8,128)(2,1)} %select_select_fusion.feature_ref, ...), custom_call_target="tpu_custom_call" | custom-call | flops 1048576 | bytes 1048576 | tf_op jit(solution)/shard_map/pallas_call | solution.py:510
  462.0 3.1 collective-permute-done.15
  473.3 5.6 collective-permute-done.16
  478.9 8.3 %collective-permute-done.17 = bf16[64,2560]{1,0:T(8,128)(2,1)S(1)} collective-permute-done((bf16[64,2560]{1,0:T(8,128)(2,1)}, bf16[64,2560]{1,0:T(8,128)(2,1)S(1)}, u32[]{:S(2)}, u32[]{:S(2)}) %collective-permute-start.17) | collective-permute-done | bytes 327712 | tf_op jit(solution)/shard_map/ppermute | solution.py:117
  489.3 4.5 collective-permute-start.19
  496.2 5.4 multiply_reduce_fusion
  501.6 6.2 %copy.112 = bf16[8,4,3,64,512]{4,3,0,1,2:T(8,128)(2,1)} copy(bf16[8,4,3,64,512]{4,3,2,1,0:T(8,128)(2,1)} %bitcast.117) | data formatting | bytes 12582912 | tf_op jit(solution)/shard_map/optimization_barrier | solution.py:1044
  507.9 3.4 collective-permute-start.22
  520.6 8.1 %collective-permute-done.25 = bf16[64,2560]{1,0:T(8,128)(2,1)S(1)} collective-permute-done((bf16[64,2560]{1,0:T(8,128)(2,1)S(1)}, bf16[64,2560]{1,0:T(8,128)(2,1)S(1)}, u32[]{:S(2)}, u32[]{:S(2)}) %collective-permute-start.25) | collective-permute-done | bytes 327712 | tf_op jit(solution)/shard_map/ppermute | solution.py:117
  528.6 4.5 collective-permute-done.26
  534.9 2.5 collective-permute-done.28
  547.3 4.5 shard_map.588
  551.8 24.6 %shard_map.587 = bf16[512,512]{1,0:T(8,128)(2,1)} custom-call(s32[2]{0:T(128)} %pad_add_fusion.1.choice_ref, f32[1,1]{1,0:T(1,128)} %bitcast.54.factor_ref, bf16[3,2048,512]{2,1,0:T(8,128)(2,1)} %bitcast.114, bf16[512,2560]{1,0:T(8,128)(2,1)} %pad_maximum_fusion.1.qkv_ref, bf16[4608,512]{1,0:T(8,128)(2,1)} %all-reduce.5.cloned.1.call-done.proj_ref.rest_ref.up_ref.down_ref, ...), custom_call_target="tpu_custom_call" | custom-call | flops 1048576 | bytes 1048576 | tf_op jit(solution)/shard_map/pallas_call | solution.py:709
  581.3 9.5 %collective-permute-done.30 = bf16[512,512]{1,0:T(8,128)(2,1)} collective-permute-done((bf16[512,512]{1,0:T(8,128)(2,1)}, bf16[512,512]{1,0:T(8,128)(2,1)}, u32[]{:S(2)}, u32[]{:S(2)}) %collective-permute-start.30) | collective-permute-done | bytes 524320 | tf_op jit(solution)/shard_map/ppermute | solution.py:117
  592.9 2.6 select_select_fusion.2
  595.5 6.4 %shard_map.589 = (f32[512,512]{1,0:T(8,128)}, f32[512,512]{1,0:T(8,128)}, f32[512,512]{1,0:T(8,128)}, f32[512,512]{1,0:T(8,128)}, f32[512,512]{1,0:T(8,128)}, /*index=5*/f32[512,512]{1,0:T(8,128)}) custom-call(bf16[512,512]{1,0:T(8,128)(2,1)} %get-tuple-element.162.refs_0_, bf16[512,512]{1,0:T(8,128)(2,1)} %get-tuple-element.161.refs_1_, ...), custom_call_target="tpu_custom_call" | custom-call | flops 1048576 | bytes 1048576 | tf_op jit(solution)/shard_map/pallas_call | solution.py:814
  (309 shorter events, 102.1 us)
Async XLA Ops:
  7.2 69.8 %all-gather.6.cloned.1.call-start = ((), (), s32[]{:S(2)}) async-start(), calls=%async_computation | async-start | bytes 1966080 | tf_op jit(solution)/shard_map/all_gather | solution.py:921
  7.3 32.3 %collective-permute-start = (s32[4,1024]{1,0:T(4,128)}, s32[4,1024]{1,0:T(4,128)}, u32[]{:S(2)}, u32[]{:S(2)}) collective-permute-start(s32[4,1024]{1,0:T(4,128)} %bitcast.139), channel_id=1, source_target_pairs={{1,0},{2,1},{3,2},{0,3},{5,4},{6,5},{7,6},{4,7},{9,8},{10,9},{11,1... | collective-permute-start | bytes 49160 | tf_op jit(solution)/shard_map/ppermute | solution.py:178
  12.4 27.2 %collective-permute-start.1 = (s32[4,1024]{1,0:T(4,128)}, s32[4,1024]{1,0:T(4,128)}, u32[]{:S(2)}, u32[]{:S(2)}) collective-permute-start(s32[4,1024]{1,0:T(4,128)} %bitcast.140), channel_id=1, source_target_pairs={{2,0},{3,1},{0,2},{1,3},{6,4},{7,5},{4,6},{5,7},{10,8},{11,9},{8,1... | collective-permute-start | bytes 49160 | tf_op jit(solution)/shard_map/ppermute | solution.py:178
  12.4 27.2 %collective-permute-start.2 = (s32[4,1024]{1,0:T(4,128)}, s32[4,1024]{1,0:T(4,128)}, u32[]{:S(2)}, u32[]{:S(2)}) collective-permute-start(s32[4,1024]{1,0:T(4,128)} %bitcast.141), channel_id=1, source_target_pairs={{3,0},{0,1},{1,2},{2,3},{7,4},{4,5},{5,6},{6,7},{11,8},{8,9},{9,10... | collective-permute-start | bytes 49160 | tf_op jit(solution)/shard_map/ppermute | solution.py:178
  18.8 138.9 %all-gather.8.cloned.1.call-start = ((), (), s32[]{:S(2)}) async-start(), calls=%async_computation.2 | async-start | bytes 7077888 | tf_op jit(solution)/shard_map/all_gather | solution.py:923
  21.4 18.1 %copy-start.4 = (bf16[249,2048]{1,0:T(8,128)(2,1)}, bf16[249,2048]{1,0:T(8,128)(2,1)S(1)}, u32[]{:S(2)}) copy-start(bf16[249,2048]{1,0:T(8,128)(2,1)S(1)} %pad_maximum_fusion.4.feature_ref) | copy-start | bytes 3059716
  21.4 48.0 %collective-permute-start.3 = (bf16[249,2048]{1,0:T(8,128)(2,1)S(1)}, bf16[249,2048]{1,0:T(8,128)(2,1)S(1)}, u32[]{:S(2)}, u32[]{:S(2)}) collective-permute-start(bf16[249,2048]{1,0:T(8,128)(2,1)S(1)} %pad_maximum_fusion.4.feature_ref), channel_id=1, source_target_pairs={{0,1},{1,2},{2,3},{4,5},{5,6},{6,7},{8,9},{9,10},{10,11},{12,13},{... | collective-permute-start | bytes 3059720 | tf_op jit(solution)/shard_map/ppermute | solution.py:195
  26.0 51.1 %collective-permute-start.4 = (bf16[249,2048]{1,0:T(8,128)(2,1)S(1)}, bf16[249,2048]{1,0:T(8,128)(2,1)}, u32[]{:S(2)}, u32[]{:S(2)}) collective-permute-start(bf16[249,2048]{1,0:T(8,128)(2,1)S(1)} %pad_maximum_fusion.4.feature_ref), channel_id=1, source_target_pairs={{1,0},{2,1},{3,2},{5,4},{6,5},{7,6},{9,8},{10,9},{11,10},{13,12},{... | collective-permute-start | bytes 3059720 | tf_op jit(solution)/shard_map/ppermute | solution.py:198
  56.8 24.6 %copy-start.64 = (s32[4]{0:T(128)S(1)}, s32[4]{0:T(128)}, u32[]{:S(2)}) copy-start(s32[4]{0:T(128)} %constant.222.clone) | copy-start | bytes 52
  79.1 206.9 %all-gather.10.cloned.1.call-start = ((), (), s32[]{:S(2)}) async-start(), calls=%async_computation.3 | async-start | bytes 7077888 | tf_op jit(solution)/shard_map/all_gather | solution.py:925
  79.2 20.8 %collective-permute-start.5 = (bf16[249,2048]{1,0:T(8,128)(2,1)S(1)}, bf16[249,2048]{1,0:T(8,128)(2,1)S(1)}, u32[]{:S(2)}, u32[]{:S(2)}) collective-permute-start(bf16[249,2048]{1,0:T(8,128)(2,1)S(1)} %collective-permute-done.3), channel_id=1, source_target_pairs={{1,2},{2,3},{5,6},{6,7},{9,10},{10,11},{13,14},{14,15},{17,18},{18... | collective-permute-start | bytes 3059720 | tf_op jit(solution)/shard_map/ppermute | solution.py:195
  79.9 28.5 %collective-permute-start.6 = (bf16[249,2048]{1,0:T(8,128)(2,1)}, bf16[249,2048]{1,0:T(8,128)(2,1)S(1)}, u32[]{:S(2)}, u32[]{:S(2)}) collective-permute-start(bf16[249,2048]{1,0:T(8,128)(2,1)} %collective-permute-done.4), channel_id=1, source_target_pairs={{1,0},{2,1},{5,4},{6,5},{9,8},{10,9},{13,12},{14,13},{17,16},{18,1... | collective-permute-start | bytes 3059720 | tf_op jit(solution)/shard_map/ppermute | solution.py:198
  85.0 26.3 %copy-start.63 = (s32[4]{0:T(128)S(1)}, s32[4]{0:T(128)}, u32[]{:S(2)}) copy-start(s32[4]{0:T(128)} %constant.223.clone) | copy-start | bytes 52
  85.0 27.6 %copy-start.62 = (s32[4]{0:T(128)S(1)}, s32[4]{0:T(128)}, u32[]{:S(2)}) copy-start(s32[4]{0:T(128)} %constant.224.clone) | copy-start | bytes 52
  108.4 21.1 %collective-permute-start.7 = (bf16[249,2048]{1,0:T(8,128)(2,1)S(1)}, bf16[249,2048]{1,0:T(8,128)(2,1)}, u32[]{:S(2)}, u32[]{:S(2)}) collective-permute-start(bf16[249,2048]{1,0:T(8,128)(2,1)S(1)} %collective-permute-done.5), channel_id=1, source_target_pairs={{2,3},{6,7},{10,11},{14,15},{18,19},{22,23},{26,27},{30,31}} | collective-permute-start | bytes 3059720 | tf_op jit(solution)/shard_map/ppermute | solution.py:195
  110.0 26.4 %collective-permute-start.8 = (bf16[249,2048]{1,0:T(8,128)(2,1)S(1)}, bf16[249,2048]{1,0:T(8,128)(2,1)}, u32[]{:S(2)}, u32[]{:S(2)}) collective-permute-start(bf16[249,2048]{1,0:T(8,128)(2,1)S(1)} %collective-permute-done.6), channel_id=1, source_target_pairs={{1,0},{5,4},{9,8},{13,12},{17,16},{21,20},{25,24},{29,28}} | collective-permute-start | bytes 3059720 | tf_op jit(solution)/shard_map/ppermute | solution.py:198
  154.5 305.7 %all-reduce.5.cloned.1.call-start = ((), (), s32[]{:S(2)}) async-start(), calls=%async_computation.1 | async-start | bytes 9437184 | tf_op jit(solution)/shard_map/psum | solution.py:990
  154.8 66.3 %copy-start.49 = (f32[2048]{0:T(1024)}, f32[2048]{0:T(1024)S(1)}, u32[]{:S(2)}) copy-start(f32[2048]{0:T(1024)S(1)} %slice.198) | copy-start | bytes 24580
  155.6 65.5 %copy-start.47 = (f32[512]{0:T(512)}, f32[512]{0:T(512)S(1)}, u32[]{:S(2)}) copy-start(f32[512]{0:T(512)S(1)} %get-tuple-element.210) | copy-start | bytes 6148
  155.6 65.5 %copy-start.57 = (f32[512]{0:T(512)}, f32[512]{0:T(512)S(1)}, u32[]{:S(2)}) copy-start(f32[512]{0:T(512)S(1)} %get-tuple-element.211) | copy-start | bytes 6148
  220.7 78.6 %copy-start.2 = (f32[1024,512]{1,0:T(8,128)}, f32[1024,512]{1,0:T(8,128)S(1)}, u32[]{:S(2)}) copy-start(f32[1024,512]{1,0:T(8,128)S(1)} %get-tuple-element.213) | copy-start | bytes 6291460
  232.5 15.0 %collective-permute-start.10 = (bf16[83,1024]{1,0:T(8,128)(2,1)S(1)}, bf16[83,1024]{1,0:T(8,128)(2,1)S(1)}, u32[]{:S(2)}, u32[]{:S(2)}) collective-permute-start(bf16[83,1024]{1,0:T(8,128)(2,1)S(1)} %fusion.6), channel_id=1, source_target_pairs={{2,0},{3,1},{0,2},{1,3},{6,4},{7,5},{4,6},{5,7},{10,8},{11,9},{8,1... | collective-permute-start | bytes 509960 | tf_op jit(solution)/shard_map/ppermute | solution.py:178
  232.6 14.9 %collective-permute-start.11 = (bf16[83,1024]{1,0:T(8,128)(2,1)S(1)}, bf16[83,1024]{1,0:T(8,128)(2,1)S(1)}, u32[]{:S(2)}, u32[]{:S(2)}) collective-permute-start(bf16[83,1024]{1,0:T(8,128)(2,1)S(1)} %fusion.6), channel_id=1, source_target_pairs={{3,0},{0,1},{1,2},{2,3},{7,4},{4,5},{5,6},{6,7},{11,8},{8,9},{9,10... | collective-permute-start | bytes 509960 | tf_op jit(solution)/shard_map/ppermute | solution.py:178
  232.7 14.9 %collective-permute-start.9 = (bf16[83,1024]{1,0:T(8,128)(2,1)S(1)}, bf16[83,1024]{1,0:T(8,128)(2,1)S(1)}, u32[]{:S(2)}, u32[]{:S(2)}) collective-permute-start(bf16[83,1024]{1,0:T(8,128)(2,1)S(1)} %fusion.6), channel_id=1, source_target_pairs={{1,0},{2,1},{3,2},{0,3},{5,4},{6,5},{7,6},{4,7},{9,8},{10,9},{11,1... | collective-permute-start | bytes 509960 | tf_op jit(solution)/shard_map/ppermute | solution.py:178
  270.0 9.4 %collective-permute-start.12 = (bf16[83,1024]{1,0:T(8,128)(2,1)S(1)}, bf16[83,1024]{1,0:T(8,128)(2,1)S(1)}, u32[]{:S(2)}, u32[]{:S(2)}) collective-permute-start(bf16[83,1024]{1,0:T(8,128)(2,1)S(1)} %get-tuple-element.176), channel_id=1, source_target_pairs={{0,1},{1,2},{2,3},{3,0},{4,5},{5,6},{6,7},{7,4},{8,9},{9,10},{10,1... | collective-permute-start | bytes 509960 | tf_op jit(solution)/shard_map/ppermute | solution.py:225
  270.7 12.9 %collective-permute-start.13 = (bf16[83,1024]{1,0:T(8,128)(2,1)S(1)}, bf16[83,1024]{1,0:T(8,128)(2,1)S(1)}, u32[]{:S(2)}, u32[]{:S(2)}) collective-permute-start(bf16[83,1024]{1,0:T(8,128)(2,1)S(1)} %get-tuple-element.178), channel_id=1, source_target_pairs={{0,2},{1,3},{2,0},{3,1},{4,6},{5,7},{6,4},{7,5},{8,10},{9,11},{10,... | collective-permute-start | bytes 509960 | tf_op jit(solution)/shard_map/ppermute | solution.py:225
  271.2 12.5 %collective-permute-start.14 = (bf16[83,1024]{1,0:T(8,128)(2,1)S(1)}, bf16[83,1024]{1,0:T(8,128)(2,1)S(1)}, u32[]{:S(2)}, u32[]{:S(2)}) collective-permute-start(bf16[83,1024]{1,0:T(8,128)(2,1)S(1)} %get-tuple-element.177), channel_id=1, source_target_pairs={{0,3},{1,0},{2,1},{3,2},{4,7},{5,4},{6,5},{7,6},{8,11},{9,8},{10,9... | collective-permute-start | bytes 509960 | tf_op jit(solution)/shard_map/ppermute | solution.py:225
  440.0 17.4 %copy-start.27 = (f32[249,512]{1,0:T(8,128)S(1)}, f32[249,512]{1,0:T(8,128)}, u32[]{:S(2)}) copy-start(f32[249,512]{1,0:T(8,128)} %get-tuple-element.100) | copy-start | bytes 1529860
  440.0 17.4 %copy-start.28 = (f32[249,512]{1,0:T(8,128)S(1)}, f32[249,512]{1,0:T(8,128)}, u32[]{:S(2)}) copy-start(f32[249,512]{1,0:T(8,128)} %get-tuple-element.99) | copy-start | bytes 1529860
  440.1 17.4 %copy-start.29 = (f32[249,512]{1,0:T(8,128)S(1)}, f32[249,512]{1,0:T(8,128)}, u32[]{:S(2)}) copy-start(f32[249,512]{1,0:T(8,128)} %get-tuple-element.101) | copy-start | bytes 1529860
  461.9 3.2 collective-permute-start.15
  468.3 10.6 %collective-permute-start.16 = (bf16[64,2560]{1,0:T(8,128)(2,1)S(1)}, bf16[64,2560]{1,0:T(8,128)(2,1)S(1)}, u32[]{:S(2)}, u32[]{:S(2)}) collective-permute-start(bf16[64,2560]{1,0:T(8,128)(2,1)S(1)} %pad_maximum_fusion.5), channel_id=1, source_target_pairs={{0,8},{4,12},{8,0},{12,4},{16,24},{20,28},{24,16},{28,20},{1,9},{5... | collective-permute-start | bytes 983048 | tf_op jit(solution)/shard_map/ppermute | solution.py:117
  470.5 16.7 %collective-permute-start.17 = (bf16[64,2560]{1,0:T(8,128)(2,1)}, bf16[64,2560]{1,0:T(8,128)(2,1)S(1)}, u32[]{:S(2)}, u32[]{:S(2)}) collective-permute-start(bf16[64,2560]{1,0:T(8,128)(2,1)} %pad_maximum_fusion.6), channel_id=1, source_target_pairs={{0,16},{4,20},{8,24},{12,28},{16,0},{20,4},{24,8},{28,12},{1,17},{... | collective-permute-start | bytes 983048 | tf_op jit(solution)/shard_map/ppermute | solution.py:117
  472.8 14.4 %collective-permute-start.18 = (bf16[64,2560]{1,0:T(8,128)(2,1)}, bf16[64,2560]{1,0:T(8,128)(2,1)}, u32[]{:S(2)}, u32[]{:S(2)}) collective-permute-start(bf16[64,2560]{1,0:T(8,128)(2,1)} %pad_maximum_fusion.7), channel_id=1, source_target_pairs={{0,24},{4,28},{8,16},{12,20},{16,8},{20,12},{24,0},{28,4},{1,25},{... | collective-permute-start | bytes 983048 | tf_op jit(solution)/shard_map/ppermute | solution.py:117
  489.3 18.5 %collective-permute-start.19 = (bf16[16,2560]{1,0:T(8,128)(2,1)S(1)}, bf16[16,2560]{1,0:T(8,128)(2,1)S(1)}, u32[]{:S(2)}, u32[]{:S(2)}) collective-permute-start(bf16[16,2560]{1,0:T(8,128)(2,1)S(1)} %pad_maximum_fusion.9), channel_id=1, source_target_pairs={{0,1},{1,0},{2,3},{3,2},{4,5},{5,4},{6,7},{7,6},{8,9},{9,8},{10,11... | collective-permute-start | bytes 245768 | tf_op jit(solution)/shard_map/ppermute | solution.py:117
  493.8 14.0 %collective-permute-start.20 = (bf16[16,2560]{1,0:T(8,128)(2,1)S(1)}, bf16[16,2560]{1,0:T(8,128)(2,1)S(1)}, u32[]{:S(2)}, u32[]{:S(2)}) collective-permute-start(bf16[16,2560]{1,0:T(8,128)(2,1)S(1)} %pad_maximum_fusion.10), channel_id=1, source_target_pairs={{0,2},{1,3},{2,0},{3,1},{4,6},{5,7},{6,4},{7,5},{8,10},{9,11},{10,... | collective-permute-start | bytes 245768 | tf_op jit(solution)/shard_map/ppermute | solution.py:117
  495.8 12.0 %collective-permute-start.21 = (bf16[16,2560]{1,0:T(8,128)(2,1)S(1)}, bf16[16,2560]{1,0:T(8,128)(2,1)S(1)}, u32[]{:S(2)}, u32[]{:S(2)}) collective-permute-start(bf16[16,2560]{1,0:T(8,128)(2,1)S(1)} %pad_maximum_fusion.11), channel_id=1, source_target_pairs={{0,3},{1,2},{2,1},{3,0},{4,7},{5,6},{6,5},{7,4},{8,11},{9,10},{10,... | collective-permute-start | bytes 245768 | tf_op jit(solution)/shard_map/ppermute | solution.py:117
  507.9 6.7 %collective-permute-start.22 = (bf16[16,2560]{1,0:T(8,128)(2,1)S(1)}, bf16[16,2560]{1,0:T(8,128)(2,1)S(1)}, u32[]{:S(2)}, u32[]{:S(2)}) collective-permute-start(bf16[16,2560]{1,0:T(8,128)(2,1)S(1)} %pad_maximum_fusion.12), channel_id=1, source_target_pairs={{0,3},{1,2},{2,1},{3,0},{4,7},{5,6},{6,5},{7,4},{8,11},{9,10},{10,... | collective-permute-start | bytes 245768 | tf_op jit(solution)/shard_map/ppermute | solution.py:117
  511.3 5.6 collective-permute-start.23
  511.3 5.6 collective-permute-start.24
  517.0 11.6 %collective-permute-start.25 = (bf16[64,2560]{1,0:T(8,128)(2,1)S(1)}, bf16[64,2560]{1,0:T(8,128)(2,1)S(1)}, u32[]{:S(2)}, u32[]{:S(2)}) collective-permute-start(bf16[64,2560]{1,0:T(8,128)(2,1)S(1)} %pad_maximum_fusion.8), channel_id=1, source_target_pairs={{0,24},{4,28},{8,16},{12,20},{16,8},{20,12},{24,0},{28,4},{1,25},{... | collective-permute-start | bytes 983048 | tf_op jit(solution)/shard_map/ppermute | solution.py:117
  518.2 15.0 %collective-permute-start.26 = (bf16[64,2560]{1,0:T(8,128)(2,1)S(1)}, bf16[64,2560]{1,0:T(8,128)(2,1)S(1)}, u32[]{:S(2)}, u32[]{:S(2)}) collective-permute-start(bf16[64,2560]{1,0:T(8,128)(2,1)S(1)} %pad_maximum_fusion.8), channel_id=1, source_target_pairs={{0,16},{4,20},{8,24},{12,28},{16,0},{20,4},{24,8},{28,12},{1,17},{... | collective-permute-start | bytes 983048 | tf_op jit(solution)/shard_map/ppermute | solution.py:117
  519.3 14.4 %collective-permute-start.27 = (bf16[64,2560]{1,0:T(8,128)(2,1)S(1)}, bf16[64,2560]{1,0:T(8,128)(2,1)S(1)}, u32[]{:S(2)}, u32[]{:S(2)}) collective-permute-start(bf16[64,2560]{1,0:T(8,128)(2,1)S(1)} %pad_maximum_fusion.8), channel_id=1, source_target_pairs={{0,8},{4,12},{8,0},{12,4},{16,24},{20,28},{24,16},{28,20},{1,9},{5... | collective-permute-start | bytes 983048 | tf_op jit(solution)/shard_map/ppermute | solution.py:117
  534.2 3.2 collective-permute-start.28
  551.8 25.7 %copy-start.36 = (f32[512,83]{0,1:T(8,128)S(1)}, f32[512,83]{0,1:T(8,128)}, u32[]{:S(2)}) copy-start(f32[512,83]{0,1:T(8,128)} %param.70) | copy-start | bytes 509956
  576.4 14.4 %collective-permute-start.30 = (bf16[512,512]{1,0:T(8,128)(2,1)}, bf16[512,512]{1,0:T(8,128)(2,1)}, u32[]{:S(2)}, u32[]{:S(2)}) collective-permute-start(bf16[512,512]{1,0:T(8,128)(2,1)} %shard_map.587), channel_id=1, source_target_pairs={{0,8},{4,12},{8,0},{12,4},{16,24},{20,28},{24,16},{28,20},{1,9},{5... | collective-permute-start | bytes 1572872 | tf_op jit(solution)/shard_map/ppermute | solution.py:117
  577.5 15.1 %collective-permute-start.29 = (bf16[512,512]{1,0:T(8,128)(2,1)}, bf16[512,512]{1,0:T(8,128)(2,1)}, u32[]{:S(2)}, u32[]{:S(2)}) collective-permute-start(bf16[512,512]{1,0:T(8,128)(2,1)} %shard_map.587), channel_id=1, source_target_pairs={{0,4},{4,0},{8,12},{12,8},{16,20},{20,16},{24,28},{28,24},{1,5},{5... | collective-permute-start | bytes 1572872 | tf_op jit(solution)/shard_map/ppermute | solution.py:117
  590.8 2.1 collective-permute-start.31
  (55 other events, 417.2 us)
Sparse Core Ops, SparseCore 0:
  19.0 53.8 all-gather.5
  79.3 44.8 all-gather.7
  154.6 43.7 all-gather.9
  311.6 147.6 all-reduce.4

commit v5 on v4

--- a/solution.py
+++ b/solution.py
@@ -145,6 +145,8 @@
                 lax.dynamic_slice_in_dim(fine, begin, block, 0),
             )
             arrived.append(partner_swap(piece, axis_name, far << first))
+        if first == 1 and axis_name == "wide":
+            arrived, beside = lax.optimization_barrier((arrived, beside))
         coarse = lax.dynamic_slice_in_dim(coarse, mine * block, block, 0)
         fine = lax.dynamic_slice_in_dim(fine, mine * block, block, 0)
         for piece in arrived:
@@ -152,7 +154,6 @@
             coarse = coarse + more_coarse.astype(jnp.float32)
             fine = fine + more_fine
     values = joint_pieces(coarse, fine)
-    values, beside = lax.optimization_barrier((values, beside))
     for axis_name, first, width in stages[::-1]:
         members = 1 << width
         mine = (lax.axis_index(axis_name) >> first) & (members - 1)
@@ -200,12 +201,10 @@
             )
         result = use_slot(chosen, source)
         if step == size - 1:
-            return later
-        if step == 0:
-            result = (result, later)
-        from_low, from_high, result = lax.optimization_barrier((from_low, from_high, result))
-        if step == 0:
-            later = result[1]
+            return
+        from_low, from_high, _, later[step] = lax.optimization_barrier(
+            (from_low, from_high, result, later[step])
+        )
         arrived[-1 - step] = from_low
         arrived[1 + step] = from_high
         offsets = [orders[n][step] - n for n in range(size)]
@@ -216,6 +215,18 @@
             )
             chosen = jnp.where(here, arrived[offset], chosen)
         source = pos + jnp.array(offsets, jnp.int32)[pos]
+
+
+def in_order(slots):
+    size = lax.axis_size("narrow")
+    pos = lax.axis_index("narrow")
+    rows, width = slots[0].shape
+    across = jnp.zeros((size, 3, rows // 3, width), slots[0].dtype)
+    for shift, piece in enumerate(slots):
+        across = lax.dynamic_update_slice_in_dim(
+            across, piece.reshape(1, 3, rows // 3, width), (pos + shift) % size, 0
+        )
+    return across
 
 
 def ring_sum(parts):
@@ -305,31 +316,29 @@
     )(row_keys, lane_keys)
 
 
-def attend_kernel(chunk, q_ref, k_ref, v_ref, bias_ref, att_ref, mass_ref, score_ref):
+def attend_kernel(chunk, q_ref, k_ref, v_ref, bias_ref, att_ref, mass_ref):
     q = q_ref[...]
-    total = k_ref.shape[0]
-    top = None
-    for start in range(0, total, chunk):
+    top = jnp.full((q.shape[0], 1), -jnp.inf, jnp.float32)
+    mass = jnp.zeros((q.shape[0], 1), jnp.float32)
+    attended = jnp.zeros(att_ref.shape, jnp.float32)
+    for start in range(0, k_ref.shape[0], chunk):
         part = pl.ds(start, chunk)
         scores = contract_last(q, k_ref[part, :]) * SCORE_SCALE + bias_ref[:, part]
-        score_ref[:, part] = scores
-        highest = jnp.max(scores, axis=1, keepdims=True)
-        top = highest if top is None else jnp.maximum(top, highest)
-    mass = jnp.zeros((q.shape[0], 1), jnp.float32)
-    attended = jnp.zeros(att_ref.shape, jnp.float32)
-    for start in range(0, total, chunk):
-        part = pl.ds(start, chunk)
-        raised = jnp.exp2(score_ref[:, part] - top)
-        mass = mass + jnp.sum(raised, axis=1, keepdims=True)
-        attended = attended + jnp.dot(
+        higher = jnp.maximum(top, jnp.max(scores, axis=1, keepdims=True))
+        raised = jnp.exp2(scores - higher)
+        shrink = jnp.exp2(top - higher)
+        mass = mass * shrink + jnp.sum(raised, axis=1, keepdims=True)
+        attended = attended * shrink + jnp.dot(
             raised.astype(jnp.bfloat16), v_ref[part, :], preferred_element_type=jnp.float32
         )
+        top = higher
     att_ref[...] = attended / mass
     mass_ref[...] = jnp.broadcast_to(top + jnp.log2(mass), mass_ref.shape)
 
 
-def attend(queries, pairs, bias, rows=256, chunk=512):
+def attend(queries, pairs, bias, rows=1024, chunk=512):
     row_count = queries.shape[0]
+    rows = min(rows, row_count)
     total = pairs.shape[0]
     block = pl.BlockSpec((rows, HEAD_WIDTH), lambda h, r: (r, h))
     return pl.pallas_call(
@@ -343,7 +352,6 @@
         ],
         out_specs=[block, block],
         out_shape=[jax.ShapeDtypeStruct(queries.shape, jnp.float32)] * 2,
-        scratch_shapes=[pltpu.VMEM((rows, total), jnp.float32)],
         cost_estimate=small_cost(),
         compiler_params=kernel_params(),
     )(queries, pairs, pairs, bias)
@@ -531,6 +539,77 @@
     )(first.reshape(1, 1), ids, grads, features, embed_map, embed_bias)
 
 
+def pad_rows(values):
+    return jnp.pad(values, ((0, 128 - values.shape[0]), (0, 0)))
+
+
+def decode_kernel(
+    scale_ref,
+    count_ref,
+    raw_ref,
+    target_ref,
+    noise_ref,
+    pixel_ref,
+    channel_ref,
+    shift_ref,
+    spread_ref,
+    bias_ref,
+    loss_ref,
+):
+    step = pl.program_id(0)
+    noise_level, skip_scale, out_scale, loss_scale = [scale_ref[place] for place in range(4)]
+    counts = count_ref[...]
+    raw = contract_last(counts, raw_ref[...]).T * (1.0 / M2G_K) + shift_ref[...]
+    target = target_ref[...].astype(jnp.float32)
+    noisy = target + noise_level * noise_ref[...].astype(jnp.float32)
+    errors = skip_scale * noisy + out_scale * raw - target
+    weighted = channel_ref[...] * pixel_ref[...] * errors
+    grads = ((2.0 * loss_scale * out_scale) * weighted).astype(jnp.bfloat16).astype(jnp.float32)
+
+    @pl.when(step == 0)
+    def _():
+        spread_ref[...] = jnp.zeros_like(spread_ref)
+        bias_ref[...] = jnp.zeros_like(bias_ref)
+        loss_ref[...] = jnp.zeros_like(loss_ref)
+
+    row_loss = jnp.sum(weighted * errors, axis=1, keepdims=True)
+    loss_ref[...] += loss_scale * jnp.sum(row_loss, axis=0, keepdims=True)
+    bias_ref[...] += jnp.sum(grads, axis=1, keepdims=True)
+    spread_ref[...] += plain_dot(grads.astype(jnp.bfloat16), counts)
+
+
+def decode(scales, counts, raw, target, noise, pixel_weight, channels, shifts, rows=512):
+    pixel_count, node_count = counts.shape
+    wide_block = pl.BlockSpec((128, rows), lambda i: (0, i))
+    column = pl.BlockSpec((128, 1), lambda i: (0, 0))
+    return pl.pallas_call(
+        decode_kernel,
+        grid=(pixel_count // rows,),
+        in_specs=[
+            pl.BlockSpec(memory_space=pltpu.SMEM),
+            pl.BlockSpec((rows, node_count), lambda i: (i, 0)),
+            pl.BlockSpec((128, node_count), lambda i: (0, 0)),
+            wide_block,
+            wide_block,
+            pl.BlockSpec((1, rows), lambda i: (0, i)),
+            column,
+            column,
+        ],
+        out_specs=[
+            pl.BlockSpec((128, node_count), lambda i: (0, 0)),
+            column,
+            pl.BlockSpec((1, 1), lambda i: (0, 0)),
+        ],
+        out_shape=[
+            jax.ShapeDtypeStruct((128, node_count), jnp.float32),
+            jax.ShapeDtypeStruct((128, 1), jnp.float32),
+            jax.ShapeDtypeStruct((1, 1), jnp.float32),
+        ],
+        cost_estimate=small_cost(),
+        compiler_params=kernel_params(),
+    )(scales, counts, raw, target, noise, pixel_weight, channels, shifts)
+
+
 def row_norm(sums):
     values = sums * (1.0 / G2M_K)
     centred = values - jnp.mean(values, axis=1, keepdims=True)
@@ -670,15 +749,39 @@
     return dot(left[0], right[0]) + (dot(left[0], right[1]) + dot(left[1], right[0]))
 
 
-def muon_kernel(choice_ref, factor_ref, mom_ref, qkv_ref, proj_ref, rest_ref, turned_ref, full_ref):
+def muon_kernel(
+    scalar_row,
+    choice_ref,
+    square_ref,
+    mom_ref,
+    joint_ref,
+    proj_ref,
+    rest_ref,
+    turned_ref,
+    factor_ref,
+    norm_ref,
+    full_ref,
+):
     matrix, pos = choice_ref[0], choice_ref[1]
-    factor = factor_ref[0, 0]
+    width = turned_ref.shape[1]
+    coarse = joint_ref[:, pl.ds(0, 3 * width)].astype(jnp.float32)
+    fine = joint_ref[:, pl.ds(3 * width, width)].astype(jnp.float32)
+    fine = fine + joint_ref[:, pl.ds(4 * width, width)].astype(jnp.float32)
+    in_norm = lax.broadcasted_iota(jnp.int32, fine.shape, 0) < scalar_row
+    square = jnp.sum(jnp.where(in_norm, fine * fine, 0.0), axis=1, keepdims=True)
+    square = square + jnp.sum(coarse * coarse, axis=1, keepdims=True)
+    square = jnp.sum(square, axis=0, keepdims=True) + square_ref[0, 0]
+    weight_total = fine[scalar_row : scalar_row + 1, 1:2]
+    grad_norm = jnp.sqrt(square) / weight_total
+    factor = jnp.minimum(1.0, clip_bound / (grad_norm + 1e-06)) / weight_total
+    norm_ref[...] = grad_norm
+    factor_ref[...] = factor
     own, width = turned_ref.shape
     gram = jnp.zeros((width, width), jnp.float32)
     for place in range(FF // width):
         part = pl.ds(place * width, width)
         if place < 3:
-            first = qkv_ref[:, part]
+            first = joint_ref[:, part]
         else:
             first = proj_ref[...]
         grads = jnp.where(
@@ -704,47 +807,42 @@
     turned_ref[...] = turned.astype(jnp.bfloat16)
 
 
-def turn_moment(matrix, pos, factor, mom_full, sum_qkv, sum_rest, own):
+def turn_moment(matrix, pos, rest_square, scalar_row, mom_full, joint, sum_rest, own):
     rows, width = mom_full.shape[1:]
+    single = pl.BlockSpec((1, 1), lambda i, choice: (0, 0))
     return pl.pallas_call(
-        muon_kernel,
+        functools.partial(muon_kernel, scalar_row),
         grid_spec=pltpu.PrefetchScalarGridSpec(
             num_scalar_prefetch=1,
             grid=(1,),
             in_specs=[
                 pl.BlockSpec(memory_space=pltpu.SMEM),
                 pl.BlockSpec((1, rows, width), lambda i, choice: (choice[0], 0, 0)),
-                pl.BlockSpec((width, 3 * width), lambda i, choice: (0, 0)),
+                pl.BlockSpec(joint.shape, lambda i, choice: (0, 0)),
                 pl.BlockSpec((width, width), lambda i, choice: (2 * FF // width, 0)),
                 pl.BlockSpec(
                     (rows, width), lambda i, choice: (jnp.maximum(choice[0] - 1, 0), 0)
                 ),
             ],
-            out_specs=pl.BlockSpec((own, width), lambda i, choice: (0, 0)),
+            out_specs=[pl.BlockSpec((own, width), lambda i, choice: (0, 0)), single, single],
             scratch_shapes=[pltpu.VMEM((rows, width), jnp.float32)],
         ),
-        out_shape=jax.ShapeDtypeStruct((own, width), jnp.bfloat16),
+        out_shape=[
+            jax.ShapeDtypeStruct((own, width), jnp.bfloat16),
+            jax.ShapeDtypeStruct((1, 1), jnp.float32),
+            jax.ShapeDtypeStruct((1, 1), jnp.float32),
+        ],
         cost_estimate=small_cost(),
         compiler_params=kernel_params(),
-    )(jnp.stack([matrix, pos]), factor.reshape(1, 1), mom_full, sum_qkv, sum_rest, sum_rest)
-
-
-def share_turned(turned, group, moments):
+    )(jnp.stack([matrix, pos]), rest_square.reshape(1, 1), mom_full, joint, sum_rest, sum_rest)
+
+
+def share_turned(turned, moments):
     across = partner_swap(turned, "wide", 2)
     across, moments = lax.optimization_barrier((across, moments))
     beside = partner_swap(turned, "wide", 1)
     corner = partner_swap(across, "wide", 1)
-    low_side = group < 2
-    even = group % 2 == 0
-    first = jnp.where(even, turned, beside)
-    second = jnp.where(even, beside, turned)
-    far_first = jnp.where(even, across, corner)
-    far_second = jnp.where(even, corner, across)
-    return (
-        jnp.where(low_side, first, far_first),
-        jnp.where(low_side, second, far_second),
-        jnp.where(low_side, across, turned),
-    ), moments
+    return (turned, beside, across, corner), moments
 
 
 def moment_kernel(pos_ref, factor_ref, qkv_ref, proj_ref, up_ref, down_ref, *refs):
@@ -796,27 +894,41 @@
     )
 
 
-def step_kernel(*refs):
+def step_kernel(group_ref, own_ref, beside_ref, across_ref, corner_ref, *refs):
     rates = [
         muon_rate * math.sqrt(max(1.0, LATENT_WIDTH / FF)),
         muon_rate * math.sqrt(max(1.0, LATENT_WIDTH / FF)),
         muon_rate * math.sqrt(max(1.0, FF / LATENT_WIDTH)),
     ]
+    group = group_ref[0]
+    low_side = group < 2
+    even = group % 2 == 0
+    own, beside, across, corner = [
+        ref[...].astype(jnp.float32) for ref in (own_ref, beside_ref, across_ref, corner_ref)
+    ]
+    near, far = jnp.where(low_side, own, across), jnp.where(low_side, beside, corner)
+    parts = [
+        jnp.where(even, near, far),
+        jnp.where(even, far, near),
+        jnp.where(low_side, across, own),
+    ]
     for place in range(3):
-        turned = refs[place][...].astype(jnp.float32)
-        change = turned if place == 2 else turned.T
-        new = refs[3 + place][...] - rates[place] * change
-        refs[9 + place][...] = new
-        refs[12 + place][...] = ema_keep * refs[6 + place][...] + (1.0 - ema_keep) * new
-
-
-def take_step(turned, weights, averages):
+        change = parts[place] if place == 2 else parts[place].T
+        new = refs[place][...] - rates[place] * change
+        refs[6 + place][...] = new
+        refs[9 + place][...] = ema_keep * refs[3 + place][...] + (1.0 - ema_keep) * new
+
+
+def take_step(group, turned, weights, averages):
+    whole = pl.BlockSpec(memory_space=pltpu.VMEM)
     return pl.pallas_call(
         step_kernel,
+        in_specs=[pl.BlockSpec(memory_space=pltpu.SMEM)] + [whole] * 10,
+        out_specs=[whole] * 6,
         out_shape=[jax.ShapeDtypeStruct(weights[0].shape, jnp.float32)] * 6,
         cost_estimate=small_cost(),
         compiler_params=kernel_params(),
-    )(*turned, *weights, *averages)
+    )(group.reshape(1), *turned, *weights, *averages)
 
 
 def adam_update(weight, grad, first, second):
@@ -883,7 +995,6 @@
     features = jnp.concatenate(
         [prior_states[0, 0], prior_states[0, 1], (scale_in * noisy).astype(jnp.bfloat16)], axis=0
     )
-    g2m_rows = jnp.concatenate(ring_slots(g2m_edges[0].T), axis=1)
     lat_weight = lat_weights(narrow_pos * pixel_local, pixel_local, pixel_total)
     pixel_weight = lat_weight * valid_mask[0].astype(jnp.float32)
     near_ids = (neighbours[0] - narrow_pos * node_local) % node_total
@@ -907,23 +1018,56 @@
         feature_slots.append((features_here, source))
         return node_sums[-1], near_bias
 
-    g2m_cols = g2m_rows.T
     piece_rows = LATENT_WIDTH // lax.axis_size("wide")
     piece_first = lax.axis_index("wide") * piece_rows
-    low_own = jnp.stack(
+    def own_pieces(one, two, three):
+        pieces = [
+            lax.dynamic_slice_in_dim(part, piece_first, piece_rows, 1).T for part in (one, two)
+        ] + [lax.dynamic_slice_in_dim(three, piece_first, piece_rows, 0)]
+        return jnp.concatenate(pieces, axis=0).astype(jnp.bfloat16)
+
+    g2m_own = g2m_edges[0].T
+    id_rows = g2m_own.size // LATENT_WIDTH
+    packed = jnp.concatenate(
         [
-            lax.dynamic_slice_in_dim(one, piece_first, piece_rows, 0)
-            if place % 3 == 2
-            else lax.dynamic_slice_in_dim(one, piece_first, piece_rows, 1).T
-            for place, one in enumerate((w_attn, w_up, w_down, mom_attn, mom_up, mom_down))
-        ]
-    ).astype(jnp.bfloat16)
-    near_blocks = lax.all_gather(low_own, "narrow", axis=0)
-    near_blocks = line_slots(features, use_slot, near_blocks)
-    weight_all = lax.all_gather(near_blocks[:, :3], "wide", axis=0)
-    mom_near, _ = lax.optimization_barrier((near_blocks, node_sums[3]))
-    mom_all = lax.all_gather(mom_near[:, 3:], "wide", axis=0)
+            (g2m_own // 128).reshape(id_rows, LATENT_WIDTH).astype(jnp.bfloat16),
+            (g2m_own % 128).reshape(id_rows, LATENT_WIDTH).astype(jnp.bfloat16),
+            own_pieces(w_attn, w_up, w_down),
+        ],
+        axis=0,
+    )
+    padded = [
+        pad_rows(values)
+        for values in (
+            target[0],
+            noise_draw[0],
+            channel_weights.reshape(-1, 1),
+            bias_out.reshape(-1, 1),
+        )
+    ]
+    packed_slots, near_bias, padded = lax.optimization_barrier(
+        (ring_slots(packed), near_bias, padded)
+    )
+    id_slots = [
+        (
+            slot[:id_rows].astype(jnp.float32) * 128.0
+            + slot[id_rows : 2 * id_rows].astype(jnp.float32)
+        )
+        .astype(jnp.int32)
+        .reshape(g2m_own.shape)
+        for slot in packed_slots
+    ]
+    g2m_rows = jnp.concatenate(id_slots, axis=1)
+    g2m_cols = g2m_rows.T
+    weight_near = in_order([slot[2 * id_rows :] for slot in packed_slots])
+    weight_all = lax.all_gather(weight_near, "wide", axis=0)
     weight_full = weight_all.transpose(2, 1, 0, 3, 4).reshape(3, -1, LATENT_WIDTH)
+    later = [() for _ in range(narrow_count)]
+    later[narrow_count - 2] = own_pieces(mom_attn, mom_up, mom_down)
+    later[max(narrow_count - 3, 0)] = weight_full
+    line_slots(features, use_slot, later)
+    mom_near = in_order(ring_slots(later[narrow_count - 2]))
+    weight_full = later[max(narrow_count - 3, 0)]
     attn_rows, up_rows, down_full = weight_full[0], weight_full[1], weight_full[2]
     conditioning = cond_features(noise_level)
     modulation = jnp.dot(conditioning, w_cond, precision=highest_precision)
@@ -932,6 +1076,8 @@
     node_sum = node_sums[-1]
     proj_map = attn_rows[3 * LATENT_WIDTH :]
     attn_in, query_rows, pair_rows = project(node_sum, shifts, attn_rows, node_local)
+    pair_rows, mom_near = lax.optimization_barrier((pair_rows, mom_near))
+    mom_all = lax.all_gather(mom_near, "wide", axis=0)
     attended, mass = attend(query_rows, pair_rows, near_bias)
     attended_rows = attended.astype(jnp.bfloat16)
     node_mid = node_sum[:node_local] / G2M_K + contract_last(attended_rows, proj_map)
@@ -944,14 +1090,21 @@
     node_raw = lax.dot_general(
         dec_low, node_low, (((0,), (1,)), ((), ())), preferred_element_type=jnp.float32
     ).astype(jnp.bfloat16)
+    node_raw, mom_all = lax.optimization_barrier((node_raw, mom_all))
     all_raw = jnp.concatenate(ring_slots(node_raw), axis=1)
-    raw_output = contract_last(all_raw, m2g_counts) / M2G_K + bias_out[:, None]
-    errors = skip_scale * noisy + out_scale * raw_output - target_rows
-    weighted = channel_weights[:, None] * pixel_weight[None, :]
-    loss_local = loss_scale * jnp.sum(weighted * errors * errors)
-    grad_raw = (2.0 * loss_scale * out_scale * weighted * errors).astype(jnp.bfloat16)
-    grad_out_bias = jnp.sum(grad_raw.astype(jnp.float32), axis=1)
-    raw_spread = jnp.dot(grad_raw, m2g_counts, preferred_element_type=jnp.float32)
+    raw_spread, out_bias_sum, loss_sum_local = decode(
+        jnp.stack([noise_level, skip_scale, out_scale, loss_scale]),
+        m2g_counts,
+        pad_rows(all_raw),
+        padded[0],
+        padded[1],
+        pixel_weight.reshape(1, pixel_local),
+        padded[2],
+        padded[3],
+    )
+    loss_local = loss_sum_local[0, 0]
+    grad_out_bias = out_bias_sum[: bias_out.shape[0], 0]
+    raw_spread = raw_spread[: bias_out.shape[0]]
     grad_node_raw = (
         ring_sum(
             [
@@ -973,7 +1126,6 @@
         (((0,), (1,)), ((), ())),
         precision=highest_precision,
     )
-    grad_node_out, mom_all = lax.optimization_barrier((grad_node_out, mom_all))
     grad_mlp = grad_node_out.astype(jnp.bfloat16)
     grad_down = contract_rows(hidden, grad_mlp)
     grad_hidden = contract_last(grad_mlp, down_full)
@@ -1044,7 +1196,7 @@
     late_rows, mom_all = lax.optimization_barrier((late_rows, mom_all))
     mom_full = mom_all.transpose(2, 1, 0, 3, 4).reshape(3, -1, LATENT_WIDTH)
     joint, early_square, mom_full = joint_sum(grad_qkv, late_rows, (early_square, mom_full))
-    sum_qkv, late_rows = joint_split(joint, 3 * LATENT_WIDTH)
+    _, late_rows = joint_split(joint, 3 * LATENT_WIDTH)
     embed_rows = w_embed.shape[0]
     sum_embed = late_rows[:embed_rows]
     place = embed_rows
@@ -1058,24 +1210,25 @@
     sum_cond = jnp.concatenate(
         [late_rows[place + COND * part : place + COND * (part + 1)] for part in range(4)], axis=1
     )
-    square_sum = (
-        jnp.sum(jnp.square(late_rows[:scalar_row]))
-        + jnp.sum(jnp.square(sum_qkv.astype(jnp.float32)))
-        + early_square
-    )
-    grad_norm = jnp.sqrt(square_sum) / weight_total
-    factor = jnp.minimum(1.0, clip_bound / (grad_norm + 1e-06)) / weight_total
     group = lax.axis_index("wide") % 4
-    turned = turn_moment(
-        jnp.minimum(group, 2), narrow_pos, factor, mom_full, joint, early, w_down.shape[0]
-    )
+    turned, factor, grad_norm = turn_moment(
+        jnp.minimum(group, 2),
+        narrow_pos,
+        early_square,
+        scalar_row,
+        mom_full,
+        joint,
+        early,
+        w_down.shape[0],
+    )
+    factor, grad_norm = factor[0, 0], grad_norm[0, 0]
     moments = own_moments(
         narrow_pos, factor, joint, early, (mom_attn, mom_up, mom_down)
     )
-    turned, moments = share_turned(turned, group, moments)
+    turned, moments = share_turned(turned, moments)
     moment_attn, moment_up, moment_down = moments
     new_attn, new_up, new_down, average_attn, average_up, average_down = take_step(
-        turned, (w_attn, w_up, w_down), (ema_attn, ema_up, ema_down)
+        group, turned, (w_attn, w_up, w_down), (ema_attn, ema_up, ema_down)
     )
     new_embed, first_embed, second_embed = adam_update(
         w_embed, factor * sum_embed, m_embed, v_embed

time: 619 us -> 577 us (0.932)
  waiting for transfers between devices: 92.3 us -> 62.7 us
  matrix products: 57.5 us -> 41.3 us
  Pallas kernels: 306 us -> 320 us
    pallas_call x2 -> x3, Pallas kernels: 31 us -> 49.6 us  [the longest x1 26 us: turn_moment(): pl.pallas_call(functools.partial(muon_kernel, scalar_row), grid_spec=pltp...]
    dot_general x4 -> x3, matrix products: 30.7 us -> 17.9 us  [contract_last(): lax.dot_general(left, right, (((1,), (1,)), ((), ())), preferred_element_...]
    ppermute x3, waiting for transfers between devices: 12.6 us -> 1.21 us  [line_slots(): lax.ppermute(from_low, 'narrow', [(i, i + 1) for i in range(step, size -...]
    ppermute x3, waiting for transfers between devices: 22.9 us -> 11.5 us  [line_slots(): lax.ppermute(from_high, 'narrow', [(i, i - 1) for i in range(1, size - st...]
    ppermute x17, waiting for transfers between devices: 47 us -> 37.9 us  [partner_swap(): lax.ppermute(values, axis_name, [(i, i ^ distance) for i in range(size)])]
    dot_general x1 -> x0, matrix products: 8.73 us -> none  [on_device(): jnp.dot(grad_raw, m2g_counts, preferred_element_type=jnp.float32)]
    transpose x0 -> x1, local copies, waits for them, and re-layouts: none -> 6.34 us  [on_device(): mom_full = mom_all.transpose(2, 1, 0, 3, 4).reshape(3, -1, LATENT_WIDTH)]
    ppermute x6 -> x9, starting transfers between devices: 10.4 us -> 13.7 us  [ring_slots(): lax.ppermute(values, 'narrow', [((i + shift) % size, i) for i in range(si...]
  transfers between devices with their start and end apart: 36 -> 38, of which waited for: 17 -> 17; matrix products, arithmetic and copies ran while one was open for 15% -> 13% of each run, Pallas kernels for 44% -> 48%
where the time goes in v5:
time: 577 us; the launch traced here: 568 us
  Pallas kernels  320 us (55%)
  waiting for transfers between devices  62.7 us (11%)
  starting transfers between devices  48 us (8%)
  other arithmetic  43.5 us (8%)
  matrix products  41.3 us (7%)
  local copies, waits for them, and re-layouts  33.6 us (6%)
  between operations  18.4 us (3%)
    pallas_call x4, Pallas kernels, scatter_sum(): pl.pallas_call(functools.partial(scatter_kernel, chunk), grid=(pixel_coun...  62.1 us
    pallas_call x4, Pallas kernels, gather_sum(): pl.pallas_call(functools.partial(gather_kernel, sub), grid=(row_count //...  58 us
    pallas_call x1, Pallas kernels, attend_back(): pl.pallas_call(functools.partial(attend_back_kernel, chunk), grid=(HEADS,...  55.1 us
    ppermute x17, waiting for transfers between devices, partner_swap(): lax.ppermute(values, axis_name, [(i, i ^ distance) for i in range(size)])  37.9 us
    pallas_call x1, Pallas kernels, attend(): pl.pallas_call(functools.partial(attend_kernel, chunk), grid=(HEADS, row_...  34.8 us
    pallas_call x1, Pallas kernels, turn_moment(): pl.pallas_call(functools.partial(muon_kernel, scalar_row), grid_spec=pltp...  26 us
    pallas_call x1, Pallas kernels, project_back(): pl.pallas_call(project_back_kernel, grid=(row_count // rows,), in_specs=[...  23 us
    ppermute x17, starting transfers between devices, partner_swap(): lax.ppermute(values, axis_name, [(i, i ^ distance) for i in range(size)])  19.6 us
  transfers between devices with their start and end apart: 38, of which 17 were waited for; matrix products, arithmetic and copies ran while one was open for 13% of the time, Pallas kernels for 48%

profile of v5, /device:TPU:0, one launch (start us, length us, event | category | flops | bytes accessed | tf_op | source)
XLA Modules:
  0.0 567.5 jit_solution(18092307460124631221)
XLA Ops:
  10.5 5.1 collective-permute-start
  22.1 9.5 %shard_map.573.bias_ref = f32[1024,4096]{1,0:T(8,128)} custom-call(s32[128,256]{1,0:T(8,128)} %get-tuple-element.235.row_ref, s32[128,256]{1,0:T(8,128)} %get-tuple-element.234.lane_ref), custom_call_target="tpu_custom_call" | custom-call | flops 1048576 | bytes 1048576 | tf_op jit(solution)/shard_map/pallas_call | solution.py:308
  37.5 2.9 collective-permute-start.3
  46.8 14.0 %shard_map.574.rest_0_ = f32[4096,512]{1,0:T(8,128)} custom-call(s32[1,1]{1,0:T(1,128)} %bitcast.3.first_ref, s32[4096,4]{1,0:T(8,128)} %copy.123.ids_ref, bf16[249,2048]{1,0:T(8,128)(2,1)} %copy-done.4, bf16[249,512]{1,0:T(8,128)(2,1)} %convert_element_type.341.map_ref, f32[1,512]{1,0:T(1,128)} %bitcast.174), custom_call_target="tpu_custom_call" | custom-call | flops 1048576 | bytes 1048576 | tf_op jit(solution)/shard_map/pallas_call | solution.py:463
  62.0 5.0 collective-permute-done.4
  78.6 14.7 %shard_map.575.rest_0_ = f32[4096,512]{1,0:T(8,128)} custom-call(s32[1,1]{1,0:T(1,128)} %bitcast.23.first_ref, s32[4096,4]{1,0:T(8,128)} %copy.123.ids_ref, bf16[249,2048]{1,0:T(8,128)(2,1)} %broadcast_select_fusion.2.feature_ref, bf16[249,512]{1,0:T(8,128)(2,1)} %convert_element_type.341.map_ref, f32[1,512]{1,0:T(1,128)} %bitcast.175, ...), custom_call_target="tpu_custom_call" | custom-call | flops 1048576 | bytes 1048576 | tf_op jit(solution)/shard_map/pallas_call | solution.py:463
  98.6 14.7 %shard_map.576.rest_0_ = f32[4096,512]{1,0:T(8,128)} custom-call(s32[1,1]{1,0:T(1,128)} %bitcast.35.first_ref, s32[4096,4]{1,0:T(8,128)} %copy.123.ids_ref, bf16[249,2048]{1,0:T(8,128)(2,1)} %select_select_fusion.1.feature_ref, bf16[249,512]{1,0:T(8,128)(2,1)} %convert_element_type.341.map_ref, f32[1,512]{1,0:T(1,128)} %bitcast.176, ...), custom_call_target="tpu_custom_call" | custom-call | flops 1048576 | bytes 1048576 | tf_op jit(solution)/shard_map/pallas_call | solution.py:463
  113.2 3.0 slice_bitcast_fusion.map_ref
  116.3 5.4 collective-permute-done.8
  126.0 14.6 %shard_map.577.sum_ref = f32[4096,512]{1,0:T(8,128)} custom-call(s32[1,1]{1,0:T(1,128)} %bitcast.15.first_ref, s32[4096,4]{1,0:T(8,128)} %copy.123.ids_ref, bf16[249,2048]{1,0:T(8,128)(2,1)} %select_select_fusion.feature_ref, bf16[249,512]{1,0:T(8,128)(2,1)} %convert_element_type.341.map_ref, f32[1,512]{1,0:T(1,128)} %bitcast.177, ...), custom_call_target="tpu_custom_call" | custom-call | flops 1048576 | bytes 1048576 | tf_op jit(solution)/shard_map/pallas_call | solution.py:463
  140.7 13.2 %shard_map.578 = (bf16[4096,512]{1,0:T(8,128)(2,1)}, bf16[1024,512]{1,0:T(8,128)(2,1)}, bf16[4096,1024]{1,0:T(8,128)(2,1)}) custom-call(f32[4096,512]{1,0:T(8,128)} %shard_map.577.sum_ref, f32[4,512]{1,0:T(4,128)} %broadcast_add_fusion.shift_ref, bf16[2048,512]{1,0:T(8,128)(2,1)} %slice_bitcast_fusion.map_ref), custom_call_target="tpu_custom_call" | custom-call | flops 1048576 | bytes 1048576 | tf_op jit(solution)/shard_map/pallas_call | solution.py:638
  157.0 34.8 %shard_map.579 = (f32[1024,512]{1,0:T(8,128)}, f32[1024,512]{1,0:T(8,128)}) custom-call(bf16[1024,512]{1,0:T(8,128)(2,1)} %get-tuple-element.111.q_ref, bf16[4096,1024]{1,0:T(8,128)(2,1)} %get-tuple-element.114.k_ref.v_ref, bf16[4096,1024]{1,0:T(8,128)(2,1)} %get-tuple-element.114.k_ref.v_ref, f32[1024,4096]{1,0:T(8,128)} %shard_map.573.bias_ref), custom_call_target="tpu_custom_call" | custom-call | flops 1048576 | bytes 1048576 | tf_op jit(solution)/shard_map/pallas_call | solution.py:344
  191.8 3.2 fusion.72
  195.5 7.6 %multiply_convert_fusion.1 = (bf16[1024,2048]{1,0:T(8,128)(2,1)S(1)}, f32[1024,2048]{1,0:T(8,128)}) fusion(f32[2048]{0:T(1024)S(1)} %slice.239, bf16[3,2048,512]{2,1,0:T(8,128)(2,1)} %bitcast.156, f32[1024,512]{1,0:T(8,128)S(1)} %get-tuple-element.243, f32[512]{0:T(512)S(1)} %get-tuple-element.241, f32[512]{0:T(512)S(1)} %get-tuple-element.240, ...), kind=kOutput, calls=%fused_computation.3 | convolution fusion | flops 2162688000 | bytes 16797696 | tf_op jit(solution)/shard_map/dot_general | solution.py:90
  203.1 5.5 add_convert_fusion
  209.0 3.1 collective-permute-start.12
  215.5 9.5 %shard_map.580.count_ref = bf16[2048,4096]{1,0:T(8,128)(2,1)} custom-call(s32[2048,3]{1,0:T(8,128)} %add_select_fusion.ids_ref), custom_call_target="tpu_custom_call" | custom-call | flops 1048576 | bytes 1048576 | tf_op jit(solution)/shard_map/pallas_call | solution.py:274
  227.8 16.8 %shard_map.581 = (f32[128,4096]{1,0:T(8,128)}, f32[128,1]{1,0:T(8,128)}, f32[1,1]{1,0:T(1,128)}) custom-call(f32[4]{0:T(128)} %pad_maximum_fusion.16.scale_ref, bf16[2048,4096]{1,0:T(8,128)(2,1)} %shard_map.580.count_ref, bf16[128,4096]{1,0:T(8,128)(2,1)} %fusion.22.raw_ref, bf16[128,2048]{1,0:T(8,128)(2,1)} %pad.30.target_ref, ...), custom_call_target="tpu_custom_call" | custom-call | flops 1048576 | bytes 1048576 | tf_op jit(solution)/shard_map/pallas_call | solution.py:585
  247.4 2.4 collective-permute-start.16
  251.2 4.5 collective-permute-done.15
  255.7 4.3 collective-permute-done.16
  262.8 7.0 %convert_reduce_fusion = (f32[2048]{0:T(1024)S(1)}, bf16[1024,2048]{1,0:T(8,128)(2,1)S(1)}) fusion(f32[1024,2048]{1,0:T(8,128)} %get-tuple-element.245, f32[2048]{0:T(1024)S(1)} %slice.239, bf16[3,2048,512]{2,1,0:T(8,128)(2,1)} %bitcast.158, f32[1024,512]{1,0:T(8,128)S(1)} %fusion.45), kind=kOutput, calls=%fused_computation.1 | convolution fusion | flops 2173171712 | bytes 16793600 | tf_op jit(solution)/shard_map/dot_general | solution.py:90
  269.9 4.5 multiply_reduce_fusion.1
  274.4 2.6 convolution_convert_fusion.1
  277.0 2.5 convolution_convert_fusion
  280.5 3.3 convolution_convert_fusion.2.g_ref
  289.3 55.1 %shard_map.582 = (bf16[1024,512]{1,0:T(8,128)(2,1)}, bf16[4096,512]{1,0:T(8,128)(2,1)}, bf16[4096,512]{1,0:T(8,128)(2,1)}) custom-call(bf16[1024,512]{1,0:T(8,128)(2,1)} %get-tuple-element.111.q_ref, bf16[4096,1024]{1,0:T(8,128)(2,1)} %get-tuple-element.114.k_ref.v_ref, bf16[4096,1024]{1,0:T(8,128)(2,1)} %get-tuple-element.114.k_ref.v_ref, ...), custom_call_target="tpu_custom_call" | custom-call | flops 1048576 | bytes 1048576 | tf_op jit(solution)/shard_map/pallas_call | solution.py:413
  344.5 23.0 %shard_map.583 = (bf16[4096,512]{1,0:T(8,128)(2,1)}, f32[512,1536]{1,0:T(8,128)}, f32[8,512]{1,0:T(8,128)}) custom-call(bf16[1024,512]{1,0:T(8,128)(2,1)} %get-tuple-element.125.dq_ref, bf16[4096,512]{1,0:T(8,128)(2,1)} %get-tuple-element.126.dk_ref, bf16[4096,512]{1,0:T(8,128)(2,1)} %get-tuple-element.127.dv_ref, f32[4096,512]{1,0:T(8,128)} %shard_map.577.sum_ref, ...), custom_call_target="tpu_custom_call" | custom-call | flops 1048576 | bytes 1048576 | tf_op jit(solution)/shard_map/pallas_call | solution.py:710
  367.5 15.6 %shard_map.585 = (f32[249,512]{1,0:T(8,128)}, f32[1,512]{1,0:T(1,128)}) custom-call(s32[1,1]{1,0:T(1,128)} %bitcast.23.first_ref, s32[4,4096]{1,0:T(4,128)} %copy-done.10, bf16[4096,512]{1,0:T(8,128)(2,1)} %get-tuple-element.129.g_ref, bf16[249,2048]{1,0:T(8,128)(2,1)} %broadcast_select_fusion.2.feature_ref, bf16[249,512]{1,0:T(8,128)(2,1)} %convert_element_type.341.map_ref, ...), custom_call_target="tpu_custom_call" | custom-call | flops 1048576 | bytes 1048576 | tf_op jit(solution)/shard_map/pallas_call | solution.py:518
  383.0 15.5 %shard_map.584 = (f32[249,512]{1,0:T(8,128)}, f32[1,512]{1,0:T(1,128)}) custom-call(s32[1,1]{1,0:T(1,128)} %bitcast.3.first_ref, s32[4,4096]{1,0:T(4,128)} %copy-done.10, bf16[4096,512]{1,0:T(8,128)(2,1)} %get-tuple-element.129.g_ref, bf16[249,2048]{1,0:T(8,128)(2,1)} %copy-done.4, bf16[249,512]{1,0:T(8,128)(2,1)} %convert_element_type.341.map_ref, ...), custom_call_target="tpu_custom_call" | custom-call | flops 1048576 | bytes 1048576 | tf_op jit(solution)/shard_map/pallas_call | solution.py:518
  398.5 15.5 %shard_map.586 = (f32[249,512]{1,0:T(8,128)}, f32[1,512]{1,0:T(1,128)}) custom-call(s32[1,1]{1,0:T(1,128)} %bitcast.35.first_ref, s32[4,4096]{1,0:T(4,128)} %copy-done.10, bf16[4096,512]{1,0:T(8,128)(2,1)} %get-tuple-element.129.g_ref, bf16[249,2048]{1,0:T(8,128)(2,1)} %select_select_fusion.1.feature_ref, bf16[249,512]{1,0:T(8,128)(2,1)} %convert_element_type.341.map_ref, ...), custom_call_target="tpu_custom_call" | custom-call | flops 1048576 | bytes 1048576 | tf_op jit(solution)/shard_map/pallas_call | solution.py:518
  414.0 15.6 %shard_map.587 = (f32[249,512]{1,0:T(8,128)}, f32[1,512]{1,0:T(1,128)}) custom-call(s32[1,1]{1,0:T(1,128)} %bitcast.15.first_ref, s32[4,4096]{1,0:T(4,128)} %copy-done.10, bf16[4096,512]{1,0:T(8,128)(2,1)} %get-tuple-element.129.g_ref, bf16[249,2048]{1,0:T(8,128)(2,1)} %select_select_fusion.feature_ref, bf16[249,512]{1,0:T(8,128)(2,1)} %convert_element_type.341.map_ref, ...), custom_call_target="tpu_custom_call" | custom-call | flops 1048576 | bytes 1048576 | tf_op jit(solution)/shard_map/pallas_call | solution.py:518
  437.3 6.3 %copy.126 = bf16[3,4,8,64,512]{4,3,2,1,0:T(8,128)(2,1)} copy(bf16[3,4,8,64,512]{4,3,0,1,2:T(8,128)(2,1)} %bitcast.152) | data formatting | bytes 12582912 | tf_op jit(solution)/shard_map/transpose | solution.py:1197
  450.1 3.0 multiply_reduce_fusion
  453.2 4.8 collective-permute-done.21
  457.9 6.5 %collective-permute-done.20 = bf16[64,2560]{1,0:T(8,128)(2,1)S(1)} collective-permute-done((bf16[64,2560]{1,0:T(8,128)(2,1)S(1)}, bf16[64,2560]{1,0:T(8,128)(2,1)S(1)}, u32[]{:S(2)}, u32[]{:S(2)}) %collective-permute-start.20) | collective-permute-done | bytes 327712 | tf_op jit(solution)/shard_map/ppermute | solution.py:117
  464.7 2.5 collective-permute-start.22
  467.2 3.6 collective-permute-start.23
  470.8 6.5 %collective-permute-done.23 = bf16[16,2560]{1,0:T(8,128)(2,1)S(1)} collective-permute-done((bf16[16,2560]{1,0:T(8,128)(2,1)S(1)}, bf16[16,2560]{1,0:T(8,128)(2,1)S(1)}, u32[]{:S(2)}, u32[]{:S(2)}) %collective-permute-start.23) | collective-permute-done | bytes 81952 | tf_op jit(solution)/shard_map/ppermute | solution.py:117
  477.4 2.6 collective-permute-start.25
  481.9 2.7 collective-permute-done.25
  490.5 8.1 %collective-permute-done.28 = bf16[64,2560]{1,0:T(8,128)(2,1)S(1)} collective-permute-done((bf16[64,2560]{1,0:T(8,128)(2,1)S(1)}, bf16[64,2560]{1,0:T(8,128)(2,1)S(1)}, u32[]{:S(2)}, u32[]{:S(2)}) %collective-permute-start.28) | collective-permute-done | bytes 327712 | tf_op jit(solution)/shard_map/ppermute | solution.py:117
  498.6 3.8 collective-permute-done.29
  503.7 2.6 collective-permute-done.31
  510.5 26.0 %shard_map.588 = (bf16[512,512]{1,0:T(8,128)(2,1)}, f32[1,1]{1,0:T(1,128)}, f32[1,1]{1,0:T(1,128)}) custom-call(s32[2]{0:T(128)} %pad_add_fusion.choice_ref, f32[1,1]{1,0:T(1,128)} %bitcast.63.square_ref, bf16[3,2048,512]{2,1,0:T(8,128)(2,1)} %bitcast.151, bf16[512,2560]{1,0:T(8,128)(2,1)} %pad_maximum_fusion.1.joint_ref.qkv_ref, ...), custom_call_target="tpu_custom_call" | custom-call | flops 1048576 | bytes 1048576 | tf_op jit(solution)/shard_map/pallas_call | solution.py:813
  538.3 5.2 shard_map.589
  543.6 2.7 multiply_add_fusion.5
  554.0 6.8 %shard_map.590 = (f32[512,512]{1,0:T(8,128)}, f32[512,512]{1,0:T(8,128)}, f32[512,512]{1,0:T(8,128)}, f32[512,512]{1,0:T(8,128)}, f32[512,512]{1,0:T(8,128)}, /*index=5*/f32[512,512]{1,0:T(8,128)}) custom-call(s32[1]{0:T(128)} %bitcast.group_ref, bf16[512,512]{1,0:T(8,128)(2,1)} %get-tuple-element.154.own_ref, ...), custom_call_target="tpu_custom_call" | custom-call | flops 1048576 | bytes 1048576 | tf_op jit(solution)/shard_map/pallas_call | solution.py:924
  (324 shorter events, 101.6 us)
Async XLA Ops:
  7.2 87.3 %all-gather.4.cloned.1.call-start = ((), (), s32[]{:S(2)}) async-start(), calls=%async_computation | async-start | bytes 7077888 | tf_op jit(solution)/shard_map/all_gather | solution.py:1063
  10.5 21.1 %collective-permute-start = (bf16[208,512]{1,0:T(8,128)(2,1)S(1)}, bf16[208,512]{1,0:T(8,128)(2,1)S(1)}, u32[]{:S(2)}, u32[]{:S(2)}) collective-permute-start(bf16[208,512]{1,0:T(8,128)(2,1)S(1)} %fusion.44), channel_id=1, source_target_pairs={{1,0},{2,1},{3,2},{0,3},{5,4},{6,5},{7,6},{4,7},{9,8},{10,9},{11,1... | collective-permute-start | bytes 638984 | tf_op jit(solution)/shard_map/ppermute | solution.py:179
  15.6 18.1 %collective-permute-start.1 = (bf16[208,512]{1,0:T(8,128)(2,1)S(1)}, bf16[208,512]{1,0:T(8,128)(2,1)S(1)}, u32[]{:S(2)}, u32[]{:S(2)}) collective-permute-start(bf16[208,512]{1,0:T(8,128)(2,1)S(1)} %fusion.44), channel_id=1, source_target_pairs={{2,0},{3,1},{0,2},{1,3},{6,4},{7,5},{4,6},{5,7},{10,8},{11,9},{8,1... | collective-permute-start | bytes 638984 | tf_op jit(solution)/shard_map/ppermute | solution.py:179
  15.6 18.1 %collective-permute-start.2 = (bf16[208,512]{1,0:T(8,128)(2,1)S(1)}, bf16[208,512]{1,0:T(8,128)(2,1)S(1)}, u32[]{:S(2)}, u32[]{:S(2)}) collective-permute-start(bf16[208,512]{1,0:T(8,128)(2,1)S(1)} %fusion.44), channel_id=1, source_target_pairs={{3,0},{0,1},{1,2},{2,3},{7,4},{4,5},{5,6},{6,7},{11,8},{8,9},{9,10... | collective-permute-start | bytes 638984 | tf_op jit(solution)/shard_map/ppermute | solution.py:179
  34.9 174.1 %all-gather.6.cloned.1.call-start = ((), (), s32[]{:S(2)}) async-start(), calls=%async_computation.2 | async-start | bytes 7077888 | tf_op jit(solution)/shard_map/all_gather | solution.py:1080
  37.5 24.6 %collective-permute-start.3 = (bf16[249,2048]{1,0:T(8,128)(2,1)S(1)}, bf16[249,2048]{1,0:T(8,128)(2,1)S(1)}, u32[]{:S(2)}, u32[]{:S(2)}) collective-permute-start(bf16[249,2048]{1,0:T(8,128)(2,1)S(1)} %pad_maximum_fusion.4.feature_ref), channel_id=1, source_target_pairs={{0,1},{1,2},{2,3},{4,5},{5,6},{6,7},{8,9},{9,10},{10,11},{12,13},{... | collective-permute-start | bytes 3059720 | tf_op jit(solution)/shard_map/ppermute | solution.py:196
  40.3 26.7 %collective-permute-start.4 = (bf16[249,2048]{1,0:T(8,128)(2,1)S(1)}, bf16[249,2048]{1,0:T(8,128)(2,1)}, u32[]{:S(2)}, u32[]{:S(2)}) collective-permute-start(bf16[249,2048]{1,0:T(8,128)(2,1)S(1)} %pad_maximum_fusion.4.feature_ref), channel_id=1, source_target_pairs={{1,0},{2,1},{3,2},{5,4},{6,5},{7,6},{9,8},{10,9},{11,10},{13,12},{... | collective-permute-start | bytes 3059720 | tf_op jit(solution)/shard_map/ppermute | solution.py:199
  46.8 23.9 %copy-start.52 = (s32[4]{0:T(128)S(1)}, s32[4]{0:T(128)}, u32[]{:S(2)}) copy-start(s32[4]{0:T(128)} %constant.257.clone) | copy-start | bytes 52
  46.8 25.2 %copy-start.51 = (s32[4]{0:T(128)S(1)}, s32[4]{0:T(128)}, u32[]{:S(2)}) copy-start(s32[4]{0:T(128)} %constant.258.clone) | copy-start | bytes 52
  46.8 26.6 %copy-start.50 = (s32[4]{0:T(128)S(1)}, s32[4]{0:T(128)}, u32[]{:S(2)}) copy-start(s32[4]{0:T(128)} %constant.259.clone) | copy-start | bytes 52
  46.8 28.8 %copy-start.49 = (f32[4]{0:T(128)S(1)}, f32[4]{0:T(128)}, u32[]{:S(2)}) copy-start(f32[4]{0:T(128)} %constant.285) | copy-start | bytes 52
  67.0 26.3 %collective-permute-start.5 = (bf16[249,2048]{1,0:T(8,128)(2,1)S(1)}, bf16[249,2048]{1,0:T(8,128)(2,1)S(1)}, u32[]{:S(2)}, u32[]{:S(2)}) collective-permute-start(bf16[249,2048]{1,0:T(8,128)(2,1)S(1)} %collective-permute-done.3), channel_id=1, source_target_pairs={{1,2},{2,3},{5,6},{6,7},{9,10},{10,11},{13,14},{14,15},{17,18},{18... | collective-permute-start | bytes 3059720 | tf_op jit(solution)/shard_map/ppermute | solution.py:196
  67.7 26.7 %collective-permute-start.6 = (bf16[249,2048]{1,0:T(8,128)(2,1)}, bf16[249,2048]{1,0:T(8,128)(2,1)S(1)}, u32[]{:S(2)}, u32[]{:S(2)}) collective-permute-start(bf16[249,2048]{1,0:T(8,128)(2,1)} %collective-permute-done.4), channel_id=1, source_target_pairs={{1,0},{2,1},{5,4},{6,5},{9,8},{10,9},{13,12},{14,13},{17,16},{18,1... | collective-permute-start | bytes 3059720 | tf_op jit(solution)/shard_map/ppermute | solution.py:199
  94.5 21.8 %collective-permute-start.7 = (bf16[249,2048]{1,0:T(8,128)(2,1)S(1)}, bf16[249,2048]{1,0:T(8,128)(2,1)}, u32[]{:S(2)}, u32[]{:S(2)}) collective-permute-start(bf16[249,2048]{1,0:T(8,128)(2,1)S(1)} %collective-permute-done.5), channel_id=1, source_target_pairs={{2,3},{6,7},{10,11},{14,15},{18,19},{22,23},{26,27},{30,31}} | collective-permute-start | bytes 3059720 | tf_op jit(solution)/shard_map/ppermute | solution.py:196
  96.2 25.5 %collective-permute-start.8 = (bf16[249,2048]{1,0:T(8,128)(2,1)S(1)}, bf16[249,2048]{1,0:T(8,128)(2,1)}, u32[]{:S(2)}, u32[]{:S(2)}) collective-permute-start(bf16[249,2048]{1,0:T(8,128)(2,1)S(1)} %collective-permute-done.6), channel_id=1, source_target_pairs={{1,0},{5,4},{9,8},{13,12},{17,16},{21,20},{25,24},{29,28}} | collective-permute-start | bytes 3059720 | tf_op jit(solution)/shard_map/ppermute | solution.py:199
  121.6 32.3 %collective-permute-start.9 = (bf16[192,512]{1,0:T(8,128)(2,1)S(1)}, bf16[192,512]{1,0:T(8,128)(2,1)S(1)}, u32[]{:S(2)}, u32[]{:S(2)}) collective-permute-start(bf16[192,512]{1,0:T(8,128)(2,1)S(1)} %pad_maximum_fusion.9), channel_id=1, source_target_pairs={{1,0},{2,1},{3,2},{0,3},{5,4},{6,5},{7,6},{4,7},{9,8},{10,9},{11,1... | collective-permute-start | bytes 589832 | tf_op jit(solution)/shard_map/ppermute | solution.py:179
  122.7 31.3 %collective-permute-start.10 = (bf16[192,512]{1,0:T(8,128)(2,1)S(1)}, bf16[192,512]{1,0:T(8,128)(2,1)S(1)}, u32[]{:S(2)}, u32[]{:S(2)}) collective-permute-start(bf16[192,512]{1,0:T(8,128)(2,1)S(1)} %pad_maximum_fusion.9), channel_id=1, source_target_pairs={{2,0},{3,1},{0,2},{1,3},{6,4},{7,5},{4,6},{5,7},{10,8},{11,9},{8,1... | collective-permute-start | bytes 589832 | tf_op jit(solution)/shard_map/ppermute | solution.py:179
  122.7 31.3 %collective-permute-start.11 = (bf16[192,512]{1,0:T(8,128)(2,1)S(1)}, bf16[192,512]{1,0:T(8,128)(2,1)S(1)}, u32[]{:S(2)}, u32[]{:S(2)}) collective-permute-start(bf16[192,512]{1,0:T(8,128)(2,1)S(1)} %pad_maximum_fusion.9), channel_id=1, source_target_pairs={{3,0},{0,1},{1,2},{2,3},{7,4},{4,5},{5,6},{6,7},{11,8},{8,9},{9,10... | collective-permute-start | bytes 589832 | tf_op jit(solution)/shard_map/ppermute | solution.py:179
  155.0 280.5 %all-reduce.10.cloned.1.call-start = ((), (), s32[]{:S(2)}) async-start(), calls=%async_computation.1 | async-start | bytes 9437184 | tf_op jit(solution)/shard_map/psum | solution.py:1142
  195.0 79.4 %copy-start.2 = (f32[1024,512]{1,0:T(8,128)}, f32[1024,512]{1,0:T(8,128)S(1)}, u32[]{:S(2)}) copy-start(f32[1024,512]{1,0:T(8,128)S(1)} %get-tuple-element.243) | copy-start | bytes 6291460
  209.0 16.6 %collective-permute-start.12 = (bf16[83,1024]{1,0:T(8,128)(2,1)S(1)}, bf16[83,1024]{1,0:T(8,128)(2,1)}, u32[]{:S(2)}, u32[]{:S(2)}) collective-permute-start(bf16[83,1024]{1,0:T(8,128)(2,1)S(1)} %fusion.18), channel_id=1, source_target_pairs={{1,0},{2,1},{3,2},{0,3},{5,4},{6,5},{7,6},{4,7},{9,8},{10,9},{11,1... | collective-permute-start | bytes 509960 | tf_op jit(solution)/shard_map/ppermute | solution.py:179
  212.1 13.5 %collective-permute-start.13 = (bf16[83,1024]{1,0:T(8,128)(2,1)S(1)}, bf16[83,1024]{1,0:T(8,128)(2,1)}, u32[]{:S(2)}, u32[]{:S(2)}) collective-permute-start(bf16[83,1024]{1,0:T(8,128)(2,1)S(1)} %fusion.18), channel_id=1, source_target_pairs={{2,0},{3,1},{0,2},{1,3},{6,4},{7,5},{4,6},{5,7},{10,8},{11,9},{8,1... | collective-permute-start | bytes 509960 | tf_op jit(solution)/shard_map/ppermute | solution.py:179
  213.6 12.0 %collective-permute-start.14 = (bf16[83,1024]{1,0:T(8,128)(2,1)S(1)}, bf16[83,1024]{1,0:T(8,128)(2,1)}, u32[]{:S(2)}, u32[]{:S(2)}) collective-permute-start(bf16[83,1024]{1,0:T(8,128)(2,1)S(1)} %fusion.18), channel_id=1, source_target_pairs={{3,0},{0,1},{1,2},{2,3},{7,4},{4,5},{5,6},{6,7},{11,8},{8,9},{9,10... | collective-permute-start | bytes 509960 | tf_op jit(solution)/shard_map/ppermute | solution.py:179
  246.3 9.4 %collective-permute-start.15 = (bf16[83,1024]{1,0:T(8,128)(2,1)S(1)}, bf16[83,1024]{1,0:T(8,128)(2,1)S(1)}, u32[]{:S(2)}, u32[]{:S(2)}) collective-permute-start(bf16[83,1024]{1,0:T(8,128)(2,1)S(1)} %get-tuple-element.206), channel_id=1, source_target_pairs={{0,1},{1,2},{2,3},{3,0},{4,5},{5,6},{6,7},{7,4},{8,9},{9,10},{10,1... | collective-permute-start | bytes 509960 | tf_op jit(solution)/shard_map/ppermute | solution.py:236
  247.4 12.7 %collective-permute-start.16 = (bf16[83,1024]{1,0:T(8,128)(2,1)S(1)}, bf16[83,1024]{1,0:T(8,128)(2,1)S(1)}, u32[]{:S(2)}, u32[]{:S(2)}) collective-permute-start(bf16[83,1024]{1,0:T(8,128)(2,1)S(1)} %get-tuple-element.208), channel_id=1, source_target_pairs={{0,2},{1,3},{2,0},{3,1},{4,6},{5,7},{6,4},{7,5},{8,10},{9,11},{10,... | collective-permute-start | bytes 509960 | tf_op jit(solution)/shard_map/ppermute | solution.py:236
  249.8 10.2 %collective-permute-start.17 = (bf16[83,1024]{1,0:T(8,128)(2,1)S(1)}, bf16[83,1024]{1,0:T(8,128)(2,1)S(1)}, u32[]{:S(2)}, u32[]{:S(2)}) collective-permute-start(bf16[83,1024]{1,0:T(8,128)(2,1)S(1)} %get-tuple-element.207), channel_id=1, source_target_pairs={{0,3},{1,0},{2,1},{3,2},{4,7},{5,4},{6,5},{7,6},{8,11},{9,8},{10,9... | collective-permute-start | bytes 509960 | tf_op jit(solution)/shard_map/ppermute | solution.py:236
  413.9 16.6 %copy-start.46 = (f32[1,512]{1,0:T(1,128)S(1)}, f32[1,512]{1,0:T(1,128)}, u32[]{:S(2)}) copy-start(f32[1,512]{1,0:T(1,128)} %get-tuple-element.134) | copy-start | bytes 6148
  413.9 16.6 %copy-start.47 = (f32[1,512]{1,0:T(1,128)S(1)}, f32[1,512]{1,0:T(1,128)}, u32[]{:S(2)}) copy-start(f32[1,512]{1,0:T(1,128)} %get-tuple-element.136) | copy-start | bytes 6148
  414.0 17.3 %copy-start.44 = (f32[32]{0:T(128)S(1)}, f32[32]{0:T(128)}, u32[]{:S(2)}) copy-start(f32[32]{0:T(128)} %copy-done.43) | copy-start | bytes 388
  414.0 17.4 %copy-start.18 = (bf16[83,1024]{1,0:T(8,128)(2,1)S(1)}, bf16[83,1024]{1,0:T(8,128)(2,1)}, u32[]{:S(2)}) copy-start(bf16[83,1024]{1,0:T(8,128)(2,1)} %copy-done.17) | copy-start | bytes 509956
  414.0 17.4 %copy-start.20 = (bf16[83,1024]{1,0:T(8,128)(2,1)S(1)}, bf16[83,1024]{1,0:T(8,128)(2,1)}, u32[]{:S(2)}) copy-start(bf16[83,1024]{1,0:T(8,128)(2,1)} %copy-done.19) | copy-start | bytes 509956
  437.2 6.5 %collective-permute-start.18 = (bf16[256,2560]{1,0:T(8,128)(2,1)S(1)}, bf16[256,2560]{1,0:T(8,128)(2,1)}, u32[]{:S(2)}, u32[]{:S(2)}) collective-permute-start(bf16[256,2560]{1,0:T(8,128)(2,1)S(1)} %pad_maximum_fusion.2), channel_id=1, source_target_pairs={{0,4},{4,0},{8,12},{12,8},{16,20},{20,16},{24,28},{28,24},{1,5},{5... | collective-permute-start | bytes 3932168 | tf_op jit(solution)/shard_map/ppermute | solution.py:117
  446.4 11.5 %collective-permute-start.21 = (bf16[64,2560]{1,0:T(8,128)(2,1)S(1)}, bf16[64,2560]{1,0:T(8,128)(2,1)S(1)}, u32[]{:S(2)}, u32[]{:S(2)}) collective-permute-start(bf16[64,2560]{1,0:T(8,128)(2,1)S(1)} %pad_maximum_fusion.7), channel_id=1, source_target_pairs={{0,24},{4,28},{8,16},{12,20},{16,8},{20,12},{24,0},{28,4},{1,25},{... | collective-permute-start | bytes 983048 | tf_op jit(solution)/shard_map/ppermute | solution.py:117
  448.3 16.2 %collective-permute-start.20 = (bf16[64,2560]{1,0:T(8,128)(2,1)S(1)}, bf16[64,2560]{1,0:T(8,128)(2,1)S(1)}, u32[]{:S(2)}, u32[]{:S(2)}) collective-permute-start(bf16[64,2560]{1,0:T(8,128)(2,1)S(1)} %pad_maximum_fusion.6), channel_id=1, source_target_pairs={{0,16},{4,20},{8,24},{12,28},{16,0},{20,4},{24,8},{28,12},{1,17},{... | collective-permute-start | bytes 983048 | tf_op jit(solution)/shard_map/ppermute | solution.py:117
  449.1 15.3 %collective-permute-start.19 = (bf16[64,2560]{1,0:T(8,128)(2,1)S(1)}, bf16[64,2560]{1,0:T(8,128)(2,1)S(1)}, u32[]{:S(2)}, u32[]{:S(2)}) collective-permute-start(bf16[64,2560]{1,0:T(8,128)(2,1)S(1)} %pad_maximum_fusion.5), channel_id=1, source_target_pairs={{0,8},{4,12},{8,0},{12,4},{16,24},{20,28},{24,16},{28,20},{1,9},{5... | collective-permute-start | bytes 983048 | tf_op jit(solution)/shard_map/ppermute | solution.py:117
  464.7 6.1 %collective-permute-start.22 = (bf16[16,2560]{1,0:T(8,128)(2,1)S(1)}, bf16[16,2560]{1,0:T(8,128)(2,1)S(1)}, u32[]{:S(2)}, u32[]{:S(2)}) collective-permute-start(bf16[16,2560]{1,0:T(8,128)(2,1)S(1)} %pad_maximum_fusion.10), channel_id=1, source_target_pairs={{0,1},{1,0},{2,3},{3,2},{4,5},{5,4},{6,7},{7,6},{8,9},{9,8},{10,11... | collective-permute-start | bytes 245768 | tf_op jit(solution)/shard_map/ppermute | solution.py:117
  467.2 10.1 %collective-permute-start.23 = (bf16[16,2560]{1,0:T(8,128)(2,1)S(1)}, bf16[16,2560]{1,0:T(8,128)(2,1)S(1)}, u32[]{:S(2)}, u32[]{:S(2)}) collective-permute-start(bf16[16,2560]{1,0:T(8,128)(2,1)S(1)} %pad_maximum_fusion.11), channel_id=1, source_target_pairs={{0,2},{1,3},{2,0},{3,1},{4,6},{5,7},{6,4},{7,5},{8,10},{9,11},{10,... | collective-permute-start | bytes 245768 | tf_op jit(solution)/shard_map/ppermute | solution.py:117
  470.8 6.6 %collective-permute-start.24 = (bf16[16,2560]{1,0:T(8,128)(2,1)S(1)}, bf16[16,2560]{1,0:T(8,128)(2,1)S(1)}, u32[]{:S(2)}, u32[]{:S(2)}) collective-permute-start(bf16[16,2560]{1,0:T(8,128)(2,1)S(1)} %pad_maximum_fusion.12), channel_id=1, source_target_pairs={{0,3},{1,2},{2,1},{3,0},{4,7},{5,6},{6,5},{7,4},{8,11},{9,10},{10,... | collective-permute-start | bytes 245768 | tf_op jit(solution)/shard_map/ppermute | solution.py:117
  477.4 7.2 %collective-permute-start.25 = (bf16[16,2560]{1,0:T(8,128)(2,1)S(1)}, bf16[16,2560]{1,0:T(8,128)(2,1)S(1)}, u32[]{:S(2)}, u32[]{:S(2)}) collective-permute-start(bf16[16,2560]{1,0:T(8,128)(2,1)S(1)} %pad_maximum_fusion.13), channel_id=1, source_target_pairs={{0,3},{1,2},{2,1},{3,0},{4,7},{5,6},{6,5},{7,4},{8,11},{9,10},{10,... | collective-permute-start | bytes 245768 | tf_op jit(solution)/shard_map/ppermute | solution.py:117
  480.0 6.8 %collective-permute-start.26 = (bf16[16,2560]{1,0:T(8,128)(2,1)S(1)}, bf16[16,2560]{1,0:T(8,128)(2,1)S(1)}, u32[]{:S(2)}, u32[]{:S(2)}) collective-permute-start(bf16[16,2560]{1,0:T(8,128)(2,1)S(1)} %pad_maximum_fusion.13), channel_id=1, source_target_pairs={{0,2},{1,3},{2,0},{3,1},{4,6},{5,7},{6,4},{7,5},{8,10},{9,11},{10,... | collective-permute-start | bytes 245768 | tf_op jit(solution)/shard_map/ppermute | solution.py:117
  480.5 6.4 %collective-permute-start.27 = (bf16[16,2560]{1,0:T(8,128)(2,1)S(1)}, bf16[16,2560]{1,0:T(8,128)(2,1)S(1)}, u32[]{:S(2)}, u32[]{:S(2)}) collective-permute-start(bf16[16,2560]{1,0:T(8,128)(2,1)S(1)} %pad_maximum_fusion.13), channel_id=1, source_target_pairs={{0,1},{1,0},{2,3},{3,2},{4,5},{5,4},{6,7},{7,6},{8,9},{9,8},{10,11... | collective-permute-start | bytes 245768 | tf_op jit(solution)/shard_map/ppermute | solution.py:117
  487.0 11.6 %collective-permute-start.28 = (bf16[64,2560]{1,0:T(8,128)(2,1)S(1)}, bf16[64,2560]{1,0:T(8,128)(2,1)S(1)}, u32[]{:S(2)}, u32[]{:S(2)}) collective-permute-start(bf16[64,2560]{1,0:T(8,128)(2,1)S(1)} %pad_maximum_fusion.8), channel_id=1, source_target_pairs={{0,24},{4,28},{8,16},{12,20},{16,8},{20,12},{24,0},{28,4},{1,25},{... | collective-permute-start | bytes 983048 | tf_op jit(solution)/shard_map/ppermute | solution.py:117
  487.9 14.5 %collective-permute-start.29 = (bf16[64,2560]{1,0:T(8,128)(2,1)S(1)}, bf16[64,2560]{1,0:T(8,128)(2,1)S(1)}, u32[]{:S(2)}, u32[]{:S(2)}) collective-permute-start(bf16[64,2560]{1,0:T(8,128)(2,1)S(1)} %pad_maximum_fusion.8), channel_id=1, source_target_pairs={{0,16},{4,20},{8,24},{12,28},{16,0},{20,4},{24,8},{28,12},{1,17},{... | collective-permute-start | bytes 983048 | tf_op jit(solution)/shard_map/ppermute | solution.py:117
  489.9 12.5 %collective-permute-start.30 = (bf16[64,2560]{1,0:T(8,128)(2,1)S(1)}, bf16[64,2560]{1,0:T(8,128)(2,1)S(1)}, u32[]{:S(2)}, u32[]{:S(2)}) collective-permute-start(bf16[64,2560]{1,0:T(8,128)(2,1)S(1)} %pad_maximum_fusion.8), channel_id=1, source_target_pairs={{0,8},{4,12},{8,0},{12,4},{16,24},{20,28},{24,16},{28,20},{1,9},{5... | collective-permute-start | bytes 983048 | tf_op jit(solution)/shard_map/ppermute | solution.py:117
  503.0 3.2 collective-permute-start.31
  536.5 14.2 %collective-permute-start.33 = (bf16[512,512]{1,0:T(8,128)(2,1)}, bf16[512,512]{1,0:T(8,128)(2,1)S(1)}, u32[]{:S(2)}, u32[]{:S(2)}) collective-permute-start(bf16[512,512]{1,0:T(8,128)(2,1)} %get-tuple-element.154.own_ref), channel_id=1, source_target_pairs={{0,8},{4,12},{8,0},{12,4},{16,24},{20,28},{24,16},{28,20},{1,9},{5... | collective-permute-start | bytes 1572872 | tf_op jit(solution)/shard_map/ppermute | solution.py:117
  538.2 14.9 %collective-permute-start.32 = (bf16[512,512]{1,0:T(8,128)(2,1)}, bf16[512,512]{1,0:T(8,128)(2,1)}, u32[]{:S(2)}, u32[]{:S(2)}) collective-permute-start(bf16[512,512]{1,0:T(8,128)(2,1)} %get-tuple-element.154.own_ref), channel_id=1, source_target_pairs={{0,4},{4,0},{8,12},{12,8},{16,20},{20,16},{24,28},{28,24},{1,5},{5... | collective-permute-start | bytes 1572872 | tf_op jit(solution)/shard_map/ppermute | solution.py:117
  550.7 2.5 collective-permute-start.34
  (47 other events, 279.7 us)
Sparse Core Ops, SparseCore 0:
  35.0 45.9 all-gather.3
  155.1 46.0 all-gather.5
  287.2 148.2 all-reduce.9

commit v6 on v5

--- a/solution.py
+++ b/solution.py
@@ -229,17 +229,19 @@
     return across
 
 
-def ring_sum(parts):
+def ring_sum(parts, beside):
     size = lax.axis_size("narrow")
-    total = parts[0]
-    for shift in range(1, size):
-        arrived = lax.ppermute(
-            parts[shift].astype(jnp.bfloat16),
-            "narrow",
-            [(i, (i + shift) % size) for i in range(size)],
+    arrived = [
+        lax.ppermute(
+            parts[shift], "narrow", [(i, (i + shift) % size) for i in range(size)]
         )
-        total = total + arrived.astype(jnp.float32)
-    return total
+        for shift in range(1, size)
+    ]
+    arrived, beside = lax.optimization_barrier((arrived, beside))
+    total = parts[0].astype(jnp.float32)
+    for piece in arrived:
+        total = total + piece.astype(jnp.float32)
+    return total, beside
 
 
 VMEM_LIMIT = 60 * 1024 * 1024
@@ -555,6 +557,7 @@
     spread_ref,
     bias_ref,
     loss_ref,
+    total_ref,
 ):
     step = pl.program_id(0)
     noise_level, skip_scale, out_scale, loss_scale = [scale_ref[place] for place in range(4)]
@@ -568,14 +571,18 @@
 
     @pl.when(step == 0)
     def _():
-        spread_ref[...] = jnp.zeros_like(spread_ref)
+        total_ref[...] = jnp.zeros_like(total_ref)
         bias_ref[...] = jnp.zeros_like(bias_ref)
         loss_ref[...] = jnp.zeros_like(loss_ref)
 
     row_loss = jnp.sum(weighted * errors, axis=1, keepdims=True)
     loss_ref[...] += loss_scale * jnp.sum(row_loss, axis=0, keepdims=True)
     bias_ref[...] += jnp.sum(grads, axis=1, keepdims=True)
-    spread_ref[...] += plain_dot(grads.astype(jnp.bfloat16), counts)
+    total_ref[...] += plain_dot(grads.astype(jnp.bfloat16), counts)
+
+    @pl.when(step == pl.num_programs(0) - 1)
+    def _():
+        spread_ref[...] = total_ref[...].astype(jnp.bfloat16)
 
 
 def decode(scales, counts, raw, target, noise, pixel_weight, channels, shifts, rows=512):
@@ -601,10 +608,11 @@
             pl.BlockSpec((1, 1), lambda i: (0, 0)),
         ],
         out_shape=[
-            jax.ShapeDtypeStruct((128, node_count), jnp.float32),
+            jax.ShapeDtypeStruct((128, node_count), jnp.bfloat16),
             jax.ShapeDtypeStruct((128, 1), jnp.float32),
             jax.ShapeDtypeStruct((1, 1), jnp.float32),
         ],
+        scratch_shapes=[pltpu.VMEM((128, node_count), jnp.float32)],
         cost_estimate=small_cost(),
         compiler_params=kernel_params(),
     )(scales, counts, raw, target, noise, pixel_weight, channels, shifts)
@@ -1061,7 +1069,10 @@
     g2m_cols = g2m_rows.T
     weight_near = in_order([slot[2 * id_rows :] for slot in packed_slots])
     weight_all = lax.all_gather(weight_near, "wide", axis=0)
-    weight_full = weight_all.transpose(2, 1, 0, 3, 4).reshape(3, -1, LATENT_WIDTH)
+    weight_full = [
+        weight_all[:, :, place].transpose(1, 0, 2, 3).reshape(-1, LATENT_WIDTH)
+        for place in range(3)
+    ]
     later = [() for _ in range(narrow_count)]
     later[narrow_count - 2] = own_pieces(mom_attn, mom_up, mom_down)
     later[max(narrow_count - 3, 0)] = weight_full
@@ -1105,15 +1116,16 @@
     loss_local = loss_sum_local[0, 0]
     grad_out_bias = out_bias_sum[: bias_out.shape[0], 0]
     raw_spread = raw_spread[: bias_out.shape[0]]
-    grad_node_raw = (
-        ring_sum(
-            [
-                raw_spread[:, slot * node_local : (slot + 1) * node_local]
-                for slot in range(narrow_count)
-            ]
-        )
-        / M2G_K
-    )
+    raw_spread, mom_all = lax.optimization_barrier((raw_spread, mom_all))
+    mom_full = mom_all.transpose(2, 1, 0, 3, 4).reshape(3, -1, LATENT_WIDTH)
+    grad_node_raw, mom_full = ring_sum(
+        [
+            raw_spread[:, slot * node_local : (slot + 1) * node_local]
+            for slot in range(narrow_count)
+        ],
+        mom_full,
+    )
+    grad_node_raw = grad_node_raw / M2G_K
     grad_dec = lax.dot_general(
         node_low.astype(jnp.float32),
         grad_node_raw,
@@ -1193,9 +1205,7 @@
     late_rows = jnp.pad(late_rows, ((0, width - late_rows.shape[0]), (0, 0)))
     late_rows, grad_qkv, early = lax.optimization_barrier((late_rows, grad_qkv, early))
     early_square = jnp.sum(jnp.square(early.astype(jnp.float32)))
-    late_rows, mom_all = lax.optimization_barrier((late_rows, mom_all))
-    mom_full = mom_all.transpose(2, 1, 0, 3, 4).reshape(3, -1, LATENT_WIDTH)
-    joint, early_square, mom_full = joint_sum(grad_qkv, late_rows, (early_square, mom_full))
+    joint, early_square = joint_sum(grad_qkv, late_rows, (early_square,))
     _, late_rows = joint_split(joint, 3 * LATENT_WIDTH)
     embed_rows = w_embed.shape[0]
     sum_embed = late_rows[:embed_rows]

time: 577 us -> 566 us (0.981)
  matrix products: 41.3 us -> 31.5 us
    slice x0 -> x2, local copies, waits for them, and re-layouts: none -> 7.04 us  [the longest x1 5.73 us: on_device(): weight_all[:, :, place].transpose(1, 0, 2, 3).reshape(-1, LATENT_WIDTH)]
    ppermute x3, waiting for transfers between devices: 8.87 us -> 2.77 us  [ring_sum(): lax.ppermute(parts[shift], 'narrow', [(i, (i + shift) % size) for i in ra...]
  transfers between devices with their start and end apart: 38 -> 38, of which waited for: 17 -> 18; matrix products, arithmetic and copies ran while one was open for 13% -> 12% of each run, Pallas kernels for 48% -> 49%
where the time goes in v6:
time: 566 us; the launch traced here: 556 us
  Pallas kernels  320 us (57%)
  waiting for transfers between devices  59.9 us (11%)
  starting transfers between devices  47 us (8%)
  other arithmetic  41.4 us (7%)
  local copies, waits for them, and re-layouts  38.3 us (7%)
  matrix products  31.5 us (6%)
  between operations  18.5 us (3%)
    pallas_call x4, Pallas kernels, scatter_sum(): pl.pallas_call(functools.partial(scatter_kernel, chunk), grid=(pixel_coun...  62.1 us
    pallas_call x4, Pallas kernels, gather_sum(): pl.pallas_call(functools.partial(gather_kernel, sub), grid=(row_count //...  57.8 us
    pallas_call x1, Pallas kernels, attend_back(): pl.pallas_call(functools.partial(attend_back_kernel, chunk), grid=(HEADS,...  55 us
    ppermute x17, waiting for transfers between devices, partner_swap(): lax.ppermute(values, axis_name, [(i, i ^ distance) for i in range(size)])  40.2 us
    pallas_call x1, Pallas kernels, attend(): pl.pallas_call(functools.partial(attend_kernel, chunk), grid=(HEADS, row_...  35 us
    pallas_call x1, Pallas kernels, turn_moment(): pl.pallas_call(functools.partial(muon_kernel, scalar_row), grid_spec=pltp...  26 us
    pallas_call x1, Pallas kernels, project_back(): pl.pallas_call(project_back_kernel, grid=(row_count // rows,), in_specs=[...  23.1 us
    ppermute x17, starting transfers between devices, partner_swap(): lax.ppermute(values, axis_name, [(i, i ^ distance) for i in range(size)])  19.5 us
  transfers between devices with their start and end apart: 38, of which 18 were waited for; matrix products, arithmetic and copies ran while one was open for 12% of the time, Pallas kernels for 49%

profile of v6, /device:TPU:0, one launch (start us, length us, event | category | flops | bytes accessed | tf_op | source)
XLA Modules:
  0.0 556.4 jit_solution(18037222171286060653)
XLA Ops:
  10.5 5.1 collective-permute-start
  22.1 9.4 %shard_map.573.bias_ref = f32[1024,4096]{1,0:T(8,128)} custom-call(s32[128,256]{1,0:T(8,128)} %get-tuple-element.248.row_ref, s32[128,256]{1,0:T(8,128)} %get-tuple-element.247.lane_ref), custom_call_target="tpu_custom_call" | custom-call | flops 1048576 | bytes 1048576 | tf_op jit(solution)/shard_map/pallas_call | solution.py:310
  37.4 2.9 collective-permute-start.3
  45.3 13.9 %shard_map.574.rest_0_ = f32[4096,512]{1,0:T(8,128)} custom-call(s32[1,1]{1,0:T(1,128)} %bitcast.3.first_ref, s32[4096,4]{1,0:T(8,128)} %copy.123.ids_ref, bf16[249,2048]{1,0:T(8,128)(2,1)} %copy-done.4, bf16[249,512]{1,0:T(8,128)(2,1)} %convert_element_type.341.map_ref, f32[1,512]{1,0:T(1,128)} %bitcast.164), custom_call_target="tpu_custom_call" | custom-call | flops 1048576 | bytes 1048576 | tf_op jit(solution)/shard_map/pallas_call | solution.py:465
  59.2 2.8 collective-permute-done.3
  62.0 5.0 collective-permute-done.4
  73.3 14.7 %shard_map.575.rest_0_ = f32[4096,512]{1,0:T(8,128)} custom-call(s32[1,1]{1,0:T(1,128)} %bitcast.23.first_ref, s32[4096,4]{1,0:T(8,128)} %copy.123.ids_ref, bf16[249,2048]{1,0:T(8,128)(2,1)} %broadcast_select_fusion.2.feature_ref, bf16[249,512]{1,0:T(8,128)(2,1)} %convert_element_type.341.map_ref, f32[1,512]{1,0:T(1,128)} %bitcast.165, ...), custom_call_target="tpu_custom_call" | custom-call | flops 1048576 | bytes 1048576 | tf_op jit(solution)/shard_map/pallas_call | solution.py:465
  88.1 5.7 %fusion.54 = (bf16[8,4,1,64,512]{4,3,0,1,2:T(8,128)(2,1)}, bf16[8,4,1,64,512]{4,3,0,1,2:T(8,128)(2,1)}, bf16[8,4,1,64,512]{4,3,0,1,2:T(8,128)(2,1)}) fusion(bf16[8,4,3,64,512]{4,3,0,1,2:T(8,128)(2,1)} %all-gather.4.cloned.1.call-done), kind=kLoop, calls=%fused_computation.233 | loop fusion | bytes 12582912 | tf_op jit(solution)/shard_map/slice | solution.py:1073
  104.0 14.6 %shard_map.576.rest_0_ = f32[4096,512]{1,0:T(8,128)} custom-call(s32[1,1]{1,0:T(1,128)} %bitcast.42.first_ref, s32[4096,4]{1,0:T(8,128)} %copy.123.ids_ref, bf16[249,2048]{1,0:T(8,128)(2,1)} %select_select_fusion.1.feature_ref, bf16[249,512]{1,0:T(8,128)(2,1)} %convert_element_type.341.map_ref, f32[1,512]{1,0:T(1,128)} %bitcast.166, ...), custom_call_target="tpu_custom_call" | custom-call | flops 1048576 | bytes 1048576 | tf_op jit(solution)/shard_map/pallas_call | solution.py:465
  118.6 3.4 collective-permute-done.8
  126.4 2.4 select_select_fusion.feature_ref
  128.8 14.6 %shard_map.577.sum_ref = f32[4096,512]{1,0:T(8,128)} custom-call(s32[1,1]{1,0:T(1,128)} %bitcast.15.first_ref, s32[4096,4]{1,0:T(8,128)} %copy.123.ids_ref, bf16[249,2048]{1,0:T(8,128)(2,1)} %select_select_fusion.feature_ref, bf16[249,512]{1,0:T(8,128)(2,1)} %convert_element_type.341.map_ref, f32[1,512]{1,0:T(1,128)} %bitcast.167, ...), custom_call_target="tpu_custom_call" | custom-call | flops 1048576 | bytes 1048576 | tf_op jit(solution)/shard_map/pallas_call | solution.py:465
  143.4 13.2 %shard_map.578 = (bf16[4096,512]{1,0:T(8,128)(2,1)}, bf16[1024,512]{1,0:T(8,128)(2,1)}, bf16[4096,1024]{1,0:T(8,128)(2,1)}) custom-call(f32[4096,512]{1,0:T(8,128)} %shard_map.577.sum_ref, f32[4,512]{1,0:T(4,128)} %broadcast_add_fusion.shift_ref, bf16[2048,512]{1,0:T(8,128)(2,1)} %bitcast.140), custom_call_target="tpu_custom_call" | custom-call | flops 1048576 | bytes 1048576 | tf_op jit(solution)/shard_map/pallas_call | solution.py:646
  159.7 35.0 %shard_map.579 = (f32[1024,512]{1,0:T(8,128)}, f32[1024,512]{1,0:T(8,128)}) custom-call(bf16[1024,512]{1,0:T(8,128)(2,1)} %get-tuple-element.116.q_ref, bf16[4096,1024]{1,0:T(8,128)(2,1)} %get-tuple-element.119.k_ref.v_ref, bf16[4096,1024]{1,0:T(8,128)(2,1)} %get-tuple-element.119.k_ref.v_ref, f32[1024,4096]{1,0:T(8,128)} %shard_map.573.bias_ref), custom_call_target="tpu_custom_call" | custom-call | flops 1048576 | bytes 1048576 | tf_op jit(solution)/shard_map/pallas_call | solution.py:346
  194.7 3.3 fusion.61
  200.4 5.7 %multiply_convert_fusion.1 = (bf16[1024,2048]{1,0:T(8,128)(2,1)S(1)}, f32[1024,2048]{1,0:T(8,128)}) fusion(f32[2048]{0:T(1024)S(1)} %slice.230, bf16[2048,512]{1,0:T(8,128)(2,1)S(1)} %bitcast.146, f32[1024,512]{1,0:T(8,128)S(1)} %get-tuple-element.256, f32[512]{0:T(512)S(1)} %get-tuple-element.254, f32[512]{0:T(512)S(1)} %get-tuple-element.253, ...), kind=kOutput, calls=%fused_computation.3 | convolution fusion | flops 2162688000 | bytes 16797696 | tf_op jit(solution)/shard_map/dot_general | solution.py:90
  212.1 9.5 %shard_map.580.count_ref = bf16[2048,4096]{1,0:T(8,128)(2,1)} custom-call(s32[2048,3]{1,0:T(8,128)} %add_select_fusion.ids_ref), custom_call_target="tpu_custom_call" | custom-call | flops 1048576 | bytes 1048576 | tf_op jit(solution)/shard_map/pallas_call | solution.py:276
  226.1 16.5 %shard_map.581 = (bf16[128,4096]{1,0:T(8,128)(2,1)}, f32[128,1]{1,0:T(8,128)}, f32[1,1]{1,0:T(1,128)}) custom-call(f32[4]{0:T(128)} %pad_maximum_fusion.16.scale_ref, bf16[2048,4096]{1,0:T(8,128)(2,1)} %shard_map.580.count_ref, bf16[128,4096]{1,0:T(8,128)(2,1)} %fusion.9.raw_ref, bf16[128,2048]{1,0:T(8,128)(2,1)} %pad.30.target_ref, ...), custom_call_target="tpu_custom_call" | custom-call | flops 1048576 | bytes 1048576 | tf_op jit(solution)/shard_map/pallas_call | solution.py:592
  246.2 2.7 collective-permute-start.17
  248.9 6.3 %copy.126 = bf16[3,4,8,64,512]{4,3,2,1,0:T(8,128)(2,1)} copy(bf16[3,4,8,64,512]{4,3,0,1,2:T(8,128)(2,1)} %bitcast.145) | data formatting | bytes 12582912 | tf_op jit(solution)/shard_map/transpose | solution.py:1120
  255.2 2.8 collective-permute-done.16
  259.1 4.9 convert_reduce_fusion
  264.1 2.9 multiply_reduce_fusion.1
  267.0 2.6 convolution_convert_fusion.1
  269.6 2.5 convolution_convert_fusion
  273.1 3.3 convolution_convert_fusion.2.g_ref
  277.2 2.3 pad_maximum_fusion
  281.9 55.0 %shard_map.582 = (bf16[1024,512]{1,0:T(8,128)(2,1)}, bf16[4096,512]{1,0:T(8,128)(2,1)}, bf16[4096,512]{1,0:T(8,128)(2,1)}) custom-call(bf16[1024,512]{1,0:T(8,128)(2,1)} %get-tuple-element.116.q_ref, bf16[4096,1024]{1,0:T(8,128)(2,1)} %get-tuple-element.119.k_ref.v_ref, bf16[4096,1024]{1,0:T(8,128)(2,1)} %get-tuple-element.119.k_ref.v_ref, ...), custom_call_target="tpu_custom_call" | custom-call | flops 1048576 | bytes 1048576 | tf_op jit(solution)/shard_map/pallas_call | solution.py:415
  336.9 23.1 %shard_map.583 = (bf16[4096,512]{1,0:T(8,128)(2,1)}, f32[512,1536]{1,0:T(8,128)}, f32[8,512]{1,0:T(8,128)}) custom-call(bf16[1024,512]{1,0:T(8,128)(2,1)} %get-tuple-element.138.dq_ref, bf16[4096,512]{1,0:T(8,128)(2,1)} %get-tuple-element.139.dk_ref, bf16[4096,512]{1,0:T(8,128)(2,1)} %get-tuple-element.140.dv_ref, f32[4096,512]{1,0:T(8,128)} %shard_map.577.sum_ref, ...), custom_call_target="tpu_custom_call" | custom-call | flops 1048576 | bytes 1048576 | tf_op jit(solution)/shard_map/pallas_call | solution.py:718
  360.0 15.6 %shard_map.585 = (f32[249,512]{1,0:T(8,128)}, f32[1,512]{1,0:T(1,128)}) custom-call(s32[1,1]{1,0:T(1,128)} %bitcast.23.first_ref, s32[4,4096]{1,0:T(4,128)} %copy-done.15, bf16[4096,512]{1,0:T(8,128)(2,1)} %get-tuple-element.142.g_ref, bf16[249,2048]{1,0:T(8,128)(2,1)} %broadcast_select_fusion.2.feature_ref, bf16[249,512]{1,0:T(8,128)(2,1)} %convert_element_type.341.map_ref, ...), custom_call_target="tpu_custom_call" | custom-call | flops 1048576 | bytes 1048576 | tf_op jit(solution)/shard_map/pallas_call | solution.py:520
  375.5 15.5 %shard_map.584 = (f32[249,512]{1,0:T(8,128)}, f32[1,512]{1,0:T(1,128)}) custom-call(s32[1,1]{1,0:T(1,128)} %bitcast.3.first_ref, s32[4,4096]{1,0:T(4,128)} %copy-done.15, bf16[4096,512]{1,0:T(8,128)(2,1)} %get-tuple-element.142.g_ref, bf16[249,2048]{1,0:T(8,128)(2,1)} %copy-done.4, bf16[249,512]{1,0:T(8,128)(2,1)} %convert_element_type.341.map_ref, ...), custom_call_target="tpu_custom_call" | custom-call | flops 1048576 | bytes 1048576 | tf_op jit(solution)/shard_map/pallas_call | solution.py:520
  391.0 15.5 %shard_map.586 = (f32[249,512]{1,0:T(8,128)}, f32[1,512]{1,0:T(1,128)}) custom-call(s32[1,1]{1,0:T(1,128)} %bitcast.42.first_ref, s32[4,4096]{1,0:T(4,128)} %copy-done.15, bf16[4096,512]{1,0:T(8,128)(2,1)} %get-tuple-element.142.g_ref, bf16[249,2048]{1,0:T(8,128)(2,1)} %select_select_fusion.1.feature_ref, bf16[249,512]{1,0:T(8,128)(2,1)} %convert_element_type.341.map_ref, ...), custom_call_target="tpu_custom_call" | custom-call | flops 1048576 | bytes 1048576 | tf_op jit(solution)/shard_map/pallas_call | solution.py:520
  406.5 15.6 %shard_map.587 = (f32[249,512]{1,0:T(8,128)}, f32[1,512]{1,0:T(1,128)}) custom-call(s32[1,1]{1,0:T(1,128)} %bitcast.15.first_ref, s32[4,4096]{1,0:T(4,128)} %copy-done.15, bf16[4096,512]{1,0:T(8,128)(2,1)} %get-tuple-element.142.g_ref, bf16[249,2048]{1,0:T(8,128)(2,1)} %select_select_fusion.feature_ref, bf16[249,512]{1,0:T(8,128)(2,1)} %convert_element_type.341.map_ref, ...), custom_call_target="tpu_custom_call" | custom-call | flops 1048576 | bytes 1048576 | tf_op jit(solution)/shard_map/pallas_call | solution.py:520
  430.0 3.1 collective-permute-done.18
  440.0 3.0 multiply_reduce_fusion
  443.0 4.8 collective-permute-done.21
  447.8 6.2 %collective-permute-done.20 = bf16[64,2560]{1,0:T(8,128)(2,1)S(1)} collective-permute-done((bf16[64,2560]{1,0:T(8,128)(2,1)S(1)}, bf16[64,2560]{1,0:T(8,128)(2,1)S(1)}, u32[]{:S(2)}, u32[]{:S(2)}) %collective-permute-start.20) | collective-permute-done | bytes 327712 | tf_op jit(solution)/shard_map/ppermute | solution.py:117
  454.3 3.8 collective-permute-start.22
  460.5 6.8 %collective-permute-done.23 = bf16[16,2560]{1,0:T(8,128)(2,1)S(1)} collective-permute-done((bf16[16,2560]{1,0:T(8,128)(2,1)S(1)}, bf16[16,2560]{1,0:T(8,128)(2,1)S(1)}, u32[]{:S(2)}, u32[]{:S(2)}) %collective-permute-start.23) | collective-permute-done | bytes 81952 | tf_op jit(solution)/shard_map/ppermute | solution.py:117
  471.8 2.4 collective-permute-done.25
  480.1 7.9 %collective-permute-done.28 = bf16[64,2560]{1,0:T(8,128)(2,1)S(1)} collective-permute-done((bf16[64,2560]{1,0:T(8,128)(2,1)S(1)}, bf16[64,2560]{1,0:T(8,128)(2,1)S(1)}, u32[]{:S(2)}, u32[]{:S(2)}) %collective-permute-start.28) | collective-permute-done | bytes 327712 | tf_op jit(solution)/shard_map/ppermute | solution.py:117
  487.9 3.4 collective-permute-done.29
  492.6 2.6 collective-permute-done.31
  499.3 26.0 %shard_map.588 = (bf16[512,512]{1,0:T(8,128)(2,1)}, f32[1,1]{1,0:T(1,128)}, f32[1,1]{1,0:T(1,128)}) custom-call(s32[2]{0:T(128)} %pad_add_fusion.choice_ref, f32[1,1]{1,0:T(1,128)} %bitcast.66.square_ref, bf16[3,2048,512]{2,1,0:T(8,128)(2,1)} %bitcast.144, bf16[512,2560]{1,0:T(8,128)(2,1)} %pad_maximum_fusion.1.joint_ref.qkv_ref, ...), custom_call_target="tpu_custom_call" | custom-call | flops 1048576 | bytes 1048576 | tf_op jit(solution)/shard_map/pallas_call | solution.py:821
  526.9 5.2 shard_map.589
  532.1 2.7 multiply_add_fusion.5
  536.2 2.4 multiply_add_fusion.1
  542.8 6.8 %shard_map.590 = (f32[512,512]{1,0:T(8,128)}, f32[512,512]{1,0:T(8,128)}, f32[512,512]{1,0:T(8,128)}, f32[512,512]{1,0:T(8,128)}, f32[512,512]{1,0:T(8,128)}, /*index=5*/f32[512,512]{1,0:T(8,128)}) custom-call(s32[1]{0:T(128)} %bitcast.group_ref, bf16[512,512]{1,0:T(8,128)(2,1)} %get-tuple-element.164.own_ref, ...), custom_call_target="tpu_custom_call" | custom-call | flops 1048576 | bytes 1048576 | tf_op jit(solution)/shard_map/pallas_call | solution.py:932
  (335 shorter events, 102.7 us)
Async XLA Ops:
  7.2 80.8 %all-gather.4.cloned.1.call-start = ((), (), s32[]{:S(2)}) async-start(), calls=%async_computation | async-start | bytes 7077888 | tf_op jit(solution)/shard_map/all_gather | solution.py:1071
  10.5 21.1 %collective-permute-start = (bf16[208,512]{1,0:T(8,128)(2,1)S(1)}, bf16[208,512]{1,0:T(8,128)(2,1)S(1)}, u32[]{:S(2)}, u32[]{:S(2)}) collective-permute-start(bf16[208,512]{1,0:T(8,128)(2,1)S(1)} %fusion.31), channel_id=1, source_target_pairs={{1,0},{2,1},{3,2},{0,3},{5,4},{6,5},{7,6},{4,7},{9,8},{10,9},{11,1... | collective-permute-start | bytes 638984 | tf_op jit(solution)/shard_map/ppermute | solution.py:179
  15.6 18.1 %collective-permute-start.1 = (bf16[208,512]{1,0:T(8,128)(2,1)S(1)}, bf16[208,512]{1,0:T(8,128)(2,1)S(1)}, u32[]{:S(2)}, u32[]{:S(2)}) collective-permute-start(bf16[208,512]{1,0:T(8,128)(2,1)S(1)} %fusion.31), channel_id=1, source_target_pairs={{2,0},{3,1},{0,2},{1,3},{6,4},{7,5},{4,6},{5,7},{10,8},{11,9},{8,1... | collective-permute-start | bytes 638984 | tf_op jit(solution)/shard_map/ppermute | solution.py:179
  15.6 18.1 %collective-permute-start.2 = (bf16[208,512]{1,0:T(8,128)(2,1)S(1)}, bf16[208,512]{1,0:T(8,128)(2,1)S(1)}, u32[]{:S(2)}, u32[]{:S(2)}) collective-permute-start(bf16[208,512]{1,0:T(8,128)(2,1)S(1)} %fusion.31), channel_id=1, source_target_pairs={{3,0},{0,1},{1,2},{2,3},{7,4},{4,5},{5,6},{6,7},{11,8},{8,9},{9,10... | collective-permute-start | bytes 638984 | tf_op jit(solution)/shard_map/ppermute | solution.py:179
  34.9 174.0 %all-gather.6.cloned.1.call-start = ((), (), s32[]{:S(2)}) async-start(), calls=%async_computation.2 | async-start | bytes 7077888 | tf_op jit(solution)/shard_map/all_gather | solution.py:1091
  37.4 24.6 %collective-permute-start.3 = (bf16[249,2048]{1,0:T(8,128)(2,1)S(1)}, bf16[249,2048]{1,0:T(8,128)(2,1)S(1)}, u32[]{:S(2)}, u32[]{:S(2)}) collective-permute-start(bf16[249,2048]{1,0:T(8,128)(2,1)S(1)} %pad_maximum_fusion.4.feature_ref), channel_id=1, source_target_pairs={{0,1},{1,2},{2,3},{4,5},{5,6},{6,7},{8,9},{9,10},{10,11},{12,13},{... | collective-permute-start | bytes 3059720 | tf_op jit(solution)/shard_map/ppermute | solution.py:196
  40.3 26.7 %collective-permute-start.4 = (bf16[249,2048]{1,0:T(8,128)(2,1)S(1)}, bf16[249,2048]{1,0:T(8,128)(2,1)}, u32[]{:S(2)}, u32[]{:S(2)}) collective-permute-start(bf16[249,2048]{1,0:T(8,128)(2,1)S(1)} %pad_maximum_fusion.4.feature_ref), channel_id=1, source_target_pairs={{1,0},{2,1},{3,2},{5,4},{6,5},{7,6},{9,8},{10,9},{11,10},{13,12},{... | collective-permute-start | bytes 3059720 | tf_op jit(solution)/shard_map/ppermute | solution.py:199
  43.1 26.4 %copy-start.46 = (f32[32]{0:T(128)}, f32[32]{0:T(128)S(1)}, u32[]{:S(2)}) copy-start(f32[32]{0:T(128)S(1)} %pad_maximum_fusion.15) | copy-start | bytes 388
  45.3 24.2 %copy-start.19 = (f32[32,2048]{1,0:T(8,128)S(1)}, f32[32,2048]{1,0:T(8,128)}, u32[]{:S(2)}) copy-start(f32[32,2048]{1,0:T(8,128)} %param.48) | copy-start | bytes 786436
  45.3 24.5 %copy-start.55 = (s32[4]{0:T(128)S(1)}, s32[4]{0:T(128)}, u32[]{:S(2)}) copy-start(s32[4]{0:T(128)} %constant.257.clone) | copy-start | bytes 52
  67.0 26.8 %collective-permute-start.5 = (bf16[249,2048]{1,0:T(8,128)(2,1)S(1)}, bf16[249,2048]{1,0:T(8,128)(2,1)S(1)}, u32[]{:S(2)}, u32[]{:S(2)}) collective-permute-start(bf16[249,2048]{1,0:T(8,128)(2,1)S(1)} %collective-permute-done.3), channel_id=1, source_target_pairs={{1,2},{2,3},{5,6},{6,7},{9,10},{10,11},{13,14},{14,15},{17,18},{18... | collective-permute-start | bytes 3059720 | tf_op jit(solution)/shard_map/ppermute | solution.py:196
  67.7 26.7 %collective-permute-start.6 = (bf16[249,2048]{1,0:T(8,128)(2,1)}, bf16[249,2048]{1,0:T(8,128)(2,1)S(1)}, u32[]{:S(2)}, u32[]{:S(2)}) collective-permute-start(bf16[249,2048]{1,0:T(8,128)(2,1)} %collective-permute-done.4), channel_id=1, source_target_pairs={{1,0},{2,1},{5,4},{6,5},{9,8},{10,9},{13,12},{14,13},{17,16},{18,1... | collective-permute-start | bytes 3059720 | tf_op jit(solution)/shard_map/ppermute | solution.py:199
  94.5 24.1 %collective-permute-start.7 = (bf16[249,2048]{1,0:T(8,128)(2,1)S(1)}, bf16[249,2048]{1,0:T(8,128)(2,1)}, u32[]{:S(2)}, u32[]{:S(2)}) collective-permute-start(bf16[249,2048]{1,0:T(8,128)(2,1)S(1)} %collective-permute-done.5), channel_id=1, source_target_pairs={{2,3},{6,7},{10,11},{14,15},{18,19},{22,23},{26,27},{30,31}} | collective-permute-start | bytes 3059720 | tf_op jit(solution)/shard_map/ppermute | solution.py:196
  96.1 25.9 %collective-permute-start.8 = (bf16[249,2048]{1,0:T(8,128)(2,1)S(1)}, bf16[249,2048]{1,0:T(8,128)(2,1)}, u32[]{:S(2)}, u32[]{:S(2)}) collective-permute-start(bf16[249,2048]{1,0:T(8,128)(2,1)S(1)} %collective-permute-done.6), channel_id=1, source_target_pairs={{1,0},{5,4},{9,8},{13,12},{17,16},{21,20},{25,24},{29,28}} | collective-permute-start | bytes 3059720 | tf_op jit(solution)/shard_map/ppermute | solution.py:199
  122.0 34.7 %collective-permute-start.9 = (bf16[192,512]{1,0:T(8,128)(2,1)S(1)}, bf16[192,512]{1,0:T(8,128)(2,1)S(1)}, u32[]{:S(2)}, u32[]{:S(2)}) collective-permute-start(bf16[192,512]{1,0:T(8,128)(2,1)S(1)} %pad_maximum_fusion.9), channel_id=1, source_target_pairs={{1,0},{2,1},{3,2},{0,3},{5,4},{6,5},{7,6},{4,7},{9,8},{10,9},{11,1... | collective-permute-start | bytes 589832 | tf_op jit(solution)/shard_map/ppermute | solution.py:179
  123.2 33.5 %collective-permute-start.10 = (bf16[192,512]{1,0:T(8,128)(2,1)S(1)}, bf16[192,512]{1,0:T(8,128)(2,1)S(1)}, u32[]{:S(2)}, u32[]{:S(2)}) collective-permute-start(bf16[192,512]{1,0:T(8,128)(2,1)S(1)} %pad_maximum_fusion.9), channel_id=1, source_target_pairs={{2,0},{3,1},{0,2},{1,3},{6,4},{7,5},{4,6},{5,7},{10,8},{11,9},{8,1... | collective-permute-start | bytes 589832 | tf_op jit(solution)/shard_map/ppermute | solution.py:179
  124.4 32.3 %collective-permute-start.11 = (bf16[192,512]{1,0:T(8,128)(2,1)S(1)}, bf16[192,512]{1,0:T(8,128)(2,1)S(1)}, u32[]{:S(2)}, u32[]{:S(2)}) collective-permute-start(bf16[192,512]{1,0:T(8,128)(2,1)S(1)} %pad_maximum_fusion.9), channel_id=1, source_target_pairs={{3,0},{0,1},{1,2},{2,3},{7,4},{4,5},{5,6},{6,7},{11,8},{8,9},{9,10... | collective-permute-start | bytes 589832 | tf_op jit(solution)/shard_map/ppermute | solution.py:179
  157.7 270.4 %all-reduce.10.cloned.1.call-start = ((), (), s32[]{:S(2)}) async-start(), calls=%async_computation.1 | async-start | bytes 9437184 | tf_op jit(solution)/shard_map/psum | solution.py:1154
  198.0 69.0 %copy-start.2 = (f32[1024,512]{1,0:T(8,128)}, f32[1024,512]{1,0:T(8,128)S(1)}, u32[]{:S(2)}) copy-start(f32[1024,512]{1,0:T(8,128)S(1)} %get-tuple-element.256) | copy-start | bytes 6291460
  208.9 13.4 %collective-permute-start.12 = (bf16[83,1024]{1,0:T(8,128)(2,1)S(1)}, bf16[83,1024]{1,0:T(8,128)(2,1)}, u32[]{:S(2)}, u32[]{:S(2)}) collective-permute-start(bf16[83,1024]{1,0:T(8,128)(2,1)S(1)} %fusion.5), channel_id=1, source_target_pairs={{1,0},{2,1},{3,2},{0,3},{5,4},{6,5},{7,6},{4,7},{9,8},{10,9},{11,1... | collective-permute-start | bytes 509960 | tf_op jit(solution)/shard_map/ppermute | solution.py:179
  210.6 13.4 %collective-permute-start.13 = (bf16[83,1024]{1,0:T(8,128)(2,1)S(1)}, bf16[83,1024]{1,0:T(8,128)(2,1)}, u32[]{:S(2)}, u32[]{:S(2)}) collective-permute-start(bf16[83,1024]{1,0:T(8,128)(2,1)S(1)} %fusion.5), channel_id=1, source_target_pairs={{2,0},{3,1},{0,2},{1,3},{6,4},{7,5},{4,6},{5,7},{10,8},{11,9},{8,1... | collective-permute-start | bytes 509960 | tf_op jit(solution)/shard_map/ppermute | solution.py:179
  210.6 13.4 %collective-permute-start.14 = (bf16[83,1024]{1,0:T(8,128)(2,1)S(1)}, bf16[83,1024]{1,0:T(8,128)(2,1)}, u32[]{:S(2)}, u32[]{:S(2)}) collective-permute-start(bf16[83,1024]{1,0:T(8,128)(2,1)S(1)} %fusion.5), channel_id=1, source_target_pairs={{3,0},{0,1},{1,2},{2,3},{7,4},{4,5},{5,6},{6,7},{11,8},{8,9},{9,10... | collective-permute-start | bytes 509960 | tf_op jit(solution)/shard_map/ppermute | solution.py:179
  244.0 11.2 %collective-permute-start.15 = (bf16[83,1024]{1,0:T(8,128)(2,1)S(1)}, bf16[83,1024]{1,0:T(8,128)(2,1)S(1)}, u32[]{:S(2)}, u32[]{:S(2)}) collective-permute-start(bf16[83,1024]{1,0:T(8,128)(2,1)S(1)} %get-tuple-element.221), channel_id=1, source_target_pairs={{0,1},{1,2},{2,3},{3,0},{4,5},{5,6},{6,7},{7,4},{8,9},{9,10},{10,1... | collective-permute-start | bytes 509960 | tf_op jit(solution)/shard_map/ppermute | solution.py:235
  245.2 12.7 %collective-permute-start.16 = (bf16[83,1024]{1,0:T(8,128)(2,1)S(1)}, bf16[83,1024]{1,0:T(8,128)(2,1)S(1)}, u32[]{:S(2)}, u32[]{:S(2)}) collective-permute-start(bf16[83,1024]{1,0:T(8,128)(2,1)S(1)} %get-tuple-element.220), channel_id=1, source_target_pairs={{0,2},{1,3},{2,0},{3,1},{4,6},{5,7},{6,4},{7,5},{8,10},{9,11},{10,... | collective-permute-start | bytes 509960 | tf_op jit(solution)/shard_map/ppermute | solution.py:235
  246.2 11.8 %collective-permute-start.17 = (bf16[83,1024]{1,0:T(8,128)(2,1)S(1)}, bf16[83,1024]{1,0:T(8,128)(2,1)S(1)}, u32[]{:S(2)}, u32[]{:S(2)}) collective-permute-start(bf16[83,1024]{1,0:T(8,128)(2,1)S(1)} %get-tuple-element.219), channel_id=1, source_target_pairs={{0,3},{1,0},{2,1},{3,2},{4,7},{5,4},{6,5},{7,6},{8,11},{9,8},{10,9... | collective-permute-start | bytes 509960 | tf_op jit(solution)/shard_map/ppermute | solution.py:235
  406.5 16.6 %copy-start.48 = (f32[1,512]{1,0:T(1,128)S(1)}, f32[1,512]{1,0:T(1,128)}, u32[]{:S(2)}) copy-start(f32[1,512]{1,0:T(1,128)} %get-tuple-element.148) | copy-start | bytes 6148
  406.5 16.6 %copy-start.49 = (f32[1,512]{1,0:T(1,128)S(1)}, f32[1,512]{1,0:T(1,128)}, u32[]{:S(2)}) copy-start(f32[1,512]{1,0:T(1,128)} %get-tuple-element.147) | copy-start | bytes 6148
  406.5 16.6 %copy-start.50 = (f32[1,512]{1,0:T(1,128)S(1)}, f32[1,512]{1,0:T(1,128)}, u32[]{:S(2)}) copy-start(f32[1,512]{1,0:T(1,128)} %get-tuple-element.149) | copy-start | bytes 6148
  406.5 17.3 %copy-start.47 = (f32[32]{0:T(128)S(1)}, f32[32]{0:T(128)}, u32[]{:S(2)}) copy-start(f32[32]{0:T(128)} %copy-done.46) | copy-start | bytes 388
  406.5 17.4 %copy-start.22 = (bf16[83,1024]{1,0:T(8,128)(2,1)S(1)}, bf16[83,1024]{1,0:T(8,128)(2,1)}, u32[]{:S(2)}) copy-start(bf16[83,1024]{1,0:T(8,128)(2,1)} %copy-done.21) | copy-start | bytes 509956
  406.5 17.4 %copy-start.24 = (bf16[83,1024]{1,0:T(8,128)(2,1)S(1)}, bf16[83,1024]{1,0:T(8,128)(2,1)}, u32[]{:S(2)}) copy-start(bf16[83,1024]{1,0:T(8,128)(2,1)} %copy-done.23) | copy-start | bytes 509956
  429.9 3.2 collective-permute-start.18
  436.3 11.6 %collective-permute-start.21 = (bf16[64,2560]{1,0:T(8,128)(2,1)S(1)}, bf16[64,2560]{1,0:T(8,128)(2,1)S(1)}, u32[]{:S(2)}, u32[]{:S(2)}) collective-permute-start(bf16[64,2560]{1,0:T(8,128)(2,1)S(1)} %pad_maximum_fusion.7), channel_id=1, source_target_pairs={{0,24},{4,28},{8,16},{12,20},{16,8},{20,12},{24,0},{28,4},{1,25},{... | collective-permute-start | bytes 983048 | tf_op jit(solution)/shard_map/ppermute | solution.py:117
  438.0 16.0 %collective-permute-start.20 = (bf16[64,2560]{1,0:T(8,128)(2,1)S(1)}, bf16[64,2560]{1,0:T(8,128)(2,1)S(1)}, u32[]{:S(2)}, u32[]{:S(2)}) collective-permute-start(bf16[64,2560]{1,0:T(8,128)(2,1)S(1)} %pad_maximum_fusion.6), channel_id=1, source_target_pairs={{0,16},{4,20},{8,24},{12,28},{16,0},{20,4},{24,8},{28,12},{1,17},{... | collective-permute-start | bytes 983048 | tf_op jit(solution)/shard_map/ppermute | solution.py:117
  439.1 14.9 %collective-permute-start.19 = (bf16[64,2560]{1,0:T(8,128)(2,1)S(1)}, bf16[64,2560]{1,0:T(8,128)(2,1)S(1)}, u32[]{:S(2)}, u32[]{:S(2)}) collective-permute-start(bf16[64,2560]{1,0:T(8,128)(2,1)S(1)} %pad_maximum_fusion.5), channel_id=1, source_target_pairs={{0,8},{4,12},{8,0},{12,4},{16,24},{20,28},{24,16},{28,20},{1,9},{5... | collective-permute-start | bytes 983048 | tf_op jit(solution)/shard_map/ppermute | solution.py:117
  454.3 6.2 %collective-permute-start.22 = (bf16[16,2560]{1,0:T(8,128)(2,1)S(1)}, bf16[16,2560]{1,0:T(8,128)(2,1)S(1)}, u32[]{:S(2)}, u32[]{:S(2)}) collective-permute-start(bf16[16,2560]{1,0:T(8,128)(2,1)S(1)} %pad_maximum_fusion.10), channel_id=1, source_target_pairs={{0,1},{1,0},{2,3},{3,2},{4,5},{5,4},{6,7},{7,6},{8,9},{9,8},{10,11... | collective-permute-start | bytes 245768 | tf_op jit(solution)/shard_map/ppermute | solution.py:117
  458.0 9.2 %collective-permute-start.23 = (bf16[16,2560]{1,0:T(8,128)(2,1)S(1)}, bf16[16,2560]{1,0:T(8,128)(2,1)S(1)}, u32[]{:S(2)}, u32[]{:S(2)}) collective-permute-start(bf16[16,2560]{1,0:T(8,128)(2,1)S(1)} %pad_maximum_fusion.11), channel_id=1, source_target_pairs={{0,2},{1,3},{2,0},{3,1},{4,6},{5,7},{6,4},{7,5},{8,10},{9,11},{10,... | collective-permute-start | bytes 245768 | tf_op jit(solution)/shard_map/ppermute | solution.py:117
  460.3 7.0 %collective-permute-start.24 = (bf16[16,2560]{1,0:T(8,128)(2,1)S(1)}, bf16[16,2560]{1,0:T(8,128)(2,1)S(1)}, u32[]{:S(2)}, u32[]{:S(2)}) collective-permute-start(bf16[16,2560]{1,0:T(8,128)(2,1)S(1)} %pad_maximum_fusion.12), channel_id=1, source_target_pairs={{0,3},{1,2},{2,1},{3,0},{4,7},{5,6},{6,5},{7,4},{8,11},{9,10},{10,... | collective-permute-start | bytes 245768 | tf_op jit(solution)/shard_map/ppermute | solution.py:117
  467.4 6.9 %collective-permute-start.25 = (bf16[16,2560]{1,0:T(8,128)(2,1)S(1)}, bf16[16,2560]{1,0:T(8,128)(2,1)S(1)}, u32[]{:S(2)}, u32[]{:S(2)}) collective-permute-start(bf16[16,2560]{1,0:T(8,128)(2,1)S(1)} %pad_maximum_fusion.13), channel_id=1, source_target_pairs={{0,3},{1,2},{2,1},{3,0},{4,7},{5,6},{6,5},{7,4},{8,11},{9,10},{10,... | collective-permute-start | bytes 245768 | tf_op jit(solution)/shard_map/ppermute | solution.py:117
  469.6 6.8 %collective-permute-start.26 = (bf16[16,2560]{1,0:T(8,128)(2,1)S(1)}, bf16[16,2560]{1,0:T(8,128)(2,1)S(1)}, u32[]{:S(2)}, u32[]{:S(2)}) collective-permute-start(bf16[16,2560]{1,0:T(8,128)(2,1)S(1)} %pad_maximum_fusion.13), channel_id=1, source_target_pairs={{0,2},{1,3},{2,0},{3,1},{4,6},{5,7},{6,4},{7,5},{8,10},{9,11},{10,... | collective-permute-start | bytes 245768 | tf_op jit(solution)/shard_map/ppermute | solution.py:117
  470.3 6.1 %collective-permute-start.27 = (bf16[16,2560]{1,0:T(8,128)(2,1)S(1)}, bf16[16,2560]{1,0:T(8,128)(2,1)S(1)}, u32[]{:S(2)}, u32[]{:S(2)}) collective-permute-start(bf16[16,2560]{1,0:T(8,128)(2,1)S(1)} %pad_maximum_fusion.13), channel_id=1, source_target_pairs={{0,1},{1,0},{2,3},{3,2},{4,5},{5,4},{6,7},{7,6},{8,9},{9,8},{10,11... | collective-permute-start | bytes 245768 | tf_op jit(solution)/shard_map/ppermute | solution.py:117
  476.5 11.4 %collective-permute-start.28 = (bf16[64,2560]{1,0:T(8,128)(2,1)S(1)}, bf16[64,2560]{1,0:T(8,128)(2,1)S(1)}, u32[]{:S(2)}, u32[]{:S(2)}) collective-permute-start(bf16[64,2560]{1,0:T(8,128)(2,1)S(1)} %pad_maximum_fusion.8), channel_id=1, source_target_pairs={{0,24},{4,28},{8,16},{12,20},{16,8},{20,12},{24,0},{28,4},{1,25},{... | collective-permute-start | bytes 983048 | tf_op jit(solution)/shard_map/ppermute | solution.py:117
  477.3 14.0 %collective-permute-start.29 = (bf16[64,2560]{1,0:T(8,128)(2,1)S(1)}, bf16[64,2560]{1,0:T(8,128)(2,1)S(1)}, u32[]{:S(2)}, u32[]{:S(2)}) collective-permute-start(bf16[64,2560]{1,0:T(8,128)(2,1)S(1)} %pad_maximum_fusion.8), channel_id=1, source_target_pairs={{0,16},{4,20},{8,24},{12,28},{16,0},{20,4},{24,8},{28,12},{1,17},{... | collective-permute-start | bytes 983048 | tf_op jit(solution)/shard_map/ppermute | solution.py:117
  479.5 11.9 %collective-permute-start.30 = (bf16[64,2560]{1,0:T(8,128)(2,1)S(1)}, bf16[64,2560]{1,0:T(8,128)(2,1)S(1)}, u32[]{:S(2)}, u32[]{:S(2)}) collective-permute-start(bf16[64,2560]{1,0:T(8,128)(2,1)S(1)} %pad_maximum_fusion.8), channel_id=1, source_target_pairs={{0,8},{4,12},{8,0},{12,4},{16,24},{20,28},{24,16},{28,20},{1,9},{5... | collective-permute-start | bytes 983048 | tf_op jit(solution)/shard_map/ppermute | solution.py:117
  491.9 3.2 collective-permute-start.31
  525.4 14.1 %collective-permute-start.33 = (bf16[512,512]{1,0:T(8,128)(2,1)}, bf16[512,512]{1,0:T(8,128)(2,1)S(1)}, u32[]{:S(2)}, u32[]{:S(2)}) collective-permute-start(bf16[512,512]{1,0:T(8,128)(2,1)} %get-tuple-element.164.own_ref), channel_id=1, source_target_pairs={{0,8},{4,12},{8,0},{12,4},{16,24},{20,28},{24,16},{28,20},{1,9},{5... | collective-permute-start | bytes 1572872 | tf_op jit(solution)/shard_map/ppermute | solution.py:117
  526.8 15.2 %collective-permute-start.32 = (bf16[512,512]{1,0:T(8,128)(2,1)}, bf16[512,512]{1,0:T(8,128)(2,1)}, u32[]{:S(2)}, u32[]{:S(2)}) collective-permute-start(bf16[512,512]{1,0:T(8,128)(2,1)} %get-tuple-element.164.own_ref), channel_id=1, source_target_pairs={{0,4},{4,0},{8,12},{12,8},{16,20},{20,16},{24,28},{28,24},{1,5},{5... | collective-permute-start | bytes 1572872 | tf_op jit(solution)/shard_map/ppermute | solution.py:117
  539.5 2.5 collective-permute-start.34
  (52 other events, 333.2 us)
Sparse Core Ops, SparseCore 0:
  35.0 45.9 all-gather.3
  157.8 45.0 all-gather.5
  279.7 148.3 all-reduce.9
